TPU v7x, 32 devices: a whole 2x2x4 slice. The times are simulated.
32 devices in a mesh: gx: 4 (over z), gy: 8 (over y, x, core).
Axes of the slice: x: 2, y: 2, z: 4, core: 2. Of those that a mesh axis runs over, the one named last changes fastest.
Arguments:
- multipoles: float32 [35, 131072], P(None, ('gx', 'gy')), may hold values from -6 to 6
- proxy_list: int32 [32, 8, 512], P(('gx', 'gy')), may hold values from 0 to 4095
- proxy_count: int32 [32, 8], P(('gx', 'gy')), may hold values from 1 to 512, as said below
- pair_source: int32 [2097152], P(('gx', 'gy')), may hold values from 0 to 9215
- pair_target: int32 [2097152], P(('gx', 'gy')), may hold values from 0 to 8191, as said below
- block_class: int32 [32768], P(('gx', 'gy')), may hold values from 0 to 188
- m2l_ops: float32 [189, 35, 35], replicated, may hold values from -1 to 1
- cell_mesh: int32 [131072], P(('gx', 'gy')), may hold values from 0 to 2097151
- pm_density: float32 [64, 1024, 1024], P('gy', None, 'gx'), may hold values from -6 to 6
Outputs:
- field_tensors: float32 [35, 131072], P(None, ('gx', 'gy'))
- pm_spectrum: float32 [2, 64, 1024, 1024], P(None, 'gy', 'gx')
Inputs may be any that keep to these rules, and one draw needn't show every extreme that they name: `proxy_count`: some neighbour slot of every domain holds all 512 slots live. `pair_target`: pairs are ordered by target: the pairs of block b of a domain target each column w * 64 to w * 64 + 63 exactly once, with w = (b * 128) // 1024.
All inputs are finite; a program needn't handle non-finite values.
Results may differ from a plain program's by a relative error of at most 0.000075.
Values sent between devices are 32-bit elements; how exact they have to be, the bound alone decides.
No kernel may reach another device: no remote copies, remote signals or barrier semaphores. Data moves between devices by JAX's collectives and lax.ppermute only.
A program may use at most 128 MiB of HBM per device.

v0:
```python
import jax
import jax.numpy as jnp
from jax import lax
from jax.sharding import PartitionSpec as P

TOP = 32
BLOCK = 64


DEPOSIT_SCALE = 8.0


def padded_2(cells, sides, width):
    for axis, dim in sides:
        count = lax.axis_size(axis)
        head = lax.slice_in_dim(cells, 0, width, axis=dim)
        tail = lax.slice_in_dim(cells, cells.shape[dim] - width, cells.shape[dim], axis=dim)
        cells = jnp.concatenate(
            [
                lax.ppermute(tail, axis, [(i, (i + 1) % count) for i in range(count)]),
                cells,
                lax.ppermute(head, axis, [((i + 1) % count, i) for i in range(count)]),
            ],
            axis=dim,
        )
    return cells


def fourier_rows(pencil_rows):
    length = pencil_rows.shape[-1]
    positions = jnp.arange(length, dtype=jnp.int32)
    product = positions[:, None] * positions[None, :] % length
    angles = product.astype(jnp.float32) * (2.0 * jnp.pi / length)
    scale = 1.0 / jnp.sqrt(jnp.float32(length))
    flat_rows = pencil_rows.reshape(-1, length)
    real_part = (
        jnp.dot(
            flat_rows,
            jnp.cos(angles),
            precision=lax.Precision.HIGHEST,
            preferred_element_type=jnp.float32,
        )
        * scale
    )
    imag_part = (
        -jnp.dot(
            flat_rows,
            jnp.sin(angles),
            precision=lax.Precision.HIGHEST,
            preferred_element_type=jnp.float32,
        )
        * scale
    )
    return jnp.stack([real_part, imag_part]).reshape((2,) + pencil_rows.shape)


def slots_to_grid(columns, slot_count):
    coef_count = columns.shape[0]
    shaped = columns.reshape(coef_count, 8, slot_count)
    middle = jnp.zeros((coef_count, 1, slot_count), columns.dtype)
    return jnp.concatenate([shaped[:, :4], middle, shaped[:, 4:]], axis=1).reshape(
        coef_count, 3, 3, slot_count
    )


def grid_to_slots(slot_grid):
    coef_count = slot_grid.shape[0]
    slot_count = slot_grid.shape[3]
    shaped = slot_grid.reshape(coef_count, 9, slot_count)
    return jnp.concatenate([shaped[:, :4], shaped[:, 5:]], axis=1).reshape(
        coef_count, 8 * slot_count
    )


def deliver(slot_grid):
    padded = padded_2(slot_grid, (("gx", 1), ("gy", 2)), 1)
    return padded[:, 0::2, 0::2]


def on_device(
    multipoles,
    proxy_list,
    proxy_count,
    pair_source,
    pair_target,
    block_class,
    m2l_ops,
    cell_mesh,
    pm_density,
):
    coef_count = multipoles.shape[0]
    cell_count = multipoles.shape[1]
    slot_count = proxy_list.shape[2]
    slot_ids = proxy_list[0].reshape(-1)
    live_mask = (
        (jnp.arange(slot_count, dtype=jnp.int32)[None, :] < proxy_count[0][:, None])
        .astype(jnp.float32)
        .reshape(-1)
    )
    outgoing = jnp.take(multipoles, slot_ids, axis=1) * live_mask[None, :]
    arrived = grid_to_slots(deliver(slots_to_grid(outgoing, slot_count)))
    top_table = lax.all_gather(multipoles[:, :TOP], ("gx", "gy"), axis=1, tiled=True)
    density = (
        pm_density.reshape(-1)
        .at[cell_mesh]
        .add(DEPOSIT_SCALE * multipoles[0])
        .reshape(pm_density.shape)
    )
    pencils_whole = lax.all_to_all(density, "gx", split_axis=1, concat_axis=2, tiled=True)
    pm_spectrum = fourier_rows(pencils_whole)
    table = jnp.concatenate([multipoles, arrived, top_table], axis=1)
    acc_columns = cell_count + 8 * slot_count
    window_total = acc_columns // BLOCK
    block_total = block_class.shape[0]
    pair_groups = 8
    group_sources = pair_source.reshape(pair_groups, -1)
    group_targets = pair_target.reshape(pair_groups, -1, BLOCK)
    group_classes = block_class.reshape(pair_groups, -1)
    group_blocks = jnp.arange(block_total, dtype=jnp.int32).reshape(pair_groups, -1)
    blocks_each = group_classes.shape[1]
    lanes = jnp.arange(BLOCK, dtype=jnp.int32)
    window_ids = jnp.arange(window_total, dtype=jnp.int32)

    def add_group(partial_sum, group):
        source_ids, target_ids, class_ids, block_ids = group
        gathered = jnp.take(table, source_ids, axis=1).reshape(coef_count, blocks_each, BLOCK)
        operators = jnp.take(m2l_ops, class_ids, axis=0)
        terms = jnp.einsum("bkj,jbi->kbi", operators, gathered, precision=lax.Precision.HIGHEST)
        windows = block_ids * window_total // block_total
        offsets = target_ids - windows[:, None] * BLOCK
        placing = (offsets[:, :, None] == lanes[None, None, :]).astype(jnp.float32)
        placed = jnp.einsum("kbi,bic->kbc", terms, placing, precision=lax.Precision.HIGHEST)
        membership = (window_ids[:, None] == windows[None, :]).astype(jnp.float32)
        summed = jnp.einsum("wb,kbc->kwc", membership, placed, precision=lax.Precision.HIGHEST)
        return (partial_sum + summed, None)

    initial = jnp.zeros((coef_count, window_total, BLOCK), jnp.float32)
    windowed, unused = lax.scan(
        add_group, initial, (group_sources, group_targets, group_classes, group_blocks)
    )
    accumulated = windowed.reshape(coef_count, acc_columns)
    slot_fields = (
        grid_to_slots(deliver(slots_to_grid(accumulated[:, cell_count:], slot_count)))
        * live_mask[None, :]
    )
    extra = jnp.zeros((coef_count, cell_count), jnp.float32).at[:, slot_ids].add(slot_fields)
    field_tensors = accumulated[:, :cell_count] + extra
    return (field_tensors, pm_spectrum)


def solution(mesh):
    placed = (
        P(None, ("gx", "gy")),
        P(("gx", "gy"), None, None),
        P(("gx", "gy"), None),
        P(("gx", "gy")),
        P(("gx", "gy")),
        P(("gx", "gy")),
        P(),
        P(("gx", "gy")),
        P("gy", None, "gx"),
    )
    return jax.shard_map(
        on_device,
        mesh=mesh,
        in_specs=placed,
        out_specs=(P(None, ("gx", "gy")), P(None, "gy", "gx", None)),
        check_vma=False,
    )
```

profile of v0, /device:TPU:8, one launch (start us, length us, event | category | flops | bytes accessed | tf_op | source)
XLA Modules:
  0.0 934.6 jit_solution(13194135016611925667)
XLA Ops:
  3.9 14.2 %gather_fusion.2 = f32[4096,35]{1,0:T(8,128)} fusion(f32[35,4096]{0,1:T(8,128)S(1)} %copy.134, s32[4096]{0:T(1024)S(1)} %broadcast_clamp_fusion.1), kind=kCustom, calls=%fused_computation.2 | custom fusion | bytes 1163264 | tf_op jit(solution)/shard_map/jit(_take)/gather | solution.py:100
  18.2 3.1 copy.135
  25.4 13.1 %copy.179 = f32[1024,2,8,128]{3,1,2,0:T(2,128)} copy(f32[1024,2,8,128]{3,2,1,0:T(8,128)} %bitcast.126) | data formatting | bytes 16777216
  43.6 26.8 %scatter_fusion.1 = f32[2097152]{0:T(1024)} fusion(f32[2097152]{0:T(1024)} %bitcast.117, s32[4096]{0:T(1024)S(1)} %compare_select_fusion.11, f32[4096]{0:T(1024)S(1)} %bitcast.142), kind=kCustom, calls=%fused_computation.4 | custom fusion | flops 4096 | bytes 65536 | tf_op jit(solution)/shard_map/scatter-add | solution.py:106
  70.4 9.9 %reshape.291 = f32[8,1024,256]{2,1,0:T(8,128)} reshape(f32[2097152]{0:T(1024)} %scatter_fusion.1) | data formatting | bytes 16777216 | tf_op jit(solution)/shard_map/reshape | solution.py:107
  80.2 11.6 %copy.164 = f32[8,1024,256]{2,0,1:T(8,128)} copy(f32[8,1024,256]{2,1,0:T(8,128)} %reshape.291) | data formatting | bytes 16777216 | tf_op jit(solution)/shard_map/reshape | solution.py:107
  91.9 8.4 all-to-all-start
  104.0 204.1 %all_gather.3 = f32[35,1024]{0,1:T(8,128)S(1)} all-gather(f32[35,32]{0,1:T(8,128)S(1)} %slice.100), channel_id=1, replica_groups=mesh['gx'=4,'gy'=8] {'gx','gy'}, dimensions={1}, use_global_device_ids=true | all-gather | bytes 147840 | tf_op jit(solution)/shard_map/all_gather | solution.py:102
  308.9 5.0 copy.149
  317.4 3.1 copy.148
  320.5 454.9 %while.13 = (s32[]{:T(128)}, f32[35,128,64]{1,2,0:T(8,128)}, s32[8,128,64]{2,1,0:T(8,128)}, s32[8,128]{1,0:T(8,128)S(1)}, s32[8,8192]{1,0:T(8,128)}, /*index=5*/...) while((s32[]{:T(128)}, f32[35,128,64]{1,2,0:T(8,128)}, ...), condition=%wide.region_1.2_spmd.clone, body=%wide.region_0.1_spmd.clone.sunk | while | flops 782679424 | bytes 24124876 | solution.py:138
  325.1 4.3 gather_fusion
  329.4 30.1 %gather_fusion.1 = f32[8192,35]{1,0:T(8,128)} fusion(f32[35,9216]{0,1:T(8,128)} %get-tuple-element.333, s32[8192]{0:T(1024)S(1)} %broadcast_clamp_fusion.3), kind=kCustom, calls=%fused_computation.clone.clone.1 | custom fusion | bytes 2326528 | tf_op jit(solution)/shard_map/while/body/eval_jaxpr/jit(_take)/gather | solution.py:126
  359.5 4.1 copy.190
  363.6 6.4 fusion.89
  369.9 4.2 fusion.91
  374.1 2.2 fusion.93
  381.9 4.3 gather_fusion
  386.3 30.1 %gather_fusion.1 = f32[8192,35]{1,0:T(8,128)} fusion(f32[35,9216]{0,1:T(8,128)} %get-tuple-element.333, s32[8192]{0:T(1024)S(1)} %broadcast_clamp_fusion.3), kind=kCustom, calls=%fused_computation.clone.clone.1 | custom fusion | bytes 2326528 | tf_op jit(solution)/shard_map/while/body/eval_jaxpr/jit(_take)/gather | solution.py:126
  416.4 4.1 copy.190
  420.4 6.4 fusion.89
  426.8 4.2 fusion.91
  438.8 4.3 gather_fusion
  443.1 30.1 %gather_fusion.1 = f32[8192,35]{1,0:T(8,128)} fusion(f32[35,9216]{0,1:T(8,128)} %get-tuple-element.333, s32[8192]{0:T(1024)S(1)} %broadcast_clamp_fusion.3), kind=kCustom, calls=%fused_computation.clone.clone.1 | custom fusion | bytes 2326528 | tf_op jit(solution)/shard_map/while/body/eval_jaxpr/jit(_take)/gather | solution.py:126
  473.2 4.1 copy.190
  477.3 6.4 fusion.89
  483.7 4.2 fusion.91
  495.7 4.3 gather_fusion
  500.0 30.1 %gather_fusion.1 = f32[8192,35]{1,0:T(8,128)} fusion(f32[35,9216]{0,1:T(8,128)} %get-tuple-element.333, s32[8192]{0:T(1024)S(1)} %broadcast_clamp_fusion.3), kind=kCustom, calls=%fused_computation.clone.clone.1 | custom fusion | bytes 2326528 | tf_op jit(solution)/shard_map/while/body/eval_jaxpr/jit(_take)/gather | solution.py:126
  530.1 4.1 copy.190
  534.2 6.4 fusion.89
  540.5 4.2 fusion.91
  552.5 4.3 gather_fusion
  556.9 30.1 %gather_fusion.1 = f32[8192,35]{1,0:T(8,128)} fusion(f32[35,9216]{0,1:T(8,128)} %get-tuple-element.333, s32[8192]{0:T(1024)S(1)} %broadcast_clamp_fusion.3), kind=kCustom, calls=%fused_computation.clone.clone.1 | custom fusion | bytes 2326528 | tf_op jit(solution)/shard_map/while/body/eval_jaxpr/jit(_take)/gather | solution.py:126
  587.0 4.1 copy.190
  591.0 6.4 fusion.89
  597.4 4.2 fusion.91
  609.4 4.3 gather_fusion
  613.7 30.1 %gather_fusion.1 = f32[8192,35]{1,0:T(8,128)} fusion(f32[35,9216]{0,1:T(8,128)} %get-tuple-element.333, s32[8192]{0:T(1024)S(1)} %broadcast_clamp_fusion.3), kind=kCustom, calls=%fused_computation.clone.clone.1 | custom fusion | bytes 2326528 | tf_op jit(solution)/shard_map/while/body/eval_jaxpr/jit(_take)/gather | solution.py:126
  643.8 4.1 copy.190
  647.9 6.4 fusion.89
  654.3 4.2 fusion.91
  666.2 4.3 gather_fusion
  670.6 30.1 %gather_fusion.1 = f32[8192,35]{1,0:T(8,128)} fusion(f32[35,9216]{0,1:T(8,128)} %get-tuple-element.333, s32[8192]{0:T(1024)S(1)} %broadcast_clamp_fusion.3), kind=kCustom, calls=%fused_computation.clone.clone.1 | custom fusion | bytes 2326528 | tf_op jit(solution)/shard_map/while/body/eval_jaxpr/jit(_take)/gather | solution.py:126
  700.7 4.1 copy.190
  704.7 6.4 fusion.89
  711.1 4.2 fusion.91
  715.3 2.2 fusion.93
  723.1 4.3 gather_fusion
  727.5 30.1 %gather_fusion.1 = f32[8192,35]{1,0:T(8,128)} fusion(f32[35,9216]{0,1:T(8,128)} %get-tuple-element.333, s32[8192]{0:T(1024)S(1)} %broadcast_clamp_fusion.3), kind=kCustom, calls=%fused_computation.clone.clone.1 | custom fusion | bytes 2326528 | tf_op jit(solution)/shard_map/while/body/eval_jaxpr/jit(_take)/gather | solution.py:126
  757.6 4.1 copy.190
  761.6 6.4 fusion.89
  768.0 4.2 fusion.91
  775.4 5.7 copy.150
  781.1 2.5 fusion.53
  789.6 2.5 collective-permute-start.4
  792.1 16.2 %fusion.70 = f32[1024,1024]{1,0:T(8,128)} fusion(), kind=kLoop, calls=%fused_computation.62.clone.1 | loop fusion | flops 14680064 | bytes 4194304 | tf_op jit(solution)/shard_map/dot_general | solution.py:37
  809.8 16.3 %fusion.68 = f32[1024,1024]{1,0:T(8,128)} fusion(), kind=kLoop, calls=%fused_computation.61.clone.1 | loop fusion | flops 14680064 | bytes 4194304 | tf_op jit(solution)/shard_map/dot_general | solution.py:46
  829.6 23.4 %scatter_fusion = f32[35,4096]{0,1:T(8,128)S(1)} fusion(f32[35,4096]{0,1:T(8,128)S(1)} %get-tuple-element.239, s32[4096]{0:T(1024)S(1)} %bitcast.141, f32[4096,35]{1,0:T(8,128)} %copy.163), kind=kCustom, calls=%fused_computation.3 | custom fusion | flops 143360 | bytes 1736704 | tf_op jit(solution)/shard_map/scatter-add | solution.py:146
  854.5 10.6 %copy.166 = f32[8,256,4,256]{1,0,3,2:T(8,128)} copy(f32[8,256,4,256]{3,0,1,2:T(8,128)} %bitcast.16) | data formatting | bytes 16777216 | tf_op jit(solution)/shard_map/all_to_all | solution.py:109
  865.1 7.7 copy.180
  872.8 27.3 %negate_multiply_fusion = f32[2048,1024]{1,0:T(8,128)S(1)} fusion(f32[2048,1024]{0,1:T(8,128)S(1)} %bitcast.127, f32[1024,1024]{1,0:T(8,128)S(1)} %copy-done.3), kind=kOutput, calls=%fused_computation.53 | convolution fusion | flops 25773998080 | bytes 20971520 | tf_op jit(solution)/shard_map/dot_general | solution.py:46
  900.1 27.7 %convolution_multiply_fusion = f32[2048,1024]{1,0:T(8,128)S(1)} fusion(f32[2048,1024]{0,1:T(8,128)S(1)} %bitcast.128, f32[1024,1024]{1,0:T(8,128)S(1)} %copy-done.2), kind=kOutput, calls=%fused_computation.57 | convolution fusion | flops 25771900928 | bytes 20971520 | tf_op jit(solution)/shard_map/dot_general | solution.py:37
  927.8 6.4 pad_maximum_fusion
  (226 shorter events, 90.1 us)
Async XLA Ops:
  18.2 7.2 copy-start.4
  22.6 0.7 copy-start.11
  23.0 15.5 %collective-permute-start.1 = (f32[35,1,3,512]{3,1,2,0:T(1,128)S(1)}, f32[35,1,3,512]{3,1,2,0:T(1,128)S(1)}, u32[]{:S(2)}, u32[]{:S(2)}) collective-permute-start(f32[35,1,3,512]{3,1,2,0:T(1,128)S(1)} %copy.137), channel_id=1, source_target_pairs={{8,0},{16,8},{24,16},{0,24},{9,1},{17,9},{25,17},{1,25},{10,2},{18... | collective-permute-start | bytes 645128 | tf_op jit(solution)/shard_map/ppermute | solution.py:22
  23.3 15.3 %collective-permute-start = (f32[35,1,3,512]{3,1,2,0:T(1,128)S(1)}, f32[35,1,3,512]{3,1,2,0:T(1,128)S(1)}, u32[]{:S(2)}, u32[]{:S(2)}) collective-permute-start(f32[35,1,3,512]{3,1,2,0:T(1,128)S(1)} %copy.136), channel_id=1, source_target_pairs={{0,8},{8,16},{16,24},{24,0},{1,9},{9,17},{17,25},{25,1},{2,10},{10... | collective-permute-start | bytes 645128 | tf_op jit(solution)/shard_map/ppermute | solution.py:20
  38.5 5.0 copy-start.10
  38.5 0.7 copy-start.5
  39.2 0.7 copy-start.7
  42.2 271.7 %collective-permute-start.3 = (f32[35,5,1,512]{3,2,1,0:T(1,128)}, f32[35,5,1,512]{3,2,1,0:T(1,128)}, u32[]{:S(2)}, u32[]{:S(2)}) collective-permute-start(f32[35,5,1,512]{3,2,1,0:T(1,128)} %copy.141), channel_id=1, source_target_pairs={{1,0},{2,1},{3,2},{4,3},{5,4},{6,5},{7,6},{0,7},{9,8},{10,9},{11,1... | collective-permute-start | bytes 1075208 | tf_op jit(solution)/shard_map/ppermute | solution.py:22
  43.5 271.4 %collective-permute-start.2 = (f32[35,5,1,512]{3,2,1,0:T(1,128)}, f32[35,5,1,512]{3,2,1,0:T(1,128)}, u32[]{:S(2)}, u32[]{:S(2)}) collective-permute-start(f32[35,5,1,512]{3,2,1,0:T(1,128)} %copy.140), channel_id=1, source_target_pairs={{0,1},{1,2},{2,3},{3,4},{4,5},{5,6},{6,7},{7,0},{8,9},{9,10},{10,1... | collective-permute-start | bytes 1075208 | tf_op jit(solution)/shard_map/ppermute | solution.py:20
  91.9 762.6 %all-to-all-start = ((f32[8,1024,256]{2,0,1:T(8,128)}), f32[8,1024,256]{2,0,1:T(8,128)}, u32[]{:S(2)}, u32[]{:S(2)}) async-start(f32[8,1024,256]{2,0,1:T(8,128)} %copy.164), calls=%async_computation | async-start | bytes 16777216 | tf_op jit(solution)/shard_map/all_to_all | solution.py:109
  103.9 212.0 %copy-start.6 = (f32[35,1,3,512]{3,0,2,1:T(8,128)S(1)}, f32[35,1,3,512]{3,0,2,1:T(8,128)}, u32[]{:S(2)}) copy-start(f32[35,1,3,512]{3,0,2,1:T(8,128)} %copy-done.5) | copy-start | bytes 645124
  103.9 212.0 %copy-start.8 = (f32[35,1,3,512]{3,0,2,1:T(8,128)S(1)}, f32[35,1,3,512]{3,0,2,1:T(8,128)}, u32[]{:S(2)}) copy-start(f32[35,1,3,512]{3,0,2,1:T(8,128)} %copy-done.7) | copy-start | bytes 645124
  316.2 1.1 copy-start.9
  369.9 4.2 copy-start
  376.3 1.0 copy-start.1
  426.8 4.2 copy-start
  433.2 1.0 copy-start.1
  483.7 4.2 copy-start
  490.1 1.0 copy-start.1
  540.5 4.2 copy-start
  546.9 1.0 copy-start.1
  597.4 4.2 copy-start
  603.8 1.0 copy-start.1
  654.3 4.2 copy-start
  660.7 1.0 copy-start.1
  711.1 4.2 copy-start
  717.5 1.0 copy-start.1
  768.0 4.2 copy-start
  774.4 1.0 copy-start.1
  783.6 3.9 copy-start.12
  789.1 19.2 %collective-permute-start.5 = (f32[35,1,3,512]{3,1,2,0:T(1,128)S(1)}, f32[35,1,3,512]{3,1,2,0:T(1,128)S(1)}, u32[]{:S(2)}, u32[]{:S(2)}) collective-permute-start(f32[35,1,3,512]{3,1,2,0:T(1,128)S(1)} %copy.154), channel_id=1, source_target_pairs={{8,0},{16,8},{24,16},{0,24},{9,1},{17,9},{25,17},{1,25},{10,2},{18... | collective-permute-start | bytes 645128 | tf_op jit(solution)/shard_map/ppermute | solution.py:22
  789.6 18.7 %collective-permute-start.4 = (f32[35,1,3,512]{3,1,2,0:T(1,128)S(1)}, f32[35,1,3,512]{3,1,2,0:T(1,128)S(1)}, u32[]{:S(2)}, u32[]{:S(2)}) collective-permute-start(f32[35,1,3,512]{3,1,2,0:T(1,128)S(1)} %copy.153), channel_id=1, source_target_pairs={{0,8},{8,16},{16,24},{24,0},{1,9},{9,17},{17,25},{25,1},{2,10},{10... | collective-permute-start | bytes 645128 | tf_op jit(solution)/shard_map/ppermute | solution.py:20
  809.2 16.9 %collective-permute-start.7 = (f32[35,5,1,512]{3,2,1,0:T(1,128)S(1)}, f32[35,5,1,512]{3,2,1,0:T(1,128)S(1)}, u32[]{:S(2)}, u32[]{:S(2)}) collective-permute-start(f32[35,5,1,512]{3,2,1,0:T(1,128)S(1)} %copy.158), channel_id=1, source_target_pairs={{1,0},{2,1},{3,2},{4,3},{5,4},{6,5},{7,6},{0,7},{9,8},{10,9},{11,1... | collective-permute-start | bytes 1075208 | tf_op jit(solution)/shard_map/ppermute | solution.py:22
  809.3 16.9 %collective-permute-start.6 = (f32[35,5,1,512]{3,2,1,0:T(1,128)S(1)}, f32[35,5,1,512]{3,2,1,0:T(1,128)S(1)}, u32[]{:S(2)}, u32[]{:S(2)}) collective-permute-start(f32[35,5,1,512]{3,2,1,0:T(1,128)S(1)} %copy.157), channel_id=1, source_target_pairs={{0,1},{1,2},{2,3},{3,4},{4,5},{5,6},{6,7},{7,0},{8,9},{9,10},{10,1... | collective-permute-start | bytes 1075208 | tf_op jit(solution)/shard_map/ppermute | solution.py:20
  865.1 7.7 copy-start.3
  872.8 27.3 %copy-start.2 = (f32[1024,1024]{1,0:T(8,128)S(1)}, f32[1024,1024]{1,0:T(8,128)}, u32[]{:S(2)}) copy-start(f32[1024,1024]{1,0:T(8,128)} %fusion.70) | copy-start | bytes 12582916
where the time goes:
time: 948 us; the launch traced here: 935 us
  local copies, waits for them, and re-layouts  435 us (46%)
  blocking collectives  204 us (22%)
  matrix products  157 us (17%)
  other arithmetic  121 us (13%)
  starting transfers between devices  15.4 us (2%)
    gather x16, local copies, waits for them, and re-layouts, add_group(): jnp.take(table, source_ids, axis=1).reshape(coef_count, blocks_each, BLOCK)  273 us
    all_gather x1, blocking collectives, on_device(): lax.all_gather(multipoles[:, :TOP], ('gx', 'gy'), axis=1, tiled=True)  204 us
    dot_general x8, matrix products, add_group(): jnp.einsum('bkj,jbi->kbi', operators, gathered, precision=lax.Precision.H...  51 us
    unnamed x40, local copies, waits for them, and re-layouts  38.4 us
    gather x8, local copies, waits for them, and re-layouts, add_group(): operators = jnp.take(m2l_ops, class_ids, axis=0)  34.7 us
    dot_general x8, matrix products, add_group(): jnp.einsum('kbi,bic->kbc', terms, placing, precision=lax.Precision.HIGHEST)  33.3 us
    dot_general x1, matrix products, fourier_rows(): jnp.dot(flat_rows, jnp.cos(angles), precision=lax.Precision.HIGHEST, pref...  27.7 us
    dot_general x1, matrix products, fourier_rows(): jnp.dot(flat_rows, jnp.sin(angles), precision=lax.Precision.HIGHEST, pref...  27.3 us
  transfers between devices with their start and end apart: 9, of which 0 were waited for; matrix products, arithmetic and copies ran while one was open for 64% of the time, Pallas kernels for 0%

commit v1 on v0

v1 whole, which is shorter than its diff:
```python
import functools

import jax
import jax.numpy as jnp
import ml_dtypes
import numpy as np
from jax import lax
from jax.experimental import pallas as pl
from jax.experimental.pallas import tpu as pltpu
from jax.sharding import PartitionSpec as P

TOP = 32
BLOCK = 64
LANES = 128
KPAD = 40
COPIES = 3
PER_WINDOW = 8
VMEM_BYTES = 48 * 1024 * 1024
CHUNKS = (2, 2, 2, 2)

DEPOSIT_SCALE = 8.0
OFFSETS = tuple((a, b) for a in (-1, 0, 1) for b in (-1, 0, 1) if (a, b) != (0, 0))

SMEM_WHOLE = pl.BlockSpec(memory_space=pltpu.SMEM)
VMEM_WHOLE = pl.BlockSpec(memory_space=pltpu.VMEM)


def params():
    return pltpu.CompilerParams(vmem_limit_bytes=VMEM_BYTES)


def cost(flops, nbytes):
    return pl.CostEstimate(flops=flops, bytes_accessed=nbytes, transcendentals=0)


def spread(block):
    rest = jnp.zeros((LANES - COPIES * KPAD, LANES), jnp.float32)
    return jnp.concatenate([block] * COPIES + [rest], axis=0).T


def lane_ids(shape):
    return lax.broadcasted_iota(jnp.int32, shape, len(shape) - 1)


def pack_kernel(list_ref, count_ref, cells_ref, out_ref, top_ref, table, rows):
    tiles = cells_ref.shape[1] // LANES

    @pl.loop(0, tiles)
    def _(k):
        at = pl.multiple_of(k * LANES, LANES)
        table[pl.ds(at, LANES), :] = spread(cells_ref[:, pl.ds(at, LANES)])

    top_ref[...] = table[:TOP, :]
    slot_tiles = list_ref.shape[1] // LANES

    @pl.loop(0, 8 * slot_tiles)
    def _(i):
        n = i // slot_tiles
        first = pl.multiple_of((i % slot_tiles) * LANES, LANES)
        for r in range(LANES):
            rows[pl.ds(r, 1), :] = table[pl.ds(list_ref[n, first + r], 1), :]
        live = (lane_ids((KPAD, LANES)) + first) < count_ref[n]
        out_ref[n, :, pl.ds(first, LANES)] = jnp.where(live, rows[...].T[:KPAD], 0.0)


def pack(cells, proxy_list, proxy_count):
    slots = proxy_list.shape[1]
    return pl.pallas_call(
        pack_kernel,
        out_shape=(
            jax.ShapeDtypeStruct((8, KPAD, slots), jnp.float32),
            jax.ShapeDtypeStruct((TOP, LANES), jnp.float32),
        ),
        in_specs=[SMEM_WHOLE, SMEM_WHOLE, VMEM_WHOLE],
        out_specs=(VMEM_WHOLE, VMEM_WHOLE),
        scratch_shapes=[
            pltpu.VMEM((cells.shape[1], LANES), jnp.float32),
            pltpu.VMEM((LANES, LANES), jnp.float32),
        ],
        compiler_params=params(),
        cost_estimate=cost(10**6, 16 * 10**6),
        name="pack",
    )(proxy_list, proxy_count, cells)


def exchange(blocks, n_gx, n_gy):
    arrived = [None] * 8
    for m, (a, b) in enumerate(OFFSETS):
        pairs = [
            (x * n_gy + y, (x + a) % n_gx * n_gy + (y + b) % n_gy)
            for x in range(n_gx)
            for y in range(n_gy)
        ]
        arrived[7 - m] = lax.ppermute(blocks[m], ("gx", "gy"), pairs)
    return arrived


def order_kernel(packed_ref, out_ref):
    lanes = lane_ids((LANES, LANES))
    within = lanes % BLOCK
    base = lanes - within

    @pl.loop(0, packed_ref.shape[0] // LANES)
    def _(k):
        at = pl.ds(pl.multiple_of(k * LANES, LANES), LANES)
        packed = packed_ref[at, :]

        def step(i, ordered):
            value = jnp.take_along_axis(packed, base + i, axis=1, mode="promise_in_bounds")
            return jnp.where(value % BLOCK == within, value // BLOCK, ordered)

        out_ref[at, :] = lax.fori_loop(0, BLOCK, step, jnp.zeros_like(packed), unroll=8)


def order(packed):
    return pl.pallas_call(
        order_kernel,
        out_shape=jax.ShapeDtypeStruct(packed.shape, jnp.int32),
        in_specs=[VMEM_WHOLE],
        out_specs=VMEM_WHOLE,
        compiler_params=params(),
        cost_estimate=cost(10**6, 16 * 10**6),
        name="order",
    )(packed)


def table_kernel(*refs):
    cells_ref, top_ref, out_ref = refs[0], refs[9], refs[10]
    cell_count = cells_ref.shape[1]

    @pl.loop(0, cell_count // LANES)
    def _(k):
        at = pl.multiple_of(k * LANES, LANES)
        out_ref[pl.ds(at, LANES), :] = spread(cells_ref[:, pl.ds(at, LANES)])

    for n in range(8):
        slots = refs[1 + n].shape[1]
        for k in range(slots // LANES):
            at = cell_count + n * slots + k * LANES
            out_ref[at : at + LANES, :] = spread(refs[1 + n][:, k * LANES : (k + 1) * LANES])
    out_ref[cell_count + 8 * refs[1].shape[1] :, :] = top_ref[...]


def make_table(cells, arrived, top_rows):
    rows = cells.shape[1] + 8 * arrived[0].shape[1] + top_rows.shape[0]
    return pl.pallas_call(
        table_kernel,
        out_shape=jax.ShapeDtypeStruct((rows, LANES), jnp.float32),
        in_specs=[VMEM_WHOLE] * 10,
        out_specs=VMEM_WHOLE,
        compiler_params=params(),
        cost_estimate=cost(10**6, 16 * 10**6),
        name="table",
    )(cells, *arrived, top_rows)


def m2l_kernel(source_ref, class_ref, table_ref, ops_ref, out_ref, gathered, *, turned):
    step = pl.program_id(0)
    lanes = lane_ids((1, LANES))
    in_first = lanes < KPAD
    in_second = lanes < 2 * KPAD

    def row(b, t):
        return table_ref[pl.ds(source_ref[b // 2, (b % 2) * BLOCK + t], 1), :]

    for u in range(2):

        @pl.loop(0, BLOCK, step=8)
        def _(first):
            for t in range(8):
                for g in range(3):
                    b = u * PER_WINDOW + 3 * g
                    one, two = row(b, first + t), row(b + 1, first + t)
                    three = row(b + 2, first + t) if g < 2 else two
                    gathered[g, pl.ds(u * BLOCK + first + t, 1), :] = jnp.where(
                        in_first, one, jnp.where(in_second, two, three)
                    )

    rest = jnp.zeros((LANES - COPIES * KPAD, LANES), jnp.float32)
    none = jnp.zeros((KPAD, LANES), jnp.float32)
    results = []
    for u in range(2):
        total = jnp.zeros((BLOCK, LANES), jnp.float32)
        for g in range(3):
            held = []
            for s in range(3):
                b = 3 * g + s
                if b < PER_WINDOW:
                    held.append(ops_ref[class_ref[step * 2 * PER_WINDOW + u * PER_WINDOW + b]])
                else:
                    held.append(none)
            weights = jnp.concatenate(held + [rest], axis=0).astype(jnp.bfloat16)
            values = gathered[g, u * BLOCK : (u + 1) * BLOCK, :]
            high = values.astype(jnp.bfloat16)
            low = (values - high.astype(jnp.float32)).astype(jnp.bfloat16)
            total += jnp.dot(high, weights, preferred_element_type=jnp.float32)
            total += jnp.dot(low, weights, preferred_element_type=jnp.float32)
        results.append(total)
    both = jnp.concatenate(results, axis=0)
    both = both + pltpu.roll(both, LANES - KPAD, 1)
    if turned:
        out_ref[0] = both.T[:KPAD]
    else:
        out_ref[...] = both


def m2l(sources, classes, table, ops, turned, slots):
    steps = classes.shape[0] // (2 * PER_WINDOW)
    if turned:
        per = slots // LANES
        shape = (steps // per, KPAD, slots)
        out_spec = pl.BlockSpec((1, KPAD, LANES), lambda i: (i // per, 0, i % per))
    else:
        shape = (steps * LANES, LANES)
        out_spec = pl.BlockSpec((LANES, LANES), lambda i: (i, 0))
    return pl.pallas_call(
        functools.partial(m2l_kernel, turned=turned),
        grid=(steps,),
        out_shape=jax.ShapeDtypeStruct(shape, jnp.float32),
        in_specs=[
            pl.BlockSpec((8, LANES), lambda i: (i, 0), memory_space=pltpu.SMEM),
            SMEM_WHOLE,
            VMEM_WHOLE,
            VMEM_WHOLE,
        ],
        out_specs=out_spec,
        scratch_shapes=[pltpu.VMEM((3, LANES, LANES), jnp.float32)],
        compiler_params=params(),
        cost_estimate=cost(10**6, 100 * 10**6),
        name="m2l_slots" if turned else "m2l_cells",
    )(sources, classes, table, ops)


def add_back_kernel(list_ref, count_ref, own_ref, *refs):
    slot_refs, out_ref = refs[:8], refs[8]
    rows, sums = refs[9], refs[10:]
    slots = list_ref.shape[1]
    sums[0][...] = own_ref[...]
    for held in sums[1:]:
        held[...] = jnp.zeros_like(held)
    for n in range(8):
        for k in range(slots // LANES):
            live = (lane_ids((KPAD, LANES)) + k * LANES) < count_ref[n]
            values = jnp.where(live, slot_refs[n][:, k * LANES : (k + 1) * LANES], 0.0)
            at = n * slots + k * LANES
            rows[at : at + LANES, :] = spread(values)
    for half in range(2):

        @pl.loop(0, slots, step=4)
        def _(first):
            for j in range(4):
                for s, held in enumerate(sums):
                    n = 4 * half + s
                    to = pl.ds(list_ref[n, first + j], 1)
                    held[to, :] = held[to, :] + rows[pl.ds(n * slots + first + j, 1), :]

    @pl.loop(0, own_ref.shape[0] // LANES)
    def _(k):
        at = pl.ds(pl.multiple_of(k * LANES, LANES), LANES)
        total = (sums[0][at, :] + sums[1][at, :]) + (sums[2][at, :] + sums[3][at, :])
        out_ref[:, at] = total.T[: out_ref.shape[0]]


def add_back(proxy_list, proxy_count, own_rows, slot_fields, coef_count):
    cell_count = own_rows.shape[0]
    slots = proxy_list.shape[1]
    return pl.pallas_call(
        add_back_kernel,
        out_shape=jax.ShapeDtypeStruct((coef_count, cell_count), jnp.float32),
        in_specs=[SMEM_WHOLE, SMEM_WHOLE] + [VMEM_WHOLE] * 9,
        out_specs=VMEM_WHOLE,
        scratch_shapes=[pltpu.VMEM((8 * slots, LANES), jnp.float32)]
        + [pltpu.VMEM((cell_count, LANES), jnp.float32)] * 4,
        compiler_params=params(),
        cost_estimate=cost(10**6, 30 * 10**6),
        name="add_back",
    )(proxy_list, proxy_count, own_rows, *slot_fields)


def deposit_kernel(code_ref, value_ref, *outs):
    lanes = lane_ids((1, LANES))
    for out_ref in outs:
        out_ref[...] = jnp.zeros_like(out_ref)

    @pl.loop(0, code_ref.shape[1], step=4)
    def _(first):
        for j in range(4):
            for s, out_ref in enumerate(outs):
                code = code_ref[s, first + j]
                to = pl.ds(code // LANES, 1)
                value = jnp.where(lanes == code % LANES, value_ref[s, first + j], 0.0)
                out_ref[to, :] = out_ref[to, :] + value


def deposit(codes, values, rows):
    sources = codes.shape[0]
    return pl.pallas_call(
        deposit_kernel,
        out_shape=(jax.ShapeDtypeStruct((rows, LANES), jnp.float32),) * sources,
        in_specs=[SMEM_WHOLE, SMEM_WHOLE],
        out_specs=(VMEM_WHOLE,) * sources,
        compiler_params=params(),
        cost_estimate=cost(10**6, 100 * 10**6),
        name="deposit",
    )(codes, values)


def fourier_tables(length):
    positions = np.arange(length)
    angles = (positions[:, None] * positions[None, : length // 2] % length) * (2.0 * np.pi / length)
    scale = 1.0 / np.sqrt(length)
    imag = -np.sin(angles) * scale
    imag[:, 0] = np.where(positions % 2 == 0, scale, -scale)
    whole = np.concatenate([np.cos(angles) * scale, imag], axis=1)
    high = whole.astype(ml_dtypes.bfloat16)
    low = (whole - high.astype(np.float64)).astype(ml_dtypes.bfloat16)
    return high, low


def fourier_kernel(*refs, sources, linked):
    mesh_ref, add_refs = refs[0], refs[1 : 1 + sources]
    high_ref, low_ref = refs[1 + sources], refs[2 + sources]
    out_ref = refs[-1]
    rows = mesh_ref.shape[2]
    width = mesh_ref.shape[3]
    pieces = []
    for s in range(sources):
        for h in range(width // LANES):
            pieces.append(
                mesh_ref[s, 0, :, h * LANES : (h + 1) * LANES]
                + add_refs[s][h * rows : (h + 1) * rows, :]
            )
    values = jnp.concatenate(pieces, axis=1)
    length = values.shape[1]
    high = values.astype(jnp.bfloat16)
    low = (values - high.astype(jnp.float32)).astype(jnp.bfloat16)
    half = jnp.dot(high, high_ref[...], preferred_element_type=jnp.float32)
    half += jnp.dot(low, high_ref[...], preferred_element_type=jnp.float32)
    half += jnp.dot(high, low_ref[...], preferred_element_type=jnp.float32)
    lanes = lane_ids((rows, LANES))
    is_first = lanes == 0
    mirror = (LANES - lanes) % LANES
    tiles = length // LANES
    per = tiles // 2

    def tile(part, j):
        at = (part * per + j) * LANES
        return half[:, at : at + LANES]

    for j in range(per):
        real, imag = tile(0, j), tile(1, j)
        if j == 0:
            imag = jnp.where(is_first, 0.0, imag)
        out_ref[0, 0, :, j * LANES : (j + 1) * LANES] = real
        out_ref[1, 0, :, j * LANES : (j + 1) * LANES] = imag
    for j in range(per, tiles):
        back = tiles - 1 - j
        real = jnp.take_along_axis(tile(0, back), mirror, axis=1, mode="promise_in_bounds")
        imag = -jnp.take_along_axis(tile(1, back), mirror, axis=1, mode="promise_in_bounds")
        if j == per:
            real = jnp.where(is_first, tile(1, 0), real)
            imag = jnp.where(is_first, 0.0, imag)
        else:
            real = jnp.where(is_first, tile(0, back + 1), real)
            imag = jnp.where(is_first, -tile(1, back + 1), imag)
        out_ref[0, 0, :, j * LANES : (j + 1) * LANES] = real
        out_ref[1, 0, :, j * LANES : (j + 1) * LANES] = imag


def fourier(mesh_part, adds, tables, first, planes, so_far):
    sources, count, rows, width = mesh_part.shape
    length = sources * width
    add_rows = (width // LANES) * rows
    operands = [mesh_part, *adds, *tables]
    in_specs = (
        [pl.BlockSpec((sources, 1, rows, width), lambda p: (0, p, 0, 0))]
        + [pl.BlockSpec((add_rows, LANES), lambda p: (first + p, 0))] * sources
        + [pl.BlockSpec((length, length), lambda p: (0, 0), pipeline_mode=pl.Buffered(1))] * 2
    )
    aliases = {}
    if so_far is not None:
        aliases = {len(operands): 0}
        operands.append(so_far)
        in_specs.append(pl.BlockSpec(memory_space=pl.ANY))
    return pl.pallas_call(
        functools.partial(fourier_kernel, sources=sources, linked=so_far is not None),
        grid=(count,),
        out_shape=jax.ShapeDtypeStruct((2, planes, rows, length), jnp.float32),
        in_specs=in_specs,
        out_specs=pl.BlockSpec((2, 1, rows, length), lambda p: (0, first + p, 0, 0)),
        input_output_aliases=aliases,
        compiler_params=params(),
        cost_estimate=cost(2 * count * rows * length * length * 3, count * rows * length * 16 + 4 * length * length),
        name="fourier",
    )(*operands)


def on_device(
    multipoles,
    proxy_list,
    proxy_count,
    pair_source,
    pair_target,
    block_class,
    m2l_ops,
    cell_mesh,
    pm_density,
    *,
    n_gx,
    n_gy,
):
    coef_count, cell_count = multipoles.shape
    slots = proxy_list.shape[2]
    planes, mesh_rows, width = pm_density.shape
    own_rows = mesh_rows // n_gx
    lists, counts = proxy_list[0], proxy_count[0]

    spans = []
    first = 0
    for size in CHUNKS:
        spans.append((first, size))
        first += size

    def send(span):
        part = pm_density[span[0] : span[0] + span[1]]
        part = part.reshape(span[1], n_gx, own_rows, width).transpose(1, 0, 2, 3)
        return lax.all_to_all(part, "gx", 0, 0, tiled=True)

    cells = jnp.pad(multipoles, ((0, KPAD - coef_count), (0, 0)))
    outgoing, top_own = pack(cells, lists, counts)
    arrived = exchange(outgoing, n_gx, n_gy)
    top_rows = lax.all_gather(top_own, ("gx", "gy"), axis=0, tiled=True)

    held = jnp.stack(
        [cell_mesh.astype(jnp.float32), DEPOSIT_SCALE * multipoles[0]]
    ).reshape(2, cell_count // LANES, LANES)
    near = lax.all_gather(held, "gx", axis=0)
    place = near[:, 0].reshape(n_gx, cell_count).astype(jnp.int32)
    amount = near[:, 1].reshape(n_gx, cell_count)
    plane = place // (mesh_rows * width)
    row = place // width % mesh_rows
    column = place % width
    parts = width // LANES
    add_rows = planes * parts * own_rows
    at_row = (plane * parts + column // LANES) * own_rows + row % own_rows
    mine = row // own_rows == lax.axis_index("gx")
    codes = jnp.where(mine, at_row, add_rows) * LANES + column % LANES

    packed = (pair_source * BLOCK + pair_target % BLOCK).reshape(-1, LANES)
    sources = order(packed)

    turned_ops = jnp.pad(
        m2l_ops.transpose(0, 2, 1), ((0, 0), (0, KPAD - coef_count), (0, KPAD - coef_count))
    )
    high = lax.reduce_precision(turned_ops, 8, 7)
    ops = jnp.concatenate([high, turned_ops - high], axis=2)
    ops = jnp.pad(ops, ((0, 0), (0, 0), (0, LANES - 2 * KPAD)))

    table = make_table(cells, arrived, top_rows)
    cell_blocks = cell_count // BLOCK * PER_WINDOW
    cut = cell_blocks * BLOCK // LANES
    slot_fields = m2l(sources[cut:], block_class[cell_blocks:], table, ops, True, slots)
    returned = exchange(slot_fields, n_gx, n_gy)
    own_fields = m2l(sources[:cut], block_class[:cell_blocks], table, ops, False, slots)

    adds = deposit(codes, amount, add_rows + 8)
    tables = fourier_tables(n_gx * width)
    spectrum = None
    for span in spans:
        spectrum = fourier(send(span), adds, tables, span[0], planes, spectrum)

    field_tensors = add_back(lists, counts, own_fields, returned, coef_count)
    return (field_tensors, spectrum)


def solution(mesh):
    placed = (
        P(None, ("gx", "gy")),
        P(("gx", "gy"), None, None),
        P(("gx", "gy"), None),
        P(("gx", "gy")),
        P(("gx", "gy")),
        P(("gx", "gy")),
        P(),
        P(("gx", "gy")),
        P("gy", None, "gx"),
    )
    return jax.shard_map(
        functools.partial(on_device, n_gx=mesh.shape["gx"], n_gy=mesh.shape["gy"]),
        mesh=mesh,
        in_specs=placed,
        out_specs=(P(None, ("gx", "gy")), P(None, "gy", "gx", None)),
        check_vma=False,
    )
```

time: 948 us -> 570 us (0.60); the launches traced: 935 us -> 568 us
  local copies, waits for them, and re-layouts: 435 us -> 29.3 us
  Pallas kernels: 0 us -> 311 us
  matrix products: 157 us -> 0 us
  blocking collectives: 204 us -> 83.7 us
  other arithmetic: 121 us -> 6.4 us
  waiting for transfers between devices: 0.02 us -> 83.2 us
  starting transfers between devices: 15.4 us -> 54.1 us
    gather x26 -> x0, local copies, waits for them, and re-layouts: 325 us -> none  [the longest x16 273 us: add_group(): jnp.take(table, source_ids, axis=1).reshape(coef_count, blocks_each, BLOCK)]
    pallas_call x0 -> x11, Pallas kernels: none -> 311 us  [the longest x1 116 us: deposit(): pl.pallas_call(deposit_kernel, out_shape=(jax.ShapeDtypeStruct((rows, LAN...]
    dot_general x26 -> x0, matrix products: 157 us -> none  [the longest x8 51 us: add_group(): jnp.einsum('bkj,jbi->kbi', operators, gathered, precision=lax.Precision.H...]
    all_gather x1 -> x2, blocking collectives: 204 us -> 83.7 us  [the longest x1 48.4 us: on_device(): near = lax.all_gather(held, 'gx', axis=0)]
    all_to_all x1 -> x4, waiting for transfers between devices: 0.01 us -> 83.2 us  [send(): return lax.all_to_all(part, 'gx', 0, 0, tiled=True)]
    scatter-add x2 -> x0, other arithmetic: 50.2 us -> none  [the longest x1 26.8 us: on_device(): density = pm_density.reshape(-1).at[cell_mesh].add(DEPOSIT_SCALE * multip...]
    dot_general x2 -> x0, other arithmetic: 32.5 us -> none  [the longest x1 16.3 us: fourier_rows(): jnp.dot(flat_rows, jnp.sin(angles), precision=lax.Precision.HIGHEST, pref...]
    unnamed x40 -> x48, local copies, waits for them, and re-layouts: 38.4 us -> 10.2 us
  transfers between devices with their start and end apart: 9 -> 20, of which waited for: 0 -> 2; matrix products, arithmetic and copies ran while one was open for 64% -> 4% of each run, Pallas kernels for 0% -> 53%
where the time goes in v1:
time: 570 us; the launch traced here: 568 us
  Pallas kernels  311 us (55%)
  blocking collectives  83.7 us (15%)
  waiting for transfers between devices  83.2 us (15%)
  starting transfers between devices  54.1 us (9%)
  local copies, waits for them, and re-layouts  29.3 us (5%)
  other arithmetic  6.4 us (1%)
    pallas_call x1, Pallas kernels, deposit(): pl.pallas_call(deposit_kernel, out_shape=(jax.ShapeDtypeStruct((rows, LAN...  116 us
    pallas_call x2, Pallas kernels, m2l(): pl.pallas_call(functools.partial(m2l_kernel, turned=turned), grid=(steps,...  115 us
    all_to_all x4, waiting for transfers between devices, send(): return lax.all_to_all(part, 'gx', 0, 0, tiled=True)  83.2 us
    all_gather x1, blocking collectives, on_device(): near = lax.all_gather(held, 'gx', axis=0)  48.4 us
    all_gather x1, blocking collectives, on_device(): top_rows = lax.all_gather(top_own, ('gx', 'gy'), axis=0, tiled=True)  35.3 us
    all_to_all x4, starting transfers between devices, send(): return lax.all_to_all(part, 'gx', 0, 0, tiled=True)  31.2 us
    pallas_call x4, Pallas kernels, fourier(): pl.pallas_call(functools.partial(fourier_kernel, sources=sources, linked=...  30 us
    ppermute x16, starting transfers between devices, exchange(): arrived[7 - m] = lax.ppermute(blocks[m], ('gx', 'gy'), pairs)  22.9 us
  transfers between devices with their start and end apart: 20, of which 2 were waited for; matrix products, arithmetic and copies ran while one was open for 4% of the time, Pallas kernels for 53%

profile of v1, /device:TPU:8, one launch (start us, length us, event | category | flops | bytes accessed | tf_op | source)
XLA Modules:
  0.0 568.4 jit_solution(11878687244401387871)
XLA Ops:
  0.6 6.3 %fusion.19 = (f32[2,1024,256]{2,1,0:T(8,128)S(1)}, f32[2,1024,256]{2,1,0:T(8,128)}, f32[2,1024,256]{2,1,0:T(8,128)}, f32[2,1024,256]{2,1,0:T(8,128)}) fusion(f32[8,1024,256]{2,1,0:T(8,128)} %param.19), kind=kLoop, calls=%fused_computation.77 | loop fusion | bytes 16777216 | tf_op jit(solution)/shard_map/slice | solution.py:425
  7.0 1.5 copy.32
  8.5 5.3 all-to-all-start.3
  13.8 3.1 copy.33
  16.9 41.8 %all-to-all-done.3.refs_0_ = f32[4,2,256,256]{3,2,1,0:T(8,128)S(1)} async-done(((f32[4,2,256,256]{3,2,1,0:T(8,128)}), f32[4,2,256,256]{3,2,1,0:T(8,128)S(1)}, u32[]{:S(2)}, u32[]{:S(2)}) %all-to-all-start.3) | async-done | bytes 2097184 | tf_op jit(solution)/shard_map/all_to_all | solution.py:427
  58.7 7.7 %all-to-all-start.2 = ((f32[4,2,256,256]{3,2,1,0:T(8,128)}), f32[4,2,256,256]{3,2,1,0:T(8,128)}, u32[]{:S(2)}, u32[]{:S(2)}) async-start(f32[4,2,256,256]{3,2,1,0:T(8,128)} %bitcast.91), calls=%async_computation.2 | async-start | bytes 4194304 | tf_op jit(solution)/shard_map/all_to_all | solution.py:427
  66.5 3.1 copy.34
  69.6 41.3 %all-to-all-done.2.refs_0_ = f32[4,2,256,256]{3,2,1,0:T(8,128)} async-done(((f32[4,2,256,256]{3,2,1,0:T(8,128)}), f32[4,2,256,256]{3,2,1,0:T(8,128)}, u32[]{:S(2)}, u32[]{:S(2)}) %all-to-all-start.2) | async-done | bytes 2097184 | tf_op jit(solution)/shard_map/all_to_all | solution.py:427
  110.9 7.0 %all-to-all-start.1 = ((f32[4,2,256,256]{3,2,1,0:T(8,128)}), f32[4,2,256,256]{3,2,1,0:T(8,128)S(1)}, u32[]{:S(2)}, u32[]{:S(2)}) async-start(f32[4,2,256,256]{3,2,1,0:T(8,128)} %bitcast.90), calls=%async_computation.1 | async-start | bytes 4194304 | tf_op jit(solution)/shard_map/all_to_all | solution.py:427
  117.8 1.3 pad.12.cells_ref.refs_0_
  119.1 15.0 %pack.1 = (f32[8,40,512]{2,1,0:T(8,128)S(1)}, f32[32,128]{1,0:T(8,128)S(1)}) custom-call(s32[8,512]{1,0:T(8,128)S(1)} %bitcast.84, s32[8]{0:T(128)S(1)} %bitcast.86, f32[40,4096]{1,0:T(8,128)S(1)} %pad.12.cells_ref.refs_0_), custom_call_target="tpu_custom_call" | custom-call | flops 1000000 | bytes 16000000 | tf_op jit(solution)/shard_map/pack/pallas_call | solution.py:68
  134.2 0.9 slice_bitcast_fusion.8
  135.1 0.0 collective-permute-start
  135.1 1.5 collective-permute-start.1
  136.5 3.0 collective-permute-start.2
  139.5 0.0 collective-permute-start.3
  139.5 2.6 collective-permute-start.4
  142.2 1.5 copy.35
  143.7 5.2 copy.18
  148.9 0.1 fusion.2.packed_ref
  149.0 15.5 %order.1 = s32[512,128]{1,0:T(8,128)S(1)} custom-call(s32[512,128]{1,0:T(8,128)S(1)} %fusion.2.packed_ref), custom_call_target="tpu_custom_call" | custom-call | flops 1000000 | bytes 16000000 | tf_op jit(solution)/shard_map/order/pallas_call | solution.py:116
  164.5 0.6 convert_bitcast_fusion
  165.1 35.3 %all_gather.6.refs_9_ = f32[1024,128]{1,0:T(8,128)S(1)} all-gather(f32[32,128]{1,0:T(8,128)} %copy-done.10), channel_id=1, replica_groups=mesh['gx'=4,'gy'=8] {'gx','gy'}, dimensions={0}, use_global_device_ids=true | all-gather | bytes 540672 | tf_op jit(solution)/shard_map/all_gather | solution.py:432
  200.4 1.5 slice_multiply_fusion
  201.9 0.0 all-to-all-done.1.refs_0_
  201.9 11.3 %all-to-all-start = ((f32[4,2,256,256]{3,2,1,0:T(8,128)}), f32[4,2,256,256]{3,2,1,0:T(8,128)}, u32[]{:S(2)}, u32[]{:S(2)}) async-start(f32[4,2,256,256]{3,2,1,0:T(8,128)} %bitcast.89), calls=%async_computation | async-start | bytes 4194304 | tf_op jit(solution)/shard_map/all_to_all | solution.py:427
  213.2 1.3 fusion.21
  214.6 2.6 pad_reduce-precision_fusion
  217.2 0.0 copy-start.17
  217.2 1.1 select_maximum_fusion.ops_ref
  218.3 0.0 collective-permute-done.refs_1_
  218.3 0.1 collective-permute-start.5
  218.4 0.0 collective-permute-done.1.refs_2_
  218.4 3.5 collective-permute-start.6
  221.9 0.0 collective-permute-done.2.refs_3_
  221.9 2.1 collective-permute-start.7
  224.0 48.4 %all_gather.7 = f32[4,2,32,128]{3,2,0,1:T(8,128)S(1)} all-gather(f32[1,2,32,128]{3,2,0,1:T(8,128)S(1)} %pad_maximum_fusion), channel_id=1, replica_groups=mesh['gx'=4,'gy'=8] {'gx'}, dimensions={0}, use_global_device_ids=true | all-gather | bytes 163840 | tf_op jit(solution)/shard_map/all_gather | solution.py:437
  272.4 0.0 collective-permute-done.5.refs_6_
  272.4 0.0 collective-permute-done.6.refs_7_
  272.5 7.0 %table.1.table_ref = f32[9216,128]{1,0:T(8,128)} custom-call(f32[40,4096]{1,0:T(8,128)S(1)} %pad.12.cells_ref.refs_0_, f32[40,512]{1,0:T(8,128)} %collective-permute-done.refs_1_, f32[40,512]{1,0:T(8,128)} %collective-permute-done.1.refs_2_, f32[40,512]{1,0:T(8,128)} %collective-permute-done.2.refs_3_, f32[40,512]{1,0:T(8,128)} %collective-permute-done.3.refs_4_, ...), custom_call_target="tpu_custom_call" | custom-call | flops 1000000 | bytes 16000000 | tf_op jit(solution)/shard_map/table/pallas_call | solution.py:146
  279.4 58.1 %m2l_slots.1 = f32[8,40,512]{2,1,0:T(8,128)S(1)} custom-call(s32[256,128]{1,0:T(8,128)S(1)} %get-tuple-element.36.source_ref, s32[512]{0:T(512)S(1)} %get-tuple-element.40.class_ref, f32[9216,128]{1,0:T(8,128)} %table.1.table_ref, f32[189,40,128]{2,1,0:T(8,128)S(1)} %select_maximum_fusion.ops_ref), custom_call_target="tpu_custom_call" | custom-call | flops 1000000 | bytes 100000000 | tf_op jit(solution)/shard_map/m2l_slots/pallas_call | solution.py:216
  337.6 0.1 collective-permute-start.10
  337.7 0.7 collective-permute-start.11
  338.4 2.0 collective-permute-start.12
  340.4 0.1 collective-permute-start.13
  340.5 2.8 collective-permute-start.14
  343.2 2.6 collective-permute-start.15
  345.9 2.0 collective-permute-start.9
  347.8 0.5 fusion.11.code_ref
  348.4 116.3 %deposit.1 = (f32[4104,128]{1,0:T(8,128)S(1)}, f32[4104,128]{1,0:T(8,128)S(1)}, f32[4104,128]{1,0:T(8,128)}, f32[4104,128]{1,0:T(8,128)}) custom-call(s32[4,4096]{1,0:T(4,128)S(1)} %fusion.11.code_ref, f32[4,4096]{1,0:T(4,128)S(1)} %bitcast.83), custom_call_target="tpu_custom_call" | custom-call | flops 1000000 | bytes 100000000 | tf_op jit(solution)/shard_map/deposit/pallas_call | solution.py:297
  464.6 1.4 copy-done.2
  466.0 1.4 copy-done.3
  467.4 2.1 copy-done.1
  469.5 56.7 %m2l_cells.1.own_ref = f32[4096,128]{1,0:T(8,128)S(1)} custom-call(s32[256,128]{1,0:T(8,128)S(1)} %get-tuple-element.37.source_ref, s32[512]{0:T(512)S(1)} %copy-done.11, f32[9216,128]{1,0:T(8,128)} %table.1.table_ref, f32[189,40,128]{2,1,0:T(8,128)S(1)} %copy-done.1), custom_call_target="tpu_custom_call" | custom-call | flops 1000000 | bytes 100000000 | tf_op jit(solution)/shard_map/m2l_cells/pallas_call | solution.py:216
  526.3 0.0 copy-start.4
  526.3 0.0 collective-permute-done.14.refs_6_
  526.3 0.0 collective-permute-done.15.refs_7_
  526.3 0.0 collective-permute-done.9.refs_1_
  526.3 12.0 %add_back.1 = f32[35,4096]{1,0:T(8,128)} custom-call(s32[8,512]{1,0:T(8,128)S(1)} %bitcast.85, s32[8]{0:T(128)S(1)} %bitcast.87, f32[4096,128]{1,0:T(8,128)S(1)} %m2l_cells.1.own_ref, f32[40,512]{1,0:T(8,128)S(1)} %collective-permute-done.8.refs_0_, f32[40,512]{1,0:T(8,128)S(1)} %collective-permute-done.9.refs_1_, ...), custom_call_target="tpu_custom_call" | custom-call | flops 1000000 | bytes 30000000 | tf_op jit(solution)/shard_map/add_back/pallas_call | solution.py:267
  538.4 7.3 %fourier.4.refs_7_ = f32[2,8,256,1024]{3,2,1,0:T(8,128)} custom-call(f32[4,2,256,256]{3,2,1,0:T(8,128)S(1)} %copy-done.6, f32[4104,128]{1,0:T(8,128)} %copy-done.2, f32[4104,128]{1,0:T(8,128)} %copy-done.3, f32[4104,128]{1,0:T(8,128)} %get-tuple-element.12.refs_3_, f32[4104,128]{1,0:T(8,128)} %get-tuple-element.13.refs_4_, bf16[1024,1024]{1,0:T(8,128)(2,1)S(1)} %copy-done.4, ...), custom_call_target="tpu_custom_call" | custom-call | flops 3221225472 | bytes 12582912 | tf_op jit(solution)/shard_map/fourier/pallas_call | solution.py:385
  545.7 7.7 %fourier.5.refs_7_ = f32[2,8,256,1024]{3,2,1,0:T(8,128)} custom-call(f32[4,2,256,256]{3,2,1,0:T(8,128)} %all-to-all-done.2.refs_0_, f32[4104,128]{1,0:T(8,128)} %copy-done.2, f32[4104,128]{1,0:T(8,128)} %copy-done.3, f32[4104,128]{1,0:T(8,128)} %get-tuple-element.12.refs_3_, f32[4104,128]{1,0:T(8,128)} %get-tuple-element.13.refs_4_, ...), custom_call_target="tpu_custom_call", output_to_operand_aliasing={{}: (7, {})} | custom-call | flops 3221225472 | bytes 12582912 | tf_op jit(solution)/shard_map/fourier/pallas_call | solution.py:385
  553.4 7.4 %fourier.6.refs_7_ = f32[2,8,256,1024]{3,2,1,0:T(8,128)} custom-call(f32[4,2,256,256]{3,2,1,0:T(8,128)S(1)} %copy-done.8, f32[4104,128]{1,0:T(8,128)} %copy-done.2, f32[4104,128]{1,0:T(8,128)} %copy-done.3, f32[4104,128]{1,0:T(8,128)} %get-tuple-element.12.refs_3_, f32[4104,128]{1,0:T(8,128)} %get-tuple-element.13.refs_4_, ...), custom_call_target="tpu_custom_call", output_to_operand_aliasing={{}: (7, {})} | custom-call | flops 3221225472 | bytes 12582912 | tf_op jit(solution)/shard_map/fourier/pallas_call | solution.py:385
  560.8 0.0 all-to-all-done.refs_0_
  560.8 7.6 %fourier.7 = f32[2,8,256,1024]{3,2,1,0:T(8,128)} custom-call(f32[4,2,256,256]{3,2,1,0:T(8,128)} %all-to-all-done.refs_0_, f32[4104,128]{1,0:T(8,128)} %copy-done.2, f32[4104,128]{1,0:T(8,128)} %copy-done.3, f32[4104,128]{1,0:T(8,128)} %get-tuple-element.12.refs_3_, f32[4104,128]{1,0:T(8,128)} %get-tuple-element.13.refs_4_, ...), custom_call_target="tpu_custom_call", output_to_operand_aliasing={{}: (7, {})} | custom-call | flops 3221225472 | bytes 12582912 | tf_op jit(solution)/shard_map/fourier/pallas_call | solution.py:385
  (55 shorter events, 0.2 us)
Async XLA Ops:
  8.5 50.2 %all-to-all-start.3 = ((f32[4,2,256,256]{3,2,1,0:T(8,128)}), f32[4,2,256,256]{3,2,1,0:T(8,128)S(1)}, u32[]{:S(2)}, u32[]{:S(2)}) async-start(f32[4,2,256,256]{3,2,1,0:T(8,128)} %bitcast.92), calls=%async_computation.3 | async-start | bytes 4194304 | tf_op jit(solution)/shard_map/all_to_all | solution.py:427
  58.7 10.8 %copy-start.5 = (f32[4,2,256,256]{3,2,1,0:T(8,128)}, f32[4,2,256,256]{3,2,1,0:T(8,128)S(1)}, u32[]{:S(2)}) copy-start(f32[4,2,256,256]{3,2,1,0:T(8,128)S(1)} %all-to-all-done.3.refs_0_) | copy-start | bytes 6291460
  58.7 52.1 %all-to-all-start.2 = ((f32[4,2,256,256]{3,2,1,0:T(8,128)}), f32[4,2,256,256]{3,2,1,0:T(8,128)}, u32[]{:S(2)}, u32[]{:S(2)}) async-start(f32[4,2,256,256]{3,2,1,0:T(8,128)} %bitcast.91), calls=%async_computation.2 | async-start | bytes 4194304 | tf_op jit(solution)/shard_map/all_to_all | solution.py:427
  66.4 52.7 %copy-start.9 = (s32[1,8,512]{2,1,0:T(8,128)S(1)}, s32[1,8,512]{2,1,0:T(8,128)}, u32[]{:S(2)}) copy-start(s32[1,8,512]{2,1,0:T(8,128)} %param.12) | copy-start | bytes 49156
  66.4 52.7 %copy-start.12 = (s32[1,8]{1,0:T(1,128)S(1)}, s32[1,8]{1,0:T(1,128)}, u32[]{:S(2)}) copy-start(s32[1,8]{1,0:T(1,128)} %param.13) | copy-start | bytes 100
  110.9 91.1 %all-to-all-start.1 = ((f32[4,2,256,256]{3,2,1,0:T(8,128)}), f32[4,2,256,256]{3,2,1,0:T(8,128)S(1)}, u32[]{:S(2)}, u32[]{:S(2)}) async-start(f32[4,2,256,256]{3,2,1,0:T(8,128)} %bitcast.90), calls=%async_computation.1 | async-start | bytes 4194304 | tf_op jit(solution)/shard_map/all_to_all | solution.py:427
  117.8 24.3 %copy-start.14 = (f32[2,1024,256]{2,1,0:T(8,128)S(1)}, f32[2,1024,256]{2,1,0:T(8,128)}, u32[]{:S(2)}) copy-start(f32[2,1024,256]{2,1,0:T(8,128)} %get-tuple-element.16) | copy-start | bytes 6291460
  134.2 14.7 %copy-start.10 = (f32[32,128]{1,0:T(8,128)}, f32[32,128]{1,0:T(8,128)S(1)}, u32[]{:S(2)}) copy-start(f32[32,128]{1,0:T(8,128)S(1)} %get-tuple-element.9) | copy-start | bytes 49156
  135.1 83.2 %collective-permute-start = (f32[40,512]{1,0:T(8,128)}, f32[40,512]{1,0:T(8,128)}, u32[]{:S(2)}, u32[]{:S(2)}) collective-permute-start(f32[40,512]{1,0:T(8,128)} %get-tuple-element.35), channel_id=1, source_target_pairs={{0,9},{1,10},{2,11},{3,12},{4,13},{5,14},{6,15},{7,8},{8,17},{9,18... | collective-permute-start | bytes 245768 | tf_op jit(solution)/shard_map/ppermute | solution.py:94
  135.1 83.3 %collective-permute-start.1 = (f32[40,512]{1,0:T(8,128)}, f32[40,512]{1,0:T(8,128)}, u32[]{:S(2)}, u32[]{:S(2)}) collective-permute-start(f32[40,512]{1,0:T(8,128)} %get-tuple-element.34), channel_id=1, source_target_pairs={{0,8},{1,9},{2,10},{3,11},{4,12},{5,13},{6,14},{7,15},{8,16},{9,17... | collective-permute-start | bytes 245768 | tf_op jit(solution)/shard_map/ppermute | solution.py:94
  136.5 85.3 %collective-permute-start.2 = (f32[40,512]{1,0:T(8,128)}, f32[40,512]{1,0:T(8,128)}, u32[]{:S(2)}, u32[]{:S(2)}) collective-permute-start(f32[40,512]{1,0:T(8,128)} %get-tuple-element.33), channel_id=1, source_target_pairs={{0,15},{1,8},{2,9},{3,10},{4,11},{5,12},{6,13},{7,14},{8,23},{9,16... | collective-permute-start | bytes 245768 | tf_op jit(solution)/shard_map/ppermute | solution.py:94
  139.5 132.9 %collective-permute-start.3 = (f32[40,512]{1,0:T(8,128)}, f32[40,512]{1,0:T(8,128)}, u32[]{:S(2)}, u32[]{:S(2)}) collective-permute-start(f32[40,512]{1,0:T(8,128)} %get-tuple-element.32), channel_id=1, source_target_pairs={{0,1},{1,2},{2,3},{3,4},{4,5},{5,6},{6,7},{7,0},{8,9},{9,10},{10,1... | collective-permute-start | bytes 245768 | tf_op jit(solution)/shard_map/ppermute | solution.py:94
  139.5 132.9 %collective-permute-start.4 = (f32[40,512]{1,0:T(8,128)}, f32[40,512]{1,0:T(8,128)}, u32[]{:S(2)}, u32[]{:S(2)}) collective-permute-start(f32[40,512]{1,0:T(8,128)} %get-tuple-element.31), channel_id=1, source_target_pairs={{0,7},{1,0},{2,1},{3,2},{4,3},{5,4},{6,5},{7,6},{8,15},{9,8},{10,9... | collective-permute-start | bytes 245768 | tf_op jit(solution)/shard_map/ppermute | solution.py:94
  142.2 6.7 %copy-start.15 = (s32[65536]{0:T(1024)S(1)}, s32[65536]{0:T(1024)}, u32[]{:S(2)}) copy-start(s32[65536]{0:T(1024)} %param.14) | copy-start | bytes 786436
  142.2 6.7 %copy-start.16 = (s32[65536]{0:T(1024)S(1)}, s32[65536]{0:T(1024)}, u32[]{:S(2)}) copy-start(s32[65536]{0:T(1024)} %param.15) | copy-start | bytes 786436
  143.7 20.8 %copy-start.22 = (s32[4096]{0:T(1024)S(1)}, s32[4096]{0:T(1024)}, u32[]{:S(2)}) copy-start(s32[4096]{0:T(1024)} %param.18) | copy-start | bytes 49156
  201.9 15.2 %copy-start.7 = (f32[4,2,256,256]{3,2,1,0:T(8,128)}, f32[4,2,256,256]{3,2,1,0:T(8,128)S(1)}, u32[]{:S(2)}) copy-start(f32[4,2,256,256]{3,2,1,0:T(8,128)S(1)} %all-to-all-done.1.refs_0_) | copy-start | bytes 6291460
  201.9 358.8 %all-to-all-start = ((f32[4,2,256,256]{3,2,1,0:T(8,128)}), f32[4,2,256,256]{3,2,1,0:T(8,128)}, u32[]{:S(2)}, u32[]{:S(2)}) async-start(f32[4,2,256,256]{3,2,1,0:T(8,128)} %bitcast.89), calls=%async_computation | async-start | bytes 4194304 | tf_op jit(solution)/shard_map/all_to_all | solution.py:427
  217.2 1.1 copy-start.19
  217.2 1.2 copy-start.18
  217.2 4.7 copy-start.17
  217.2 6.8 %copy-start.20 = (f32[1,1,32,128]{3,2,0,1:T(8,128)S(1)}, f32[1,1,32,128]{3,2,0,1:T(8,128)}, u32[]{:S(2)}) copy-start(f32[1,1,32,128]{3,2,0,1:T(8,128)} %convert_bitcast_fusion) | copy-start | bytes 49156
  217.2 6.8 %copy-start.21 = (f32[1,4096]{1,0:T(1,128)S(1)}, f32[1,4096]{1,0:T(1,128)}, u32[]{:S(2)}) copy-start(f32[1,4096]{1,0:T(1,128)} %slice_multiply_fusion) | copy-start | bytes 49156
  218.3 119.3 %copy-start = (f32[189,40,128]{2,1,0:T(8,128)}, f32[189,40,128]{2,1,0:T(8,128)S(1)}, u32[]{:S(2)}) copy-start(f32[189,40,128]{2,1,0:T(8,128)S(1)} %select_maximum_fusion.ops_ref) | copy-start | bytes 11612164
  218.3 54.1 %collective-permute-start.5 = (f32[40,512]{1,0:T(8,128)S(1)}, f32[40,512]{1,0:T(8,128)S(1)}, u32[]{:S(2)}, u32[]{:S(2)}) collective-permute-start(f32[40,512]{1,0:T(8,128)S(1)} %copy-done.19), channel_id=1, source_target_pairs={{0,25},{1,26},{2,27},{3,28},{4,29},{5,30},{6,31},{7,24},{8,1},{9,2... | collective-permute-start | bytes 245768 | tf_op jit(solution)/shard_map/ppermute | solution.py:94
  218.4 54.0 %collective-permute-start.6 = (f32[40,512]{1,0:T(8,128)S(1)}, f32[40,512]{1,0:T(8,128)S(1)}, u32[]{:S(2)}, u32[]{:S(2)}) collective-permute-start(f32[40,512]{1,0:T(8,128)S(1)} %copy-done.18), channel_id=1, source_target_pairs={{0,24},{1,25},{2,26},{3,27},{4,28},{5,29},{6,30},{7,31},{8,0},{9,1... | collective-permute-start | bytes 245768 | tf_op jit(solution)/shard_map/ppermute | solution.py:94
  221.9 50.6 %collective-permute-start.7 = (f32[40,512]{1,0:T(8,128)S(1)}, f32[40,512]{1,0:T(8,128)S(1)}, u32[]{:S(2)}, u32[]{:S(2)}) collective-permute-start(f32[40,512]{1,0:T(8,128)S(1)} %copy-done.17), channel_id=1, source_target_pairs={{0,31},{1,24},{2,25},{3,26},{4,27},{5,28},{6,29},{7,30},{8,7},{9,0... | collective-permute-start | bytes 245768 | tf_op jit(solution)/shard_map/ppermute | solution.py:94
  279.4 188.0 %copy-start.11 = (s32[512]{0:T(512)S(1)}, s32[512]{0:T(512)}, u32[]{:S(2)}) copy-start(s32[512]{0:T(512)} %get-tuple-element.41.class_ref) | copy-start | bytes 6148
  337.6 5.6 collective-permute-start.10
  337.7 8.1 %collective-permute-start.11 = (f32[40,512]{1,0:T(8,128)S(1)}, f32[40,512]{1,0:T(8,128)S(1)}, u32[]{:S(2)}, u32[]{:S(2)}) collective-permute-start(f32[40,512]{1,0:T(8,128)S(1)} %get-tuple-element.24), channel_id=1, source_target_pairs={{0,1},{1,2},{2,3},{3,4},{4,5},{5,6},{6,7},{7,0},{8,9},{9,10},{10,1... | collective-permute-start | bytes 245768 | tf_op jit(solution)/shard_map/ppermute | solution.py:94
  338.4 7.5 %collective-permute-start.12 = (f32[40,512]{1,0:T(8,128)S(1)}, f32[40,512]{1,0:T(8,128)S(1)}, u32[]{:S(2)}, u32[]{:S(2)}) collective-permute-start(f32[40,512]{1,0:T(8,128)S(1)} %get-tuple-element.23), channel_id=1, source_target_pairs={{0,7},{1,0},{2,1},{3,2},{4,3},{5,4},{6,5},{7,6},{8,15},{9,8},{10,9... | collective-permute-start | bytes 245768 | tf_op jit(solution)/shard_map/ppermute | solution.py:94
  340.4 185.9 %collective-permute-start.13 = (f32[40,512]{1,0:T(8,128)S(1)}, f32[40,512]{1,0:T(8,128)S(1)}, u32[]{:S(2)}, u32[]{:S(2)}) collective-permute-start(f32[40,512]{1,0:T(8,128)S(1)} %get-tuple-element.22), channel_id=1, source_target_pairs={{0,25},{1,26},{2,27},{3,28},{4,29},{5,30},{6,31},{7,24},{8,1},{9,2... | collective-permute-start | bytes 245768 | tf_op jit(solution)/shard_map/ppermute | solution.py:94
  340.5 185.8 %collective-permute-start.14 = (f32[40,512]{1,0:T(8,128)S(1)}, f32[40,512]{1,0:T(8,128)S(1)}, u32[]{:S(2)}, u32[]{:S(2)}) collective-permute-start(f32[40,512]{1,0:T(8,128)S(1)} %get-tuple-element.21), channel_id=1, source_target_pairs={{0,24},{1,25},{2,26},{3,27},{4,28},{5,29},{6,30},{7,31},{8,0},{9,1... | collective-permute-start | bytes 245768 | tf_op jit(solution)/shard_map/ppermute | solution.py:94
  343.2 183.0 %collective-permute-start.15 = (f32[40,512]{1,0:T(8,128)S(1)}, f32[40,512]{1,0:T(8,128)S(1)}, u32[]{:S(2)}, u32[]{:S(2)}) collective-permute-start(f32[40,512]{1,0:T(8,128)S(1)} %get-tuple-element.20), channel_id=1, source_target_pairs={{0,31},{1,24},{2,25},{3,26},{4,27},{5,28},{6,29},{7,30},{8,7},{9,0... | collective-permute-start | bytes 245768 | tf_op jit(solution)/shard_map/ppermute | solution.py:94
  345.8 180.5 %collective-permute-start.8 = (f32[40,512]{1,0:T(8,128)S(1)}, f32[40,512]{1,0:T(8,128)S(1)}, u32[]{:S(2)}, u32[]{:S(2)}) collective-permute-start(f32[40,512]{1,0:T(8,128)S(1)} %get-tuple-element.27), channel_id=1, source_target_pairs={{0,9},{1,10},{2,11},{3,12},{4,13},{5,14},{6,15},{7,8},{8,17},{9,18... | collective-permute-start | bytes 245768 | tf_op jit(solution)/shard_map/ppermute | solution.py:94
  345.9 180.5 %collective-permute-start.9 = (f32[40,512]{1,0:T(8,128)S(1)}, f32[40,512]{1,0:T(8,128)S(1)}, u32[]{:S(2)}, u32[]{:S(2)}) collective-permute-start(f32[40,512]{1,0:T(8,128)S(1)} %get-tuple-element.26), channel_id=1, source_target_pairs={{0,8},{1,9},{2,10},{3,11},{4,12},{5,13},{6,14},{7,15},{8,16},{9,17... | collective-permute-start | bytes 245768 | tf_op jit(solution)/shard_map/ppermute | solution.py:94
  464.6 1.4 copy-start.2
  466.0 1.4 copy-start.3
  467.4 2.1 copy-start.1
  469.5 56.8 %copy-start.13 = (s32[1,8]{1,0:T(1,128)S(1)}, s32[1,8]{1,0:T(1,128)}, u32[]{:S(2)}) copy-start(s32[1,8]{1,0:T(1,128)} %param.13) | copy-start | bytes 100
  469.5 68.8 %copy-start.6 = (f32[4,2,256,256]{3,2,1,0:T(8,128)S(1)}, f32[4,2,256,256]{3,2,1,0:T(8,128)}, u32[]{:S(2)}) copy-start(f32[4,2,256,256]{3,2,1,0:T(8,128)} %copy-done.5) | copy-start | bytes 6291460
  526.3 12.1 %copy-start.4 = (bf16[1024,1024]{1,0:T(8,128)(2,1)S(1)}, bf16[1024,1024]{1,0:T(8,128)(2,1)}, u32[]{:S(2)}) copy-start(bf16[1024,1024]{1,0:T(8,128)(2,1)} %constant.117.clone.refs_5_) | copy-start | bytes 6291460
  545.7 7.7 %copy-start.8 = (f32[4,2,256,256]{3,2,1,0:T(8,128)S(1)}, f32[4,2,256,256]{3,2,1,0:T(8,128)}, u32[]{:S(2)}) copy-start(f32[4,2,256,256]{3,2,1,0:T(8,128)} %copy-done.7) | copy-start | bytes 6291460

commit v2 on v1

v2 whole, which is shorter than its diff:
```python
import functools

import jax
import jax.numpy as jnp
import ml_dtypes
import numpy as np
from jax import lax
from jax.experimental import pallas as pl
from jax.experimental.pallas import tpu as pltpu
from jax.sharding import PartitionSpec as P

TOP = 32
BLOCK = 64
LANES = 128
KPAD = 40
COPIES = 3
PER_WINDOW = 8
SHIFT = 6
LANE_SHIFT = 7
VMEM_BYTES = 48 * 1024 * 1024
CHUNKS = (1, 3, 3, 1)
TOP_ROWS = TOP // 2

DEPOSIT_SCALE = 8.0
OFFSETS = tuple((a, b) for a in (-1, 0, 1) for b in (-1, 0, 1) if (a, b) != (0, 0))

SMEM_WHOLE = pl.BlockSpec(memory_space=pltpu.SMEM)
VMEM_WHOLE = pl.BlockSpec(memory_space=pltpu.VMEM)


def params():
    return pltpu.CompilerParams(vmem_limit_bytes=VMEM_BYTES)


def cost(flops, nbytes):
    return pl.CostEstimate(flops=flops, bytes_accessed=nbytes, transcendentals=0)


def spread(block):
    rest = jnp.zeros((LANES - COPIES * KPAD, LANES), jnp.float32)
    return jnp.concatenate([block] * COPIES + [rest], axis=0).T


def lane_ids(shape):
    return lax.broadcasted_iota(jnp.int32, shape, len(shape) - 1)


def own_table_kernel(cells_ref, out_ref, top_ref):
    @pl.loop(0, cells_ref.shape[1] // LANES)
    def _(k):
        at = pl.multiple_of(k * LANES, LANES)
        out_ref[pl.ds(at, LANES), :] = spread(cells_ref[:, pl.ds(at, LANES)])

    is_first = lane_ids((TOP_ROWS, LANES)) < KPAD
    top_ref[...] = jnp.where(is_first, out_ref[:TOP_ROWS, :], out_ref[TOP_ROWS : 2 * TOP_ROWS, :])


def own_table(cells, rows):
    count = cells.shape[1]
    return pl.pallas_call(
        own_table_kernel,
        grid=(1,),
        out_shape=(
            jax.ShapeDtypeStruct((rows, LANES), jnp.float32),
            jax.ShapeDtypeStruct((TOP_ROWS, LANES), jnp.float32),
        ),
        in_specs=[pl.BlockSpec((KPAD, count), lambda i: (0, 0))],
        out_specs=(
            pl.BlockSpec((count, LANES), lambda i: (0, 0)),
            pl.BlockSpec((TOP_ROWS, LANES), lambda i: (0, 0)),
        ),
        compiler_params=params(),
        cost_estimate=cost(10**6, 12 * 10**6),
        name="own_table",
    )(cells)


def whole_table_kernel(*refs, slot_steps):
    top_ref, out_ref = refs[8], refs[10]
    step = pl.program_id(0)
    for k in range(slot_steps):

        @pl.when(step == k)
        def _():
            at = 0
            for n in (2 * k, 2 * k + 1):
                for c in range(refs[n].shape[1] // LANES):
                    out_ref[at : at + LANES, :] = spread(refs[n][:, c * LANES : (c + 1) * LANES])
                    at += LANES

    rows = out_ref.shape[0]
    total = top_ref.shape[0]
    lanes = lane_ids((rows, LANES))
    for k in range(2 * total // rows):

        @pl.when(step == slot_steps + k)
        def _():
            pieces = []
            for first in range(k * rows, (k + 1) * rows, min(rows, total)):
                group, at = first // total, first % total
                value = top_ref[at : at + min(rows, total), :]
                pieces.append(pltpu.roll(value, LANES - KPAD, 1) if group else value)
            value = jnp.concatenate(pieces, axis=0) if len(pieces) > 1 else pieces[0]
            value = jnp.where(lanes < KPAD, value, 0.0)
            out_ref[...] = value + pltpu.roll(value, KPAD, 1) + pltpu.roll(value, 2 * KPAD, 1)


def whole_table(table, arrived, top_rows):
    slots = arrived[0].shape[1]
    rows = 2 * slots
    own = table.shape[0] - 8 * slots - 2 * top_rows.shape[0]
    first = own // rows
    steps = 4 + 2 * top_rows.shape[0] // rows
    return pl.pallas_call(
        functools.partial(whole_table_kernel, slot_steps=4),
        grid=(steps,),
        out_shape=jax.ShapeDtypeStruct(table.shape, jnp.float32),
        in_specs=[VMEM_WHOLE] * 9 + [pl.BlockSpec(memory_space=pl.ANY)],
        out_specs=pl.BlockSpec((rows, LANES), lambda i: (first + i, 0)),
        input_output_aliases={9: 0},
        compiler_params=params(),
        cost_estimate=cost(10**6, 16 * 10**6),
        name="whole_table",
    )(*arrived, top_rows, table)


def as_rows(table):
    return table.reshape(table.shape[0], 1, LANES)


def pack_kernel(list_ref, count_ref, table_ref, *refs):
    outs, rows = refs[:8], refs[8]
    slot_tiles = list_ref.shape[1] // LANES
    for n in range(8):

        @pl.loop(0, slot_tiles)
        def _(i):
            first = pl.multiple_of(i * LANES, LANES)
            for r in range(LANES):
                rows[r : r + 1, :] = table_ref[list_ref[n, first + r]]
            live = (lane_ids((KPAD, LANES)) + first) < count_ref[n]
            outs[n][:, pl.ds(first, LANES)] = jnp.where(live, rows[...].T[:KPAD], 0.0)


def pack(table, cell_count, proxy_list, proxy_count):
    slots = proxy_list.shape[1]
    return pl.pallas_call(
        pack_kernel,
        grid=(1,),
        out_shape=(jax.ShapeDtypeStruct((KPAD, slots), jnp.float32),) * 8,
        in_specs=[
            SMEM_WHOLE,
            SMEM_WHOLE,
            pl.BlockSpec((cell_count, 1, LANES), lambda i: (0, 0, 0)),
        ],
        out_specs=(pl.BlockSpec((KPAD, slots), lambda i: (0, 0)),) * 8,
        scratch_shapes=[pltpu.VMEM((LANES, LANES), jnp.float32)],
        compiler_params=params(),
        cost_estimate=cost(10**6, 25 * 10**6),
        name="pack",
    )(proxy_list, proxy_count, as_rows(table))


def exchange(blocks, n_gx, n_gy):
    arrived = [None] * 8
    for m, (a, b) in enumerate(OFFSETS):
        pairs = [
            (x * n_gy + y, (x + a) % n_gx * n_gy + (y + b) % n_gy)
            for x in range(n_gx)
            for y in range(n_gy)
        ]
        arrived[7 - m] = lax.ppermute(blocks[m], ("gx", "gy"), pairs)
    return arrived


def order_kernel(packed_ref, out_ref):
    lanes = lane_ids((LANES, LANES))
    within = lanes & (BLOCK - 1)
    base = lanes - within

    @pl.loop(0, packed_ref.shape[0] // LANES)
    def _(k):
        at = pl.ds(pl.multiple_of(k * LANES, LANES), LANES)
        packed = packed_ref[at, :]

        def step(i, ordered):
            value = jnp.take_along_axis(packed, base + i, axis=1, mode="promise_in_bounds")
            return jnp.where((value & (BLOCK - 1)) == within, value, ordered)

        ordered = lax.fori_loop(0, BLOCK, step, jnp.zeros_like(packed), unroll=8)
        out_ref[at, :] = ordered >> SHIFT


def order(packed):
    return pl.pallas_call(
        order_kernel,
        out_shape=jax.ShapeDtypeStruct(packed.shape, jnp.int32),
        in_specs=[VMEM_WHOLE],
        out_specs=VMEM_WHOLE,
        compiler_params=params(),
        cost_estimate=cost(10**6, 20 * 10**6),
        name="order",
    )(packed)


def m2l_kernel(source_ref, class_ref, table_ref, ops_ref, out_ref, *gathered, first, turned):
    step = first + pl.program_id(0)
    lanes = lane_ids((1, LANES))
    in_first = lanes < KPAD
    in_second = lanes < 2 * KPAD

    def row(b, t):
        return table_ref[source_ref[b // 2, (b % 2) * BLOCK + t]]

    for u in range(2):
        for t in range(BLOCK):
            for g in range(3):
                b = u * PER_WINDOW + 3 * g
                one, two = row(b, t), row(b + 1, t)
                three = row(b + 2, t) if g < 2 else two
                gathered[u][g, t : t + 1, :] = jnp.where(
                    in_first, one, jnp.where(in_second, two, three)
                )

    rest = jnp.zeros((LANES - COPIES * KPAD, LANES), jnp.float32)
    none = jnp.zeros((KPAD, LANES), jnp.float32)
    results = []
    for u in range(2):
        total = jnp.zeros((BLOCK, LANES), jnp.float32)
        for g in range(3):
            held = []
            for s in range(3):
                b = 3 * g + s
                if b < PER_WINDOW:
                    held.append(ops_ref[class_ref[step * 2 * PER_WINDOW + u * PER_WINDOW + b]])
                else:
                    held.append(none)
            weights = jnp.concatenate(held + [rest], axis=0).astype(jnp.bfloat16)
            values = gathered[u][g]
            high = values.astype(jnp.bfloat16)
            low = (values - high.astype(jnp.float32)).astype(jnp.bfloat16)
            total += jnp.dot(high, weights, preferred_element_type=jnp.float32)
            total += jnp.dot(low, weights, preferred_element_type=jnp.float32)
        results.append(total)
    both = jnp.concatenate(results, axis=0)
    both = both + pltpu.roll(both, LANES - KPAD, 1)
    if turned:
        out_ref[0] = both.T[:KPAD]
    else:
        out_ref[...] = both


def m2l(sources, classes, table, ops, first, steps, turned, slots):
    if turned:
        per = slots // LANES
        shape = (steps // per, KPAD, slots)
        out_spec = pl.BlockSpec((1, KPAD, LANES), lambda i: (i // per, 0, i % per))
    else:
        shape = (steps * LANES, LANES)
        out_spec = pl.BlockSpec((LANES, LANES), lambda i: (i, 0))
    return pl.pallas_call(
        functools.partial(m2l_kernel, first=first, turned=turned),
        grid=(steps,),
        out_shape=jax.ShapeDtypeStruct(shape, jnp.float32),
        in_specs=[
            pl.BlockSpec((8, LANES), lambda i: (first + i, 0), memory_space=pltpu.SMEM),
            SMEM_WHOLE,
            VMEM_WHOLE,
            VMEM_WHOLE,
        ],
        out_specs=out_spec,
        scratch_shapes=[pltpu.VMEM((3, BLOCK, LANES), jnp.float32)] * 2,
        compiler_params=params(),
        cost_estimate=cost(10**6, 150 * 10**6),
        name="m2l_slots" if turned else "m2l_cells",
    )(sources, classes, as_rows(table), ops)


def add_back_kernel(list_ref, count_ref, own_ref, *refs):
    slot_refs, out_ref = refs[:8], refs[8]
    rows, sums = refs[9], refs[10:]
    slots = list_ref.shape[1]
    sums[0][...] = own_ref[...]
    for held in sums[1:]:
        held[...] = jnp.zeros_like(held)
    for n in range(8):
        for k in range(slots // LANES):
            live = (lane_ids((KPAD, LANES)) + k * LANES) < count_ref[n]
            values = jnp.where(live, slot_refs[n][:, k * LANES : (k + 1) * LANES], 0.0)
            at = n * slots + k * LANES
            rows[at : at + LANES, :] = spread(values)

    @pl.loop(0, slots, step=4)
    def _(first):
        for j in range(4):
            to = [pl.ds(list_ref[n, first + j], 1) for n in range(8)]
            old = [sums[n][to[n], :] for n in range(8)]
            new = [old[n] + rows[pl.ds(n * slots + first + j, 1), :] for n in range(8)]
            for n in range(8):
                sums[n][to[n], :] = new[n]

    @pl.loop(0, own_ref.shape[0] // LANES)
    def _(k):
        at = pl.ds(pl.multiple_of(k * LANES, LANES), LANES)
        parts = [held[at, :] for held in sums]
        while len(parts) > 1:
            parts = [a + b for a, b in zip(parts[::2], parts[1::2])]
        out_ref[:, at] = parts[0].T[: out_ref.shape[0]]


def add_back(proxy_list, proxy_count, own_rows, slot_fields, coef_count):
    cell_count = own_rows.shape[0]
    slots = proxy_list.shape[1]
    return pl.pallas_call(
        add_back_kernel,
        out_shape=jax.ShapeDtypeStruct((coef_count, cell_count), jnp.float32),
        in_specs=[SMEM_WHOLE, SMEM_WHOLE] + [VMEM_WHOLE] * 9,
        out_specs=VMEM_WHOLE,
        scratch_shapes=[pltpu.VMEM((8 * slots, LANES), jnp.float32)]
        + [pltpu.VMEM((cell_count, LANES), jnp.float32)] * 8,
        compiler_params=params(),
        cost_estimate=cost(10**6, 30 * 10**6),
        name="add_back",
    )(proxy_list, proxy_count, own_rows, *slot_fields)


def carve_kernel(mesh_ref, out_ref, sems, *, first):
    sources, count, rows, width = out_ref.shape
    copies = [
        pltpu.make_async_copy(
            mesh_ref.at[pl.ds(first, count), pl.ds(s * rows, rows), :], out_ref.at[s], sems.at[s]
        )
        for s in range(sources)
    ]
    for copy in copies:
        copy.start()
    for copy in copies:
        copy.wait()


def carve(mesh, first, count, sources):
    rows, width = mesh.shape[1] // sources, mesh.shape[2]
    return pl.pallas_call(
        functools.partial(carve_kernel, first=first),
        out_shape=jax.ShapeDtypeStruct((sources, count, rows, width), jnp.float32),
        in_specs=[pl.BlockSpec(memory_space=pl.ANY)],
        out_specs=pl.BlockSpec(memory_space=pl.ANY),
        scratch_shapes=[pltpu.SemaphoreType.DMA((sources,))],
        compiler_params=params(),
        cost_estimate=cost(0, 8 * count * sources * rows * width),
        name="carve",
    )(mesh)


def deposit_kernel(code_ref, value_ref, *refs):
    sources = code_ref.shape[0]
    outs, others = refs[:sources], refs[sources:]
    lanes = lane_ids((1, LANES))
    for held in refs:
        held[...] = jnp.zeros_like(held)
    half = code_ref.shape[1] // 2

    @pl.loop(0, half, step=4)
    def _(first):
        for j in range(4):
            at = [(s, first + j + h * half) for h in range(2) for s in range(sources)]
            codes = [code_ref[i] for i in at]
            to = [pl.ds(code >> LANE_SHIFT, 1) for code in codes]
            old = [held[rows, :] for held, rows in zip(refs, to)]
            new = [
                row + jnp.where(lanes == (code & (LANES - 1)), value_ref[i], 0.0)
                for row, code, i in zip(old, codes, at)
            ]
            for held, rows, row in zip(refs, to, new):
                held[rows, :] = row

    for out_ref, held in zip(outs, others):
        out_ref[...] = out_ref[...] + held[...]


def deposit(codes, values, rows):
    sources = codes.shape[0]
    return pl.pallas_call(
        deposit_kernel,
        out_shape=(jax.ShapeDtypeStruct((rows, LANES), jnp.float32),) * sources,
        in_specs=[SMEM_WHOLE, SMEM_WHOLE],
        out_specs=(VMEM_WHOLE,) * sources,
        scratch_shapes=[pltpu.VMEM((rows, LANES), jnp.float32)] * sources,
        compiler_params=params(),
        cost_estimate=cost(10**6, 75 * 10**6),
        name="deposit",
    )(codes, values)


def fourier_tables(length):
    points, half = length // 2, length // 4
    positions = np.arange(points)
    scale = 1.0 / np.sqrt(length)
    parts = []
    for odd in range(2):
        ks = 2 * np.arange(half) + odd
        angles = (positions[:, None] * ks[None, :] % length) * (2.0 * np.pi / length)
        imag = -np.sin(angles) * scale
        if not odd:
            imag[:, 0] = np.where(positions % 2 == 0, scale, -scale)
        parts.append(np.concatenate([np.cos(angles) * scale, imag], axis=1))
    whole = np.stack(parts)
    high = whole.astype(ml_dtypes.bfloat16)
    low = (whole - high.astype(np.float64)).astype(ml_dtypes.bfloat16)
    return high, low


def fourier_kernel(*refs, sources):
    mesh_ref, add_refs = refs[0], refs[1 : 1 + sources]
    high_ref, low_ref = refs[1 + sources], refs[2 + sources]
    out_ref = refs[-1]
    rows, width = mesh_ref.shape[1:]
    pieces = []
    for s in range(sources):
        for h in range(width // LANES):
            pieces.append(
                mesh_ref[s, :, h * LANES : (h + 1) * LANES]
                + add_refs[s][h * rows : (h + 1) * rows, :]
            )
    mid = len(pieces) // 2
    halves = []
    for odd in range(2):
        if odd:
            folded = [a - b for a, b in zip(pieces[:mid], pieces[mid:])]
        else:
            folded = [a + b for a, b in zip(pieces[:mid], pieces[mid:])]
        values = jnp.concatenate(folded, axis=1)
        high = values.astype(jnp.bfloat16)
        low = (values - high.astype(jnp.float32)).astype(jnp.bfloat16)
        both = jnp.dot(
            jnp.concatenate([high, low], axis=0), high_ref[odd], preferred_element_type=jnp.float32
        )
        halves.append(
            both[:rows]
            + both[rows:]
            + jnp.dot(high, low_ref[odd], preferred_element_type=jnp.float32)
        )
    lanes = lane_ids((rows, LANES))
    is_first = lanes == 0
    is_odd = (lanes & 1) == 1
    steps = lanes >> 1
    tiles = len(pieces)
    per = tiles // 4

    def tile(odd, part, j):
        at = (part * per + j) * LANES
        return halves[odd][:, at : at + LANES]

    def pick(value, lane):
        return jnp.take_along_axis(value, lane, axis=1, mode="promise_in_bounds")

    for j in range(tiles):
        for part in range(2):
            if j < tiles // 2:
                at = BLOCK * j
                lane = (at % LANES) + steps
                even = pick(tile(0, part, at // LANES), lane)
                odd = pick(tile(1, part, at // LANES), lane)
                if j == 0 and part == 1:
                    even = jnp.where(is_first, 0.0, even)
            else:
                at = BLOCK * (tiles - j)
                last = (at - 1) // LANES
                even = pick(tile(0, part, last), (at - steps) & (LANES - 1))
                odd = pick(tile(1, part, last), ((at - 1) % LANES) - steps)
                if at % LANES == 0 and j > tiles // 2:
                    even = jnp.where(is_first, tile(0, part, at // LANES), even)
                if part == 1:
                    even, odd = -even, -odd
                if j == tiles // 2:
                    even = jnp.where(is_first, 0.0 if part else tile(0, 1, 0), even)
            out_ref[part, 0, :, j * LANES : (j + 1) * LANES] = jnp.where(is_odd, odd, even)


def fourier(mesh_part, count, adds, tables, first, planes, so_far, rows):
    sources, _, width = mesh_part.shape
    length = sources * width
    add_rows = (width // LANES) * rows
    operands = [mesh_part, *adds, *tables]
    in_specs = (
        [pl.BlockSpec((sources, rows, width), lambda p: (0, p, 0))]
        + [pl.BlockSpec((add_rows, LANES), lambda p: (first + p, 0))] * sources
        + [
            pl.BlockSpec((2, length // 2, length // 2), lambda p: (0, 0, 0), pipeline_mode=pl.Buffered(1))
        ]
        * 2
    )
    aliases = {}
    if so_far is not None:
        aliases = {len(operands): 0}
        operands.append(so_far)
        in_specs.append(pl.BlockSpec(memory_space=pl.ANY))
    return pl.pallas_call(
        functools.partial(fourier_kernel, sources=sources),
        grid=(count,),
        out_shape=jax.ShapeDtypeStruct((2, planes, rows, length), jnp.float32),
        in_specs=in_specs,
        out_specs=pl.BlockSpec((2, 1, rows, length), lambda p: (0, first + p, 0, 0)),
        input_output_aliases=aliases,
        compiler_params=params(),
        cost_estimate=cost(10**6, count * 10 * 10**6),
        name="fourier",
    )(*operands)


def after(value, *others):
    return lax.optimization_barrier((value, *others))[0]


def on_device(
    multipoles,
    proxy_list,
    proxy_count,
    pair_source,
    pair_target,
    block_class,
    m2l_ops,
    cell_mesh,
    pm_density,
    *,
    n_gx,
    n_gy,
):
    coef_count, cell_count = multipoles.shape
    slots = proxy_list.shape[2]
    planes, mesh_rows, width = pm_density.shape
    own_rows = mesh_rows // n_gx
    domains = n_gx * n_gy
    lists, counts = proxy_list[0], proxy_count[0]

    def send(part):
        return lax.all_to_all(part, "gx", 0, 0, tiled=True)

    spans = []
    first = 0
    for size in CHUNKS:
        spans.append((first, size))
        first += size

    held = jnp.stack([cell_mesh.astype(jnp.float32), DEPOSIT_SCALE * multipoles[0]])
    held = held.reshape(1, -1, width)
    start = pm_density[0].reshape(n_gx, own_rows, width)
    parts = [send(jnp.concatenate([start, jnp.broadcast_to(held, (n_gx, *held.shape[1:]))], axis=1))]
    carved = [
        carve(pm_density, at, size, n_gx).reshape(n_gx, size * own_rows, width)
        for at, size in spans[1:]
    ]

    cells = jnp.pad(multipoles, ((0, KPAD - coef_count), (0, 0)))
    base = cell_count + 8 * slots
    table, top_own = own_table(cells, base + TOP * domains)
    outgoing = pack(table, cell_count, lists, counts)
    arrived = exchange(outgoing, n_gx, n_gy)

    top = pair_source - base
    top = base + ((top >> 4) & 1) * (TOP_ROWS * domains) + (top >> 5) * TOP_ROWS + (top & 15)
    wanted = jnp.where(pair_source < base, pair_source, top)
    sources = order(((wanted << SHIFT) | (pair_target & (BLOCK - 1))).reshape(-1, LANES))

    turned_ops = jnp.pad(
        m2l_ops.transpose(0, 2, 1), ((0, 0), (0, KPAD - coef_count), (0, KPAD - coef_count))
    )
    high = lax.reduce_precision(turned_ops, 8, 7)
    ops = jnp.concatenate([high, turned_ops - high], axis=2)
    ops = jnp.pad(ops, ((0, 0), (0, 0), (0, LANES - 2 * KPAD)))

    tops = jnp.broadcast_to(top_own, (domains, TOP_ROWS, LANES))
    tops = after(tops, parts[0], outgoing[0], sources, ops)
    tops = lax.all_to_all(tops, ("gx", "gy"), 0, 0, tiled=True)
    parts.append(send(after(carved[0], tops)))

    near = parts[0][:, own_rows:].reshape(n_gx, 2, cell_count)
    place = near[:, 0].astype(jnp.int32)
    plane = place // (mesh_rows * width)
    row = place // width % mesh_rows
    column = place % width
    tiles = width // LANES
    add_rows = planes * tiles * own_rows
    at_row = (plane * tiles + column // LANES) * own_rows + row % own_rows
    mine = row // own_rows == lax.axis_index("gx")
    codes = jnp.where(mine, at_row, add_rows) * LANES + column % LANES
    adds = deposit(codes, near[:, 1], add_rows + 8)

    table = whole_table(table, arrived, tops.reshape(-1, LANES))
    cell_steps = cell_count // LANES
    slot_steps = 8 * slots // LANES
    slot_fields = m2l(sources, block_class, table, ops, cell_steps, slot_steps, True, slots)
    returned = exchange([slot_fields[m] for m in range(8)], n_gx, n_gy)
    parts.append(send(after(carved[1], parts[1], slot_fields, adds[0])))
    own_fields = m2l(sources, block_class, table, ops, 0, cell_steps, False, slots)

    tables = fourier_tables(n_gx * width)
    spectrum = None
    for i, (at, size) in enumerate(spans):
        if i == 2:
            parts.append(send(after(carved[2], parts[2], own_fields, spectrum)))
        spectrum = fourier(parts[i], size, adds, tables, at, planes, spectrum, own_rows)

    field_tensors = add_back(lists, counts, own_fields, returned, coef_count)
    return (field_tensors, spectrum)


def solution(mesh):
    placed = (
        P(None, ("gx", "gy")),
        P(("gx", "gy"), None, None),
        P(("gx", "gy"), None),
        P(("gx", "gy")),
        P(("gx", "gy")),
        P(("gx", "gy")),
        P(),
        P(("gx", "gy")),
        P("gy", None, "gx"),
    )
    return jax.shard_map(
        functools.partial(on_device, n_gx=mesh.shape["gx"], n_gy=mesh.shape["gy"]),
        mesh=mesh,
        in_specs=placed,
        out_specs=(P(None, ("gx", "gy")), P(None, "gy", "gx", None)),
        check_vma=False,
    )
```

time: 570 us -> 476 us (0.84)
  blocking collectives: 83.7 us -> 0 us
  Pallas kernels: 311 us -> 290 us
  waiting for transfers between devices: 83.2 us -> 101 us
  local copies, waits for them, and re-layouts: 29.3 us -> 22.7 us
    ppermute x16, waiting for transfers between devices: 0.04 us -> 91.6 us  [exchange(): arrived[7 - m] = lax.ppermute(blocks[m], ('gx', 'gy'), pairs)]
    all_gather x2 -> x0, blocking collectives: 83.7 us -> none  [the longest x1 48.4 us: on_device(): near = lax.all_gather(held, 'gx', axis=0)]
    all_to_all x4, waiting for transfers between devices: 83.2 us -> 9.84 us  [send(): return lax.all_to_all(part, 'gx', 0, 0, tiled=True)]
    pallas_call x1, Pallas kernels: 116 us -> 45.9 us  [deposit(): pl.pallas_call(deposit_kernel, out_shape=(jax.ShapeDtypeStruct((rows, LAN...]
    pallas_call x8 -> x12, Pallas kernels: 167 us -> 225 us  [the longest x3 99.7 us: carve(): pl.pallas_call(functools.partial(carve_kernel, first=first), out_shape=ja...]
    reshape x4 -> x1, local copies, waits for them, and re-layouts: 9.23 us -> 0.09 us  [on_device(): near = parts[0][:, own_rows:].reshape(n_gx, 2, cell_count)]
    pallas_call x1, Pallas kernels: 15.5 us -> 7.39 us  [order(): pl.pallas_call(order_kernel, out_shape=jax.ShapeDtypeStruct(packed.shape,...]
    unnamed x48 -> x70, local copies, waits for them, and re-layouts: 10.2 us -> 18.1 us
  transfers between devices with their start and end apart: 20 -> 21, of which waited for: 2 -> 9; matrix products, arithmetic and copies ran while one was open for 4% -> 2% of each run, Pallas kernels for 53% -> 60%
where the time goes in v2:
time: 476 us; the launch traced here: 472 us
  Pallas kernels  290 us (61%)
  waiting for transfers between devices  101 us (21%)
  starting transfers between devices  50.4 us (11%)
  local copies, waits for them, and re-layouts  22.7 us (5%)
  other arithmetic  6.98 us (1%)
    pallas_call x3, Pallas kernels, carve(): pl.pallas_call(functools.partial(carve_kernel, first=first), out_shape=ja...  99.7 us
    ppermute x16, waiting for transfers between devices, exchange(): arrived[7 - m] = lax.ppermute(blocks[m], ('gx', 'gy'), pairs)  91.6 us
    pallas_call x2, Pallas kernels, m2l(): pl.pallas_call(functools.partial(m2l_kernel, first=first, turned=turned),...  80 us
    pallas_call x1, Pallas kernels, deposit(): pl.pallas_call(deposit_kernel, out_shape=(jax.ShapeDtypeStruct((rows, LAN...  45.9 us
    pallas_call x4, Pallas kernels, fourier(): pl.pallas_call(functools.partial(fourier_kernel, sources=sources), grid=(...  28.2 us
    all_to_all x4, starting transfers between devices, send(): return lax.all_to_all(part, 'gx', 0, 0, tiled=True)  26.4 us
    ppermute x16, starting transfers between devices, exchange(): arrived[7 - m] = lax.ppermute(blocks[m], ('gx', 'gy'), pairs)  18.2 us
    unnamed x70, local copies, waits for them, and re-layouts  18.1 us
  transfers between devices with their start and end apart: 21, of which 9 were waited for; matrix products, arithmetic and copies ran while one was open for 2% of the time, Pallas kernels for 60%

profile of v2, /device:TPU:8, one launch (start us, length us, event | category | flops | bytes accessed | tf_op | source)
XLA Modules:
  0.0 472.2 jit_solution(5230081691100370895)
XLA Ops:
  0.6 0.8 convert_element_type.15
  1.4 0.9 slice_multiply_fusion
  2.4 1.4 slice.39
  3.9 1.1 pad_maximum_fusion
  5.0 5.3 %all-to-all-start = ((f32[4,288,256]{2,1,0:T(8,128)}), f32[4,288,256]{2,1,0:T(8,128)}, u32[]{:S(2)}, u32[]{:S(2)}) async-start(f32[4,288,256]{2,1,0:T(8,128)} %pad_maximum_fusion), calls=%async_computation | async-start | bytes 2359296 | tf_op jit(solution)/shard_map/all_to_all | solution.py:537
  10.4 4.2 copy.17
  14.6 0.1 fusion.2.packed_ref
  14.8 7.4 %order.1.source_ref = s32[512,128]{1,0:T(8,128)S(1)} custom-call(s32[512,128]{1,0:T(8,128)S(1)} %fusion.2.packed_ref), custom_call_target="tpu_custom_call" | custom-call | flops 1000000 | bytes 20000000 | tf_op jit(solution)/shard_map/order/pallas_call | solution.py:195
  22.2 3.3 own_table.1
  25.6 11.2 %pack.1 = (f32[40,512]{1,0:T(8,128)}, f32[40,512]{1,0:T(8,128)S(1)}, f32[40,512]{1,0:T(8,128)S(1)}, f32[40,512]{1,0:T(8,128)S(1)}, f32[40,512]{1,0:T(8,128)S(1)}...) custom-call(s32[8,512]{1,0:T(8,128)S(1)} %bitcast.42, s32[8]{0:T(128)S(1)} %bitcast.44, ...), custom_call_target="tpu_custom_call" | custom-call | flops 1000000 | bytes 25000000 | tf_op jit(solution)/shard_map/pack/pallas_call | solution.py:147
  36.8 0.5 pad_reduce-precision_fusion
  37.4 0.1 copy-done.17
  37.4 0.1 copy-done.19
  37.5 0.1 copy-done.23
  37.6 3.0 select_maximum_fusion.ops_ref
  40.6 0.7 broadcast_in_dim.14
  41.3 5.9 %all-to-all-start.1 = ((f32[32,16,128]{2,1,0:T(8,128)}), f32[32,16,128]{2,1,0:T(8,128)}, u32[]{:S(2)}, u32[]{:S(2)}) async-start(f32[32,16,128]{2,1,0:T(8,128)} %broadcast_in_dim.14), calls=%async_computation.1 | async-start | bytes 524288 | tf_op jit(solution)/shard_map/all_to_all | solution.py:574
  47.2 96.4 %carve.5 = f32[4,3,256,256]{3,2,1,0:T(8,128)} custom-call(f32[8,1024,256]{2,1,0:T(8,128)} %mesh_ref.5), custom_call_target="tpu_custom_call" | custom-call | bytes 6291456 | tf_op jit(solution)/shard_map/carve/pallas_call | solution.py:343
  143.7 5.3 %all-to-all-start.2 = ((f32[4,768,256]{2,1,0:T(8,128)}), f32[4,768,256]{2,1,0:T(8,128)}, u32[]{:S(2)}, u32[]{:S(2)}) async-start(f32[4,768,256]{2,1,0:T(8,128)} %bitcast.19), calls=%async_computation.2 | async-start | bytes 6291456 | tf_op jit(solution)/shard_map/all_to_all | solution.py:537
  149.0 1.7 collective-permute-start.7
  150.7 0.1 collective-permute-start
  150.7 1.6 collective-permute-start.1
  152.4 5.9 %collective-permute-start.2 = (f32[40,512]{1,0:T(8,128)S(1)}, f32[40,512]{1,0:T(8,128)}, u32[]{:S(2)}, u32[]{:S(2)}) collective-permute-start(f32[40,512]{1,0:T(8,128)S(1)} %copy-done.24), channel_id=1, source_target_pairs={{0,15},{1,8},{2,9},{3,10},{4,11},{5,12},{6,13},{7,14},{8,23},{9,16... | collective-permute-start | bytes 245768 | tf_op jit(solution)/shard_map/ppermute | solution.py:172
  158.3 1.9 carve.4
  160.2 1.6 copy-done.9
  161.9 0.9 slice.60
  162.8 0.1 reshape.39
  162.9 0.1 fusion.21
  163.0 59.9 %collective-permute-done.refs_0_ = f32[40,512]{1,0:T(8,128)} collective-permute-done((f32[40,512]{1,0:T(8,128)S(1)}, f32[40,512]{1,0:T(8,128)}, u32[]{:S(2)}, u32[]{:S(2)}) %collective-permute-start) | collective-permute-done | bytes 81952 | tf_op jit(solution)/shard_map/ppermute | solution.py:172
  222.9 0.5 collective-permute-start.4
  223.4 1.1 collective-permute-done.1.refs_1_
  224.6 0.9 collective-permute-done.2.refs_2_
  225.5 0.5 fusion.14.code_ref
  226.0 45.9 %deposit.1 = (f32[4104,128]{1,0:T(8,128)S(1)}, f32[4104,128]{1,0:T(8,128)S(1)}, f32[4104,128]{1,0:T(8,128)}, f32[4104,128]{1,0:T(8,128)}) custom-call(s32[4,4096]{1,0:T(4,128)S(1)} %fusion.14.code_ref, f32[4,4096]{1,0:T(4,128)S(1)} %bitcast.41), custom_call_target="tpu_custom_call" | custom-call | flops 1000000 | bytes 75000000 | tf_op jit(solution)/shard_map/deposit/pallas_call | solution.py:383
  271.9 1.4 copy-done.4
  273.3 2.3 copy-done.1
  275.6 2.6 whole_table.1
  278.3 2.2 copy-done.2
  280.4 40.1 %m2l_slots.1 = f32[8,40,512]{2,1,0:T(8,128)S(1)} custom-call(s32[512,128]{1,0:T(8,128)S(1)} %order.1.source_ref, s32[1024]{0:T(1024)S(1)} %copy-done.15, f32[9216,1,128]{2,1,0:T(1,128)} %bitcast.37, f32[189,40,128]{2,1,0:T(8,128)S(1)} %copy-done.3), custom_call_target="tpu_custom_call" | custom-call | flops 1000000 | bytes 150000000 | tf_op jit(solution)/shard_map/m2l_slots/pallas_call | solution.py:261
  320.5 0.8 copy-done.13
  321.3 8.0 %all-to-all-start.3 = ((f32[4,768,256]{2,1,0:T(8,128)}), f32[4,768,256]{2,1,0:T(8,128)}, u32[]{:S(2)}, u32[]{:S(2)}) async-start(f32[4,768,256]{2,1,0:T(8,128)} %bitcast.39), calls=%async_computation.3 | async-start | bytes 6291456 | tf_op jit(solution)/shard_map/all_to_all | solution.py:537
  329.3 1.4 carve.3
  330.7 1.0 copy-done.12
  331.7 4.9 %fourier.4.refs_7_ = f32[2,8,256,1024]{3,2,1,0:T(8,128)} custom-call(f32[4,288,256]{2,1,0:T(8,128)} %all-to-all-done.refs_0_, f32[4104,128]{1,0:T(8,128)S(1)} %get-tuple-element.32.refs_1_, f32[4104,128]{1,0:T(8,128)} %copy-done.4, f32[4104,128]{1,0:T(8,128)} %get-tuple-element.35.refs_3_, f32[4104,128]{1,0:T(8,128)} %get-tuple-element.36.refs_4_, ...), custom_call_target="tpu_custom_call" | custom-call | flops 1000000 | bytes 10000000 | tf_op jit(solution)/shard_map/fourier/pallas_call | solution.py:498
  336.6 39.9 %m2l_cells.1.own_ref = f32[4096,128]{1,0:T(8,128)S(1)} custom-call(s32[512,128]{1,0:T(8,128)S(1)} %order.1.source_ref, s32[1024]{0:T(1024)S(1)} %copy-done.15, f32[9216,1,128]{2,1,0:T(1,128)} %bitcast.38, f32[189,40,128]{2,1,0:T(8,128)} %select_maximum_fusion.ops_ref), custom_call_target="tpu_custom_call" | custom-call | flops 1000000 | bytes 150000000 | tf_op jit(solution)/shard_map/m2l_cells/pallas_call | solution.py:261
  376.5 1.3 copy-done.10
  377.9 9.2 %fourier.5.refs_7_ = f32[2,8,256,1024]{3,2,1,0:T(8,128)} custom-call(f32[4,768,256]{2,1,0:T(8,128)} %all-to-all-done.2.refs_0_, f32[4104,128]{1,0:T(8,128)S(1)} %get-tuple-element.32.refs_1_, f32[4104,128]{1,0:T(8,128)} %copy-done.4, f32[4104,128]{1,0:T(8,128)} %get-tuple-element.35.refs_3_, ...), custom_call_target="tpu_custom_call", output_to_operand_aliasing={{}: (7, {})} | custom-call | flops 1000000 | bytes 30000000 | tf_op jit(solution)/shard_map/fourier/pallas_call | solution.py:498
  387.1 9.8 %all-to-all-done.3.refs_0_ = f32[4,768,256]{2,1,0:T(8,128)} async-done(((f32[4,768,256]{2,1,0:T(8,128)}), f32[4,768,256]{2,1,0:T(8,128)}, u32[]{:S(2)}, u32[]{:S(2)}) %all-to-all-start.3) | async-done | bytes 3145760 | tf_op jit(solution)/shard_map/all_to_all | solution.py:537
  396.9 7.8 %all-to-all-start.4 = ((f32[4,256,256]{2,1,0:T(8,128)}), f32[4,256,256]{2,1,0:T(8,128)}, u32[]{:S(2)}, u32[]{:S(2)}) async-start(f32[4,256,256]{2,1,0:T(8,128)} %bitcast.40), calls=%async_computation.4 | async-start | bytes 2097152 | tf_op jit(solution)/shard_map/all_to_all | solution.py:537
  404.7 1.3 slice_bitcast_fusion
  406.0 1.9 collective-permute-start.15
  407.9 3.5 collective-permute-start.14
  411.4 2.6 collective-permute-start.12
  414.1 19.6 %collective-permute-done.15.refs_7_ = f32[40,512]{1,0:T(8,128)S(1)} collective-permute-done((f32[40,512]{1,0:T(8,128)S(1)}, f32[40,512]{1,0:T(8,128)S(1)}, u32[]{:S(2)}, u32[]{:S(2)}) %collective-permute-start.15) | collective-permute-done | bytes 81952 | tf_op jit(solution)/shard_map/ppermute | solution.py:172
  433.7 0.3 collective-permute-start.10
  434.0 1.7 collective-permute-done.14.refs_6_
  435.7 2.7 collective-permute-done.13.refs_5_
  438.4 2.4 collective-permute-done.9.refs_1_
  440.8 3.3 collective-permute-done.8.refs_0_
  444.0 1.6 copy-done.11
  445.6 11.2 %add_back.1 = f32[35,4096]{1,0:T(8,128)} custom-call(s32[8,512]{1,0:T(8,128)S(1)} %bitcast.43, s32[8]{0:T(128)S(1)} %bitcast.45, f32[4096,128]{1,0:T(8,128)S(1)} %copy-done.11, f32[40,512]{1,0:T(8,128)S(1)} %collective-permute-done.8.refs_0_, f32[40,512]{1,0:T(8,128)S(1)} %collective-permute-done.9.refs_1_, f32[40,512]{1,0:T(8,128)S(1)} %collective-permute-done.10.refs_2_, ...), custom_call_target="tpu_custom_call" | custom-call | flops 1000000 | bytes 30000000 | tf_op jit(solution)/shard_map/add_back/pallas_call | solution.py:314
  456.8 9.2 %fourier.6.refs_7_ = f32[2,8,256,1024]{3,2,1,0:T(8,128)} custom-call(f32[4,768,256]{2,1,0:T(8,128)} %all-to-all-done.3.refs_0_, f32[4104,128]{1,0:T(8,128)S(1)} %get-tuple-element.32.refs_1_, f32[4104,128]{1,0:T(8,128)} %copy-done.4, f32[4104,128]{1,0:T(8,128)} %get-tuple-element.35.refs_3_, ...), custom_call_target="tpu_custom_call", output_to_operand_aliasing={{}: (7, {})} | custom-call | flops 1000000 | bytes 30000000 | tf_op jit(solution)/shard_map/fourier/pallas_call | solution.py:498
  466.1 1.2 copy-done.8
  467.3 4.9 %fourier.7 = f32[2,8,256,1024]{3,2,1,0:T(8,128)} custom-call(f32[4,256,256]{2,1,0:T(8,128)} %all-to-all-done.4.refs_0_, f32[4104,128]{1,0:T(8,128)S(1)} %get-tuple-element.32.refs_1_, f32[4104,128]{1,0:T(8,128)} %copy-done.4, f32[4104,128]{1,0:T(8,128)} %get-tuple-element.35.refs_3_, ...), custom_call_target="tpu_custom_call", output_to_operand_aliasing={{}: (7, {})} | custom-call | flops 1000000 | bytes 10000000 | tf_op jit(solution)/shard_map/fourier/pallas_call | solution.py:498
  (80 shorter events, 0.4 us)
Async XLA Ops:
  0.6 9.7 %copy-start.31 = (f32[35,4096]{1,0:T(8,128)S(1)}, f32[35,4096]{1,0:T(8,128)}, u32[]{:S(2)}) copy-start(f32[35,4096]{1,0:T(8,128)} %param.11) | copy-start | bytes 1720324
  2.4 7.9 %copy-start.30 = (f32[189,35,35]{0,2,1:T(8,128)S(1)}, f32[189,35,35]{0,2,1:T(8,128)}, u32[]{:S(2)}) copy-start(f32[189,35,35]{0,2,1:T(8,128)} %param.17) | copy-start | bytes 2778304
  5.0 35.6 %all-to-all-start = ((f32[4,288,256]{2,1,0:T(8,128)}), f32[4,288,256]{2,1,0:T(8,128)}, u32[]{:S(2)}, u32[]{:S(2)}) async-start(f32[4,288,256]{2,1,0:T(8,128)} %pad_maximum_fusion), calls=%async_computation | async-start | bytes 2359296 | tf_op jit(solution)/shard_map/all_to_all | solution.py:537
  10.3 4.3 copy-start.32
  10.3 4.3 copy-start.33
  10.4 15.2 %copy-start.14 = (s32[1,8,512]{2,1,0:T(8,128)S(1)}, s32[1,8,512]{2,1,0:T(8,128)}, u32[]{:S(2)}) copy-start(s32[1,8,512]{2,1,0:T(8,128)} %param.12) | copy-start | bytes 49156
  10.4 15.2 %copy-start.16 = (s32[1,8]{1,0:T(1,128)S(1)}, s32[1,8]{1,0:T(1,128)}, u32[]{:S(2)}) copy-start(s32[1,8]{1,0:T(1,128)} %param.13) | copy-start | bytes 100
  14.6 22.2 %copy-start.29 = (f32[189,35,35]{1,2,0:T(8,128)S(1)}, f32[189,35,35]{1,2,0:T(8,128)}, u32[]{:S(2)}) copy-start(f32[189,35,35]{1,2,0:T(8,128)} %copy.17) | copy-start | bytes 2778304
  25.5 11.8 %copy-start = (f32[9216,128]{1,0:T(8,128)}, f32[9216,128]{1,0:T(8,128)S(1)}, u32[]{:S(2)}) copy-start(f32[9216,128]{1,0:T(8,128)S(1)} %get-tuple-element.20.refs_9_) | copy-start | bytes 14155780
  36.8 0.6 copy-start.17
  36.8 0.7 copy-start.19
  36.8 0.7 copy-start.21
  36.8 0.7 copy-start.23
  36.8 0.8 copy-start.25
  36.8 0.8 copy-start.27
  41.3 102.4 %all-to-all-start.1 = ((f32[32,16,128]{2,1,0:T(8,128)}), f32[32,16,128]{2,1,0:T(8,128)}, u32[]{:S(2)}, u32[]{:S(2)}) async-start(f32[32,16,128]{2,1,0:T(8,128)} %broadcast_in_dim.14), calls=%async_computation.1 | async-start | bytes 524288 | tf_op jit(solution)/shard_map/all_to_all | solution.py:574
  143.6 7.0 %copy-start.28 = (f32[40,512]{1,0:T(8,128)S(1)}, f32[40,512]{1,0:T(8,128)}, u32[]{:S(2)}) copy-start(f32[40,512]{1,0:T(8,128)} %copy-done.27) | copy-start | bytes 245764
  143.6 7.1 %copy-start.26 = (f32[40,512]{1,0:T(8,128)S(1)}, f32[40,512]{1,0:T(8,128)}, u32[]{:S(2)}) copy-start(f32[40,512]{1,0:T(8,128)} %copy-done.25) | copy-start | bytes 245764
  143.7 8.7 %copy-start.24 = (f32[40,512]{1,0:T(8,128)S(1)}, f32[40,512]{1,0:T(8,128)}, u32[]{:S(2)}) copy-start(f32[40,512]{1,0:T(8,128)} %copy-done.23) | copy-start | bytes 245764
  143.7 14.6 %copy-start.22 = (f32[40,512]{1,0:T(8,128)S(1)}, f32[40,512]{1,0:T(8,128)}, u32[]{:S(2)}) copy-start(f32[40,512]{1,0:T(8,128)} %copy-done.21) | copy-start | bytes 245764
  143.7 176.8 %all-to-all-start.2 = ((f32[4,768,256]{2,1,0:T(8,128)}), f32[4,768,256]{2,1,0:T(8,128)}, u32[]{:S(2)}, u32[]{:S(2)}) async-start(f32[4,768,256]{2,1,0:T(8,128)} %bitcast.19), calls=%async_computation.2 | async-start | bytes 6291456 | tf_op jit(solution)/shard_map/all_to_all | solution.py:537
  149.0 124.3 %collective-permute-start.7 = (f32[40,512]{1,0:T(8,128)}, f32[40,512]{1,0:T(8,128)S(1)}, u32[]{:S(2)}, u32[]{:S(2)}) collective-permute-start(f32[40,512]{1,0:T(8,128)} %get-tuple-element.28), channel_id=1, source_target_pairs={{0,31},{1,24},{2,25},{3,26},{4,27},{5,28},{6,29},{7,30},{8,7},{9,0... | collective-permute-start | bytes 245768 | tf_op jit(solution)/shard_map/ppermute | solution.py:172
  150.7 72.3 %collective-permute-start = (f32[40,512]{1,0:T(8,128)S(1)}, f32[40,512]{1,0:T(8,128)}, u32[]{:S(2)}, u32[]{:S(2)}) collective-permute-start(f32[40,512]{1,0:T(8,128)S(1)} %copy-done.28), channel_id=1, source_target_pairs={{0,9},{1,10},{2,11},{3,12},{4,13},{5,14},{6,15},{7,8},{8,17},{9,18... | collective-permute-start | bytes 245768 | tf_op jit(solution)/shard_map/ppermute | solution.py:172
  150.7 73.9 %collective-permute-start.1 = (f32[40,512]{1,0:T(8,128)S(1)}, f32[40,512]{1,0:T(8,128)}, u32[]{:S(2)}, u32[]{:S(2)}) collective-permute-start(f32[40,512]{1,0:T(8,128)S(1)} %copy-done.26), channel_id=1, source_target_pairs={{0,8},{1,9},{2,10},{3,11},{4,12},{5,13},{6,14},{7,15},{8,16},{9,17... | collective-permute-start | bytes 245768 | tf_op jit(solution)/shard_map/ppermute | solution.py:172
  152.4 73.1 %collective-permute-start.2 = (f32[40,512]{1,0:T(8,128)S(1)}, f32[40,512]{1,0:T(8,128)}, u32[]{:S(2)}, u32[]{:S(2)}) collective-permute-start(f32[40,512]{1,0:T(8,128)S(1)} %copy-done.24), channel_id=1, source_target_pairs={{0,15},{1,8},{2,9},{3,10},{4,11},{5,12},{6,13},{7,14},{8,23},{9,16... | collective-permute-start | bytes 245768 | tf_op jit(solution)/shard_map/ppermute | solution.py:172
  158.3 115.0 %collective-permute-start.3 = (f32[40,512]{1,0:T(8,128)S(1)}, f32[40,512]{1,0:T(8,128)}, u32[]{:S(2)}, u32[]{:S(2)}) collective-permute-start(f32[40,512]{1,0:T(8,128)S(1)} %copy-done.22), channel_id=1, source_target_pairs={{0,1},{1,2},{2,3},{3,4},{4,5},{5,6},{6,7},{7,0},{8,9},{9,10},{10,1... | collective-permute-start | bytes 245768 | tf_op jit(solution)/shard_map/ppermute | solution.py:172
  158.3 64.6 %copy-start.20 = (f32[40,512]{1,0:T(8,128)S(1)}, f32[40,512]{1,0:T(8,128)}, u32[]{:S(2)}) copy-start(f32[40,512]{1,0:T(8,128)} %copy-done.19) | copy-start | bytes 245764
  158.3 66.3 %copy-start.18 = (f32[40,512]{1,0:T(8,128)S(1)}, f32[40,512]{1,0:T(8,128)}, u32[]{:S(2)}) copy-start(f32[40,512]{1,0:T(8,128)} %copy-done.17) | copy-start | bytes 245764
  160.2 1.7 copy-start.9
  222.9 50.3 %collective-permute-start.4 = (f32[40,512]{1,0:T(8,128)S(1)}, f32[40,512]{1,0:T(8,128)S(1)}, u32[]{:S(2)}, u32[]{:S(2)}) collective-permute-start(f32[40,512]{1,0:T(8,128)S(1)} %copy-done.20), channel_id=1, source_target_pairs={{0,7},{1,0},{2,1},{3,2},{4,3},{5,4},{6,5},{7,6},{8,15},{9,8},{10,9... | collective-permute-start | bytes 245768 | tf_op jit(solution)/shard_map/ppermute | solution.py:172
  224.6 48.7 %collective-permute-start.5 = (f32[40,512]{1,0:T(8,128)S(1)}, f32[40,512]{1,0:T(8,128)S(1)}, u32[]{:S(2)}, u32[]{:S(2)}) collective-permute-start(f32[40,512]{1,0:T(8,128)S(1)} %copy-done.18), channel_id=1, source_target_pairs={{0,25},{1,26},{2,27},{3,28},{4,29},{5,30},{6,31},{7,24},{8,1},{9,2... | collective-permute-start | bytes 245768 | tf_op jit(solution)/shard_map/ppermute | solution.py:172
  225.5 47.8 %collective-permute-start.6 = (f32[40,512]{1,0:T(8,128)S(1)}, f32[40,512]{1,0:T(8,128)S(1)}, u32[]{:S(2)}, u32[]{:S(2)}) collective-permute-start(f32[40,512]{1,0:T(8,128)S(1)} %get-tuple-element.27), channel_id=1, source_target_pairs={{0,24},{1,25},{2,26},{3,27},{4,28},{5,29},{6,30},{7,31},{8,0},{9,1... | collective-permute-start | bytes 245768 | tf_op jit(solution)/shard_map/ppermute | solution.py:172
  271.9 1.4 copy-start.4
  273.3 2.3 copy-start.1
  275.6 4.8 %copy-start.3 = (f32[189,40,128]{2,1,0:T(8,128)S(1)}, f32[189,40,128]{2,1,0:T(8,128)}, u32[]{:S(2)}) copy-start(f32[189,40,128]{2,1,0:T(8,128)} %select_maximum_fusion.ops_ref) | copy-start | bytes 11612164
  275.6 4.8 %copy-start.15 = (s32[1024]{0:T(1024)S(1)}, s32[1024]{0:T(1024)}, u32[]{:S(2)}) copy-start(s32[1024]{0:T(1024)} %class_ref.3) | copy-start | bytes 12292
  278.2 2.2 copy-start.2
  320.5 0.8 copy-start.13
  321.3 75.6 %all-to-all-start.3 = ((f32[4,768,256]{2,1,0:T(8,128)}), f32[4,768,256]{2,1,0:T(8,128)}, u32[]{:S(2)}, u32[]{:S(2)}) async-start(f32[4,768,256]{2,1,0:T(8,128)} %bitcast.39), calls=%async_computation.3 | async-start | bytes 6291456 | tf_op jit(solution)/shard_map/all_to_all | solution.py:537
  329.3 2.4 copy-start.5
  329.3 2.4 copy-start.6
  330.7 1.0 copy-start.12
  376.5 1.3 copy-start.10
  396.9 69.2 %all-to-all-start.4 = ((f32[4,256,256]{2,1,0:T(8,128)}), f32[4,256,256]{2,1,0:T(8,128)}, u32[]{:S(2)}, u32[]{:S(2)}) async-start(f32[4,256,256]{2,1,0:T(8,128)} %bitcast.40), calls=%async_computation.4 | async-start | bytes 2097152 | tf_op jit(solution)/shard_map/all_to_all | solution.py:537
  404.7 52.1 %copy-start.7 = (bf16[2,512,512]{2,1,0:T(8,128)(2,1)S(1)}, bf16[2,512,512]{2,1,0:T(8,128)(2,1)}, u32[]{:S(2)}) copy-start(bf16[2,512,512]{2,1,0:T(8,128)(2,1)} %constant.121.clone.refs_5_) | copy-start | bytes 3145732
  406.0 27.7 %collective-permute-start.15 = (f32[40,512]{1,0:T(8,128)S(1)}, f32[40,512]{1,0:T(8,128)S(1)}, u32[]{:S(2)}, u32[]{:S(2)}) collective-permute-start(f32[40,512]{1,0:T(8,128)S(1)} %get-tuple-element.40), channel_id=1, source_target_pairs={{0,31},{1,24},{2,25},{3,26},{4,27},{5,28},{6,29},{7,30},{8,7},{9,0... | collective-permute-start | bytes 245768 | tf_op jit(solution)/shard_map/ppermute | solution.py:172
  407.9 27.7 %collective-permute-start.14 = (f32[40,512]{1,0:T(8,128)S(1)}, f32[40,512]{1,0:T(8,128)S(1)}, u32[]{:S(2)}, u32[]{:S(2)}) collective-permute-start(f32[40,512]{1,0:T(8,128)S(1)} %get-tuple-element.41), channel_id=1, source_target_pairs={{0,24},{1,25},{2,26},{3,27},{4,28},{5,29},{6,30},{7,31},{8,0},{9,1... | collective-permute-start | bytes 245768 | tf_op jit(solution)/shard_map/ppermute | solution.py:172
  411.4 27.0 %collective-permute-start.13 = (f32[40,512]{1,0:T(8,128)S(1)}, f32[40,512]{1,0:T(8,128)S(1)}, u32[]{:S(2)}, u32[]{:S(2)}) collective-permute-start(f32[40,512]{1,0:T(8,128)S(1)} %get-tuple-element.42), channel_id=1, source_target_pairs={{0,25},{1,26},{2,27},{3,28},{4,29},{5,30},{6,31},{7,24},{8,1},{9,2... | collective-permute-start | bytes 245768 | tf_op jit(solution)/shard_map/ppermute | solution.py:172
  411.4 27.0 %collective-permute-start.12 = (f32[40,512]{1,0:T(8,128)S(1)}, f32[40,512]{1,0:T(8,128)S(1)}, u32[]{:S(2)}, u32[]{:S(2)}) collective-permute-start(f32[40,512]{1,0:T(8,128)S(1)} %get-tuple-element.43), channel_id=1, source_target_pairs={{0,7},{1,0},{2,1},{3,2},{4,3},{5,4},{6,5},{7,6},{8,15},{9,8},{10,9... | collective-permute-start | bytes 245768 | tf_op jit(solution)/shard_map/ppermute | solution.py:172
  414.1 24.3 %collective-permute-start.11 = (f32[40,512]{1,0:T(8,128)S(1)}, f32[40,512]{1,0:T(8,128)S(1)}, u32[]{:S(2)}, u32[]{:S(2)}) collective-permute-start(f32[40,512]{1,0:T(8,128)S(1)} %get-tuple-element.44), channel_id=1, source_target_pairs={{0,1},{1,2},{2,3},{3,4},{4,5},{5,6},{6,7},{7,0},{8,9},{9,10},{10,1... | collective-permute-start | bytes 245768 | tf_op jit(solution)/shard_map/ppermute | solution.py:172
  433.7 4.7 collective-permute-start.10
  435.7 5.1 %collective-permute-start.9 = (f32[40,512]{1,0:T(8,128)S(1)}, f32[40,512]{1,0:T(8,128)S(1)}, u32[]{:S(2)}, u32[]{:S(2)}) collective-permute-start(f32[40,512]{1,0:T(8,128)S(1)} %get-tuple-element.46), channel_id=1, source_target_pairs={{0,8},{1,9},{2,10},{3,11},{4,12},{5,13},{6,14},{7,15},{8,16},{9,17... | collective-permute-start | bytes 245768 | tf_op jit(solution)/shard_map/ppermute | solution.py:172
  438.4 5.7 %collective-permute-start.8 = (f32[40,512]{1,0:T(8,128)S(1)}, f32[40,512]{1,0:T(8,128)S(1)}, u32[]{:S(2)}, u32[]{:S(2)}) collective-permute-start(f32[40,512]{1,0:T(8,128)S(1)} %get-tuple-element.47), channel_id=1, source_target_pairs={{0,9},{1,10},{2,11},{3,12},{4,13},{5,14},{6,15},{7,8},{8,17},{9,18... | collective-permute-start | bytes 245768 | tf_op jit(solution)/shard_map/ppermute | solution.py:172
  444.0 1.6 copy-start.11
  466.1 1.2 copy-start.8

commit v3 on v2

--- a/solution.py
+++ b/solution.py
@@ -18,7 +18,7 @@
 SHIFT = 6
 LANE_SHIFT = 7
 VMEM_BYTES = 48 * 1024 * 1024
-CHUNKS = (1, 3, 3, 1)
+CHUNKS = (1, 2, 4, 1)
 TOP_ROWS = TOP // 2
 
 DEPOSIT_SCALE = 8.0
@@ -45,38 +45,39 @@
     return lax.broadcasted_iota(jnp.int32, shape, len(shape) - 1)
 
 
-def own_table_kernel(cells_ref, out_ref, top_ref):
+def own_table_kernel(cells_ref, out_ref):
     @pl.loop(0, cells_ref.shape[1] // LANES)
     def _(k):
         at = pl.multiple_of(k * LANES, LANES)
         out_ref[pl.ds(at, LANES), :] = spread(cells_ref[:, pl.ds(at, LANES)])
 
-    is_first = lane_ids((TOP_ROWS, LANES)) < KPAD
-    top_ref[...] = jnp.where(is_first, out_ref[:TOP_ROWS, :], out_ref[TOP_ROWS : 2 * TOP_ROWS, :])
-
 
 def own_table(cells, rows):
     count = cells.shape[1]
     return pl.pallas_call(
         own_table_kernel,
         grid=(1,),
-        out_shape=(
-            jax.ShapeDtypeStruct((rows, LANES), jnp.float32),
-            jax.ShapeDtypeStruct((TOP_ROWS, LANES), jnp.float32),
-        ),
+        out_shape=jax.ShapeDtypeStruct((rows, LANES), jnp.float32),
         in_specs=[pl.BlockSpec((KPAD, count), lambda i: (0, 0))],
-        out_specs=(
-            pl.BlockSpec((count, LANES), lambda i: (0, 0)),
-            pl.BlockSpec((TOP_ROWS, LANES), lambda i: (0, 0)),
-        ),
+        out_specs=pl.BlockSpec((count, LANES), lambda i: (0, 0)),
         compiler_params=params(),
         cost_estimate=cost(10**6, 12 * 10**6),
         name="own_table",
     )(cells)
 
 
+def cut_rows(refs, first, stop):
+    pieces, at = [], 0
+    for ref in refs:
+        low, high = max(first - at, 0), min(stop - at, ref.shape[0])
+        if low < high:
+            pieces.append(ref[low:high, :])
+        at += ref.shape[0]
+    return jnp.concatenate(pieces, axis=0) if len(pieces) > 1 else pieces[0]
+
+
 def whole_table_kernel(*refs, slot_steps):
-    top_ref, out_ref = refs[8], refs[10]
+    top_refs, out_ref = refs[8:-2], refs[-1]
     step = pl.program_id(0)
     for k in range(slot_steps):
 
@@ -89,7 +90,7 @@
                     at += LANES
 
     rows = out_ref.shape[0]
-    total = top_ref.shape[0]
+    total = sum(ref.shape[0] for ref in top_refs)
     lanes = lane_ids((rows, LANES))
     for k in range(2 * total // rows):
 
@@ -98,30 +99,29 @@
             pieces = []
             for first in range(k * rows, (k + 1) * rows, min(rows, total)):
                 group, at = first // total, first % total
-                value = top_ref[at : at + min(rows, total), :]
+                value = cut_rows(top_refs, at, at + min(rows, total))
                 pieces.append(pltpu.roll(value, LANES - KPAD, 1) if group else value)
             value = jnp.concatenate(pieces, axis=0) if len(pieces) > 1 else pieces[0]
             value = jnp.where(lanes < KPAD, value, 0.0)
             out_ref[...] = value + pltpu.roll(value, KPAD, 1) + pltpu.roll(value, 2 * KPAD, 1)
 
 
-def whole_table(table, arrived, top_rows):
+def whole_table(table, arrived, tops):
     slots = arrived[0].shape[1]
     rows = 2 * slots
-    own = table.shape[0] - 8 * slots - 2 * top_rows.shape[0]
-    first = own // rows
-    steps = 4 + 2 * top_rows.shape[0] // rows
+    top_rows = 2 * sum(part.shape[0] for part in tops)
+    first = (table.shape[0] - 8 * slots - top_rows) // rows
     return pl.pallas_call(
         functools.partial(whole_table_kernel, slot_steps=4),
-        grid=(steps,),
+        grid=(4 + top_rows // rows,),
         out_shape=jax.ShapeDtypeStruct(table.shape, jnp.float32),
-        in_specs=[VMEM_WHOLE] * 9 + [pl.BlockSpec(memory_space=pl.ANY)],
+        in_specs=[VMEM_WHOLE] * (8 + len(tops)) + [pl.BlockSpec(memory_space=pl.ANY)],
         out_specs=pl.BlockSpec((rows, LANES), lambda i: (first + i, 0)),
-        input_output_aliases={9: 0},
+        input_output_aliases={8 + len(tops): 0},
         compiler_params=params(),
         cost_estimate=cost(10**6, 16 * 10**6),
         name="whole_table",
-    )(*arrived, top_rows, table)
+    )(*arrived, *tops, table)
 
 
 def as_rows(table):
@@ -129,17 +129,19 @@
 
 
 def pack_kernel(list_ref, count_ref, table_ref, *refs):
-    outs, rows = refs[:8], refs[8]
+    outs, held = refs[:8], refs[8:]
     slot_tiles = list_ref.shape[1] // LANES
     for n in range(8):
 
-        @pl.loop(0, slot_tiles)
+        @pl.loop(0, slot_tiles, step=len(held))
         def _(i):
-            first = pl.multiple_of(i * LANES, LANES)
-            for r in range(LANES):
-                rows[r : r + 1, :] = table_ref[list_ref[n, first + r]]
-            live = (lane_ids((KPAD, LANES)) + first) < count_ref[n]
-            outs[n][:, pl.ds(first, LANES)] = jnp.where(live, rows[...].T[:KPAD], 0.0)
+            firsts = [pl.multiple_of((i + k) * LANES, LANES) for k in range(len(held))]
+            for first, rows in zip(firsts, held):
+                for r in range(LANES):
+                    rows[r : r + 1, :] = table_ref[list_ref[n, first + r]]
+            for first, rows in zip(firsts, held):
+                live = (lane_ids((KPAD, LANES)) + first) < count_ref[n]
+                outs[n][:, pl.ds(first, LANES)] = jnp.where(live, rows[...].T[:KPAD], 0.0)
 
 
 def pack(table, cell_count, proxy_list, proxy_count):
@@ -154,7 +156,7 @@
             pl.BlockSpec((cell_count, 1, LANES), lambda i: (0, 0, 0)),
         ],
         out_specs=(pl.BlockSpec((KPAD, slots), lambda i: (0, 0)),) * 8,
-        scratch_shapes=[pltpu.VMEM((LANES, LANES), jnp.float32)],
+        scratch_shapes=[pltpu.VMEM((LANES, LANES), jnp.float32)] * 2,
         compiler_params=params(),
         cost_estimate=cost(10**6, 25 * 10**6),
         name="pack",
@@ -352,18 +354,150 @@
     )(mesh)
 
 
-def deposit_kernel(code_ref, value_ref, *refs):
-    sources = code_ref.shape[0]
+def first_part_kernel(mesh_ref, place_ref, cells_ref, out_ref, ride, sems):
+    sources, whole_rows, width = out_ref.shape
+    extra = ride.shape[0]
+    rows = whole_rows - extra
+    copies = [
+        pltpu.make_async_copy(
+            mesh_ref.at[0, pl.ds(s * rows, rows), :], out_ref.at[s, pl.ds(0, rows), :], sems.at[s]
+        )
+        for s in range(sources)
+    ]
+    for copy in copies:
+        copy.start()
+    is_first = lane_ids((TOP_ROWS, LANES)) < KPAD
+    table = spread(jnp.concatenate([cells_ref[:, :LANES], jnp.zeros((KPAD - cells_ref.shape[0], LANES), jnp.float32)], axis=0))
+    top = jnp.where(is_first, table[:TOP_ROWS, :], table[TOP_ROWS : 2 * TOP_ROWS, :])
+    blocks = [place_ref[...].astype(jnp.float32), cell_lines(cells_ref), top]
+    at = 0
+    for block in blocks:
+        high = block.shape[0] * LANES // width
+        for h in range(width // LANES):
+            ride[at : at + high, h * LANES : (h + 1) * LANES] = block[h * high : (h + 1) * high, :]
+        at += high
+    more = [
+        pltpu.make_async_copy(ride, out_ref.at[s, pl.ds(rows, extra), :], sems.at[sources + s])
+        for s in range(sources)
+    ]
+    for copy in more:
+        copy.start()
+    for copy in copies + more:
+        copy.wait()
+
+
+def cell_lines(cells_ref):
+    lines = [cells_ref[0:1, k : k + LANES] for k in range(0, cells_ref.shape[1], LANES)]
+    return DEPOSIT_SCALE * jnp.concatenate(lines, axis=0)
+
+
+def first_part(mesh, place, multipoles, sources):
+    rows, width = mesh.shape[1] // sources, mesh.shape[2]
+    extra = (2 * place.size + TOP_ROWS * LANES) // width
+    return pl.pallas_call(
+        first_part_kernel,
+        out_shape=jax.ShapeDtypeStruct((sources, rows + extra, width), jnp.float32),
+        in_specs=[pl.BlockSpec(memory_space=pl.ANY), VMEM_WHOLE, VMEM_WHOLE],
+        out_specs=pl.BlockSpec(memory_space=pl.ANY),
+        scratch_shapes=[
+            pltpu.VMEM((extra, width), jnp.float32),
+            pltpu.SemaphoreType.DMA((2 * sources,)),
+        ],
+        compiler_params=params(),
+        cost_estimate=cost(0, 8 * sources * rows * width),
+        name="first_part",
+    )(mesh, place.reshape(-1, LANES), multipoles)
+
+
+def log2(value):
+    return value.bit_length() - 1
+
+
+def sift_kernel(mine_ref, part_ref, code_ref, value_ref, bound_ref, top_ref, ride, sem, *, planes, rows):
+    sources, extra, width = ride.shape
+    lines = code_ref.shape[0] // sources
+    copy = pltpu.make_async_copy(part_ref.at[:, pl.ds(rows, extra), :], ride, sem)
+    copy.start()
+    copy.wait()
+
+    def unfold(first, count):
+        high = count * LANES // width
+        return jnp.concatenate(
+            [
+                ride[s, first : first + high, h * LANES : (h + 1) * LANES]
+                for s in range(sources)
+                for h in range(width // LANES)
+            ],
+            axis=0,
+        )
+
+    step = lines * LANES // width
+    place = unfold(0, lines).astype(jnp.int32)
+    value = unfold(step, lines)
+    top_ref[...] = unfold(2 * step, TOP_ROWS)
+
+    row_at, mesh_rows = log2(width), rows * sources
+    plane = place >> (row_at + log2(mesh_rows))
+    row = (place >> row_at) & (mesh_rows - 1)
+    column = place & (width - 1)
+    tiles = width // LANES
+    target = (plane * tiles + (column >> LANE_SHIFT)) * rows + (row & (rows - 1))
+    none = planes * tiles * rows * LANES
+    mine = (row >> log2(rows)) == mine_ref[0]
+    lanes = lane_ids(place.shape)
+    code = jnp.where(mine, target * LANES + (column & (LANES - 1)), none)
+    value = jnp.where(mine, value, 0.0)
+    ahead = jnp.where(mine, 1, 0)
+    for b in range(LANE_SHIFT):
+        ahead = ahead + jnp.where(lanes >= (1 << b), pltpu.roll(ahead, 1 << b, 1), 0)
+    shift = jnp.where(mine, lanes + 1 - ahead, 0)
+    for b in range(LANE_SHIFT):
+        back = LANES - (1 << b)
+        moves = (shift >> b) & 1
+        comes = pltpu.roll(moves, back, 1) == 1
+        goes = moves == 1
+        code = jnp.where(comes, pltpu.roll(code, back, 1), jnp.where(goes, none, code))
+        value = jnp.where(comes, pltpu.roll(value, back, 1), jnp.where(goes, 0.0, value))
+        shift = jnp.where(comes, pltpu.roll(shift, back, 1), jnp.where(goes, 0, shift))
+    code_ref[...] = code
+    value_ref[...] = value
+    counts = jnp.sum(jnp.where(mine, 1.0, 0.0), axis=1, keepdims=True)
+    counts = jnp.broadcast_to(counts, mine.shape).reshape(2 * sources, lines // 2, LANES)
+    bound_ref[...] = jnp.max(counts, axis=0).astype(jnp.int32)
+
+
+def sift(part, mine, planes, rows, lines):
+    sources, whole_rows, width = part.shape
+    extra = whole_rows - rows
+    shape = (sources * lines, LANES)
+    return pl.pallas_call(
+        functools.partial(sift_kernel, planes=planes, rows=rows),
+        out_shape=(
+            jax.ShapeDtypeStruct(shape, jnp.int32),
+            jax.ShapeDtypeStruct(shape, jnp.float32),
+            jax.ShapeDtypeStruct((lines // 2, LANES), jnp.int32),
+            jax.ShapeDtypeStruct((sources * TOP_ROWS, LANES), jnp.float32),
+        ),
+        in_specs=[SMEM_WHOLE, pl.BlockSpec(memory_space=pl.ANY)],
+        out_specs=(VMEM_WHOLE,) * 4,
+        scratch_shapes=[pltpu.VMEM((sources, extra, width), jnp.float32), pltpu.SemaphoreType.DMA],
+        compiler_params=params(),
+        cost_estimate=cost(10**6, 8 * 10**6),
+        name="sift",
+    )(mine, part)
+
+
+def deposit_kernel(code_ref, value_ref, bound_ref, *refs):
+    sources = len(refs) // 2
     outs, others = refs[:sources], refs[sources:]
+    lines = code_ref.shape[0] // (2 * sources)
     lanes = lane_ids((1, LANES))
     for held in refs:
         held[...] = jnp.zeros_like(held)
-    half = code_ref.shape[1] // 2
-
-    @pl.loop(0, half, step=4)
-    def _(first):
-        for j in range(4):
-            at = [(s, first + j + h * half) for h in range(2) for s in range(sources)]
+
+    def line(g, _):
+        def one(j, _):
+            at = [((2 * s + h) * lines + g, j) for h in range(2) for s in range(sources)]
             codes = [code_ref[i] for i in at]
             to = [pl.ds(code >> LANE_SHIFT, 1) for code in codes]
             old = [held[rows, :] for held, rows in zip(refs, to)]
@@ -373,23 +507,26 @@
             ]
             for held, rows, row in zip(refs, to, new):
                 held[rows, :] = row
-
+            return 0
+
+        return lax.fori_loop(0, bound_ref[g, 0], one, 0)
+
+    lax.fori_loop(0, lines, line, 0)
     for out_ref, held in zip(outs, others):
         out_ref[...] = out_ref[...] + held[...]
 
 
-def deposit(codes, values, rows):
-    sources = codes.shape[0]
+def deposit(codes, values, bounds, rows, sources):
     return pl.pallas_call(
         deposit_kernel,
         out_shape=(jax.ShapeDtypeStruct((rows, LANES), jnp.float32),) * sources,
-        in_specs=[SMEM_WHOLE, SMEM_WHOLE],
+        in_specs=[SMEM_WHOLE] * 3,
         out_specs=(VMEM_WHOLE,) * sources,
         scratch_shapes=[pltpu.VMEM((rows, LANES), jnp.float32)] * sources,
         compiler_params=params(),
-        cost_estimate=cost(10**6, 75 * 10**6),
+        cost_estimate=cost(10**6, 40 * 10**6),
         name="deposit",
-    )(codes, values)
+    )(codes, values, bounds)
 
 
 def fourier_tables(length):
@@ -542,10 +679,7 @@
         spans.append((first, size))
         first += size
 
-    held = jnp.stack([cell_mesh.astype(jnp.float32), DEPOSIT_SCALE * multipoles[0]])
-    held = held.reshape(1, -1, width)
-    start = pm_density[0].reshape(n_gx, own_rows, width)
-    parts = [send(jnp.concatenate([start, jnp.broadcast_to(held, (n_gx, *held.shape[1:]))], axis=1))]
+    parts = [send(first_part(pm_density, cell_mesh, multipoles, n_gx))]
     carved = [
         carve(pm_density, at, size, n_gx).reshape(n_gx, size * own_rows, width)
         for at, size in spans[1:]
@@ -553,12 +687,15 @@
 
     cells = jnp.pad(multipoles, ((0, KPAD - coef_count), (0, 0)))
     base = cell_count + 8 * slots
-    table, top_own = own_table(cells, base + TOP * domains)
+    table = own_table(cells, base + TOP * domains)
     outgoing = pack(table, cell_count, lists, counts)
     arrived = exchange(outgoing, n_gx, n_gy)
 
     top = pair_source - base
-    top = base + ((top >> 4) & 1) * (TOP_ROWS * domains) + (top >> 5) * TOP_ROWS + (top & 15)
+    domain = top >> log2(TOP)
+    along = (domain & (n_gy - 1)) ^ lax.axis_index("gy")
+    place = (along * n_gx + (domain >> log2(n_gy))) * TOP_ROWS + (top & (TOP_ROWS - 1))
+    top = base + ((top >> log2(TOP_ROWS)) & 1) * (TOP_ROWS * domains) + place
     wanted = jnp.where(pair_source < base, pair_source, top)
     sources = order(((wanted << SHIFT) | (pair_target & (BLOCK - 1))).reshape(-1, LANES))
 
@@ -569,29 +706,23 @@
     ops = jnp.concatenate([high, turned_ops - high], axis=2)
     ops = jnp.pad(ops, ((0, 0), (0, 0), (0, LANES - 2 * KPAD)))
 
-    tops = jnp.broadcast_to(top_own, (domains, TOP_ROWS, LANES))
-    tops = after(tops, parts[0], outgoing[0], sources, ops)
-    tops = lax.all_to_all(tops, ("gx", "gy"), 0, 0, tiled=True)
-    parts.append(send(after(carved[0], tops)))
-
-    near = parts[0][:, own_rows:].reshape(n_gx, 2, cell_count)
-    place = near[:, 0].astype(jnp.int32)
-    plane = place // (mesh_rows * width)
-    row = place // width % mesh_rows
-    column = place % width
     tiles = width // LANES
     add_rows = planes * tiles * own_rows
-    at_row = (plane * tiles + column // LANES) * own_rows + row % own_rows
-    mine = row // own_rows == lax.axis_index("gx")
-    codes = jnp.where(mine, at_row, add_rows) * LANES + column % LANES
-    adds = deposit(codes, near[:, 1], add_rows + 8)
-
-    table = whole_table(table, arrived, tops.reshape(-1, LANES))
+    mine = lax.axis_index("gx").astype(jnp.int32).reshape(1)
+    codes, amounts, bounds, top_own = sift(parts[0], mine, planes, own_rows, cell_count // LANES)
+    tops = [top_own]
+    for bit in range(log2(n_gy)):
+        held = jnp.concatenate(tops, axis=0) if bit else top_own
+        tops.append(lax.ppermute(held, "gy", [(i, i ^ (1 << bit)) for i in range(n_gy)]))
+
+    parts.append(send(after(carved[0], parts[0], sources, ops, *arrived)))
+    adds = deposit(codes, amounts, bounds, add_rows + 8, n_gx)
+    table = whole_table(table, arrived, tops)
     cell_steps = cell_count // LANES
     slot_steps = 8 * slots // LANES
     slot_fields = m2l(sources, block_class, table, ops, cell_steps, slot_steps, True, slots)
     returned = exchange([slot_fields[m] for m in range(8)], n_gx, n_gy)
-    parts.append(send(after(carved[1], parts[1], slot_fields, adds[0])))
+    parts.append(send(after(carved[1], parts[1], adds[0], *returned)))
     own_fields = m2l(sources, block_class, table, ops, 0, cell_steps, False, slots)
 
     tables = fourier_tables(n_gx * width)

time: 476 us -> 396 us (0.83)
  waiting for transfers between devices: 101 us -> 44.3 us
  Pallas kernels: 290 us -> 265 us
  local copies, waits for them, and re-layouts: 22.7 us -> 27.9 us
    ppermute x16, waiting for transfers between devices: 91.6 us -> 0.04 us  [exchange(): arrived[7 - m] = lax.ppermute(blocks[m], ('gx', 'gy'), pairs)]
    pallas_call x1 -> x3, Pallas kernels: 3.34 us -> 37.6 us  [the longest x1 32.9 us: first_part(): pl.pallas_call(first_part_kernel, out_shape=jax.ShapeDtypeStruct((sources...]
    pallas_call x3, Pallas kernels: 99.7 us -> 68.2 us  [carve(): pl.pallas_call(functools.partial(carve_kernel, first=first), out_shape=ja...]
    all_to_all x4, waiting for transfers between devices: 9.84 us -> 35.4 us  [send(): return lax.all_to_all(part, 'gx', 0, 0, tiled=True)]
    pallas_call x1, Pallas kernels: 45.9 us -> 21.6 us  [deposit(): pl.pallas_call(deposit_kernel, out_shape=(jax.ShapeDtypeStruct((rows, LAN...]
    unnamed x70 -> x79, local copies, waits for them, and re-layouts: 18.1 us -> 27.8 us
    ppermute x0 -> x3, waiting for transfers between devices: none -> 8.85 us  [on_device(): lax.ppermute(held, 'gy', [(i, i ^ 1 << bit) for i in range(n_gy)])]
    all_to_all x1 -> x0, starting transfers between devices: 5.87 us -> none  [on_device(): tops = lax.all_to_all(tops, ('gx', 'gy'), 0, 0, tiled=True)]
  transfers between devices with their start and end apart: 21 -> 23, of which waited for: 9 -> 4; matrix products, arithmetic and copies ran while one was open for 2% -> 3% of each run, Pallas kernels for 60% -> 58%
where the time goes in v3:
time: 396 us; the launch traced here: 393 us
  Pallas kernels  265 us (67%)
  starting transfers between devices  48.8 us (12%)
  waiting for transfers between devices  44.3 us (11%)
  local copies, waits for them, and re-layouts  27.9 us (7%)
  other arithmetic  5.78 us (1%)
    pallas_call x2, Pallas kernels, m2l(): pl.pallas_call(functools.partial(m2l_kernel, first=first, turned=turned),...  80 us
    pallas_call x3, Pallas kernels, carve(): pl.pallas_call(functools.partial(carve_kernel, first=first), out_shape=ja...  68.2 us
    all_to_all x4, waiting for transfers between devices, send(): return lax.all_to_all(part, 'gx', 0, 0, tiled=True)  35.4 us
    pallas_call x1, Pallas kernels, first_part(): pl.pallas_call(first_part_kernel, out_shape=jax.ShapeDtypeStruct((sources...  32.9 us
    pallas_call x4, Pallas kernels, fourier(): pl.pallas_call(functools.partial(fourier_kernel, sources=sources), grid=(...  28.1 us
    unnamed x79, local copies, waits for them, and re-layouts  27.8 us
    ppermute x16, starting transfers between devices, exchange(): arrived[7 - m] = lax.ppermute(blocks[m], ('gx', 'gy'), pairs)  23.6 us
    all_to_all x4, starting transfers between devices, send(): return lax.all_to_all(part, 'gx', 0, 0, tiled=True)  23.5 us
  transfers between devices with their start and end apart: 23, of which 4 were waited for; matrix products, arithmetic and copies ran while one was open for 3% of the time, Pallas kernels for 58%

profile of v3, /device:TPU:8, one launch (start us, length us, event | category | flops | bytes accessed | tf_op | source)
XLA Modules:
  0.0 393.3 jit_solution(7633201127066592544)
XLA Ops:
  0.6 1.1 copy-done.17
  1.7 0.7 copy-done.34
  2.4 32.9 %first_part.1 = f32[4,296,256]{2,1,0:T(8,128)} custom-call(f32[8,1024,256]{2,1,0:T(8,128)} %mesh_ref.7, s32[32,128]{1,0:T(8,128)S(1)} %bitcast.35, f32[35,4096]{1,0:T(8,128)S(1)} %copy-done.17), custom_call_target="tpu_custom_call" | custom-call | bytes 2097152 | tf_op jit(solution)/shard_map/first_part/pallas_call | solution.py:397
  35.4 5.3 %all-to-all-start = ((f32[4,296,256]{2,1,0:T(8,128)}), f32[4,296,256]{2,1,0:T(8,128)S(1)}, u32[]{:S(2)}, u32[]{:S(2)}) async-start(f32[4,296,256]{2,1,0:T(8,128)} %first_part.1), calls=%async_computation | async-start | bytes 2424832 | tf_op jit(solution)/shard_map/all_to_all | solution.py:674
  40.8 3.3 own_table.1.refs_12_
  44.1 10.0 %pack.1 = (f32[40,512]{1,0:T(8,128)S(1)}, f32[40,512]{1,0:T(8,128)S(1)}, f32[40,512]{1,0:T(8,128)S(1)}, f32[40,512]{1,0:T(8,128)S(1)}, f32[40,512]{1,0:T(8,128)S...) custom-call(s32[8,512]{1,0:T(8,128)S(1)} %bitcast.33, s32[8]{0:T(128)S(1)} %bitcast.36, ...), custom_call_target="tpu_custom_call" | custom-call | flops 1000000 | bytes 25000000 | tf_op jit(solution)/shard_map/pack/pallas_call | solution.py:149
  54.1 2.2 copy-done
  56.3 0.3 collective-permute-start
  56.7 1.5 collective-permute-start.1
  58.1 2.6 collective-permute-start.2
  60.8 2.6 collective-permute-start.4
  63.4 5.2 %copy.17 = f32[189,35,35]{1,2,0:T(8,128)} copy(f32[189,35,35]{0,2,1:T(8,128)} %param.17) | data formatting | bytes 1852200 | tf_op args[6]
  68.6 2.7 pad_reduce-precision_fusion
  71.3 0.2 fusion.2.packed_ref
  71.5 0.1 collective-permute-start.5
  71.6 1.8 collective-permute-start.6
  73.4 4.1 %collective-permute-start.7 = (f32[40,512]{1,0:T(8,128)S(1)}, f32[40,512]{1,0:T(8,128)S(1)}, u32[]{:S(2)}, u32[]{:S(2)}) collective-permute-start(f32[40,512]{1,0:T(8,128)S(1)} %get-tuple-element.28), channel_id=1, source_target_pairs={{0,31},{1,24},{2,25},{3,26},{4,27},{5,28},{6,29},{7,30},{8,7},{9,0... | collective-permute-start | bytes 245768 | tf_op jit(solution)/shard_map/ppermute | solution.py:174
  77.4 2.9 select_maximum_fusion.ops_ref
  80.4 64.7 %carve.5 = f32[4,2,256,256]{3,2,1,0:T(8,128)} custom-call(f32[8,1024,256]{2,1,0:T(8,128)} %mesh_ref.7), custom_call_target="tpu_custom_call" | custom-call | bytes 4194304 | tf_op jit(solution)/shard_map/carve/pallas_call | solution.py:345
  145.0 7.4 %order.1.source_ref = s32[512,128]{1,0:T(8,128)S(1)} custom-call(s32[512,128]{1,0:T(8,128)S(1)} %fusion.2.packed_ref), custom_call_target="tpu_custom_call" | custom-call | flops 1000000 | bytes 20000000 | tf_op jit(solution)/shard_map/order/pallas_call | solution.py:197
  152.5 4.8 %all-to-all-start.1 = ((f32[4,512,256]{2,1,0:T(8,128)}), f32[4,512,256]{2,1,0:T(8,128)}, u32[]{:S(2)}, u32[]{:S(2)}) async-start(f32[4,512,256]{2,1,0:T(8,128)} %bitcast.18), calls=%async_computation.1 | async-start | bytes 4194304 | tf_op jit(solution)/shard_map/all_to_all | solution.py:674
  157.3 1.3 sift.1
  158.6 0.1 collective-permute-start.8
  158.7 1.2 collective-permute-done.8.refs_9_
  159.9 0.1 collective-permute-start.9
  160.0 4.2 %collective-permute-done.9.refs_10_ = f32[128,128]{1,0:T(8,128)S(1)} collective-permute-done((f32[128,128]{1,0:T(8,128)S(1)}, f32[128,128]{1,0:T(8,128)S(1)}, u32[]{:S(2)}, u32[]{:S(2)}) %collective-permute-start.9) | collective-permute-done | bytes 65568 | tf_op jit(solution)/shard_map/ppermute | solution.py:716
  164.2 1.6 collective-permute-start.10
  165.8 3.4 collective-permute-done.10.refs_11_
  169.2 2.3 copy-done.1
  171.6 1.3 whole_table.1
  172.9 2.2 copy-done.2
  175.1 40.1 %m2l_slots.1 = f32[8,40,512]{2,1,0:T(8,128)S(1)} custom-call(s32[512,128]{1,0:T(8,128)S(1)} %order.1.source_ref, s32[1024]{0:T(1024)S(1)} %copy-done.35, f32[9216,1,128]{2,1,0:T(1,128)} %bitcast.29, f32[189,40,128]{2,1,0:T(8,128)S(1)} %copy-done.3), custom_call_target="tpu_custom_call" | custom-call | flops 1000000 | bytes 150000000 | tf_op jit(solution)/shard_map/m2l_slots/pallas_call | solution.py:263
  215.2 0.1 collective-permute-start.18
  215.3 3.2 collective-permute-start.17
  218.4 0.7 collective-permute-start.16
  219.1 2.3 collective-permute-start.15
  221.4 3.2 collective-permute-start.13
  224.6 0.6 copy-done.19
  225.3 1.2 collective-permute-start.12
  226.4 0.6 copy-done.21
  227.1 2.2 carve.4
  229.3 2.1 copy-done.7
  231.4 21.6 %deposit.1 = (f32[4104,128]{1,0:T(8,128)S(1)}, f32[4104,128]{1,0:T(8,128)S(1)}, f32[4104,128]{1,0:T(8,128)}, f32[4104,128]{1,0:T(8,128)}) custom-call(s32[128,128]{1,0:T(8,128)S(1)} %get-tuple-element.31.code_ref, f32[128,128]{1,0:T(8,128)S(1)} %get-tuple-element.32.value_ref, s32[16,128]{1,0:T(8,128)S(1)} %get-tuple-element.33.bound_ref), custom_call_target="tpu_custom_call" | custom-call | flops 1000000 | bytes 40000000 | tf_op jit(solution)/shard_map/deposit/pallas_call | solution.py:520
  253.0 1.3 copy-done.6
  254.4 0.6 copy-done.23
  255.1 0.1 copy-done.31
  255.1 5.6 %all-to-all-start.2 = ((f32[4,1024,256]{2,1,0:T(8,128)}), f32[4,1024,256]{2,1,0:T(8,128)}, u32[]{:S(2)}, u32[]{:S(2)}) async-start(f32[4,1024,256]{2,1,0:T(8,128)} %bitcast.31), calls=%async_computation.2 | async-start | bytes 8388608 | tf_op jit(solution)/shard_map/all_to_all | solution.py:674
  260.7 1.4 carve.3
  262.1 1.0 copy-done.16
  263.1 4.6 %fourier.4.refs_7_ = f32[2,8,256,1024]{3,2,1,0:T(8,128)} custom-call(f32[4,296,256]{2,1,0:T(8,128)S(1)} %copy-done.13, f32[4104,128]{1,0:T(8,128)S(1)} %get-tuple-element.34.refs_1_, f32[4104,128]{1,0:T(8,128)} %copy-done.6, f32[4104,128]{1,0:T(8,128)} %get-tuple-element.37.refs_3_, f32[4104,128]{1,0:T(8,128)} %get-tuple-element.38.refs_4_, ...), custom_call_target="tpu_custom_call" | custom-call | flops 1000000 | bytes 10000000 | tf_op jit(solution)/shard_map/fourier/pallas_call | solution.py:635
  267.7 39.9 %m2l_cells.1.own_ref = f32[4096,128]{1,0:T(8,128)S(1)} custom-call(s32[512,128]{1,0:T(8,128)S(1)} %order.1.source_ref, s32[1024]{0:T(1024)S(1)} %copy-done.35, f32[9216,1,128]{2,1,0:T(1,128)} %bitcast.30, f32[189,40,128]{2,1,0:T(8,128)} %select_maximum_fusion.ops_ref), custom_call_target="tpu_custom_call" | custom-call | flops 1000000 | bytes 150000000 | tf_op jit(solution)/shard_map/m2l_cells/pallas_call | solution.py:263
  307.6 1.3 copy-done.14
  309.0 7.2 %fourier.5.refs_7_ = f32[2,8,256,1024]{3,2,1,0:T(8,128)} custom-call(f32[4,512,256]{2,1,0:T(8,128)} %all-to-all-done.1.refs_0_, f32[4104,128]{1,0:T(8,128)} %copy-done.4, f32[4104,128]{1,0:T(8,128)} %copy-done.6, f32[4104,128]{1,0:T(8,128)} %get-tuple-element.37.refs_3_, f32[4104,128]{1,0:T(8,128)} %get-tuple-element.38.refs_4_, ...), custom_call_target="tpu_custom_call", output_to_operand_aliasing={{}: (7, {})} | custom-call | flops 1000000 | bytes 20000000 | tf_op jit(solution)/shard_map/fourier/pallas_call | solution.py:635
  316.1 35.4 %all-to-all-done.2.refs_0_ = f32[4,1024,256]{2,1,0:T(8,128)} async-done(((f32[4,1024,256]{2,1,0:T(8,128)}), f32[4,1024,256]{2,1,0:T(8,128)}, u32[]{:S(2)}, u32[]{:S(2)}) %all-to-all-start.2) | async-done | bytes 4194336 | tf_op jit(solution)/shard_map/all_to_all | solution.py:674
  351.6 7.8 %all-to-all-start.3 = ((f32[4,256,256]{2,1,0:T(8,128)}), f32[4,256,256]{2,1,0:T(8,128)}, u32[]{:S(2)}, u32[]{:S(2)}) async-start(f32[4,256,256]{2,1,0:T(8,128)} %bitcast.32), calls=%async_computation.3 | async-start | bytes 2097152 | tf_op jit(solution)/shard_map/all_to_all | solution.py:674
  359.4 1.6 copy-done.15
  361.0 0.9 copy-done.26
  361.9 0.9 copy-done.28
  362.7 0.9 copy-done.30
  363.6 0.9 copy-done.32
  364.5 11.2 %add_back.1 = f32[35,4096]{1,0:T(8,128)} custom-call(s32[8,512]{1,0:T(8,128)S(1)} %bitcast.34, s32[8]{0:T(128)S(1)} %bitcast.37, f32[4096,128]{1,0:T(8,128)S(1)} %copy-done.15, f32[40,512]{1,0:T(8,128)S(1)} %copy-done.32, f32[40,512]{1,0:T(8,128)S(1)} %copy-done.30, f32[40,512]{1,0:T(8,128)S(1)} %copy-done.28, f32[40,512]{1,0:T(8,128)S(1)} %copy-done.26, ...), custom_call_target="tpu_custom_call" | custom-call | flops 1000000 | bytes 30000000 | tf_op jit(solution)/shard_map/add_back/pallas_call | solution.py:316
  375.8 11.5 %fourier.6.refs_7_ = f32[2,8,256,1024]{3,2,1,0:T(8,128)} custom-call(f32[4,1024,256]{2,1,0:T(8,128)} %all-to-all-done.2.refs_0_, f32[4104,128]{1,0:T(8,128)S(1)} %copy-done.5, f32[4104,128]{1,0:T(8,128)} %copy-done.6, f32[4104,128]{1,0:T(8,128)} %get-tuple-element.37.refs_3_, f32[4104,128]{1,0:T(8,128)} %get-tuple-element.38.refs_4_, ...), custom_call_target="tpu_custom_call", output_to_operand_aliasing={{}: (7, {})} | custom-call | flops 1000000 | bytes 40000000 | tf_op jit(solution)/shard_map/fourier/pallas_call | solution.py:635
  387.2 1.2 copy-done.11
  388.4 4.9 %fourier.7 = f32[2,8,256,1024]{3,2,1,0:T(8,128)} custom-call(f32[4,256,256]{2,1,0:T(8,128)} %all-to-all-done.3.refs_0_, f32[4104,128]{1,0:T(8,128)S(1)} %copy-done.5, f32[4104,128]{1,0:T(8,128)} %copy-done.6, f32[4104,128]{1,0:T(8,128)} %get-tuple-element.37.refs_3_, f32[4104,128]{1,0:T(8,128)} %get-tuple-element.38.refs_4_, ...), custom_call_target="tpu_custom_call", output_to_operand_aliasing={{}: (7, {})} | custom-call | flops 1000000 | bytes 10000000 | tf_op jit(solution)/shard_map/fourier/pallas_call | solution.py:635
  (85 shorter events, 0.3 us)
Async XLA Ops:
  0.6 1.1 copy-start.17
  1.7 0.7 copy-start.34
  2.4 38.3 %copy-start.18 = (f32[35,4096]{1,0:T(8,128)S(1)}, f32[35,4096]{1,0:T(8,128)}, u32[]{:S(2)}) copy-start(f32[35,4096]{1,0:T(8,128)} %cells_ref.1) | copy-start | bytes 1720324
  35.4 117.1 %all-to-all-start = ((f32[4,296,256]{2,1,0:T(8,128)}), f32[4,296,256]{2,1,0:T(8,128)S(1)}, u32[]{:S(2)}, u32[]{:S(2)}) async-start(f32[4,296,256]{2,1,0:T(8,128)} %first_part.1), calls=%async_computation | async-start | bytes 2424832 | tf_op jit(solution)/shard_map/all_to_all | solution.py:674
  40.7 3.4 copy-start.33
  40.7 3.4 copy-start.36
  54.1 2.2 copy-start
  56.3 15.2 %collective-permute-start = (f32[40,512]{1,0:T(8,128)S(1)}, f32[40,512]{1,0:T(8,128)S(1)}, u32[]{:S(2)}, u32[]{:S(2)}) collective-permute-start(f32[40,512]{1,0:T(8,128)S(1)} %get-tuple-element.21), channel_id=1, source_target_pairs={{0,9},{1,10},{2,11},{3,12},{4,13},{5,14},{6,15},{7,8},{8,17},{9,18... | collective-permute-start | bytes 245768 | tf_op jit(solution)/shard_map/ppermute | solution.py:174
  56.7 14.9 %collective-permute-start.1 = (f32[40,512]{1,0:T(8,128)S(1)}, f32[40,512]{1,0:T(8,128)S(1)}, u32[]{:S(2)}, u32[]{:S(2)}) collective-permute-start(f32[40,512]{1,0:T(8,128)S(1)} %get-tuple-element.22), channel_id=1, source_target_pairs={{0,8},{1,9},{2,10},{3,11},{4,12},{5,13},{6,14},{7,15},{8,16},{9,17... | collective-permute-start | bytes 245768 | tf_op jit(solution)/shard_map/ppermute | solution.py:174
  58.1 15.2 %collective-permute-start.2 = (f32[40,512]{1,0:T(8,128)S(1)}, f32[40,512]{1,0:T(8,128)S(1)}, u32[]{:S(2)}, u32[]{:S(2)}) collective-permute-start(f32[40,512]{1,0:T(8,128)S(1)} %get-tuple-element.23), channel_id=1, source_target_pairs={{0,15},{1,8},{2,9},{3,10},{4,11},{5,12},{6,13},{7,14},{8,23},{9,16... | collective-permute-start | bytes 245768 | tf_op jit(solution)/shard_map/ppermute | solution.py:174
  60.8 91.7 %collective-permute-start.3 = (f32[40,512]{1,0:T(8,128)S(1)}, f32[40,512]{1,0:T(8,128)S(1)}, u32[]{:S(2)}, u32[]{:S(2)}) collective-permute-start(f32[40,512]{1,0:T(8,128)S(1)} %get-tuple-element.24), channel_id=1, source_target_pairs={{0,1},{1,2},{2,3},{3,4},{4,5},{5,6},{6,7},{7,0},{8,9},{9,10},{10,1... | collective-permute-start | bytes 245768 | tf_op jit(solution)/shard_map/ppermute | solution.py:174
  60.8 91.7 %collective-permute-start.4 = (f32[40,512]{1,0:T(8,128)S(1)}, f32[40,512]{1,0:T(8,128)S(1)}, u32[]{:S(2)}, u32[]{:S(2)}) collective-permute-start(f32[40,512]{1,0:T(8,128)S(1)} %get-tuple-element.25), channel_id=1, source_target_pairs={{0,7},{1,0},{2,1},{3,2},{4,3},{5,4},{6,5},{7,6},{8,15},{9,8},{10,9... | collective-permute-start | bytes 245768 | tf_op jit(solution)/shard_map/ppermute | solution.py:174
  68.6 2.7 copy-start.37
  68.6 2.7 copy-start.38
  71.5 81.0 %collective-permute-start.5 = (f32[40,512]{1,0:T(8,128)S(1)}, f32[40,512]{1,0:T(8,128)S(1)}, u32[]{:S(2)}, u32[]{:S(2)}) collective-permute-start(f32[40,512]{1,0:T(8,128)S(1)} %get-tuple-element.26), channel_id=1, source_target_pairs={{0,25},{1,26},{2,27},{3,28},{4,29},{5,30},{6,31},{7,24},{8,1},{9,2... | collective-permute-start | bytes 245768 | tf_op jit(solution)/shard_map/ppermute | solution.py:174
  71.6 80.9 %collective-permute-start.6 = (f32[40,512]{1,0:T(8,128)S(1)}, f32[40,512]{1,0:T(8,128)S(1)}, u32[]{:S(2)}, u32[]{:S(2)}) collective-permute-start(f32[40,512]{1,0:T(8,128)S(1)} %get-tuple-element.27), channel_id=1, source_target_pairs={{0,24},{1,25},{2,26},{3,27},{4,28},{5,29},{6,30},{7,31},{8,0},{9,1... | collective-permute-start | bytes 245768 | tf_op jit(solution)/shard_map/ppermute | solution.py:174
  73.4 79.1 %collective-permute-start.7 = (f32[40,512]{1,0:T(8,128)S(1)}, f32[40,512]{1,0:T(8,128)S(1)}, u32[]{:S(2)}, u32[]{:S(2)}) collective-permute-start(f32[40,512]{1,0:T(8,128)S(1)} %get-tuple-element.28), channel_id=1, source_target_pairs={{0,31},{1,24},{2,25},{3,26},{4,27},{5,28},{6,29},{7,30},{8,7},{9,0... | collective-permute-start | bytes 245768 | tf_op jit(solution)/shard_map/ppermute | solution.py:174
  152.5 20.4 %copy-start.12 = (f32[4,296,256]{2,1,0:T(8,128)}, f32[4,296,256]{2,1,0:T(8,128)S(1)}, u32[]{:S(2)}) copy-start(f32[4,296,256]{2,1,0:T(8,128)S(1)} %all-to-all-done.part_ref.refs_0_) | copy-start | bytes 3637252
  152.5 101.9 %all-to-all-start.1 = ((f32[4,512,256]{2,1,0:T(8,128)}), f32[4,512,256]{2,1,0:T(8,128)}, u32[]{:S(2)}, u32[]{:S(2)}) async-start(f32[4,512,256]{2,1,0:T(8,128)} %bitcast.18), calls=%async_computation.1 | async-start | bytes 4194304 | tf_op jit(solution)/shard_map/all_to_all | solution.py:674
  158.6 1.3 collective-permute-start.8
  159.9 4.3 %collective-permute-start.9 = (f32[128,128]{1,0:T(8,128)S(1)}, f32[128,128]{1,0:T(8,128)S(1)}, u32[]{:S(2)}, u32[]{:S(2)}) collective-permute-start(f32[128,128]{1,0:T(8,128)S(1)} %pad_maximum_fusion.1), channel_id=1, source_target_pairs={{0,2},{1,3},{2,0},{3,1},{4,6},{5,7},{6,4},{7,5},{8,10},{9,11},{10,... | collective-permute-start | bytes 196616 | tf_op jit(solution)/shard_map/ppermute | solution.py:716
  164.2 10.9 %copy-start.35 = (s32[1024]{0:T(1024)S(1)}, s32[1024]{0:T(1024)}, u32[]{:S(2)}) copy-start(s32[1024]{0:T(1024)} %class_ref.3) | copy-start | bytes 12292
  164.2 5.0 %collective-permute-start.10 = (f32[256,128]{1,0:T(8,128)S(1)}, f32[256,128]{1,0:T(8,128)S(1)}, u32[]{:S(2)}, u32[]{:S(2)}) collective-permute-start(f32[256,128]{1,0:T(8,128)S(1)} %pad_maximum_fusion), channel_id=1, source_target_pairs={{0,4},{1,5},{2,6},{3,7},{4,0},{5,1},{6,2},{7,3},{8,12},{9,13},{10,... | collective-permute-start | bytes 393224 | tf_op jit(solution)/shard_map/ppermute | solution.py:716
  169.2 2.3 copy-start.1
  171.6 3.5 copy-start.3
  172.9 2.2 copy-start.2
  215.2 6.2 %collective-permute-start.18 = (f32[40,512]{1,0:T(8,128)S(1)}, f32[40,512]{1,0:T(8,128)S(1)}, u32[]{:S(2)}, u32[]{:S(2)}) collective-permute-start(f32[40,512]{1,0:T(8,128)S(1)} %get-tuple-element.42), channel_id=1, source_target_pairs={{0,31},{1,24},{2,25},{3,26},{4,27},{5,28},{6,29},{7,30},{8,7},{9,0... | collective-permute-start | bytes 245768 | tf_op jit(solution)/shard_map/ppermute | solution.py:174
  215.3 9.4 %collective-permute-start.17 = (f32[40,512]{1,0:T(8,128)S(1)}, f32[40,512]{1,0:T(8,128)S(1)}, u32[]{:S(2)}, u32[]{:S(2)}) collective-permute-start(f32[40,512]{1,0:T(8,128)S(1)} %get-tuple-element.43), channel_id=1, source_target_pairs={{0,24},{1,25},{2,26},{3,27},{4,28},{5,29},{6,30},{7,31},{8,0},{9,1... | collective-permute-start | bytes 245768 | tf_op jit(solution)/shard_map/ppermute | solution.py:174
  218.4 8.0 %collective-permute-start.16 = (f32[40,512]{1,0:T(8,128)S(1)}, f32[40,512]{1,0:T(8,128)S(1)}, u32[]{:S(2)}, u32[]{:S(2)}) collective-permute-start(f32[40,512]{1,0:T(8,128)S(1)} %get-tuple-element.44), channel_id=1, source_target_pairs={{0,25},{1,26},{2,27},{3,28},{4,29},{5,30},{6,31},{7,24},{8,1},{9,2... | collective-permute-start | bytes 245768 | tf_op jit(solution)/shard_map/ppermute | solution.py:174
  219.1 35.2 %collective-permute-start.15 = (f32[40,512]{1,0:T(8,128)S(1)}, f32[40,512]{1,0:T(8,128)S(1)}, u32[]{:S(2)}, u32[]{:S(2)}) collective-permute-start(f32[40,512]{1,0:T(8,128)S(1)} %get-tuple-element.45), channel_id=1, source_target_pairs={{0,7},{1,0},{2,1},{3,2},{4,3},{5,4},{6,5},{7,6},{8,15},{9,8},{10,9... | collective-permute-start | bytes 245768 | tf_op jit(solution)/shard_map/ppermute | solution.py:174
  221.4 32.9 %collective-permute-start.14 = (f32[40,512]{1,0:T(8,128)S(1)}, f32[40,512]{1,0:T(8,128)S(1)}, u32[]{:S(2)}, u32[]{:S(2)}) collective-permute-start(f32[40,512]{1,0:T(8,128)S(1)} %get-tuple-element.46), channel_id=1, source_target_pairs={{0,1},{1,2},{2,3},{3,4},{4,5},{5,6},{6,7},{7,0},{8,9},{9,10},{10,1... | collective-permute-start | bytes 245768 | tf_op jit(solution)/shard_map/ppermute | solution.py:174
  221.4 32.9 %collective-permute-start.13 = (f32[40,512]{1,0:T(8,128)S(1)}, f32[40,512]{1,0:T(8,128)S(1)}, u32[]{:S(2)}, u32[]{:S(2)}) collective-permute-start(f32[40,512]{1,0:T(8,128)S(1)} %get-tuple-element.47), channel_id=1, source_target_pairs={{0,15},{1,8},{2,9},{3,10},{4,11},{5,12},{6,13},{7,14},{8,23},{9,16... | collective-permute-start | bytes 245768 | tf_op jit(solution)/shard_map/ppermute | solution.py:174
  224.6 0.6 copy-start.19
  225.3 29.1 %collective-permute-start.12 = (f32[40,512]{1,0:T(8,128)S(1)}, f32[40,512]{1,0:T(8,128)S(1)}, u32[]{:S(2)}, u32[]{:S(2)}) collective-permute-start(f32[40,512]{1,0:T(8,128)S(1)} %get-tuple-element.48), channel_id=1, source_target_pairs={{0,8},{1,9},{2,10},{3,11},{4,12},{5,13},{6,14},{7,15},{8,16},{9,17... | collective-permute-start | bytes 245768 | tf_op jit(solution)/shard_map/ppermute | solution.py:174
  226.4 0.6 copy-start.21
  227.1 27.3 %collective-permute-start.11 = (f32[40,512]{1,0:T(8,128)S(1)}, f32[40,512]{1,0:T(8,128)S(1)}, u32[]{:S(2)}, u32[]{:S(2)}) collective-permute-start(f32[40,512]{1,0:T(8,128)S(1)} %get-tuple-element.49), channel_id=1, source_target_pairs={{0,9},{1,10},{2,11},{3,12},{4,13},{5,14},{6,15},{7,8},{8,17},{9,18... | collective-permute-start | bytes 245768 | tf_op jit(solution)/shard_map/ppermute | solution.py:174
  229.3 2.1 copy-start.7
  253.0 1.3 copy-start.6
  254.3 8.8 %copy-start.4 = (f32[4104,128]{1,0:T(8,128)}, f32[4104,128]{1,0:T(8,128)S(1)}, u32[]{:S(2)}) copy-start(f32[4104,128]{1,0:T(8,128)S(1)} %get-tuple-element.34.refs_1_) | copy-start | bytes 6303748
  254.3 0.7 copy-start.23
  254.3 0.7 copy-start.25
  254.3 0.7 copy-start.27
  254.4 0.7 copy-start.29
  254.4 0.8 copy-start.31
  255.1 96.4 %all-to-all-start.2 = ((f32[4,1024,256]{2,1,0:T(8,128)}), f32[4,1024,256]{2,1,0:T(8,128)}, u32[]{:S(2)}, u32[]{:S(2)}) async-start(f32[4,1024,256]{2,1,0:T(8,128)} %bitcast.31), calls=%async_computation.2 | async-start | bytes 8388608 | tf_op jit(solution)/shard_map/all_to_all | solution.py:674
  260.7 2.4 copy-start.8
  260.7 2.4 copy-start.9
  260.7 2.4 copy-start.13
  262.1 1.0 copy-start.16
  307.6 1.3 copy-start.14
  309.0 50.4 %copy-start.20 = (f32[40,512]{1,0:T(8,128)S(1)}, f32[40,512]{1,0:T(8,128)}, u32[]{:S(2)}) copy-start(f32[40,512]{1,0:T(8,128)} %copy-done.19) | copy-start | bytes 245764
  309.0 50.4 %copy-start.22 = (f32[40,512]{1,0:T(8,128)S(1)}, f32[40,512]{1,0:T(8,128)}, u32[]{:S(2)}) copy-start(f32[40,512]{1,0:T(8,128)} %copy-done.21) | copy-start | bytes 245764
  309.0 50.4 %copy-start.24 = (f32[40,512]{1,0:T(8,128)S(1)}, f32[40,512]{1,0:T(8,128)}, u32[]{:S(2)}) copy-start(f32[40,512]{1,0:T(8,128)} %copy-done.23) | copy-start | bytes 245764
  316.1 59.6 %copy-start.5 = (f32[4104,128]{1,0:T(8,128)S(1)}, f32[4104,128]{1,0:T(8,128)}, u32[]{:S(2)}) copy-start(f32[4104,128]{1,0:T(8,128)} %copy-done.4) | copy-start | bytes 6303748
  351.6 35.6 %all-to-all-start.3 = ((f32[4,256,256]{2,1,0:T(8,128)}), f32[4,256,256]{2,1,0:T(8,128)}, u32[]{:S(2)}, u32[]{:S(2)}) async-start(f32[4,256,256]{2,1,0:T(8,128)} %bitcast.32), calls=%async_computation.3 | async-start | bytes 2097152 | tf_op jit(solution)/shard_map/all_to_all | solution.py:674
  359.4 1.6 copy-start.15
  361.0 0.9 copy-start.26
  361.9 0.9 copy-start.28
  362.7 0.9 copy-start.30
  363.6 0.9 copy-start.32
  364.5 11.2 %copy-start.10 = (bf16[2,512,512]{2,1,0:T(8,128)(2,1)S(1)}, bf16[2,512,512]{2,1,0:T(8,128)(2,1)}, u32[]{:S(2)}) copy-start(bf16[2,512,512]{2,1,0:T(8,128)(2,1)} %constant.39.clone.refs_5_) | copy-start | bytes 3145732
  387.2 1.2 copy-start.11

commit v4 on v3

--- a/solution.py
+++ b/solution.py
@@ -18,11 +18,13 @@
 SHIFT = 6
 LANE_SHIFT = 7
 VMEM_BYTES = 48 * 1024 * 1024
-CHUNKS = (1, 2, 4, 1)
+CHUNKS = (1, 3, 3, 1)
 TOP_ROWS = TOP // 2
 
 DEPOSIT_SCALE = 8.0
-OFFSETS = tuple((a, b) for a in (-1, 0, 1) for b in (-1, 0, 1) if (a, b) != (0, 0))
+SENT = ((0, 0), (2, 0), (1, 0), (0, 1), (1, 1), (0, 2), (2, 1), (1, 2))
+GOT = ((3, 2), (3, 1), (3, 0), (1, 1), (0, 1), (2, 2), (2, 1), (2, 0))
+IN_ROW = 0x57241360
 
 SMEM_WHOLE = pl.BlockSpec(memory_space=pltpu.SMEM)
 VMEM_WHOLE = pl.BlockSpec(memory_space=pltpu.VMEM)
@@ -77,7 +79,7 @@
 
 
 def whole_table_kernel(*refs, slot_steps):
-    top_refs, out_ref = refs[8:-2], refs[-1]
+    top_refs, out_ref = refs[4:-2], refs[-1]
     step = pl.program_id(0)
     for k in range(slot_steps):
 
@@ -85,8 +87,10 @@
         def _():
             at = 0
             for n in (2 * k, 2 * k + 1):
-                for c in range(refs[n].shape[1] // LANES):
-                    out_ref[at : at + LANES, :] = spread(refs[n][:, c * LANES : (c + 1) * LANES])
+                part, place = GOT[n]
+                for c in range(refs[part].shape[2] // LANES):
+                    block = refs[part][place, :, c * LANES : (c + 1) * LANES]
+                    out_ref[at : at + LANES, :] = spread(block)
                     at += LANES
 
     rows = out_ref.shape[0]
@@ -107,7 +111,7 @@
 
 
 def whole_table(table, arrived, tops):
-    slots = arrived[0].shape[1]
+    slots = arrived[0].shape[2]
     rows = 2 * slots
     top_rows = 2 * sum(part.shape[0] for part in tops)
     first = (table.shape[0] - 8 * slots - top_rows) // rows
@@ -115,9 +119,9 @@
         functools.partial(whole_table_kernel, slot_steps=4),
         grid=(4 + top_rows // rows,),
         out_shape=jax.ShapeDtypeStruct(table.shape, jnp.float32),
-        in_specs=[VMEM_WHOLE] * (8 + len(tops)) + [pl.BlockSpec(memory_space=pl.ANY)],
+        in_specs=[VMEM_WHOLE] * (4 + len(tops)) + [pl.BlockSpec(memory_space=pl.ANY)],
         out_specs=pl.BlockSpec((rows, LANES), lambda i: (first + i, 0)),
-        input_output_aliases={8 + len(tops): 0},
+        input_output_aliases={4 + len(tops): 0},
         compiler_params=params(),
         cost_estimate=cost(10**6, 16 * 10**6),
         name="whole_table",
@@ -129,7 +133,7 @@
 
 
 def pack_kernel(list_ref, count_ref, table_ref, *refs):
-    outs, held = refs[:8], refs[8:]
+    outs, held = refs[:3], refs[3:]
     slot_tiles = list_ref.shape[1] // LANES
     for n in range(8):
 
@@ -141,7 +145,8 @@
                     rows[r : r + 1, :] = table_ref[list_ref[n, first + r]]
             for first, rows in zip(firsts, held):
                 live = (lane_ids((KPAD, LANES)) + first) < count_ref[n]
-                outs[n][:, pl.ds(first, LANES)] = jnp.where(live, rows[...].T[:KPAD], 0.0)
+                part, at = SENT[n]
+                outs[part][at, :, pl.ds(first, LANES)] = jnp.where(live, rows[...].T[:KPAD], 0.0)
 
 
 def pack(table, cell_count, proxy_list, proxy_count):
@@ -149,13 +154,15 @@
     return pl.pallas_call(
         pack_kernel,
         grid=(1,),
-        out_shape=(jax.ShapeDtypeStruct((KPAD, slots), jnp.float32),) * 8,
+        out_shape=tuple(jax.ShapeDtypeStruct((size, KPAD, slots), jnp.float32) for size in (3, 3, 2)),
         in_specs=[
             SMEM_WHOLE,
             SMEM_WHOLE,
             pl.BlockSpec((cell_count, 1, LANES), lambda i: (0, 0, 0)),
         ],
-        out_specs=(pl.BlockSpec((KPAD, slots), lambda i: (0, 0)),) * 8,
+        out_specs=tuple(
+            pl.BlockSpec((size, KPAD, slots), lambda i: (0, 0, 0)) for size in (3, 3, 2)
+        ),
         scratch_shapes=[pltpu.VMEM((LANES, LANES), jnp.float32)] * 2,
         compiler_params=params(),
         cost_estimate=cost(10**6, 25 * 10**6),
@@ -163,16 +170,15 @@
     )(proxy_list, proxy_count, as_rows(table))
 
 
-def exchange(blocks, n_gx, n_gy):
-    arrived = [None] * 8
-    for m, (a, b) in enumerate(OFFSETS):
-        pairs = [
-            (x * n_gy + y, (x + a) % n_gx * n_gy + (y + b) % n_gy)
-            for x in range(n_gx)
-            for y in range(n_gy)
-        ]
-        arrived[7 - m] = lax.ppermute(blocks[m], ("gx", "gy"), pairs)
-    return arrived
+def exchange(down, up, mid):
+    def shift(value, axis, by):
+        count = lax.axis_size(axis)
+        return lax.ppermute(value, axis, [(i, (i + by) % count) for i in range(count)])
+
+    down, up = shift(down, "gy", -1), shift(up, "gy", 1)
+    left = shift(jnp.stack([down[0], mid[0], up[0]]), "gx", -1)
+    right = shift(jnp.stack([down[2], mid[1], up[2]]), "gx", 1)
+    return down, up, left, right
 
 
 def order_kernel(packed_ref, out_ref):
@@ -256,7 +262,9 @@
     if turned:
         per = slots // LANES
         shape = (steps // per, KPAD, slots)
-        out_spec = pl.BlockSpec((1, KPAD, LANES), lambda i: (i // per, 0, i % per))
+        out_spec = pl.BlockSpec(
+            (1, KPAD, LANES), lambda i: ((IN_ROW >> (4 * (i // per))) & 7, 0, i % per)
+        )
     else:
         shape = (steps * LANES, LANES)
         out_spec = pl.BlockSpec((LANES, LANES), lambda i: (i, 0))
@@ -279,8 +287,8 @@
 
 
 def add_back_kernel(list_ref, count_ref, own_ref, *refs):
-    slot_refs, out_ref = refs[:8], refs[8]
-    rows, sums = refs[9], refs[10:]
+    slot_refs, out_ref = refs[:4], refs[4]
+    rows, sums = refs[5], refs[6:]
     slots = list_ref.shape[1]
     sums[0][...] = own_ref[...]
     for held in sums[1:]:
@@ -288,7 +296,8 @@
     for n in range(8):
         for k in range(slots // LANES):
             live = (lane_ids((KPAD, LANES)) + k * LANES) < count_ref[n]
-            values = jnp.where(live, slot_refs[n][:, k * LANES : (k + 1) * LANES], 0.0)
+            part, place = GOT[n]
+            values = jnp.where(live, slot_refs[part][place, :, k * LANES : (k + 1) * LANES], 0.0)
             at = n * slots + k * LANES
             rows[at : at + LANES, :] = spread(values)
 
@@ -316,7 +325,7 @@
     return pl.pallas_call(
         add_back_kernel,
         out_shape=jax.ShapeDtypeStruct((coef_count, cell_count), jnp.float32),
-        in_specs=[SMEM_WHOLE, SMEM_WHOLE] + [VMEM_WHOLE] * 9,
+        in_specs=[SMEM_WHOLE, SMEM_WHOLE] + [VMEM_WHOLE] * 5,
         out_specs=VMEM_WHOLE,
         scratch_shapes=[pltpu.VMEM((8 * slots, LANES), jnp.float32)]
         + [pltpu.VMEM((cell_count, LANES), jnp.float32)] * 8,
@@ -346,7 +355,7 @@
         functools.partial(carve_kernel, first=first),
         out_shape=jax.ShapeDtypeStruct((sources, count, rows, width), jnp.float32),
         in_specs=[pl.BlockSpec(memory_space=pl.ANY)],
-        out_specs=pl.BlockSpec(memory_space=pl.ANY),
+        out_specs=VMEM_WHOLE,
         scratch_shapes=[pltpu.SemaphoreType.DMA((sources,))],
         compiler_params=params(),
         cost_estimate=cost(0, 8 * count * sources * rows * width),
@@ -354,10 +363,8 @@
     )(mesh)
 
 
-def first_part_kernel(mesh_ref, place_ref, cells_ref, out_ref, ride, sems):
-    sources, whole_rows, width = out_ref.shape
-    extra = ride.shape[0]
-    rows = whole_rows - extra
+def first_part_kernel(mesh_ref, place_ref, cells_ref, out_ref, sems, *, rows):
+    sources, _, width = out_ref.shape
     copies = [
         pltpu.make_async_copy(
             mesh_ref.at[0, pl.ds(s * rows, rows), :], out_ref.at[s, pl.ds(0, rows), :], sems.at[s]
@@ -367,22 +374,20 @@
     for copy in copies:
         copy.start()
     is_first = lane_ids((TOP_ROWS, LANES)) < KPAD
-    table = spread(jnp.concatenate([cells_ref[:, :LANES], jnp.zeros((KPAD - cells_ref.shape[0], LANES), jnp.float32)], axis=0))
+    rest = jnp.zeros((KPAD - cells_ref.shape[0], LANES), jnp.float32)
+    table = spread(jnp.concatenate([cells_ref[:, :LANES], rest], axis=0))
     top = jnp.where(is_first, table[:TOP_ROWS, :], table[TOP_ROWS : 2 * TOP_ROWS, :])
     blocks = [place_ref[...].astype(jnp.float32), cell_lines(cells_ref), top]
-    at = 0
+    at = rows
     for block in blocks:
         high = block.shape[0] * LANES // width
         for h in range(width // LANES):
-            ride[at : at + high, h * LANES : (h + 1) * LANES] = block[h * high : (h + 1) * high, :]
+            for s in range(sources):
+                out_ref[s, at : at + high, h * LANES : (h + 1) * LANES] = block[
+                    h * high : (h + 1) * high, :
+                ]
         at += high
-    more = [
-        pltpu.make_async_copy(ride, out_ref.at[s, pl.ds(rows, extra), :], sems.at[sources + s])
-        for s in range(sources)
-    ]
-    for copy in more:
-        copy.start()
-    for copy in copies + more:
+    for copy in copies:
         copy.wait()
 
 
@@ -395,13 +400,12 @@
     rows, width = mesh.shape[1] // sources, mesh.shape[2]
     extra = (2 * place.size + TOP_ROWS * LANES) // width
     return pl.pallas_call(
-        first_part_kernel,
+        functools.partial(first_part_kernel, rows=rows),
         out_shape=jax.ShapeDtypeStruct((sources, rows + extra, width), jnp.float32),
         in_specs=[pl.BlockSpec(memory_space=pl.ANY), VMEM_WHOLE, VMEM_WHOLE],
-        out_specs=pl.BlockSpec(memory_space=pl.ANY),
+        out_specs=VMEM_WHOLE,
         scratch_shapes=[
-            pltpu.VMEM((extra, width), jnp.float32),
-            pltpu.SemaphoreType.DMA((2 * sources,)),
+            pltpu.SemaphoreType.DMA((sources,)),
         ],
         compiler_params=params(),
         cost_estimate=cost(0, 8 * sources * rows * width),
@@ -496,7 +500,7 @@
         held[...] = jnp.zeros_like(held)
 
     def line(g, _):
-        def one(j, _):
+        def one(j):
             at = [((2 * s + h) * lines + g, j) for h in range(2) for s in range(sources)]
             codes = [code_ref[i] for i in at]
             to = [pl.ds(code >> LANE_SHIFT, 1) for code in codes]
@@ -507,9 +511,13 @@
             ]
             for held, rows, row in zip(refs, to, new):
                 held[rows, :] = row
+
+        def four(i, _):
+            for j in range(4):
+                one(4 * i + j)
             return 0
 
-        return lax.fori_loop(0, bound_ref[g, 0], one, 0)
+        return lax.fori_loop(0, (bound_ref[g, 0] + 3) >> 2, four, 0)
 
     lax.fori_loop(0, lines, line, 0)
     for out_ref, held in zip(outs, others):
@@ -689,7 +697,7 @@
     base = cell_count + 8 * slots
     table = own_table(cells, base + TOP * domains)
     outgoing = pack(table, cell_count, lists, counts)
-    arrived = exchange(outgoing, n_gx, n_gy)
+    arrived = exchange(*outgoing)
 
     top = pair_source - base
     domain = top >> log2(TOP)
@@ -715,21 +723,21 @@
         held = jnp.concatenate(tops, axis=0) if bit else top_own
         tops.append(lax.ppermute(held, "gy", [(i, i ^ (1 << bit)) for i in range(n_gy)]))
 
-    parts.append(send(after(carved[0], parts[0], sources, ops, *arrived)))
+    parts.append(send(after(carved[0], parts[0], *arrived)))
     adds = deposit(codes, amounts, bounds, add_rows + 8, n_gx)
     table = whole_table(table, arrived, tops)
     cell_steps = cell_count // LANES
     slot_steps = 8 * slots // LANES
     slot_fields = m2l(sources, block_class, table, ops, cell_steps, slot_steps, True, slots)
-    returned = exchange([slot_fields[m] for m in range(8)], n_gx, n_gy)
-    parts.append(send(after(carved[1], parts[1], adds[0], *returned)))
+    returned = exchange(slot_fields[:3], slot_fields[3:6], slot_fields[6:])
+    parts.append(send(after(carved[1], parts[1], slot_fields)))
     own_fields = m2l(sources, block_class, table, ops, 0, cell_steps, False, slots)
 
     tables = fourier_tables(n_gx * width)
     spectrum = None
     for i, (at, size) in enumerate(spans):
         if i == 2:
-            parts.append(send(after(carved[2], parts[2], own_fields, spectrum)))
+            parts.append(send(after(carved[2], parts[2], own_fields, spectrum, *returned)))
         spectrum = fourier(parts[i], size, adds, tables, at, planes, spectrum, own_rows)
 
     field_tensors = add_back(lists, counts, own_fields, returned, coef_count)

time: 396 us -> 267 us (0.67)
  Pallas kernels: 265 us -> 176 us
  waiting for transfers between devices: 44.3 us -> 26.5 us
  starting transfers between devices: 48.8 us -> 32.6 us
  local copies, waits for them, and re-layouts: 27.9 us -> 19.5 us
    pallas_call x3, Pallas kernels: 68.2 us -> 8.85 us  [carve(): pl.pallas_call(functools.partial(carve_kernel, first=first), out_shape=ja...]
    all_to_all x4, waiting for transfers between devices: 35.4 us -> 0.01 us  [send(): return lax.all_to_all(part, 'gx', 0, 0, tiled=True)]
    pallas_call x2, Pallas kernels: 42.9 us -> 12.3 us  [the longest x1 9.99 us: pack(): pl.pallas_call(pack_kernel, grid=(1,), out_shape=tuple((jax.ShapeDtypeStr...]
    ppermute x16 -> x8, waiting for transfers between devices: 0.04 us -> 25.7 us  [shift(): lax.ppermute(value, axis, [(i, (i + by) % count) for i in range(count)])]
    ppermute x16 -> x8, starting transfers between devices: 23.6 us -> 6.2 us  [shift(): lax.ppermute(value, axis, [(i, (i + by) % count) for i in range(count)])]
    unnamed x79 -> x69, local copies, waits for them, and re-layouts: 27.8 us -> 19.3 us
    ppermute x3, waiting for transfers between devices: 8.85 us -> 0.87 us  [on_device(): lax.ppermute(held, 'gy', [(i, i ^ 1 << bit) for i in range(n_gy)])]
  transfers between devices with their start and end apart: 23 -> 15, of which waited for: 4 -> 7; matrix products, arithmetic and copies ran while one was open for 3% -> 6% of each run, Pallas kernels for 58% -> 64%
where the time goes in v4:
time: 267 us; the launch traced here: 265 us
  Pallas kernels  176 us (66%)
  starting transfers between devices  32.6 us (12%)
  waiting for transfers between devices  26.5 us (10%)
  local copies, waits for them, and re-layouts  19.5 us (7%)
  other arithmetic  9.2 us (3%)
    pallas_call x2, Pallas kernels, m2l(): pl.pallas_call(functools.partial(m2l_kernel, first=first, turned=turned),...  80 us
    pallas_call x4, Pallas kernels, fourier(): pl.pallas_call(functools.partial(fourier_kernel, sources=sources), grid=(...  28.6 us
    ppermute x8, waiting for transfers between devices, shift(): lax.ppermute(value, axis, [(i, (i + by) % count) for i in range(count)])  25.7 us
    all_to_all x4, starting transfers between devices, send(): return lax.all_to_all(part, 'gx', 0, 0, tiled=True)  23.3 us
    pallas_call x1, Pallas kernels, deposit(): pl.pallas_call(deposit_kernel, out_shape=(jax.ShapeDtypeStruct((rows, LAN...  21.3 us
    unnamed x69, local copies, waits for them, and re-layouts  19.3 us
    pallas_call x1, Pallas kernels, add_back(): pl.pallas_call(add_back_kernel, out_shape=jax.ShapeDtypeStruct((coef_coun...  11.2 us
    pallas_call x1, Pallas kernels, pack(): pl.pallas_call(pack_kernel, grid=(1,), out_shape=tuple((jax.ShapeDtypeStr...  9.99 us
  transfers between devices with their start and end apart: 15, of which 7 were waited for; matrix products, arithmetic and copies ran while one was open for 6% of the time, Pallas kernels for 64%

profile of v4, /device:TPU:8, one launch (start us, length us, event | category | flops | bytes accessed | tf_op | source)
XLA Modules:
  0.0 264.6 jit_solution(11063868733353843013)
XLA Ops:
  0.6 1.1 copy-done.13
  1.7 0.7 copy-done.26
  2.4 2.4 first_part.1
  4.8 5.3 %all-to-all-start = ((f32[4,296,256]{2,1,0:T(8,128)}), f32[4,296,256]{2,1,0:T(8,128)S(1)}, u32[]{:S(2)}, u32[]{:S(2)}) async-start(f32[4,296,256]{2,1,0:T(8,128)} %first_part.1), calls=%async_computation | async-start | bytes 2424832 | tf_op jit(solution)/shard_map/all_to_all | solution.py:682
  10.2 3.3 %own_table.1.refs_8_ = f32[9216,128]{1,0:T(8,128)S(1)} custom-call(f32[40,4096]{1,0:T(8,128)S(1)} %pad.12.cells_ref), custom_call_target="tpu_custom_call" | custom-call | flops 1000000 | bytes 12000000 | tf_op jit(solution)/shard_map/own_table/pallas_call | solution.py:59
  13.5 0.0 copy-start
  13.6 10.0 %pack.1 = (f32[3,40,512]{2,1,0:T(8,128)S(1)}, f32[3,40,512]{2,1,0:T(8,128)S(1)}, f32[2,40,512]{2,1,0:T(8,128)S(1)}) custom-call(s32[8,512]{1,0:T(8,128)S(1)} %bitcast.18, s32[8]{0:T(128)S(1)} %bitcast.21, f32[9216,1,128]{2,1,0:T(1,128)S(1)} %bitcast.12), custom_call_target="tpu_custom_call" | custom-call | flops 1000000 | bytes 25000000 | tf_op jit(solution)/shard_map/pack/pallas_call | solution.py:154
  23.6 1.4 collective-permute-start
  24.9 6.0 %collective-permute-done.refs_0_ = f32[3,40,512]{2,1,0:T(8,128)S(1)} collective-permute-done((f32[3,40,512]{2,1,0:T(8,128)S(1)}, f32[3,40,512]{2,1,0:T(8,128)S(1)}, u32[]{:S(2)}, u32[]{:S(2)}) %collective-permute-start) | collective-permute-done | bytes 245792 | tf_op jit(solution)/shard_map/ppermute | solution.py:176
  30.9 1.9 collective-permute-done.1.refs_1_
  32.9 1.5 collective-permute-start.3
  34.4 0.6 collective-permute-start.2
  35.1 3.6 %carve.5 = f32[4,3,256,256]{3,2,1,0:T(8,128)} custom-call(f32[8,1024,256]{2,1,0:T(8,128)} %mesh_ref.7), custom_call_target="tpu_custom_call" | custom-call | bytes 6291456 | tf_op jit(solution)/shard_map/carve/pallas_call | solution.py:354
  38.6 7.9 %collective-permute-done.3.refs_3_ = f32[3,40,512]{2,1,0:T(8,128)S(1)} collective-permute-done((f32[3,40,512]{2,1,0:T(8,128)S(1)}, f32[3,40,512]{2,1,0:T(8,128)S(1)}, u32[]{:S(2)}, u32[]{:S(2)}) %collective-permute-start.3) | collective-permute-done | bytes 245792 | tf_op jit(solution)/shard_map/ppermute | solution.py:176
  46.6 1.9 collective-permute-done.2.refs_2_
  48.5 0.0 all-to-all-done.part_ref.refs_0_
  48.5 6.1 %all-to-all-start.1 = ((f32[4,768,256]{2,1,0:T(8,128)}), f32[4,768,256]{2,1,0:T(8,128)}, u32[]{:S(2)}, u32[]{:S(2)}) async-start(f32[4,768,256]{2,1,0:T(8,128)} %bitcast.10), calls=%async_computation.1 | async-start | bytes 6291456 | tf_op jit(solution)/shard_map/all_to_all | solution.py:682
  54.5 5.2 %copy.17 = f32[189,35,35]{1,2,0:T(8,128)} copy(f32[189,35,35]{0,2,1:T(8,128)} %param.17) | data formatting | bytes 1852200 | tf_op args[6]
  59.8 1.4 sift.1
  61.1 0.6 copy-done.24
  61.8 5.7 %pad_reduce-precision_fusion = (f32[189,40,40]{2,1,0:T(8,128)}, f32[189,40,40]{2,1,0:T(8,128)}) fusion(f32[189,35,35]{2,1,0:T(8,128)} %bitcast.23), kind=kLoop, calls=%fused_computation.3 | loop fusion | flops 604800 | bytes 3345300 | tf_op jit(solution)/shard_map/reduce_precision | solution.py:713
  67.5 0.0 collective-permute-done.4.refs_5_
  67.5 1.6 collective-permute-start.5
  69.1 0.2 fusion.2.packed_ref
  69.2 3.7 %carve.4 = f32[4,3,256,256]{3,2,1,0:T(8,128)} custom-call(f32[8,1024,256]{2,1,0:T(8,128)} %mesh_ref.7), custom_call_target="tpu_custom_call" | custom-call | bytes 6291456 | tf_op jit(solution)/shard_map/carve/pallas_call | solution.py:354
  73.0 0.0 slice-start
  73.0 7.4 %order.1.source_ref = s32[512,128]{1,0:T(8,128)S(1)} custom-call(s32[512,128]{1,0:T(8,128)S(1)} %fusion.2.packed_ref), custom_call_target="tpu_custom_call" | custom-call | flops 1000000 | bytes 20000000 | tf_op jit(solution)/shard_map/order/pallas_call | solution.py:203
  80.4 0.0 collective-permute-done.5.refs_6_
  80.4 1.6 collective-permute-start.6
  82.0 3.2 %select_maximum_fusion.ops_ref = f32[189,40,128]{2,1,0:T(8,128)S(1)} fusion(f32[189,40,40]{2,1,0:T(8,128)} %get-tuple-element.31, f32[189,40,40]{2,1,0:T(8,128)S(1)} %copy-done.29), kind=kLoop, calls=%fused_computation | loop fusion | flops 3870720 | bytes 6289920 | tf_op jit(solution)/shard_map/concatenate | solution.py:714
  85.3 0.0 copy-start.27
  85.3 0.9 collective-permute-done.6.refs_7_
  86.1 1.3 whole_table.1
  87.5 2.2 copy-done.1
  89.7 40.1 %m2l_slots.1 = f32[8,40,512]{2,1,0:T(8,128)S(1)} custom-call(s32[512,128]{1,0:T(8,128)S(1)} %order.1.source_ref, s32[1024]{0:T(1024)S(1)} %copy-done.27, f32[9216,1,128]{2,1,0:T(1,128)} %bitcast.15, f32[189,40,128]{2,1,0:T(8,128)S(1)} %select_maximum_fusion.ops_ref), custom_call_target="tpu_custom_call" | custom-call | flops 1000000 | bytes 150000000 | tf_op jit(solution)/shard_map/m2l_slots/pallas_call | solution.py:271
  129.8 0.0 all-to-all-done.1.refs_0_
  129.8 5.1 %all-to-all-start.2 = ((f32[4,768,256]{2,1,0:T(8,128)}), f32[4,768,256]{2,1,0:T(8,128)}, u32[]{:S(2)}, u32[]{:S(2)}) async-start(f32[4,768,256]{2,1,0:T(8,128)} %bitcast.9), calls=%async_computation.2 | async-start | bytes 6291456 | tf_op jit(solution)/shard_map/all_to_all | solution.py:682
  134.9 0.2 collective-permute-start.7
  135.1 0.3 collective-permute-start.8
  135.5 6.0 %collective-permute-done.7.refs_0_ = f32[3,40,512]{2,1,0:T(8,128)S(1)} collective-permute-done((f32[3,40,512]{2,1,0:T(8,128)S(1)}, f32[3,40,512]{2,1,0:T(8,128)S(1)}, u32[]{:S(2)}, u32[]{:S(2)}) %collective-permute-start.7) | collective-permute-done | bytes 245792 | tf_op jit(solution)/shard_map/ppermute | solution.py:176
  141.5 2.0 collective-permute-done.8.refs_1_
  143.5 1.5 collective-permute-start.10
  145.0 0.0 copy-start.4
  145.0 0.0 copy-start.5
  145.1 0.6 collective-permute-start.9
  145.7 1.5 carve.3
  147.2 1.0 copy-done.12
  148.2 21.3 %deposit.1 = (f32[4104,128]{1,0:T(8,128)S(1)}, f32[4104,128]{1,0:T(8,128)S(1)}, f32[4104,128]{1,0:T(8,128)}, f32[4104,128]{1,0:T(8,128)}) custom-call(s32[128,128]{1,0:T(8,128)S(1)} %get-tuple-element.22.code_ref, f32[128,128]{1,0:T(8,128)S(1)} %copy-done.25, s32[16,128]{1,0:T(8,128)S(1)} %get-tuple-element.24.bound_ref), custom_call_target="tpu_custom_call" | custom-call | flops 1000000 | bytes 40000000 | tf_op jit(solution)/shard_map/deposit/pallas_call | solution.py:528
  169.5 1.3 copy-done.3
  170.9 4.6 %fourier.4.refs_7_ = f32[2,8,256,1024]{3,2,1,0:T(8,128)} custom-call(f32[4,296,256]{2,1,0:T(8,128)S(1)} %copy-done.9, f32[4104,128]{1,0:T(8,128)S(1)} %get-tuple-element.25.refs_1_, f32[4104,128]{1,0:T(8,128)} %copy-done.3, f32[4104,128]{1,0:T(8,128)} %get-tuple-element.27.refs_3_, f32[4104,128]{1,0:T(8,128)} %get-tuple-element.28.refs_4_, ...), custom_call_target="tpu_custom_call" | custom-call | flops 1000000 | bytes 10000000 | tf_op jit(solution)/shard_map/fourier/pallas_call | solution.py:643
  175.4 39.9 %m2l_cells.1.own_ref = f32[4096,128]{1,0:T(8,128)S(1)} custom-call(s32[512,128]{1,0:T(8,128)S(1)} %order.1.source_ref, s32[1024]{0:T(1024)S(1)} %copy-done.27, f32[9216,1,128]{2,1,0:T(1,128)} %bitcast.16, f32[189,40,128]{2,1,0:T(8,128)} %copy-done.2), custom_call_target="tpu_custom_call" | custom-call | flops 1000000 | bytes 150000000 | tf_op jit(solution)/shard_map/m2l_cells/pallas_call | solution.py:271
  215.4 0.0 copy-start.16
  215.4 10.0 %fourier.5.refs_7_ = f32[2,8,256,1024]{3,2,1,0:T(8,128)} custom-call(f32[4,768,256]{2,1,0:T(8,128)} %all-to-all-done.1.refs_0_, f32[4104,128]{1,0:T(8,128)S(1)} %get-tuple-element.25.refs_1_, f32[4104,128]{1,0:T(8,128)} %copy-done.3, f32[4104,128]{1,0:T(8,128)} %get-tuple-element.27.refs_3_, ...), custom_call_target="tpu_custom_call", output_to_operand_aliasing={{}: (7, {})} | custom-call | flops 1000000 | bytes 30000000 | tf_op jit(solution)/shard_map/fourier/pallas_call | solution.py:643
  225.4 0.7 copy-done.19
  226.1 0.7 copy-done.21
  226.8 6.8 %all-to-all-start.3 = ((f32[4,256,256]{2,1,0:T(8,128)}), f32[4,256,256]{2,1,0:T(8,128)}, u32[]{:S(2)}, u32[]{:S(2)}) async-start(f32[4,256,256]{2,1,0:T(8,128)} %bitcast.17), calls=%async_computation.3 | async-start | bytes 2097152 | tf_op jit(solution)/shard_map/all_to_all | solution.py:682
  233.6 1.6 copy-done.11
  235.2 0.9 copy-done.18
  236.2 0.9 copy-done.20
  237.1 0.9 copy-done.22
  238.1 11.2 %add_back.1 = f32[35,4096]{1,0:T(8,128)} custom-call(s32[8,512]{1,0:T(8,128)S(1)} %bitcast.19, s32[8]{0:T(128)S(1)} %bitcast.22, f32[4096,128]{1,0:T(8,128)S(1)} %copy-done.11, f32[3,40,512]{2,1,0:T(8,128)S(1)} %copy-done.16, f32[3,40,512]{2,1,0:T(8,128)S(1)} %copy-done.18, f32[3,40,512]{2,1,0:T(8,128)S(1)} %copy-done.22, f32[3,40,512]{2,1,0:T(8,128)S(1)} %copy-done.20), custom_call_target="tpu_custom_call" | custom-call | flops 1000000 | bytes 30000000 | tf_op jit(solution)/shard_map/add_back/pallas_call | solution.py:325
  249.3 9.2 %fourier.6.refs_7_ = f32[2,8,256,1024]{3,2,1,0:T(8,128)} custom-call(f32[4,768,256]{2,1,0:T(8,128)} %all-to-all-done.2.refs_0_, f32[4104,128]{1,0:T(8,128)S(1)} %get-tuple-element.25.refs_1_, f32[4104,128]{1,0:T(8,128)} %copy-done.3, f32[4104,128]{1,0:T(8,128)} %get-tuple-element.27.refs_3_, ...), custom_call_target="tpu_custom_call", output_to_operand_aliasing={{}: (7, {})} | custom-call | flops 1000000 | bytes 30000000 | tf_op jit(solution)/shard_map/fourier/pallas_call | solution.py:643
  258.5 1.2 copy-done.7
  259.7 4.9 %fourier.7 = f32[2,8,256,1024]{3,2,1,0:T(8,128)} custom-call(f32[4,256,256]{2,1,0:T(8,128)} %all-to-all-done.3.refs_0_, f32[4104,128]{1,0:T(8,128)S(1)} %get-tuple-element.25.refs_1_, f32[4104,128]{1,0:T(8,128)} %copy-done.3, f32[4104,128]{1,0:T(8,128)} %get-tuple-element.27.refs_3_, ...), custom_call_target="tpu_custom_call", output_to_operand_aliasing={{}: (7, {})} | custom-call | flops 1000000 | bytes 10000000 | tf_op jit(solution)/shard_map/fourier/pallas_call | solution.py:643
  (70 shorter events, 0.3 us)
Async XLA Ops:
  0.6 1.1 copy-start.13
  1.7 0.7 copy-start.26
  2.4 7.7 %copy-start.14 = (f32[35,4096]{1,0:T(8,128)S(1)}, f32[35,4096]{1,0:T(8,128)}, u32[]{:S(2)}) copy-start(f32[35,4096]{1,0:T(8,128)} %cells_ref.1) | copy-start | bytes 1720324
  4.8 43.7 %all-to-all-start = ((f32[4,296,256]{2,1,0:T(8,128)}), f32[4,296,256]{2,1,0:T(8,128)S(1)}, u32[]{:S(2)}, u32[]{:S(2)}) async-start(f32[4,296,256]{2,1,0:T(8,128)} %first_part.1), calls=%async_computation | async-start | bytes 2424832 | tf_op jit(solution)/shard_map/all_to_all | solution.py:682
  10.1 3.4 %copy-start.23 = (s32[1,8,512]{2,1,0:T(8,128)S(1)}, s32[1,8,512]{2,1,0:T(8,128)}, u32[]{:S(2)}) copy-start(s32[1,8,512]{2,1,0:T(8,128)} %param.12) | copy-start | bytes 49156
  10.1 3.4 %copy-start.28 = (s32[1,8]{1,0:T(1,128)S(1)}, s32[1,8]{1,0:T(1,128)}, u32[]{:S(2)}) copy-start(s32[1,8]{1,0:T(1,128)} %param.13) | copy-start | bytes 100
  13.5 25.1 %copy-start = (f32[9216,128]{1,0:T(8,128)}, f32[9216,128]{1,0:T(8,128)S(1)}, u32[]{:S(2)}) copy-start(f32[9216,128]{1,0:T(8,128)S(1)} %own_table.1.refs_8_) | copy-start | bytes 14155780
  23.6 7.4 %collective-permute-start = (f32[3,40,512]{2,1,0:T(8,128)S(1)}, f32[3,40,512]{2,1,0:T(8,128)S(1)}, u32[]{:S(2)}, u32[]{:S(2)}) collective-permute-start(f32[3,40,512]{2,1,0:T(8,128)S(1)} %get-tuple-element.16), channel_id=1, source_target_pairs={{0,7},{1,0},{2,1},{3,2},{4,3},{5,4},{6,5},{7,6},{8,15},{9,8},{10,9... | collective-permute-start | bytes 737288 | tf_op jit(solution)/shard_map/ppermute | solution.py:176
  24.9 7.9 %collective-permute-start.1 = (f32[3,40,512]{2,1,0:T(8,128)S(1)}, f32[3,40,512]{2,1,0:T(8,128)S(1)}, u32[]{:S(2)}, u32[]{:S(2)}) collective-permute-start(f32[3,40,512]{2,1,0:T(8,128)S(1)} %get-tuple-element.17), channel_id=1, source_target_pairs={{0,1},{1,2},{2,3},{3,4},{4,5},{5,6},{6,7},{7,0},{8,9},{9,10},{10,1... | collective-permute-start | bytes 737288 | tf_op jit(solution)/shard_map/ppermute | solution.py:176
  32.9 13.7 %collective-permute-start.3 = (f32[3,40,512]{2,1,0:T(8,128)S(1)}, f32[3,40,512]{2,1,0:T(8,128)S(1)}, u32[]{:S(2)}, u32[]{:S(2)}) collective-permute-start(f32[3,40,512]{2,1,0:T(8,128)S(1)} %pad_maximum_fusion.1), channel_id=1, source_target_pairs={{0,8},{8,16},{16,24},{24,0},{1,9},{9,17},{17,25},{25,1},{2,10},{10... | collective-permute-start | bytes 737288 | tf_op jit(solution)/shard_map/ppermute | solution.py:176
  34.4 14.0 %collective-permute-start.2 = (f32[3,40,512]{2,1,0:T(8,128)S(1)}, f32[3,40,512]{2,1,0:T(8,128)S(1)}, u32[]{:S(2)}, u32[]{:S(2)}) collective-permute-start(f32[3,40,512]{2,1,0:T(8,128)S(1)} %pad_maximum_fusion), channel_id=1, source_target_pairs={{0,24},{8,0},{16,8},{24,16},{1,25},{9,1},{17,9},{25,17},{2,26},{10... | collective-permute-start | bytes 737288 | tf_op jit(solution)/shard_map/ppermute | solution.py:176
  48.5 11.3 %copy-start.8 = (f32[4,296,256]{2,1,0:T(8,128)}, f32[4,296,256]{2,1,0:T(8,128)S(1)}, u32[]{:S(2)}) copy-start(f32[4,296,256]{2,1,0:T(8,128)S(1)} %all-to-all-done.part_ref.refs_0_) | copy-start | bytes 3637252
  48.5 81.3 %all-to-all-start.1 = ((f32[4,768,256]{2,1,0:T(8,128)}), f32[4,768,256]{2,1,0:T(8,128)}, u32[]{:S(2)}, u32[]{:S(2)}) async-start(f32[4,768,256]{2,1,0:T(8,128)} %bitcast.10), calls=%async_computation.1 | async-start | bytes 6291456 | tf_op jit(solution)/shard_map/all_to_all | solution.py:682
  61.1 0.6 copy-start.24
  61.8 5.7 %collective-permute-start.4 = (f32[64,128]{1,0:T(8,128)S(1)}, f32[64,128]{1,0:T(8,128)S(1)}, u32[]{:S(2)}, u32[]{:S(2)}) collective-permute-start(f32[64,128]{1,0:T(8,128)S(1)} %get-tuple-element.19.refs_4_), channel_id=1, source_target_pairs={{0,1},{1,0},{2,3},{3,2},{4,5},{5,4},{6,7},{7,6},{8,9},{9,8},{10,11... | collective-permute-start | bytes 98312 | tf_op jit(solution)/shard_map/ppermute | solution.py:724
  61.8 7.3 %copy-start.30 = (s32[65536]{0:T(1024)S(1)}, s32[65536]{0:T(1024)}, u32[]{:S(2)}) copy-start(s32[65536]{0:T(1024)} %param.14) | copy-start | bytes 786436
  61.8 7.3 %copy-start.31 = (s32[65536]{0:T(1024)S(1)}, s32[65536]{0:T(1024)}, u32[]{:S(2)}) copy-start(s32[65536]{0:T(1024)} %param.15) | copy-start | bytes 786436
  67.5 12.9 %collective-permute-start.5 = (f32[128,128]{1,0:T(8,128)S(1)}, f32[128,128]{1,0:T(8,128)S(1)}, u32[]{:S(2)}, u32[]{:S(2)}) collective-permute-start(f32[128,128]{1,0:T(8,128)S(1)} %pad_maximum_fusion.5), channel_id=1, source_target_pairs={{0,2},{1,3},{2,0},{3,1},{4,6},{5,7},{6,4},{7,5},{8,10},{9,11},{10,... | collective-permute-start | bytes 196616 | tf_op jit(solution)/shard_map/ppermute | solution.py:724
  69.2 12.8 %copy-start.29 = (f32[189,40,40]{2,1,0:T(8,128)S(1)}, f32[189,40,40]{2,1,0:T(8,128)}, u32[]{:S(2)}) copy-start(f32[189,40,40]{2,1,0:T(8,128)} %get-tuple-element.30) | copy-start | bytes 3628804
  73.0 13.1 %slice-start = ((s8[4718592]{0:T(1024)(128)(4,1)}), s8[4194304]{0:T(1024)(128)(4,1)S(1)}, s32[]{:S(2)}) async-start(s8[4718592]{0:T(1024)(128)(4,1)} %bitcast.13), calls=%async_computation.4 | async-start | bytes 8388608
  80.4 5.7 %collective-permute-start.6 = (f32[256,128]{1,0:T(8,128)S(1)}, f32[256,128]{1,0:T(8,128)S(1)}, u32[]{:S(2)}, u32[]{:S(2)}) collective-permute-start(f32[256,128]{1,0:T(8,128)S(1)} %pad_maximum_fusion.4), channel_id=1, source_target_pairs={{0,4},{1,5},{2,6},{3,7},{4,0},{5,1},{6,2},{7,3},{8,12},{9,13},{10,... | collective-permute-start | bytes 393224 | tf_op jit(solution)/shard_map/ppermute | solution.py:724
  82.0 4.1 %slice-start.1 = ((s8[4718592]{0:T(1024)(128)(4,1)}), s8[524288]{0:T(1024)(128)(4,1)S(1)}, s32[]{:S(2)}) async-start(s8[4718592]{0:T(1024)(128)(4,1)} %bitcast.13), calls=%async_computation.5 | async-start | bytes 1048576
  85.2 4.4 %copy-start.2 = (f32[189,40,128]{2,1,0:T(8,128)}, f32[189,40,128]{2,1,0:T(8,128)S(1)}, u32[]{:S(2)}) copy-start(f32[189,40,128]{2,1,0:T(8,128)S(1)} %select_maximum_fusion.ops_ref) | copy-start | bytes 11612164
  85.3 4.4 %copy-start.27 = (s32[1024]{0:T(1024)S(1)}, s32[1024]{0:T(1024)}, u32[]{:S(2)}) copy-start(s32[1024]{0:T(1024)} %class_ref.3) | copy-start | bytes 12292
  87.5 2.2 copy-start.1
  129.8 97.1 %all-to-all-start.2 = ((f32[4,768,256]{2,1,0:T(8,128)}), f32[4,768,256]{2,1,0:T(8,128)}, u32[]{:S(2)}, u32[]{:S(2)}) async-start(f32[4,768,256]{2,1,0:T(8,128)} %bitcast.9), calls=%async_computation.2 | async-start | bytes 6291456 | tf_op jit(solution)/shard_map/all_to_all | solution.py:682
  134.9 6.5 %collective-permute-start.7 = (f32[3,40,512]{2,1,0:T(8,128)S(1)}, f32[3,40,512]{2,1,0:T(8,128)S(1)}, u32[]{:S(2)}, u32[]{:S(2)}) collective-permute-start(f32[3,40,512]{2,1,0:T(8,128)S(1)} %get-tuple-element.35), channel_id=1, source_target_pairs={{0,7},{1,0},{2,1},{3,2},{4,3},{5,4},{6,5},{7,6},{8,15},{9,8},{10,9... | collective-permute-start | bytes 737288 | tf_op jit(solution)/shard_map/ppermute | solution.py:176
  135.1 8.3 %collective-permute-start.8 = (f32[3,40,512]{2,1,0:T(8,128)S(1)}, f32[3,40,512]{2,1,0:T(8,128)S(1)}, u32[]{:S(2)}, u32[]{:S(2)}) collective-permute-start(f32[3,40,512]{2,1,0:T(8,128)S(1)} %get-tuple-element.34), channel_id=1, source_target_pairs={{0,1},{1,2},{2,3},{3,4},{4,5},{5,6},{6,7},{7,0},{8,9},{9,10},{10,1... | collective-permute-start | bytes 737288 | tf_op jit(solution)/shard_map/ppermute | solution.py:176
  141.4 3.6 %copy-start.15 = (f32[3,40,512]{2,1,0:T(8,128)}, f32[3,40,512]{2,1,0:T(8,128)S(1)}, u32[]{:S(2)}) copy-start(f32[3,40,512]{2,1,0:T(8,128)S(1)} %collective-permute-done.7.refs_0_) | copy-start | bytes 737284
  143.4 1.6 copy-start.17
  143.5 81.9 %collective-permute-start.10 = (f32[3,40,512]{2,1,0:T(8,128)S(1)}, f32[3,40,512]{2,1,0:T(8,128)S(1)}, u32[]{:S(2)}, u32[]{:S(2)}) collective-permute-start(f32[3,40,512]{2,1,0:T(8,128)S(1)} %pad_maximum_fusion.3), channel_id=1, source_target_pairs={{0,8},{8,16},{16,24},{24,0},{1,9},{9,17},{17,25},{25,1},{2,10},{10... | collective-permute-start | bytes 737288 | tf_op jit(solution)/shard_map/ppermute | solution.py:176
  145.0 3.2 %copy-start.25 = (f32[128,128]{1,0:T(8,128)S(1)}, f32[128,128]{1,0:T(8,128)}, u32[]{:S(2)}) copy-start(f32[128,128]{1,0:T(8,128)} %copy-done.24) | copy-start | bytes 196612
  145.0 25.8 %copy-start.4 = (bf16[2,512,512]{2,1,0:T(8,128)(2,1)S(1)}, bf16[2,512,512]{2,1,0:T(8,128)(2,1)}, u32[]{:S(2)}) copy-start(bf16[2,512,512]{2,1,0:T(8,128)(2,1)} %constant.39.clone.refs_5_) | copy-start | bytes 3145732
  145.0 25.8 %copy-start.5 = (bf16[2,512,512]{2,1,0:T(8,128)(2,1)S(1)}, bf16[2,512,512]{2,1,0:T(8,128)(2,1)}, u32[]{:S(2)}) copy-start(bf16[2,512,512]{2,1,0:T(8,128)(2,1)} %constant.40.clone.refs_6_) | copy-start | bytes 3145732
  145.1 25.8 %copy-start.9 = (f32[4,296,256]{2,1,0:T(8,128)S(1)}, f32[4,296,256]{2,1,0:T(8,128)}, u32[]{:S(2)}) copy-start(f32[4,296,256]{2,1,0:T(8,128)} %copy-done.8) | copy-start | bytes 3637252
  145.1 81.0 %collective-permute-start.9 = (f32[3,40,512]{2,1,0:T(8,128)S(1)}, f32[3,40,512]{2,1,0:T(8,128)S(1)}, u32[]{:S(2)}, u32[]{:S(2)}) collective-permute-start(f32[3,40,512]{2,1,0:T(8,128)S(1)} %pad_maximum_fusion.2), channel_id=1, source_target_pairs={{0,24},{8,0},{16,8},{24,16},{1,25},{9,1},{17,9},{25,17},{2,26},{10... | collective-permute-start | bytes 737288 | tf_op jit(solution)/shard_map/ppermute | solution.py:176
  147.2 1.0 copy-start.12
  169.5 1.3 copy-start.3
  215.4 10.0 %copy-start.10 = (f32[4096,128]{1,0:T(8,128)}, f32[4096,128]{1,0:T(8,128)S(1)}, u32[]{:S(2)}) copy-start(f32[4096,128]{1,0:T(8,128)S(1)} %m2l_cells.1.own_ref) | copy-start | bytes 6291460
  215.4 18.3 %copy-start.16 = (f32[3,40,512]{2,1,0:T(8,128)S(1)}, f32[3,40,512]{2,1,0:T(8,128)}, u32[]{:S(2)}) copy-start(f32[3,40,512]{2,1,0:T(8,128)} %copy-done.15) | copy-start | bytes 737284
  225.4 0.7 copy-start.19
  226.1 0.7 copy-start.21
  226.8 31.6 %all-to-all-start.3 = ((f32[4,256,256]{2,1,0:T(8,128)}), f32[4,256,256]{2,1,0:T(8,128)}, u32[]{:S(2)}, u32[]{:S(2)}) async-start(f32[4,256,256]{2,1,0:T(8,128)} %bitcast.17), calls=%async_computation.3 | async-start | bytes 2097152 | tf_op jit(solution)/shard_map/all_to_all | solution.py:682
  233.6 1.6 copy-start.11
  235.2 0.9 copy-start.18
  236.2 0.9 copy-start.20
  237.1 0.9 copy-start.22
  238.1 11.2 %copy-start.6 = (bf16[2,512,512]{2,1,0:T(8,128)(2,1)S(1)}, bf16[2,512,512]{2,1,0:T(8,128)(2,1)}, u32[]{:S(2)}) copy-start(bf16[2,512,512]{2,1,0:T(8,128)(2,1)} %constant.40.clone.refs_6_) | copy-start | bytes 3145732
  258.5 1.2 copy-start.7

commit v5 on v4

--- a/solution.py
+++ b/solution.py
@@ -18,7 +18,7 @@
 SHIFT = 6
 LANE_SHIFT = 7
 VMEM_BYTES = 48 * 1024 * 1024
-CHUNKS = (1, 3, 3, 1)
+CHUNKS = (2, 4, 2)
 TOP_ROWS = TOP // 2
 
 DEPOSIT_SCALE = 8.0
@@ -170,12 +170,14 @@
     )(proxy_list, proxy_count, as_rows(table))
 
 
-def exchange(down, up, mid):
+def exchange(down, up, mid, *before_gx):
     def shift(value, axis, by):
         count = lax.axis_size(axis)
         return lax.ppermute(value, axis, [(i, (i + by) % count) for i in range(count)])
 
     down, up = shift(down, "gy", -1), shift(up, "gy", 1)
+    if before_gx:
+        mid = after(mid, *before_gx)
     left = shift(jnp.stack([down[0], mid[0], up[0]]), "gx", -1)
     right = shift(jnp.stack([down[2], mid[1], up[2]]), "gx", 1)
     return down, up, left, right
@@ -211,79 +213,105 @@
     )(packed)
 
 
+def split_kernel(ops_ref, out_ref, *, group):
+    coefs = ops_ref.shape[1]
+
+    @pl.loop(0, ops_ref.shape[0], step=group)
+    def _(c):
+        at = pl.ds(c, group)
+        value = ops_ref[at]
+        high = value.astype(jnp.bfloat16).astype(jnp.float32)
+        out_ref[at] = jnp.zeros((group, KPAD, LANES), jnp.float32)
+        out_ref[at, :coefs, :coefs] = high
+        out_ref[at, :coefs, KPAD : KPAD + coefs] = value - high
+
+
+def split(turned_ops):
+    classes = turned_ops.shape[0]
+    group = max(size for size in range(1, 10) if classes % size == 0)
+    return pl.pallas_call(
+        functools.partial(split_kernel, group=group),
+        out_shape=jax.ShapeDtypeStruct((classes, KPAD, LANES), jnp.float32),
+        in_specs=[VMEM_WHOLE],
+        out_specs=VMEM_WHOLE,
+        compiler_params=params(),
+        cost_estimate=cost(10**6, 12 * 10**6),
+        name="split",
+    )(turned_ops)
+
+
 def m2l_kernel(source_ref, class_ref, table_ref, ops_ref, out_ref, *gathered, first, turned):
-    step = first + pl.program_id(0)
+    steps = source_ref.shape[0] // 8
     lanes = lane_ids((1, LANES))
     in_first = lanes < KPAD
     in_second = lanes < 2 * KPAD
-
-    def row(b, t):
-        return table_ref[source_ref[b // 2, (b % 2) * BLOCK + t]]
-
-    for u in range(2):
-        for t in range(BLOCK):
-            for g in range(3):
-                b = u * PER_WINDOW + 3 * g
+    rest = jnp.zeros((LANES - COPIES * KPAD, LANES), jnp.float32)
+    none = jnp.zeros((KPAD, LANES), jnp.float32)
+
+    def one_step(step, _):
+        def row(b, t):
+            return table_ref[source_ref[step * 8 + b // 2, (b % 2) * BLOCK + t]]
+
+        def gather(u, g):
+            b = u * PER_WINDOW + COPIES * g
+            for t in range(BLOCK):
                 one, two = row(b, t), row(b + 1, t)
                 three = row(b + 2, t) if g < 2 else two
-                gathered[u][g, t : t + 1, :] = jnp.where(
+                gathered[3 * u + g][t : t + 1, :] = jnp.where(
                     in_first, one, jnp.where(in_second, two, three)
                 )
 
-    rest = jnp.zeros((LANES - COPIES * KPAD, LANES), jnp.float32)
-    none = jnp.zeros((KPAD, LANES), jnp.float32)
-    results = []
-    for u in range(2):
-        total = jnp.zeros((BLOCK, LANES), jnp.float32)
-        for g in range(3):
+        def product(u, g):
             held = []
-            for s in range(3):
-                b = 3 * g + s
+            for b in range(COPIES * g, COPIES * g + COPIES):
                 if b < PER_WINDOW:
-                    held.append(ops_ref[class_ref[step * 2 * PER_WINDOW + u * PER_WINDOW + b]])
+                    block = (first + step) * 2 * PER_WINDOW + u * PER_WINDOW + b
+                    held.append(ops_ref[class_ref[block]])
                 else:
                     held.append(none)
             weights = jnp.concatenate(held + [rest], axis=0).astype(jnp.bfloat16)
-            values = gathered[u][g]
+            values = gathered[3 * u + g][...]
             high = values.astype(jnp.bfloat16)
             low = (values - high.astype(jnp.float32)).astype(jnp.bfloat16)
-            total += jnp.dot(high, weights, preferred_element_type=jnp.float32)
-            total += jnp.dot(low, weights, preferred_element_type=jnp.float32)
-        results.append(total)
-    both = jnp.concatenate(results, axis=0)
-    both = both + pltpu.roll(both, LANES - KPAD, 1)
-    if turned:
-        out_ref[0] = both.T[:KPAD]
-    else:
-        out_ref[...] = both
+            return jnp.dot(high, weights, preferred_element_type=jnp.float32) + jnp.dot(
+                low, weights, preferred_element_type=jnp.float32
+            )
+
+        order = [(u, g) for u in range(2) for g in range(3)]
+        terms = []
+        for i, pair in enumerate(order):
+            gather(*pair)
+            if i:
+                terms.append(product(*order[i - 1]))
+        terms.append(product(*order[-1]))
+        both = jnp.concatenate([terms[0] + terms[1] + terms[2], terms[3] + terms[4] + terms[5]], axis=0)
+        both = both + pltpu.roll(both, LANES - KPAD, 1)
+        if turned:
+            per = out_ref.shape[2] // LANES
+            slot = (IN_ROW >> (4 * (step // per))) & 7
+            out_ref[slot, :, pl.ds(pl.multiple_of((step % per) * LANES, LANES), LANES)] = both.T[:KPAD]
+        else:
+            out_ref[pl.ds(pl.multiple_of(step * LANES, LANES), LANES), :] = both
+        return 0
+
+    lax.fori_loop(0, steps, one_step, 0)
 
 
 def m2l(sources, classes, table, ops, first, steps, turned, slots):
     if turned:
-        per = slots // LANES
-        shape = (steps // per, KPAD, slots)
-        out_spec = pl.BlockSpec(
-            (1, KPAD, LANES), lambda i: ((IN_ROW >> (4 * (i // per))) & 7, 0, i % per)
-        )
+        shape = (steps * LANES // slots, KPAD, slots)
     else:
         shape = (steps * LANES, LANES)
-        out_spec = pl.BlockSpec((LANES, LANES), lambda i: (i, 0))
     return pl.pallas_call(
         functools.partial(m2l_kernel, first=first, turned=turned),
-        grid=(steps,),
         out_shape=jax.ShapeDtypeStruct(shape, jnp.float32),
-        in_specs=[
-            pl.BlockSpec((8, LANES), lambda i: (first + i, 0), memory_space=pltpu.SMEM),
-            SMEM_WHOLE,
-            VMEM_WHOLE,
-            VMEM_WHOLE,
-        ],
-        out_specs=out_spec,
-        scratch_shapes=[pltpu.VMEM((3, BLOCK, LANES), jnp.float32)] * 2,
-        compiler_params=params(),
-        cost_estimate=cost(10**6, 150 * 10**6),
+        in_specs=[SMEM_WHOLE, SMEM_WHOLE, VMEM_WHOLE, VMEM_WHOLE],
+        out_specs=VMEM_WHOLE,
+        scratch_shapes=[pltpu.VMEM((BLOCK, LANES), jnp.float32)] * 6,
+        compiler_params=params(),
+        cost_estimate=cost(10**6, 120 * 10**6),
         name="m2l_slots" if turned else "m2l_cells",
-    )(sources, classes, as_rows(table), ops)
+    )(sources[first * 8 : (first + steps) * 8], classes, as_rows(table), ops)
 
 
 def add_back_kernel(list_ref, count_ref, own_ref, *refs):
@@ -363,12 +391,15 @@
     )(mesh)
 
 
-def first_part_kernel(mesh_ref, place_ref, cells_ref, out_ref, sems, *, rows):
+def first_part_kernel(mesh_ref, place_ref, cells_ref, out_ref, sems, *, count, rows):
     sources, _, width = out_ref.shape
     copies = [
         pltpu.make_async_copy(
-            mesh_ref.at[0, pl.ds(s * rows, rows), :], out_ref.at[s, pl.ds(0, rows), :], sems.at[s]
+            mesh_ref.at[p, pl.ds(s * rows, rows), :],
+            out_ref.at[s, pl.ds(p * rows, rows), :],
+            sems.at[p, s],
         )
+        for p in range(count)
         for s in range(sources)
     ]
     for copy in copies:
@@ -378,7 +409,7 @@
     table = spread(jnp.concatenate([cells_ref[:, :LANES], rest], axis=0))
     top = jnp.where(is_first, table[:TOP_ROWS, :], table[TOP_ROWS : 2 * TOP_ROWS, :])
     blocks = [place_ref[...].astype(jnp.float32), cell_lines(cells_ref), top]
-    at = rows
+    at = count * rows
     for block in blocks:
         high = block.shape[0] * LANES // width
         for h in range(width // LANES):
@@ -396,16 +427,16 @@
     return DEPOSIT_SCALE * jnp.concatenate(lines, axis=0)
 
 
-def first_part(mesh, place, multipoles, sources):
+def first_part(mesh, place, multipoles, sources, count):
     rows, width = mesh.shape[1] // sources, mesh.shape[2]
     extra = (2 * place.size + TOP_ROWS * LANES) // width
     return pl.pallas_call(
-        functools.partial(first_part_kernel, rows=rows),
-        out_shape=jax.ShapeDtypeStruct((sources, rows + extra, width), jnp.float32),
+        functools.partial(first_part_kernel, count=count, rows=rows),
+        out_shape=jax.ShapeDtypeStruct((sources, count * rows + extra, width), jnp.float32),
         in_specs=[pl.BlockSpec(memory_space=pl.ANY), VMEM_WHOLE, VMEM_WHOLE],
         out_specs=VMEM_WHOLE,
         scratch_shapes=[
-            pltpu.SemaphoreType.DMA((sources,)),
+            pltpu.SemaphoreType.DMA((count, sources)),
         ],
         compiler_params=params(),
         cost_estimate=cost(0, 8 * sources * rows * width),
@@ -417,10 +448,10 @@
     return value.bit_length() - 1
 
 
-def sift_kernel(mine_ref, part_ref, code_ref, value_ref, bound_ref, top_ref, ride, sem, *, planes, rows):
+def sift_kernel(mine_ref, part_ref, code_ref, lane_ref, value_ref, bound_ref, top_ref, ride, sem, *, count, planes, rows):
     sources, extra, width = ride.shape
     lines = code_ref.shape[0] // sources
-    copy = pltpu.make_async_copy(part_ref.at[:, pl.ds(rows, extra), :], ride, sem)
+    copy = pltpu.make_async_copy(part_ref.at[:, pl.ds(count * rows, extra), :], ride, sem)
     copy.start()
     copy.wait()
 
@@ -463,27 +494,29 @@
         code = jnp.where(comes, pltpu.roll(code, back, 1), jnp.where(goes, none, code))
         value = jnp.where(comes, pltpu.roll(value, back, 1), jnp.where(goes, 0.0, value))
         shift = jnp.where(comes, pltpu.roll(shift, back, 1), jnp.where(goes, 0, shift))
-    code_ref[...] = code
+    code_ref[...] = code >> LANE_SHIFT
+    lane_ref[...] = (code & (LANES - 1)).astype(jnp.float32)
     value_ref[...] = value
     counts = jnp.sum(jnp.where(mine, 1.0, 0.0), axis=1, keepdims=True)
     counts = jnp.broadcast_to(counts, mine.shape).reshape(2 * sources, lines // 2, LANES)
     bound_ref[...] = jnp.max(counts, axis=0).astype(jnp.int32)
 
 
-def sift(part, mine, planes, rows, lines):
+def sift(part, mine, count, planes, rows, lines):
     sources, whole_rows, width = part.shape
-    extra = whole_rows - rows
+    extra = whole_rows - count * rows
     shape = (sources * lines, LANES)
     return pl.pallas_call(
-        functools.partial(sift_kernel, planes=planes, rows=rows),
+        functools.partial(sift_kernel, count=count, planes=planes, rows=rows),
         out_shape=(
             jax.ShapeDtypeStruct(shape, jnp.int32),
+            jax.ShapeDtypeStruct(shape, jnp.float32),
             jax.ShapeDtypeStruct(shape, jnp.float32),
             jax.ShapeDtypeStruct((lines // 2, LANES), jnp.int32),
             jax.ShapeDtypeStruct((sources * TOP_ROWS, LANES), jnp.float32),
         ),
         in_specs=[SMEM_WHOLE, pl.BlockSpec(memory_space=pl.ANY)],
-        out_specs=(VMEM_WHOLE,) * 4,
+        out_specs=(VMEM_WHOLE,) * 5,
         scratch_shapes=[pltpu.VMEM((sources, extra, width), jnp.float32), pltpu.SemaphoreType.DMA],
         compiler_params=params(),
         cost_estimate=cost(10**6, 8 * 10**6),
@@ -491,26 +524,39 @@
     )(mine, part)
 
 
-def deposit_kernel(code_ref, value_ref, bound_ref, *refs):
+def deposit_kernel(target_ref, lane_ref, value_ref, bound_ref, *refs):
     sources = len(refs) // 2
-    outs, others = refs[:sources], refs[sources:]
-    lines = code_ref.shape[0] // (2 * sources)
-    lanes = lane_ids((1, LANES))
-    for held in refs:
-        held[...] = jnp.zeros_like(held)
+    outs, others, ready = refs[:sources], refs[sources:-1], refs[-1]
+    held = outs + others
+    whole = lane_ref.shape[0]
+    lines = whole // (2 * sources)
+    for ref in held:
+        ref[...] = jnp.zeros_like(ref)
+
+    lanes = lane_ids((LANES, LANES))
+    spots = lanes.astype(jnp.float32)
+    for first in range(0, whole, LANES):
+        turned_lane = lane_ref[first : first + LANES, :].T
+        turned_value = value_ref[first : first + LANES, :].T
+
+        @pl.loop(0, LANES)
+        def _(k):
+            pick = jnp.zeros((LANES, LANES), jnp.int32) + k
+            lane = jnp.take_along_axis(turned_lane, pick, axis=1, mode="promise_in_bounds")
+            value = jnp.take_along_axis(turned_value, pick, axis=1, mode="promise_in_bounds")
+            at = pl.multiple_of((first + k) * LANES, LANES)
+            ready[pl.ds(at, LANES), :] = jnp.where(spots == lane, value, 0.0)
 
     def line(g, _):
         def one(j):
-            at = [((2 * s + h) * lines + g, j) for h in range(2) for s in range(sources)]
-            codes = [code_ref[i] for i in at]
-            to = [pl.ds(code >> LANE_SHIFT, 1) for code in codes]
-            old = [held[rows, :] for held, rows in zip(refs, to)]
+            at = [(2 * s + h) * lines + g for h in range(2) for s in range(sources)]
+            to = [pl.ds(target_ref[i, j], 1) for i in at]
             new = [
-                row + jnp.where(lanes == (code & (LANES - 1)), value_ref[i], 0.0)
-                for row, code, i in zip(old, codes, at)
+                ref[rows, :] + ready[pl.ds(i * LANES + j, 1), :]
+                for ref, rows, i in zip(held, to, at)
             ]
-            for held, rows, row in zip(refs, to, new):
-                held[rows, :] = row
+            for ref, rows, row in zip(held, to, new):
+                ref[rows, :] = row
 
         def four(i, _):
             for j in range(4):
@@ -520,21 +566,22 @@
         return lax.fori_loop(0, (bound_ref[g, 0] + 3) >> 2, four, 0)
 
     lax.fori_loop(0, lines, line, 0)
-    for out_ref, held in zip(outs, others):
-        out_ref[...] = out_ref[...] + held[...]
-
-
-def deposit(codes, values, bounds, rows, sources):
+    for out_ref, other in zip(outs, others):
+        out_ref[...] = out_ref[...] + other[...]
+
+
+def deposit(targets, lanes, values, bounds, rows, sources):
     return pl.pallas_call(
         deposit_kernel,
         out_shape=(jax.ShapeDtypeStruct((rows, LANES), jnp.float32),) * sources,
-        in_specs=[SMEM_WHOLE] * 3,
+        in_specs=[SMEM_WHOLE, VMEM_WHOLE, VMEM_WHOLE, SMEM_WHOLE],
         out_specs=(VMEM_WHOLE,) * sources,
-        scratch_shapes=[pltpu.VMEM((rows, LANES), jnp.float32)] * sources,
+        scratch_shapes=[pltpu.VMEM((rows, LANES), jnp.float32)] * sources
+        + [pltpu.VMEM((values.size, LANES), jnp.float32)],
         compiler_params=params(),
         cost_estimate=cost(10**6, 40 * 10**6),
         name="deposit",
-    )(codes, values, bounds)
+    )(targets, lanes, values, bounds)
 
 
 def fourier_tables(length):
@@ -687,7 +734,7 @@
         spans.append((first, size))
         first += size
 
-    parts = [send(first_part(pm_density, cell_mesh, multipoles, n_gx))]
+    parts = [send(first_part(pm_density, cell_mesh, multipoles, n_gx, spans[0][1]))]
     carved = [
         carve(pm_density, at, size, n_gx).reshape(n_gx, size * own_rows, width)
         for at, size in spans[1:]
@@ -707,38 +754,33 @@
     wanted = jnp.where(pair_source < base, pair_source, top)
     sources = order(((wanted << SHIFT) | (pair_target & (BLOCK - 1))).reshape(-1, LANES))
 
-    turned_ops = jnp.pad(
-        m2l_ops.transpose(0, 2, 1), ((0, 0), (0, KPAD - coef_count), (0, KPAD - coef_count))
-    )
-    high = lax.reduce_precision(turned_ops, 8, 7)
-    ops = jnp.concatenate([high, turned_ops - high], axis=2)
-    ops = jnp.pad(ops, ((0, 0), (0, 0), (0, LANES - 2 * KPAD)))
+    ops = split(m2l_ops.transpose(0, 2, 1))
 
     tiles = width // LANES
     add_rows = planes * tiles * own_rows
     mine = lax.axis_index("gx").astype(jnp.int32).reshape(1)
-    codes, amounts, bounds, top_own = sift(parts[0], mine, planes, own_rows, cell_count // LANES)
+    targets, spots, amounts, bounds, top_own = sift(
+        parts[0], mine, spans[0][1], planes, own_rows, cell_count // LANES
+    )
     tops = [top_own]
     for bit in range(log2(n_gy)):
         held = jnp.concatenate(tops, axis=0) if bit else top_own
         tops.append(lax.ppermute(held, "gy", [(i, i ^ (1 << bit)) for i in range(n_gy)]))
 
-    parts.append(send(after(carved[0], parts[0], *arrived)))
-    adds = deposit(codes, amounts, bounds, add_rows + 8, n_gx)
+    parts.append(send(after(carved[0], parts[0], sources, ops, *arrived)))
+    adds = deposit(targets, spots, amounts, bounds, add_rows + 8, n_gx)
     table = whole_table(table, arrived, tops)
     cell_steps = cell_count // LANES
     slot_steps = 8 * slots // LANES
     slot_fields = m2l(sources, block_class, table, ops, cell_steps, slot_steps, True, slots)
-    returned = exchange(slot_fields[:3], slot_fields[3:6], slot_fields[6:])
-    parts.append(send(after(carved[1], parts[1], slot_fields)))
+    returned = exchange(slot_fields[:3], slot_fields[3:6], slot_fields[6:], adds[0])
     own_fields = m2l(sources, block_class, table, ops, 0, cell_steps, False, slots)
+    parts.append(send(after(carved[1], parts[1], own_fields, *returned)))
 
     tables = fourier_tables(n_gx * width)
     spectrum = None
-    for i, (at, size) in enumerate(spans):
-        if i == 2:
-            parts.append(send(after(carved[2], parts[2], own_fields, spectrum, *returned)))
-        spectrum = fourier(parts[i], size, adds, tables, at, planes, spectrum, own_rows)
+    for part, (at, size) in zip(parts, spans):
+        spectrum = fourier(part, size, adds, tables, at, planes, spectrum, own_rows)
 
     field_tensors = add_back(lists, counts, own_fields, returned, coef_count)
     return (field_tensors, spectrum)

time: 267 us -> 281 us (1.052); the launches traced: 265 us -> 276 us
  waiting for transfers between devices: 26.5 us -> 42 us
  other arithmetic: 9.2 us -> 1.65 us
  local copies, waits for them, and re-layouts: 19.5 us -> 25.9 us
  starting transfers between devices: 32.6 us -> 27.2 us
    all_to_all x4 -> x3, waiting for transfers between devices: 0.01 us -> 14.3 us  [send(): return lax.all_to_all(part, 'gx', 0, 0, tiled=True)]
    all_to_all x4 -> x3, starting transfers between devices: 23.3 us -> 15.9 us  [send(): return lax.all_to_all(part, 'gx', 0, 0, tiled=True)]
    pallas_call x1, Pallas kernels: 21.3 us -> 28.1 us  [deposit(): pl.pallas_call(deposit_kernel, out_shape=(jax.ShapeDtypeStruct((rows, LAN...]
    ppermute x3, waiting for transfers between devices: 0.87 us -> 7.4 us  [on_device(): lax.ppermute(held, 'gy', [(i, i ^ 1 << bit) for i in range(n_gy)])]
    unnamed x69 -> x63, local copies, waits for them, and re-layouts: 19.3 us -> 25.7 us
    reduce_precision x1 -> x0, other arithmetic: 5.72 us -> none  [on_device(): high = lax.reduce_precision(turned_ops, 8, 7)]
    ppermute x8, waiting for transfers between devices: 25.7 us -> 20.3 us  [shift(): lax.ppermute(value, axis, [(i, (i + by) % count) for i in range(count)])]
    pallas_call x3 -> x2, Pallas kernels: 8.85 us -> 3.75 us  [carve(): pl.pallas_call(functools.partial(carve_kernel, first=first), out_shape=ja...]
  transfers between devices with their start and end apart: 15 -> 14, of which waited for: 7 -> 8; matrix products, arithmetic and copies ran while one was open for 6% -> 3% of each run, Pallas kernels for 64% -> 61%
where the time goes in v5:
time: 281 us; the launch traced here: 276 us
  Pallas kernels  178 us (63%)
  waiting for transfers between devices  42 us (15%)
  starting transfers between devices  27.2 us (10%)
  local copies, waits for them, and re-layouts  25.9 us (9%)
    pallas_call x2, Pallas kernels, m2l(): pl.pallas_call(functools.partial(m2l_kernel, first=first, turned=turned),...  78.2 us
    pallas_call x1, Pallas kernels, deposit(): pl.pallas_call(deposit_kernel, out_shape=(jax.ShapeDtypeStruct((rows, LAN...  28.1 us
    pallas_call x3, Pallas kernels, fourier(): pl.pallas_call(functools.partial(fourier_kernel, sources=sources), grid=(...  25.9 us
    unnamed x63, local copies, waits for them, and re-layouts  25.7 us
    ppermute x8, waiting for transfers between devices, shift(): lax.ppermute(value, axis, [(i, (i + by) % count) for i in range(count)])  20.3 us
    all_to_all x3, starting transfers between devices, send(): return lax.all_to_all(part, 'gx', 0, 0, tiled=True)  15.9 us
    all_to_all x3, waiting for transfers between devices, send(): return lax.all_to_all(part, 'gx', 0, 0, tiled=True)  14.3 us
    pallas_call x1, Pallas kernels, add_back(): pl.pallas_call(add_back_kernel, out_shape=jax.ShapeDtypeStruct((coef_coun...  11.2 us
  transfers between devices with their start and end apart: 14, of which 8 were waited for; matrix products, arithmetic and copies ran while one was open for 3% of the time, Pallas kernels for 61%

profile of v5, /device:TPU:8, one launch (start us, length us, event | category | flops | bytes accessed | tf_op | source)
XLA Modules:
  0.0 275.7 jit_solution(18382352383545314700)
XLA Ops:
  0.6 0.0 copy-start.17
  0.6 1.1 copy-done.17
  1.7 0.7 copy-done.26
  2.4 1.6 first_part.1
  4.0 1.4 copy-done.13
  5.4 5.4 %all-to-all-start = ((f32[4,552,256]{2,1,0:T(8,128)}), f32[4,552,256]{2,1,0:T(8,128)S(1)}, u32[]{:S(2)}, u32[]{:S(2)}) async-start(f32[4,552,256]{2,1,0:T(8,128)} %copy-done.13), calls=%async_computation | async-start | bytes 4521984 | tf_op jit(solution)/shard_map/all_to_all | solution.py:729
  11.0 3.3 %own_table.1.refs_8_ = f32[9216,128]{1,0:T(8,128)S(1)} custom-call(f32[40,4096]{1,0:T(8,128)S(1)} %pad.4.cells_ref), custom_call_target="tpu_custom_call" | custom-call | flops 1000000 | bytes 12000000 | tf_op jit(solution)/shard_map/own_table/pallas_call | solution.py:59
  14.3 10.0 %pack.1 = (f32[3,40,512]{2,1,0:T(8,128)S(1)}, f32[3,40,512]{2,1,0:T(8,128)S(1)}, f32[2,40,512]{2,1,0:T(8,128)S(1)}) custom-call(s32[8,512]{1,0:T(8,128)S(1)} %bitcast.16, s32[8]{0:T(128)S(1)} %bitcast.19, f32[9216,1,128]{2,1,0:T(1,128)S(1)} %bitcast.11), custom_call_target="tpu_custom_call" | custom-call | flops 1000000 | bytes 25000000 | tf_op jit(solution)/shard_map/pack/pallas_call | solution.py:154
  24.3 2.2 copy-done
  26.5 1.3 collective-permute-start
  27.8 0.0 collective-permute-start.1
  27.8 5.9 %collective-permute-done.refs_0_ = f32[3,40,512]{2,1,0:T(8,128)S(1)} collective-permute-done((f32[3,40,512]{2,1,0:T(8,128)S(1)}, f32[3,40,512]{2,1,0:T(8,128)S(1)}, u32[]{:S(2)}, u32[]{:S(2)}) %collective-permute-start) | collective-permute-done | bytes 245792 | tf_op jit(solution)/shard_map/ppermute | solution.py:176
  33.8 2.0 collective-permute-done.1.refs_1_
  35.8 0.7 pad_maximum_fusion
  36.5 0.0 collective-permute-start.2
  36.5 0.7 pad_maximum_fusion.1
  37.2 2.0 collective-permute-start.3
  39.2 2.2 carve.3
  41.4 2.0 copy-done.8
  43.4 5.3 %copy.16 = f32[189,35,35]{1,2,0:T(8,128)} copy(f32[189,35,35]{0,2,1:T(8,128)} %param.17) | data formatting | bytes 1852200 | tf_op args[6]
  48.7 0.2 fusion.2.packed_ref
  48.9 7.4 %order.1 = s32[512,128]{1,0:T(8,128)S(1)} custom-call(s32[512,128]{1,0:T(8,128)S(1)} %fusion.2.packed_ref), custom_call_target="tpu_custom_call" | custom-call | flops 1000000 | bytes 20000000 | tf_op jit(solution)/shard_map/order/pallas_call | solution.py:205
  56.3 4.7 %split.1.ops_ref = f32[189,40,128]{2,1,0:T(8,128)S(1)} custom-call(f32[189,35,35]{2,1,0:T(8,128)} %bitcast.21), custom_call_target="tpu_custom_call" | custom-call | flops 1000000 | bytes 12000000 | tf_op jit(solution)/shard_map/split/pallas_call | solution.py:232
  61.0 2.0 copy-done.3
  62.9 8.8 %collective-permute-done.2.refs_2_ = f32[3,40,512]{2,1,0:T(8,128)S(1)} collective-permute-done((f32[3,40,512]{2,1,0:T(8,128)}, f32[3,40,512]{2,1,0:T(8,128)S(1)}, u32[]{:S(2)}, u32[]{:S(2)}) %collective-permute-start.2) | collective-permute-done | bytes 245792 | tf_op jit(solution)/shard_map/ppermute | solution.py:176
  71.7 0.0 collective-permute-done.3.refs_3_
  71.7 0.0 all-to-all-done.part_ref.refs_0_
  71.7 4.9 %all-to-all-start.1 = ((f32[4,1024,256]{2,1,0:T(8,128)}), f32[4,1024,256]{2,1,0:T(8,128)}, u32[]{:S(2)}, u32[]{:S(2)}) async-start(f32[4,1024,256]{2,1,0:T(8,128)} %bitcast.14), calls=%async_computation.1 | async-start | bytes 8388608 | tf_op jit(solution)/shard_map/all_to_all | solution.py:729
  76.6 1.4 sift.1
  77.9 0.1 collective-permute-start.4
  78.0 1.2 collective-permute-done.4.refs_5_
  79.2 1.5 collective-permute-start.5
  80.7 2.8 %collective-permute-done.5.refs_6_ = f32[128,128]{1,0:T(8,128)S(1)} collective-permute-done((f32[128,128]{1,0:T(8,128)S(1)}, f32[128,128]{1,0:T(8,128)S(1)}, u32[]{:S(2)}, u32[]{:S(2)}) %collective-permute-start.5) | collective-permute-done | bytes 65568 | tf_op jit(solution)/shard_map/ppermute | solution.py:768
  83.5 1.6 collective-permute-start.6
  85.1 3.4 %collective-permute-done.6.refs_7_ = f32[256,128]{1,0:T(8,128)S(1)} collective-permute-done((f32[256,128]{1,0:T(8,128)S(1)}, f32[256,128]{1,0:T(8,128)S(1)}, u32[]{:S(2)}, u32[]{:S(2)}) %collective-permute-start.6) | collective-permute-done | bytes 131104 | tf_op jit(solution)/shard_map/ppermute | solution.py:768
  88.5 2.3 copy-done.1
  90.9 2.4 whole_table.1
  93.3 0.0 copy-start.2
  93.3 2.2 copy-done.2
  95.5 39.9 %m2l_slots.1 = f32[8,40,512]{2,1,0:T(8,128)S(1)} custom-call(s32[256,128]{1,0:T(8,128)S(1)} %get-tuple-element.34.source_ref, s32[1024]{0:T(1024)S(1)} %copy-done.27, f32[9216,1,128]{2,1,0:T(1,128)} %bitcast.12, f32[189,40,128]{2,1,0:T(8,128)S(1)} %copy-done.4), custom_call_target="tpu_custom_call" | custom-call | flops 1000000 | bytes 120000000 | tf_op jit(solution)/shard_map/m2l_slots/pallas_call | solution.py:305
  135.4 0.2 collective-permute-start.8
  135.7 28.1 %deposit.1 = (f32[4104,128]{1,0:T(8,128)S(1)}, f32[4104,128]{1,0:T(8,128)S(1)}, f32[4104,128]{1,0:T(8,128)}, f32[4104,128]{1,0:T(8,128)}) custom-call(s32[128,128]{1,0:T(8,128)S(1)} %get-tuple-element.21.target_ref, f32[128,128]{1,0:T(8,128)S(1)} %get-tuple-element.22.lane_ref, f32[128,128]{1,0:T(8,128)S(1)} %get-tuple-element.23.value_ref, ...), custom_call_target="tpu_custom_call" | custom-call | flops 1000000 | bytes 40000000 | tf_op jit(solution)/shard_map/deposit/pallas_call | solution.py:574
  163.8 2.4 collective-permute-start.7
  166.3 0.0 collective-permute-done.8.refs_1_
  166.3 3.7 %collective-permute-done.7.refs_0_ = f32[3,40,512]{2,1,0:T(8,128)S(1)} collective-permute-done((f32[3,40,512]{2,1,0:T(8,128)S(1)}, f32[3,40,512]{2,1,0:T(8,128)S(1)}, u32[]{:S(2)}, u32[]{:S(2)}) %collective-permute-start.7) | collective-permute-done | bytes 245792 | tf_op jit(solution)/shard_map/ppermute | solution.py:176
  170.0 0.1 collective-permute-start.9
  170.1 2.1 collective-permute-start.10
  172.2 1.5 carve.2
  173.7 1.3 copy-done.14
  175.1 38.4 %m2l_cells.1.own_ref = f32[4096,128]{1,0:T(8,128)S(1)} custom-call(s32[256,128]{1,0:T(8,128)S(1)} %get-tuple-element.35.source_ref, s32[1024]{0:T(1024)S(1)} %copy-done.27, f32[9216,1,128]{2,1,0:T(1,128)} %bitcast.13, f32[189,40,128]{2,1,0:T(8,128)S(1)} %copy-done.4), custom_call_target="tpu_custom_call" | custom-call | flops 1000000 | bytes 120000000 | tf_op jit(solution)/shard_map/m2l_cells/pallas_call | solution.py:305
  213.5 1.3 copy-done.15
  214.8 0.0 collective-permute-done.9.refs_2_
  214.8 0.7 copy-done.21
  215.5 0.7 copy-done.23
  216.2 0.0 all-to-all-done.1.refs_0_
  216.2 5.6 %all-to-all-start.2 = ((f32[4,512,256]{2,1,0:T(8,128)}), f32[4,512,256]{2,1,0:T(8,128)}, u32[]{:S(2)}, u32[]{:S(2)}) async-start(f32[4,512,256]{2,1,0:T(8,128)} %bitcast.15), calls=%async_computation.2 | async-start | bytes 4194304 | tf_op jit(solution)/shard_map/all_to_all | solution.py:729
  221.8 1.2 copy-done.10
  223.1 7.3 %fourier.3.refs_7_ = f32[2,8,256,1024]{3,2,1,0:T(8,128)} custom-call(f32[4,552,256]{2,1,0:T(8,128)} %copy-done.5, f32[4104,128]{1,0:T(8,128)S(1)} %get-tuple-element.25.refs_1_, f32[4104,128]{1,0:T(8,128)} %copy-done.7, f32[4104,128]{1,0:T(8,128)} %get-tuple-element.30.refs_3_, f32[4104,128]{1,0:T(8,128)} %get-tuple-element.31.refs_4_, ...), custom_call_target="tpu_custom_call" | custom-call | flops 1000000 | bytes 20000000 | tf_op jit(solution)/shard_map/fourier/pallas_call | solution.py:690
  230.3 0.0 copy-start.11
  230.3 11.2 %add_back.1 = f32[35,4096]{1,0:T(8,128)} custom-call(s32[8,512]{1,0:T(8,128)S(1)} %bitcast.17, s32[8]{0:T(128)S(1)} %bitcast.20, f32[4096,128]{1,0:T(8,128)S(1)} %copy-done.16, f32[3,40,512]{2,1,0:T(8,128)S(1)} %copy-done.20, f32[3,40,512]{2,1,0:T(8,128)S(1)} %collective-permute-done.8.refs_1_, f32[3,40,512]{2,1,0:T(8,128)S(1)} %copy-done.22, ...), custom_call_target="tpu_custom_call" | custom-call | flops 1000000 | bytes 30000000 | tf_op jit(solution)/shard_map/add_back/pallas_call | solution.py:353
  241.6 11.5 %fourier.4.refs_7_ = f32[2,8,256,1024]{3,2,1,0:T(8,128)} custom-call(f32[4,1024,256]{2,1,0:T(8,128)} %all-to-all-done.1.refs_0_, f32[4104,128]{1,0:T(8,128)S(1)} %get-tuple-element.25.refs_1_, f32[4104,128]{1,0:T(8,128)} %copy-done.7, f32[4104,128]{1,0:T(8,128)} %get-tuple-element.30.refs_3_, ...), custom_call_target="tpu_custom_call", output_to_operand_aliasing={{}: (7, {})} | custom-call | flops 1000000 | bytes 40000000 | tf_op jit(solution)/shard_map/fourier/pallas_call | solution.py:690
  253.1 14.3 %all-to-all-done.2.refs_0_ = f32[4,512,256]{2,1,0:T(8,128)} async-done(((f32[4,512,256]{2,1,0:T(8,128)}), f32[4,512,256]{2,1,0:T(8,128)}, u32[]{:S(2)}, u32[]{:S(2)}) %all-to-all-start.2) | async-done | bytes 2097184 | tf_op jit(solution)/shard_map/all_to_all | solution.py:729
  267.3 1.2 copy-done.12
  268.6 7.1 %fourier.5 = f32[2,8,256,1024]{3,2,1,0:T(8,128)} custom-call(f32[4,512,256]{2,1,0:T(8,128)} %all-to-all-done.2.refs_0_, f32[4104,128]{1,0:T(8,128)} %copy-done.6, f32[4104,128]{1,0:T(8,128)} %copy-done.7, f32[4104,128]{1,0:T(8,128)} %get-tuple-element.30.refs_3_, f32[4104,128]{1,0:T(8,128)} %get-tuple-element.31.refs_4_, ...), custom_call_target="tpu_custom_call", output_to_operand_aliasing={{}: (7, {})} | custom-call | flops 1000000 | bytes 20000000 | tf_op jit(solution)/shard_map/fourier/pallas_call | solution.py:690
  (60 shorter events, 0.3 us)
Async XLA Ops:
  0.6 1.1 copy-start.17
  1.7 0.7 copy-start.26
  4.0 1.4 copy-start.13
  5.4 5.5 %copy-start.18 = (f32[35,4096]{1,0:T(8,128)S(1)}, f32[35,4096]{1,0:T(8,128)}, u32[]{:S(2)}) copy-start(f32[35,4096]{1,0:T(8,128)} %cells_ref.1) | copy-start | bytes 1720324
  5.4 66.2 %all-to-all-start = ((f32[4,552,256]{2,1,0:T(8,128)}), f32[4,552,256]{2,1,0:T(8,128)S(1)}, u32[]{:S(2)}, u32[]{:S(2)}) async-start(f32[4,552,256]{2,1,0:T(8,128)} %copy-done.13), calls=%async_computation | async-start | bytes 4521984 | tf_op jit(solution)/shard_map/all_to_all | solution.py:729
  10.9 3.4 %copy-start.25 = (s32[1,8,512]{2,1,0:T(8,128)S(1)}, s32[1,8,512]{2,1,0:T(8,128)}, u32[]{:S(2)}) copy-start(s32[1,8,512]{2,1,0:T(8,128)} %param.12) | copy-start | bytes 49156
  10.9 3.4 %copy-start.28 = (s32[1,8]{1,0:T(1,128)S(1)}, s32[1,8]{1,0:T(1,128)}, u32[]{:S(2)}) copy-start(s32[1,8]{1,0:T(1,128)} %param.13) | copy-start | bytes 100
  24.3 2.2 copy-start
  26.5 7.3 %collective-permute-start = (f32[3,40,512]{2,1,0:T(8,128)S(1)}, f32[3,40,512]{2,1,0:T(8,128)S(1)}, u32[]{:S(2)}, u32[]{:S(2)}) collective-permute-start(f32[3,40,512]{2,1,0:T(8,128)S(1)} %get-tuple-element.17), channel_id=1, source_target_pairs={{0,7},{1,0},{2,1},{3,2},{4,3},{5,4},{6,5},{7,6},{8,15},{9,8},{10,9... | collective-permute-start | bytes 737288 | tf_op jit(solution)/shard_map/ppermute | solution.py:176
  27.8 7.9 %collective-permute-start.1 = (f32[3,40,512]{2,1,0:T(8,128)S(1)}, f32[3,40,512]{2,1,0:T(8,128)S(1)}, u32[]{:S(2)}, u32[]{:S(2)}) collective-permute-start(f32[3,40,512]{2,1,0:T(8,128)S(1)} %get-tuple-element.18), channel_id=1, source_target_pairs={{0,1},{1,2},{2,3},{3,4},{4,5},{5,6},{6,7},{7,0},{8,9},{9,10},{10,1... | collective-permute-start | bytes 737288 | tf_op jit(solution)/shard_map/ppermute | solution.py:176
  36.5 35.2 %collective-permute-start.2 = (f32[3,40,512]{2,1,0:T(8,128)}, f32[3,40,512]{2,1,0:T(8,128)S(1)}, u32[]{:S(2)}, u32[]{:S(2)}) collective-permute-start(f32[3,40,512]{2,1,0:T(8,128)} %pad_maximum_fusion), channel_id=1, source_target_pairs={{0,24},{8,0},{16,8},{24,16},{1,25},{9,1},{17,9},{25,17},{2,26},{10... | collective-permute-start | bytes 737288 | tf_op jit(solution)/shard_map/ppermute | solution.py:176
  37.2 34.5 %collective-permute-start.3 = (f32[3,40,512]{2,1,0:T(8,128)}, f32[3,40,512]{2,1,0:T(8,128)}, u32[]{:S(2)}, u32[]{:S(2)}) collective-permute-start(f32[3,40,512]{2,1,0:T(8,128)} %pad_maximum_fusion.1), channel_id=1, source_target_pairs={{0,8},{8,16},{16,24},{24,0},{1,9},{9,17},{17,25},{25,1},{2,10},{10... | collective-permute-start | bytes 737288 | tf_op jit(solution)/shard_map/ppermute | solution.py:176
  41.4 2.0 copy-start.8
  43.4 5.3 %copy-start.29 = (s32[65536]{0:T(1024)S(1)}, s32[65536]{0:T(1024)}, u32[]{:S(2)}) copy-start(s32[65536]{0:T(1024)} %param.14) | copy-start | bytes 786436
  43.4 5.3 %copy-start.30 = (s32[65536]{0:T(1024)S(1)}, s32[65536]{0:T(1024)}, u32[]{:S(2)}) copy-start(s32[65536]{0:T(1024)} %param.15) | copy-start | bytes 786436
  60.9 2.0 copy-start.3
  71.7 4.9 %copy-start.5 = (f32[4,552,256]{2,1,0:T(8,128)}, f32[4,552,256]{2,1,0:T(8,128)S(1)}, u32[]{:S(2)}) copy-start(f32[4,552,256]{2,1,0:T(8,128)S(1)} %all-to-all-done.part_ref.refs_0_) | copy-start | bytes 6782980
  71.7 144.5 %all-to-all-start.1 = ((f32[4,1024,256]{2,1,0:T(8,128)}), f32[4,1024,256]{2,1,0:T(8,128)}, u32[]{:S(2)}, u32[]{:S(2)}) async-start(f32[4,1024,256]{2,1,0:T(8,128)} %bitcast.14), calls=%async_computation.1 | async-start | bytes 8388608 | tf_op jit(solution)/shard_map/all_to_all | solution.py:729
  77.9 1.3 collective-permute-start.4
  79.2 4.3 %collective-permute-start.5 = (f32[128,128]{1,0:T(8,128)S(1)}, f32[128,128]{1,0:T(8,128)S(1)}, u32[]{:S(2)}, u32[]{:S(2)}) collective-permute-start(f32[128,128]{1,0:T(8,128)S(1)} %pad_maximum_fusion.5), channel_id=1, source_target_pairs={{0,2},{1,3},{2,0},{3,1},{4,6},{5,7},{6,4},{7,5},{8,10},{9,11},{10,... | collective-permute-start | bytes 196616 | tf_op jit(solution)/shard_map/ppermute | solution.py:768
  83.5 5.0 %collective-permute-start.6 = (f32[256,128]{1,0:T(8,128)S(1)}, f32[256,128]{1,0:T(8,128)S(1)}, u32[]{:S(2)}, u32[]{:S(2)}) collective-permute-start(f32[256,128]{1,0:T(8,128)S(1)} %pad_maximum_fusion.4), channel_id=1, source_target_pairs={{0,4},{1,5},{2,6},{3,7},{4,0},{5,1},{6,2},{7,3},{8,12},{9,13},{10,... | collective-permute-start | bytes 393224 | tf_op jit(solution)/shard_map/ppermute | solution.py:768
  88.5 2.3 copy-start.1
  90.9 4.6 %copy-start.4 = (f32[189,40,128]{2,1,0:T(8,128)S(1)}, f32[189,40,128]{2,1,0:T(8,128)}, u32[]{:S(2)}) copy-start(f32[189,40,128]{2,1,0:T(8,128)} %copy-done.3) | copy-start | bytes 11612164
  90.9 4.6 %copy-start.27 = (s32[1024]{0:T(1024)S(1)}, s32[1024]{0:T(1024)}, u32[]{:S(2)}) copy-start(s32[1024]{0:T(1024)} %class_ref.3) | copy-start | bytes 12292
  93.3 2.2 copy-start.2
  135.4 30.9 %collective-permute-start.8 = (f32[3,40,512]{2,1,0:T(8,128)S(1)}, f32[3,40,512]{2,1,0:T(8,128)S(1)}, u32[]{:S(2)}, u32[]{:S(2)}) collective-permute-start(f32[3,40,512]{2,1,0:T(8,128)S(1)} %get-tuple-element.32), channel_id=1, source_target_pairs={{0,1},{1,2},{2,3},{3,4},{4,5},{5,6},{6,7},{7,0},{8,9},{9,10},{10,1... | collective-permute-start | bytes 737288 | tf_op jit(solution)/shard_map/ppermute | solution.py:176
  163.8 9.9 %copy-start.7 = (f32[4104,128]{1,0:T(8,128)}, f32[4104,128]{1,0:T(8,128)S(1)}, u32[]{:S(2)}) copy-start(f32[4104,128]{1,0:T(8,128)S(1)} %get-tuple-element.29.refs_2_) | copy-start | bytes 6303748
  163.8 77.8 %copy-start.6 = (f32[4104,128]{1,0:T(8,128)}, f32[4104,128]{1,0:T(8,128)S(1)}, u32[]{:S(2)}) copy-start(f32[4104,128]{1,0:T(8,128)S(1)} %get-tuple-element.25.refs_1_) | copy-start | bytes 6303748
  163.8 6.2 %collective-permute-start.7 = (f32[3,40,512]{2,1,0:T(8,128)S(1)}, f32[3,40,512]{2,1,0:T(8,128)S(1)}, u32[]{:S(2)}, u32[]{:S(2)}) collective-permute-start(f32[3,40,512]{2,1,0:T(8,128)S(1)} %get-tuple-element.33), channel_id=1, source_target_pairs={{0,7},{1,0},{2,1},{3,2},{4,3},{5,4},{6,5},{7,6},{8,15},{9,8},{10,9... | collective-permute-start | bytes 737288 | tf_op jit(solution)/shard_map/ppermute | solution.py:176
  170.0 3.8 %copy-start.19 = (f32[3,40,512]{2,1,0:T(8,128)}, f32[3,40,512]{2,1,0:T(8,128)S(1)}, u32[]{:S(2)}) copy-start(f32[3,40,512]{2,1,0:T(8,128)S(1)} %collective-permute-done.7.refs_0_) | copy-start | bytes 737284
  170.0 44.8 %collective-permute-start.9 = (f32[3,40,512]{2,1,0:T(8,128)S(1)}, f32[3,40,512]{2,1,0:T(8,128)S(1)}, u32[]{:S(2)}, u32[]{:S(2)}) collective-permute-start(f32[3,40,512]{2,1,0:T(8,128)S(1)} %pad_maximum_fusion.2), channel_id=1, source_target_pairs={{0,24},{8,0},{16,8},{24,16},{1,25},{9,1},{17,9},{25,17},{2,26},{10... | collective-permute-start | bytes 737288 | tf_op jit(solution)/shard_map/ppermute | solution.py:176
  170.1 45.4 %collective-permute-start.10 = (f32[3,40,512]{2,1,0:T(8,128)S(1)}, f32[3,40,512]{2,1,0:T(8,128)S(1)}, u32[]{:S(2)}, u32[]{:S(2)}) collective-permute-start(f32[3,40,512]{2,1,0:T(8,128)S(1)} %pad_maximum_fusion.3), channel_id=1, source_target_pairs={{0,8},{8,16},{16,24},{24,0},{1,9},{9,17},{17,25},{25,1},{2,10},{10... | collective-permute-start | bytes 737288 | tf_op jit(solution)/shard_map/ppermute | solution.py:176
  173.7 1.3 copy-start.14
  213.5 1.4 copy-start.15
  214.8 7.0 %copy-start.9 = (bf16[2,512,512]{2,1,0:T(8,128)(2,1)S(1)}, bf16[2,512,512]{2,1,0:T(8,128)(2,1)}, u32[]{:S(2)}) copy-start(bf16[2,512,512]{2,1,0:T(8,128)(2,1)} %constant.40.clone.refs_6_) | copy-start | bytes 3145732
  214.8 0.7 copy-start.21
  215.5 0.7 copy-start.23
  216.2 51.1 %all-to-all-start.2 = ((f32[4,512,256]{2,1,0:T(8,128)}), f32[4,512,256]{2,1,0:T(8,128)}, u32[]{:S(2)}, u32[]{:S(2)}) async-start(f32[4,512,256]{2,1,0:T(8,128)} %bitcast.15), calls=%async_computation.2 | async-start | bytes 4194304 | tf_op jit(solution)/shard_map/all_to_all | solution.py:729
  221.8 1.2 copy-start.10
  223.0 7.3 %copy-start.16 = (f32[4096,128]{1,0:T(8,128)S(1)}, f32[4096,128]{1,0:T(8,128)}, u32[]{:S(2)}) copy-start(f32[4096,128]{1,0:T(8,128)} %copy-done.15) | copy-start | bytes 6291460
  223.0 7.3 %copy-start.20 = (f32[3,40,512]{2,1,0:T(8,128)S(1)}, f32[3,40,512]{2,1,0:T(8,128)}, u32[]{:S(2)}) copy-start(f32[3,40,512]{2,1,0:T(8,128)} %copy-done.19) | copy-start | bytes 737284
  223.1 7.3 %copy-start.22 = (f32[3,40,512]{2,1,0:T(8,128)S(1)}, f32[3,40,512]{2,1,0:T(8,128)}, u32[]{:S(2)}) copy-start(f32[3,40,512]{2,1,0:T(8,128)} %copy-done.21) | copy-start | bytes 737284
  223.1 7.3 %copy-start.24 = (f32[3,40,512]{2,1,0:T(8,128)S(1)}, f32[3,40,512]{2,1,0:T(8,128)}, u32[]{:S(2)}) copy-start(f32[3,40,512]{2,1,0:T(8,128)} %copy-done.23) | copy-start | bytes 737284
  230.3 11.2 %copy-start.11 = (bf16[2,512,512]{2,1,0:T(8,128)(2,1)S(1)}, bf16[2,512,512]{2,1,0:T(8,128)(2,1)}, u32[]{:S(2)}) copy-start(bf16[2,512,512]{2,1,0:T(8,128)(2,1)} %constant.39.clone.refs_5_) | copy-start | bytes 3145732
  267.3 1.2 copy-start.12

commit v6 on v5

--- a/solution.py
+++ b/solution.py
@@ -17,8 +17,8 @@
 PER_WINDOW = 8
 SHIFT = 6
 LANE_SHIFT = 7
-VMEM_BYTES = 48 * 1024 * 1024
-CHUNKS = (2, 4, 2)
+MIB = 1024 * 1024
+CHUNKS = (2, 3, 3)
 TOP_ROWS = TOP // 2
 
 DEPOSIT_SCALE = 8.0
@@ -30,8 +30,8 @@
 VMEM_WHOLE = pl.BlockSpec(memory_space=pltpu.VMEM)
 
 
-def params():
-    return pltpu.CompilerParams(vmem_limit_bytes=VMEM_BYTES)
+def params(mebibytes):
+    return pltpu.CompilerParams(vmem_limit_bytes=mebibytes * MIB)
 
 
 def cost(flops, nbytes):
@@ -62,7 +62,7 @@
         out_shape=jax.ShapeDtypeStruct((rows, LANES), jnp.float32),
         in_specs=[pl.BlockSpec((KPAD, count), lambda i: (0, 0))],
         out_specs=pl.BlockSpec((count, LANES), lambda i: (0, 0)),
-        compiler_params=params(),
+        compiler_params=params(12),
         cost_estimate=cost(10**6, 12 * 10**6),
         name="own_table",
     )(cells)
@@ -122,7 +122,7 @@
         in_specs=[VMEM_WHOLE] * (4 + len(tops)) + [pl.BlockSpec(memory_space=pl.ANY)],
         out_specs=pl.BlockSpec((rows, LANES), lambda i: (first + i, 0)),
         input_output_aliases={4 + len(tops): 0},
-        compiler_params=params(),
+        compiler_params=params(12),
         cost_estimate=cost(10**6, 16 * 10**6),
         name="whole_table",
     )(*arrived, *tops, table)
@@ -164,7 +164,7 @@
             pl.BlockSpec((size, KPAD, slots), lambda i: (0, 0, 0)) for size in (3, 3, 2)
         ),
         scratch_shapes=[pltpu.VMEM((LANES, LANES), jnp.float32)] * 2,
-        compiler_params=params(),
+        compiler_params=params(12),
         cost_estimate=cost(10**6, 25 * 10**6),
         name="pack",
     )(proxy_list, proxy_count, as_rows(table))
@@ -207,7 +207,7 @@
         out_shape=jax.ShapeDtypeStruct(packed.shape, jnp.int32),
         in_specs=[VMEM_WHOLE],
         out_specs=VMEM_WHOLE,
-        compiler_params=params(),
+        compiler_params=params(6),
         cost_estimate=cost(10**6, 20 * 10**6),
         name="order",
     )(packed)
@@ -234,13 +234,14 @@
         out_shape=jax.ShapeDtypeStruct((classes, KPAD, LANES), jnp.float32),
         in_specs=[VMEM_WHOLE],
         out_specs=VMEM_WHOLE,
-        compiler_params=params(),
+        compiler_params=params(16),
         cost_estimate=cost(10**6, 12 * 10**6),
         name="split",
     )(turned_ops)
 
 
-def m2l_kernel(source_ref, class_ref, table_ref, ops_ref, out_ref, *gathered, first, turned):
+def m2l_kernel(source_ref, class_ref, table_ref, ops_ref, out_ref, *refs, first, turned):
+    gathered, indices, sems = refs[:6], refs[6:8], refs[8]
     steps = source_ref.shape[0] // 8
     lanes = lane_ids((1, LANES))
     in_first = lanes < KPAD
@@ -248,9 +249,13 @@
     rest = jnp.zeros((LANES - COPIES * KPAD, LANES), jnp.float32)
     none = jnp.zeros((KPAD, LANES), jnp.float32)
 
-    def one_step(step, _):
+    def fetch(step, slot):
+        rows = pl.ds(pl.multiple_of(step * 8, 8), 8)
+        return pltpu.make_async_copy(source_ref.at[rows, :], indices[slot], sems.at[slot])
+
+    def one_step(step, slot):
         def row(b, t):
-            return table_ref[source_ref[step * 8 + b // 2, (b % 2) * BLOCK + t]]
+            return table_ref[indices[slot][b // 2, (b % 2) * BLOCK + t]]
 
         def gather(u, g):
             b = u * PER_WINDOW + COPIES * g
@@ -292,9 +297,21 @@
             out_ref[slot, :, pl.ds(pl.multiple_of((step % per) * LANES, LANES), LANES)] = both.T[:KPAD]
         else:
             out_ref[pl.ds(pl.multiple_of(step * LANES, LANES), LANES), :] = both
-        return 0
-
-    lax.fori_loop(0, steps, one_step, 0)
+
+    fetch(0, 0).start()
+
+    @pl.loop(0, steps // 2)
+    def _(i):
+        fetch(2 * i, 0).wait()
+        fetch(2 * i + 1, 1).start()
+        one_step(2 * i, 0)
+        fetch(2 * i + 1, 1).wait()
+
+        @pl.when(i < steps // 2 - 1)
+        def _():
+            fetch(2 * i + 2, 0).start()
+
+        one_step(2 * i + 1, 1)
 
 
 def m2l(sources, classes, table, ops, first, steps, turned, slots):
@@ -305,10 +322,12 @@
     return pl.pallas_call(
         functools.partial(m2l_kernel, first=first, turned=turned),
         out_shape=jax.ShapeDtypeStruct(shape, jnp.float32),
-        in_specs=[SMEM_WHOLE, SMEM_WHOLE, VMEM_WHOLE, VMEM_WHOLE],
+        in_specs=[VMEM_WHOLE, SMEM_WHOLE, VMEM_WHOLE, VMEM_WHOLE],
         out_specs=VMEM_WHOLE,
-        scratch_shapes=[pltpu.VMEM((BLOCK, LANES), jnp.float32)] * 6,
-        compiler_params=params(),
+        scratch_shapes=[pltpu.VMEM((BLOCK, LANES), jnp.float32)] * 6
+        + [pltpu.SMEM((8, LANES), jnp.int32)] * 2
+        + [pltpu.SemaphoreType.DMA((2,))],
+        compiler_params=params(20),
         cost_estimate=cost(10**6, 120 * 10**6),
         name="m2l_slots" if turned else "m2l_cells",
     )(sources[first * 8 : (first + steps) * 8], classes, as_rows(table), ops)
@@ -357,7 +376,7 @@
         out_specs=VMEM_WHOLE,
         scratch_shapes=[pltpu.VMEM((8 * slots, LANES), jnp.float32)]
         + [pltpu.VMEM((cell_count, LANES), jnp.float32)] * 8,
-        compiler_params=params(),
+        compiler_params=params(30),
         cost_estimate=cost(10**6, 30 * 10**6),
         name="add_back",
     )(proxy_list, proxy_count, own_rows, *slot_fields)
@@ -385,7 +404,7 @@
         in_specs=[pl.BlockSpec(memory_space=pl.ANY)],
         out_specs=VMEM_WHOLE,
         scratch_shapes=[pltpu.SemaphoreType.DMA((sources,))],
-        compiler_params=params(),
+        compiler_params=params(12),
         cost_estimate=cost(0, 8 * count * sources * rows * width),
         name="carve",
     )(mesh)
@@ -438,7 +457,7 @@
         scratch_shapes=[
             pltpu.SemaphoreType.DMA((count, sources)),
         ],
-        compiler_params=params(),
+        compiler_params=params(10),
         cost_estimate=cost(0, 8 * sources * rows * width),
         name="first_part",
     )(mesh, place.reshape(-1, LANES), multipoles)
@@ -448,7 +467,7 @@
     return value.bit_length() - 1
 
 
-def sift_kernel(mine_ref, part_ref, code_ref, lane_ref, value_ref, bound_ref, top_ref, ride, sem, *, count, planes, rows):
+def sift_kernel(mine_ref, part_ref, code_ref, value_ref, bound_ref, top_ref, ride, sem, *, count, planes, rows):
     sources, extra, width = ride.shape
     lines = code_ref.shape[0] // sources
     copy = pltpu.make_async_copy(part_ref.at[:, pl.ds(count * rows, extra), :], ride, sem)
@@ -494,8 +513,7 @@
         code = jnp.where(comes, pltpu.roll(code, back, 1), jnp.where(goes, none, code))
         value = jnp.where(comes, pltpu.roll(value, back, 1), jnp.where(goes, 0.0, value))
         shift = jnp.where(comes, pltpu.roll(shift, back, 1), jnp.where(goes, 0, shift))
-    code_ref[...] = code >> LANE_SHIFT
-    lane_ref[...] = (code & (LANES - 1)).astype(jnp.float32)
+    code_ref[...] = code
     value_ref[...] = value
     counts = jnp.sum(jnp.where(mine, 1.0, 0.0), axis=1, keepdims=True)
     counts = jnp.broadcast_to(counts, mine.shape).reshape(2 * sources, lines // 2, LANES)
@@ -510,53 +528,39 @@
         functools.partial(sift_kernel, count=count, planes=planes, rows=rows),
         out_shape=(
             jax.ShapeDtypeStruct(shape, jnp.int32),
-            jax.ShapeDtypeStruct(shape, jnp.float32),
             jax.ShapeDtypeStruct(shape, jnp.float32),
             jax.ShapeDtypeStruct((lines // 2, LANES), jnp.int32),
             jax.ShapeDtypeStruct((sources * TOP_ROWS, LANES), jnp.float32),
         ),
         in_specs=[SMEM_WHOLE, pl.BlockSpec(memory_space=pl.ANY)],
-        out_specs=(VMEM_WHOLE,) * 5,
+        out_specs=(VMEM_WHOLE,) * 4,
         scratch_shapes=[pltpu.VMEM((sources, extra, width), jnp.float32), pltpu.SemaphoreType.DMA],
-        compiler_params=params(),
+        compiler_params=params(8),
         cost_estimate=cost(10**6, 8 * 10**6),
         name="sift",
     )(mine, part)
 
 
-def deposit_kernel(target_ref, lane_ref, value_ref, bound_ref, *refs):
+def deposit_kernel(code_ref, value_ref, bound_ref, *refs):
     sources = len(refs) // 2
-    outs, others, ready = refs[:sources], refs[sources:-1], refs[-1]
-    held = outs + others
-    whole = lane_ref.shape[0]
-    lines = whole // (2 * sources)
-    for ref in held:
-        ref[...] = jnp.zeros_like(ref)
-
-    lanes = lane_ids((LANES, LANES))
-    spots = lanes.astype(jnp.float32)
-    for first in range(0, whole, LANES):
-        turned_lane = lane_ref[first : first + LANES, :].T
-        turned_value = value_ref[first : first + LANES, :].T
-
-        @pl.loop(0, LANES)
-        def _(k):
-            pick = jnp.zeros((LANES, LANES), jnp.int32) + k
-            lane = jnp.take_along_axis(turned_lane, pick, axis=1, mode="promise_in_bounds")
-            value = jnp.take_along_axis(turned_value, pick, axis=1, mode="promise_in_bounds")
-            at = pl.multiple_of((first + k) * LANES, LANES)
-            ready[pl.ds(at, LANES), :] = jnp.where(spots == lane, value, 0.0)
+    outs, others = refs[:sources], refs[sources:]
+    lines = code_ref.shape[0] // (2 * sources)
+    lanes = lane_ids((1, LANES))
+    for held in refs:
+        held[...] = jnp.zeros_like(held)
 
     def line(g, _):
         def one(j):
-            at = [(2 * s + h) * lines + g for h in range(2) for s in range(sources)]
-            to = [pl.ds(target_ref[i, j], 1) for i in at]
+            at = [((2 * s + h) * lines + g, j) for h in range(2) for s in range(sources)]
+            codes = [code_ref[i] for i in at]
+            to = [pl.ds(code >> LANE_SHIFT, 1) for code in codes]
+            old = [held[rows, :] for held, rows in zip(refs, to)]
             new = [
-                ref[rows, :] + ready[pl.ds(i * LANES + j, 1), :]
-                for ref, rows, i in zip(held, to, at)
+                row + jnp.where(lanes == (code & (LANES - 1)), value_ref[i], 0.0)
+                for row, code, i in zip(old, codes, at)
             ]
-            for ref, rows, row in zip(held, to, new):
-                ref[rows, :] = row
+            for held, rows, row in zip(refs, to, new):
+                held[rows, :] = row
 
         def four(i, _):
             for j in range(4):
@@ -566,22 +570,21 @@
         return lax.fori_loop(0, (bound_ref[g, 0] + 3) >> 2, four, 0)
 
     lax.fori_loop(0, lines, line, 0)
-    for out_ref, other in zip(outs, others):
-        out_ref[...] = out_ref[...] + other[...]
-
-
-def deposit(targets, lanes, values, bounds, rows, sources):
+    for out_ref, held in zip(outs, others):
+        out_ref[...] = out_ref[...] + held[...]
+
+
+def deposit(codes, values, bounds, rows, sources):
     return pl.pallas_call(
         deposit_kernel,
         out_shape=(jax.ShapeDtypeStruct((rows, LANES), jnp.float32),) * sources,
-        in_specs=[SMEM_WHOLE, VMEM_WHOLE, VMEM_WHOLE, SMEM_WHOLE],
+        in_specs=[SMEM_WHOLE] * 3,
         out_specs=(VMEM_WHOLE,) * sources,
-        scratch_shapes=[pltpu.VMEM((rows, LANES), jnp.float32)] * sources
-        + [pltpu.VMEM((values.size, LANES), jnp.float32)],
-        compiler_params=params(),
+        scratch_shapes=[pltpu.VMEM((rows, LANES), jnp.float32)] * sources,
+        compiler_params=params(26),
         cost_estimate=cost(10**6, 40 * 10**6),
         name="deposit",
-    )(targets, lanes, values, bounds)
+    )(codes, values, bounds)
 
 
 def fourier_tables(length):
@@ -694,7 +697,7 @@
         in_specs=in_specs,
         out_specs=pl.BlockSpec((2, 1, rows, length), lambda p: (0, first + p, 0, 0)),
         input_output_aliases=aliases,
-        compiler_params=params(),
+        compiler_params=params(24),
         cost_estimate=cost(10**6, count * 10 * 10**6),
         name="fourier",
     )(*operands)
@@ -744,7 +747,6 @@
     base = cell_count + 8 * slots
     table = own_table(cells, base + TOP * domains)
     outgoing = pack(table, cell_count, lists, counts)
-    arrived = exchange(*outgoing)
 
     top = pair_source - base
     domain = top >> log2(TOP)
@@ -754,12 +756,14 @@
     wanted = jnp.where(pair_source < base, pair_source, top)
     sources = order(((wanted << SHIFT) | (pair_target & (BLOCK - 1))).reshape(-1, LANES))
 
+    arrived = exchange(*outgoing, sources)
+
     ops = split(m2l_ops.transpose(0, 2, 1))
 
     tiles = width // LANES
     add_rows = planes * tiles * own_rows
     mine = lax.axis_index("gx").astype(jnp.int32).reshape(1)
-    targets, spots, amounts, bounds, top_own = sift(
+    codes, amounts, bounds, top_own = sift(
         parts[0], mine, spans[0][1], planes, own_rows, cell_count // LANES
     )
     tops = [top_own]
@@ -767,15 +771,15 @@
         held = jnp.concatenate(tops, axis=0) if bit else top_own
         tops.append(lax.ppermute(held, "gy", [(i, i ^ (1 << bit)) for i in range(n_gy)]))
 
-    parts.append(send(after(carved[0], parts[0], sources, ops, *arrived)))
-    adds = deposit(targets, spots, amounts, bounds, add_rows + 8, n_gx)
+    parts.append(send(after(carved[0], parts[0], ops, *arrived)))
+    adds = deposit(codes, amounts, bounds, add_rows + 8, n_gx)
     table = whole_table(table, arrived, tops)
     cell_steps = cell_count // LANES
     slot_steps = 8 * slots // LANES
     slot_fields = m2l(sources, block_class, table, ops, cell_steps, slot_steps, True, slots)
     returned = exchange(slot_fields[:3], slot_fields[3:6], slot_fields[6:], adds[0])
     own_fields = m2l(sources, block_class, table, ops, 0, cell_steps, False, slots)
-    parts.append(send(after(carved[1], parts[1], own_fields, *returned)))
+    parts.append(send(after(carved[1], parts[1], slot_fields, adds[0])))
 
     tables = fourier_tables(n_gx * width)
     spectrum = None

time: 281 us -> 282 us (level); the launches traced: 276 us -> 281 us
  local copies, waits for them, and re-layouts: 25.9 us -> 49.1 us
  Pallas kernels: 178 us -> 167 us
  waiting for transfers between devices: 42 us -> 35.2 us
    unnamed x63 -> x89, local copies, waits for them, and re-layouts: 25.7 us -> 47 us
    all_to_all x3, waiting for transfers between devices: 14.3 us -> 0.01 us  [send(): return lax.all_to_all(part, 'gx', 0, 0, tiled=True)]
    ppermute x8, waiting for transfers between devices: 20.3 us -> 34 us  [shift(): lax.ppermute(value, axis, [(i, (i + by) % count) for i in range(count)])]
    ppermute x3, waiting for transfers between devices: 7.4 us -> 1.2 us  [on_device(): lax.ppermute(held, 'gy', [(i, i ^ 1 << bit) for i in range(n_gy)])]
    pallas_call x1, Pallas kernels: 28.1 us -> 23.1 us  [deposit(): pl.pallas_call(deposit_kernel, out_shape=(jax.ShapeDtypeStruct((rows, LAN...]
  transfers between devices with their start and end apart: 14 -> 14, of which waited for: 8 -> 4; matrix products, arithmetic and copies ran while one was open for 3% -> 4% of each run, Pallas kernels for 61% -> 56%
where the time goes in v6:
time: 282 us; the launch traced here: 281 us
  Pallas kernels  167 us (59%)
  local copies, waits for them, and re-layouts  49.1 us (17%)
  waiting for transfers between devices  35.2 us (12%)
  starting transfers between devices  26.6 us (9%)
    pallas_call x2, Pallas kernels, m2l(): pl.pallas_call(functools.partial(m2l_kernel, first=first, turned=turned),...  80.2 us
    unnamed x89, local copies, waits for them, and re-layouts  47 us
    ppermute x8, waiting for transfers between devices, shift(): lax.ppermute(value, axis, [(i, (i + by) % count) for i in range(count)])  34 us
    pallas_call x3, Pallas kernels, fourier(): pl.pallas_call(functools.partial(fourier_kernel, sources=sources), grid=(...  24.1 us
    pallas_call x1, Pallas kernels, deposit(): pl.pallas_call(deposit_kernel, out_shape=(jax.ShapeDtypeStruct((rows, LAN...  23.1 us
    all_to_all x3, starting transfers between devices, send(): return lax.all_to_all(part, 'gx', 0, 0, tiled=True)  15 us
    pallas_call x1, Pallas kernels, add_back(): pl.pallas_call(add_back_kernel, out_shape=jax.ShapeDtypeStruct((coef_coun...  11.2 us
    pallas_call x1, Pallas kernels, pack(): pl.pallas_call(pack_kernel, grid=(1,), out_shape=tuple((jax.ShapeDtypeStr...  10.6 us
  transfers between devices with their start and end apart: 14, of which 4 were waited for; matrix products, arithmetic and copies ran while one was open for 4% of the time, Pallas kernels for 56%

profile of v6, /device:TPU:8, one launch (start us, length us, event | category | flops | bytes accessed | tf_op | source)
XLA Modules:
  0.0 281.2 jit_solution(5179382656441961160)
XLA Ops:
  0.6 3.4 %copy-done.2 = f32[8,1024,256]{2,1,0:T(8,128)S(1)} copy-done((f32[8,1024,256]{2,1,0:T(8,128)S(1)}, f32[8,1024,256]{2,1,0:T(8,128)}, u32[]{:S(2)}) %copy-start.2) | copy-done | bytes 8388632
  4.0 1.1 copy-done.31
  5.1 0.7 copy-done.36
  5.8 0.3 first_part.1
  6.1 1.4 copy-done.30
  7.5 5.4 %all-to-all-start = ((f32[4,552,256]{2,1,0:T(8,128)}), f32[4,552,256]{2,1,0:T(8,128)S(1)}, u32[]{:S(2)}, u32[]{:S(2)}) async-start(f32[4,552,256]{2,1,0:T(8,128)} %copy-done.30), calls=%async_computation | async-start | bytes 4521984 | tf_op jit(solution)/shard_map/all_to_all | solution.py:732
  13.0 3.3 %own_table.1.refs_8_ = f32[9216,128]{1,0:T(8,128)S(1)} custom-call(f32[40,4096]{1,0:T(8,128)S(1)} %pad.4.cells_ref), custom_call_target="tpu_custom_call" | custom-call | flops 1000000 | bytes 12000000 | tf_op jit(solution)/shard_map/own_table/pallas_call | solution.py:59
  16.4 10.6 %pack.1 = (f32[3,40,512]{2,1,0:T(8,128)}, f32[3,40,512]{2,1,0:T(8,128)S(1)}, f32[2,40,512]{2,1,0:T(8,128)S(1)}) custom-call(s32[8,512]{1,0:T(8,128)S(1)} %bitcast.21, s32[8]{0:T(128)S(1)} %bitcast.24, f32[9216,1,128]{2,1,0:T(1,128)S(1)} %bitcast.11), custom_call_target="tpu_custom_call" | custom-call | flops 1000000 | bytes 25000000 | tf_op jit(solution)/shard_map/pack/pallas_call | solution.py:154
  27.0 2.2 copy-done
  29.2 1.3 collective-permute-start
  30.5 1.1 fusion.2.packed_ref
  31.7 7.4 %order.1 = s32[512,128]{1,0:T(8,128)S(1)} custom-call(s32[512,128]{1,0:T(8,128)S(1)} %fusion.2.packed_ref), custom_call_target="tpu_custom_call" | custom-call | flops 1000000 | bytes 20000000 | tf_op jit(solution)/shard_map/order/pallas_call | solution.py:205
  39.1 0.7 pad_maximum_fusion
  39.9 0.3 collective-permute-start.2
  40.2 0.7 pad_maximum_fusion.1
  40.9 1.7 collective-permute-start.3
  42.6 3.4 %copy-done.3 = f32[8,1024,256]{2,1,0:T(8,128)S(1)} copy-done((f32[8,1024,256]{2,1,0:T(8,128)S(1)}, f32[8,1024,256]{2,1,0:T(8,128)}, u32[]{:S(2)}) %copy-start.3) | copy-done | bytes 8388632
  46.0 0.5 carve.3
  46.5 1.7 copy-done.25
  48.2 5.3 %copy.16 = f32[189,35,35]{1,2,0:T(8,128)} copy(f32[189,35,35]{0,2,1:T(8,128)} %param.17) | data formatting | bytes 1852200 | tf_op args[6]
  53.5 2.1 copy-done.23
  55.5 2.6 split.1.ops_ref
  58.1 1.9 copy-done.5
  60.1 13.7 %collective-permute-done.2.refs_2_ = f32[3,40,512]{2,1,0:T(8,128)S(1)} collective-permute-done((f32[3,40,512]{2,1,0:T(8,128)}, f32[3,40,512]{2,1,0:T(8,128)S(1)}, u32[]{:S(2)}, u32[]{:S(2)}) %collective-permute-start.2) | collective-permute-done | bytes 245792 | tf_op jit(solution)/shard_map/ppermute | solution.py:176
  73.7 4.8 %all-to-all-start.1 = ((f32[4,768,256]{2,1,0:T(8,128)}), f32[4,768,256]{2,1,0:T(8,128)}, u32[]{:S(2)}, u32[]{:S(2)}) async-start(f32[4,768,256]{2,1,0:T(8,128)} %bitcast.20), calls=%async_computation.1 | async-start | bytes 6291456 | tf_op jit(solution)/shard_map/all_to_all | solution.py:732
  78.6 1.4 sift.1
  79.9 0.1 collective-permute-start.4
  80.0 1.2 collective-permute-done.4.refs_5_
  81.2 0.0 slice-start.1
  81.2 1.6 collective-permute-start.5
  82.8 3.4 %copy-done.4 = f32[8,1024,256]{2,1,0:T(8,128)S(1)} copy-done((f32[8,1024,256]{2,1,0:T(8,128)S(1)}, f32[8,1024,256]{2,1,0:T(8,128)}, u32[]{:S(2)}) %copy-start.4) | copy-done | bytes 8388632
  86.2 0.5 carve.2
  86.8 1.6 collective-permute-start.6
  88.3 0.7 fusion.7
  89.0 23.1 %deposit.1 = (f32[4104,128]{1,0:T(8,128)S(1)}, f32[4104,128]{1,0:T(8,128)S(1)}, f32[4104,128]{1,0:T(8,128)S(1)}, f32[4104,128]{1,0:T(8,128)S(1)}) custom-call(s32[128,128]{1,0:T(8,128)S(1)} %get-tuple-element.22.code_ref, f32[128,128]{1,0:T(8,128)S(1)} %get-tuple-element.23.value_ref, s32[16,128]{1,0:T(8,128)S(1)} %get-tuple-element.24.bound_ref), custom_call_target="tpu_custom_call" | custom-call | flops 1000000 | bytes 40000000 | tf_op jit(solution)/shard_map/deposit/pallas_call | solution.py:578
  112.2 1.3 copy-done.11
  113.5 1.4 copy-done.15
  114.8 1.4 copy-done.19
  116.3 1.3 whole_table.1
  117.6 1.5 copy-done.6
  119.1 40.1 %m2l_slots.1 = f32[8,40,512]{2,1,0:T(8,128)S(1)} custom-call(s32[256,128]{1,0:T(8,128)S(1)} %get-tuple-element.34.source_ref, s32[1024]{0:T(1024)S(1)} %copy-done.37, f32[9216,1,128]{2,1,0:T(1,128)S(1)} %bitcast.14, f32[189,40,128]{2,1,0:T(8,128)S(1)} %copy-done.6), custom_call_target="tpu_custom_call" | custom-call | flops 1000000 | bytes 120000000 | tf_op jit(solution)/shard_map/m2l_slots/pallas_call | solution.py:322
  159.2 2.2 copy-done.1
  161.4 0.8 copy-done.33
  162.2 4.8 %all-to-all-start.2 = ((f32[4,768,256]{2,1,0:T(8,128)}), f32[4,768,256]{2,1,0:T(8,128)}, u32[]{:S(2)}, u32[]{:S(2)}) async-start(f32[4,768,256]{2,1,0:T(8,128)} %bitcast.19), calls=%async_computation.2 | async-start | bytes 6291456 | tf_op jit(solution)/shard_map/all_to_all | solution.py:732
  167.0 1.2 fusion.6
  168.3 0.1 collective-permute-start.8
  168.3 2.6 collective-permute-start.7
  171.0 6.2 %collective-permute-done.8.refs_1_ = f32[3,40,512]{2,1,0:T(8,128)S(1)} collective-permute-done((f32[3,40,512]{2,1,0:T(8,128)S(1)}, f32[3,40,512]{2,1,0:T(8,128)S(1)}, u32[]{:S(2)}, u32[]{:S(2)}) %collective-permute-start.8) | collective-permute-done | bytes 245792 | tf_op jit(solution)/shard_map/ppermute | solution.py:176
  177.3 0.1 collective-permute-start.9
  177.4 2.3 collective-permute-start.10
  179.6 1.6 copy-done.12
  181.2 1.6 copy-done.16
  182.8 1.6 copy-done.20
  184.4 1.2 copy-done.27
  185.6 5.8 %fourier.3.refs_7_ = f32[2,8,256,1024]{3,2,1,0:T(8,128)} custom-call(f32[4,552,256]{2,1,0:T(8,128)S(1)} %all-to-all-done.part_ref.refs_0_, f32[4104,128]{1,0:T(8,128)S(1)} %copy-done.9, f32[4104,128]{1,0:T(8,128)S(1)} %copy-done.12, f32[4104,128]{1,0:T(8,128)S(1)} %copy-done.16, f32[4104,128]{1,0:T(8,128)S(1)} %copy-done.20, ...), custom_call_target="tpu_custom_call" | custom-call | flops 1000000 | bytes 20000000 | tf_op jit(solution)/shard_map/fourier/pallas_call | solution.py:693
  191.5 40.1 %m2l_cells.1.own_ref = f32[4096,128]{1,0:T(8,128)S(1)} custom-call(s32[256,128]{1,0:T(8,128)S(1)} %copy-done.34, s32[1024]{0:T(1024)S(1)} %copy-done.37, f32[9216,1,128]{2,1,0:T(1,128)S(1)} %bitcast.17, f32[189,40,128]{2,1,0:T(8,128)S(1)} %copy-done.7), custom_call_target="tpu_custom_call" | custom-call | flops 1000000 | bytes 120000000 | tf_op jit(solution)/shard_map/m2l_cells/pallas_call | solution.py:322
  231.6 14.1 %collective-permute-done.9.refs_2_ = f32[3,40,512]{2,1,0:T(8,128)S(1)} collective-permute-done((f32[3,40,512]{2,1,0:T(8,128)S(1)}, f32[3,40,512]{2,1,0:T(8,128)S(1)}, u32[]{:S(2)}, u32[]{:S(2)}) %collective-permute-start.9) | collective-permute-done | bytes 245792 | tf_op jit(solution)/shard_map/ppermute | solution.py:176
  245.7 11.2 %add_back.1 = f32[35,4096]{1,0:T(8,128)} custom-call(s32[8,512]{1,0:T(8,128)S(1)} %bitcast.22, s32[8]{0:T(128)S(1)} %bitcast.25, f32[4096,128]{1,0:T(8,128)S(1)} %m2l_cells.1.own_ref, f32[3,40,512]{2,1,0:T(8,128)S(1)} %collective-permute-done.7.refs_0_, f32[3,40,512]{2,1,0:T(8,128)S(1)} %collective-permute-done.8.refs_1_, ...), custom_call_target="tpu_custom_call" | custom-call | flops 1000000 | bytes 30000000 | tf_op jit(solution)/shard_map/add_back/pallas_call | solution.py:372
  256.9 9.2 %fourier.4.refs_7_ = f32[2,8,256,1024]{3,2,1,0:T(8,128)} custom-call(f32[4,768,256]{2,1,0:T(8,128)} %all-to-all-done.1.refs_0_, f32[4104,128]{1,0:T(8,128)S(1)} %copy-done.9, f32[4104,128]{1,0:T(8,128)S(1)} %copy-done.13, f32[4104,128]{1,0:T(8,128)S(1)} %copy-done.17, f32[4104,128]{1,0:T(8,128)S(1)} %copy-done.21, ...), custom_call_target="tpu_custom_call", output_to_operand_aliasing={{}: (7, {})} | custom-call | flops 1000000 | bytes 30000000 | tf_op jit(solution)/shard_map/fourier/pallas_call | solution.py:693
  266.2 1.6 copy-done.14
  267.8 1.6 copy-done.18
  269.4 1.6 copy-done.22
  271.0 1.2 copy-done.29
  272.2 9.0 %fourier.5 = f32[2,8,256,1024]{3,2,1,0:T(8,128)} custom-call(f32[4,768,256]{2,1,0:T(8,128)} %all-to-all-done.2.refs_0_, f32[4104,128]{1,0:T(8,128)S(1)} %copy-done.10, f32[4104,128]{1,0:T(8,128)S(1)} %copy-done.14, f32[4104,128]{1,0:T(8,128)S(1)} %copy-done.18, f32[4104,128]{1,0:T(8,128)S(1)} %copy-done.22, ...), custom_call_target="tpu_custom_call", output_to_operand_aliasing={{}: (7, {})} | custom-call | flops 1000000 | bytes 30000000 | tf_op jit(solution)/shard_map/fourier/pallas_call | solution.py:693
  (89 shorter events, 0.3 us)
Async XLA Ops:
  0.6 3.4 %copy-start.2 = (f32[8,1024,256]{2,1,0:T(8,128)S(1)}, f32[8,1024,256]{2,1,0:T(8,128)}, u32[]{:S(2)}) copy-start(f32[8,1024,256]{2,1,0:T(8,128)} %mesh_ref.5) | copy-start | bytes 25165828
  4.0 1.1 copy-start.31
  5.1 0.7 copy-start.36
  6.1 1.4 copy-start.30
  7.5 5.5 %copy-start.32 = (f32[35,4096]{1,0:T(8,128)S(1)}, f32[35,4096]{1,0:T(8,128)}, u32[]{:S(2)}) copy-start(f32[35,4096]{1,0:T(8,128)} %cells_ref.1) | copy-start | bytes 1720324
  7.5 66.2 %all-to-all-start = ((f32[4,552,256]{2,1,0:T(8,128)}), f32[4,552,256]{2,1,0:T(8,128)S(1)}, u32[]{:S(2)}, u32[]{:S(2)}) async-start(f32[4,552,256]{2,1,0:T(8,128)} %copy-done.30), calls=%async_computation | async-start | bytes 4521984 | tf_op jit(solution)/shard_map/all_to_all | solution.py:732
  13.0 3.4 %copy-start.35 = (s32[1,8,512]{2,1,0:T(8,128)S(1)}, s32[1,8,512]{2,1,0:T(8,128)}, u32[]{:S(2)}) copy-start(s32[1,8,512]{2,1,0:T(8,128)} %param.12) | copy-start | bytes 49156
  13.0 3.4 %copy-start.38 = (s32[1,8]{1,0:T(1,128)S(1)}, s32[1,8]{1,0:T(1,128)}, u32[]{:S(2)}) copy-start(s32[1,8]{1,0:T(1,128)} %param.13) | copy-start | bytes 100
  16.3 14.2 %copy-start.39 = (s32[65536]{0:T(1024)S(1)}, s32[65536]{0:T(1024)}, u32[]{:S(2)}) copy-start(s32[65536]{0:T(1024)} %param.14) | copy-start | bytes 786436
  27.0 2.2 copy-start
  29.2 9.9 %collective-permute-start = (f32[3,40,512]{2,1,0:T(8,128)}, f32[3,40,512]{2,1,0:T(8,128)S(1)}, u32[]{:S(2)}, u32[]{:S(2)}) collective-permute-start(f32[3,40,512]{2,1,0:T(8,128)} %get-tuple-element.17), channel_id=1, source_target_pairs={{0,7},{1,0},{2,1},{3,2},{4,3},{5,4},{6,5},{7,6},{8,15},{9,8},{10,9... | collective-permute-start | bytes 737288 | tf_op jit(solution)/shard_map/ppermute | solution.py:176
  30.5 8.6 %collective-permute-start.1 = (f32[3,40,512]{2,1,0:T(8,128)S(1)}, f32[3,40,512]{2,1,0:T(8,128)S(1)}, u32[]{:S(2)}, u32[]{:S(2)}) collective-permute-start(f32[3,40,512]{2,1,0:T(8,128)S(1)} %get-tuple-element.18), channel_id=1, source_target_pairs={{0,1},{1,2},{2,3},{3,4},{4,5},{5,6},{6,7},{7,0},{8,9},{9,10},{10,1... | collective-permute-start | bytes 737288 | tf_op jit(solution)/shard_map/ppermute | solution.py:176
  39.9 33.9 %collective-permute-start.2 = (f32[3,40,512]{2,1,0:T(8,128)}, f32[3,40,512]{2,1,0:T(8,128)S(1)}, u32[]{:S(2)}, u32[]{:S(2)}) collective-permute-start(f32[3,40,512]{2,1,0:T(8,128)} %pad_maximum_fusion), channel_id=1, source_target_pairs={{0,24},{8,0},{16,8},{24,16},{1,25},{9,1},{17,9},{25,17},{2,26},{10... | collective-permute-start | bytes 737288 | tf_op jit(solution)/shard_map/ppermute | solution.py:176
  40.9 32.9 %collective-permute-start.3 = (f32[3,40,512]{2,1,0:T(8,128)}, f32[3,40,512]{2,1,0:T(8,128)S(1)}, u32[]{:S(2)}, u32[]{:S(2)}) collective-permute-start(f32[3,40,512]{2,1,0:T(8,128)} %pad_maximum_fusion.1), channel_id=1, source_target_pairs={{0,8},{8,16},{16,24},{24,0},{1,9},{9,17},{17,25},{25,1},{2,10},{10... | collective-permute-start | bytes 737288 | tf_op jit(solution)/shard_map/ppermute | solution.py:176
  42.6 3.4 %copy-start.3 = (f32[8,1024,256]{2,1,0:T(8,128)S(1)}, f32[8,1024,256]{2,1,0:T(8,128)}, u32[]{:S(2)}) copy-start(f32[8,1024,256]{2,1,0:T(8,128)} %mesh_ref.5) | copy-start | bytes 25165828
  46.5 1.7 copy-start.25
  53.5 2.1 copy-start.23
  58.1 2.0 copy-start.5
  73.7 88.5 %all-to-all-start.1 = ((f32[4,768,256]{2,1,0:T(8,128)}), f32[4,768,256]{2,1,0:T(8,128)}, u32[]{:S(2)}, u32[]{:S(2)}) async-start(f32[4,768,256]{2,1,0:T(8,128)} %bitcast.20), calls=%async_computation.1 | async-start | bytes 6291456 | tf_op jit(solution)/shard_map/all_to_all | solution.py:732
  79.9 1.3 collective-permute-start.4
  81.2 35.0 %slice-start = ((s8[4718592]{0:T(1024)(128)(4,1)}), s8[4194304]{0:T(1024)(128)(4,1)S(1)}, s32[]{:S(2)}) async-start(s8[4718592]{0:T(1024)(128)(4,1)} %bitcast.12), calls=%async_computation.3 | async-start | bytes 8388608
  81.2 35.0 %slice-start.1 = ((s8[4718592]{0:T(1024)(128)(4,1)}), s8[524288]{0:T(1024)(128)(4,1)S(1)}, s32[]{:S(2)}) async-start(s8[4718592]{0:T(1024)(128)(4,1)} %bitcast.12), calls=%async_computation.4 | async-start | bytes 1048576
  81.2 5.5 %collective-permute-start.5 = (f32[128,128]{1,0:T(8,128)S(1)}, f32[128,128]{1,0:T(8,128)S(1)}, u32[]{:S(2)}, u32[]{:S(2)}) collective-permute-start(f32[128,128]{1,0:T(8,128)S(1)} %pad_maximum_fusion.5), channel_id=1, source_target_pairs={{0,2},{1,3},{2,0},{3,1},{4,6},{5,7},{6,4},{7,5},{8,10},{9,11},{10,... | collective-permute-start | bytes 196616 | tf_op jit(solution)/shard_map/ppermute | solution.py:772
  82.8 3.4 %copy-start.4 = (f32[8,1024,256]{2,1,0:T(8,128)S(1)}, f32[8,1024,256]{2,1,0:T(8,128)}, u32[]{:S(2)}) copy-start(f32[8,1024,256]{2,1,0:T(8,128)} %mesh_ref.5) | copy-start | bytes 25165828
  86.7 2.3 copy-start.24
  86.8 29.5 %collective-permute-start.6 = (f32[256,128]{1,0:T(8,128)S(1)}, f32[256,128]{1,0:T(8,128)S(1)}, u32[]{:S(2)}, u32[]{:S(2)}) collective-permute-start(f32[256,128]{1,0:T(8,128)S(1)} %pad_maximum_fusion.4), channel_id=1, source_target_pairs={{0,4},{1,5},{2,6},{3,7},{4,0},{5,1},{6,2},{7,3},{8,12},{9,13},{10,... | collective-permute-start | bytes 393224 | tf_op jit(solution)/shard_map/ppermute | solution.py:772
  112.1 1.3 copy-start.11
  113.5 1.4 copy-start.15
  114.8 1.4 copy-start.19
  116.2 1.4 copy-start.8
  116.2 2.9 %copy-start.6 = (f32[189,40,128]{2,1,0:T(8,128)S(1)}, f32[189,40,128]{2,1,0:T(8,128)}, u32[]{:S(2)}) copy-start(f32[189,40,128]{2,1,0:T(8,128)} %copy-done.5) | copy-start | bytes 11612164
  116.2 2.9 %copy-start.37 = (s32[1024]{0:T(1024)S(1)}, s32[1024]{0:T(1024)}, u32[]{:S(2)}) copy-start(s32[1024]{0:T(1024)} %class_ref.3) | copy-start | bytes 12292
  159.2 2.2 copy-start.1
  161.4 0.8 copy-start.33
  162.2 8.8 %slice-start.4 = ((f32[8,40,512]{2,1,0:T(8,128)}), f32[2,40,512]{2,1,0:T(8,128)S(1)}, s32[]{:S(2)}) async-start(f32[8,40,512]{2,1,0:T(8,128)} %copy-done.33), calls=%async_computation.7 | async-start | bytes 327680 | tf_op jit(solution)/shard_map/slice | solution.py:780
  162.2 17.4 %copy-start.26 = (bf16[2,512,512]{2,1,0:T(8,128)(2,1)S(1)}, bf16[2,512,512]{2,1,0:T(8,128)(2,1)}, u32[]{:S(2)}) copy-start(bf16[2,512,512]{2,1,0:T(8,128)(2,1)} %constant.40.clone.refs_6_) | copy-start | bytes 3145732
  162.2 104.0 %all-to-all-start.2 = ((f32[4,768,256]{2,1,0:T(8,128)}), f32[4,768,256]{2,1,0:T(8,128)}, u32[]{:S(2)}, u32[]{:S(2)}) async-start(f32[4,768,256]{2,1,0:T(8,128)} %bitcast.19), calls=%async_computation.2 | async-start | bytes 6291456 | tf_op jit(solution)/shard_map/all_to_all | solution.py:732
  167.0 12.6 %copy-start.9 = (f32[4104,128]{1,0:T(8,128)S(1)}, f32[4104,128]{1,0:T(8,128)}, u32[]{:S(2)}) copy-start(f32[4104,128]{1,0:T(8,128)} %copy-done.8) | copy-start | bytes 6303748
  168.3 8.9 %collective-permute-start.8 = (f32[3,40,512]{2,1,0:T(8,128)S(1)}, f32[3,40,512]{2,1,0:T(8,128)S(1)}, u32[]{:S(2)}, u32[]{:S(2)}) collective-permute-start(f32[3,40,512]{2,1,0:T(8,128)S(1)} %get-tuple-element.32), channel_id=1, source_target_pairs={{0,1},{1,2},{2,3},{3,4},{4,5},{5,6},{6,7},{7,0},{8,9},{9,10},{10,1... | collective-permute-start | bytes 737288 | tf_op jit(solution)/shard_map/ppermute | solution.py:176
  168.3 8.9 %collective-permute-start.7 = (f32[3,40,512]{2,1,0:T(8,128)S(1)}, f32[3,40,512]{2,1,0:T(8,128)S(1)}, u32[]{:S(2)}, u32[]{:S(2)}) collective-permute-start(f32[3,40,512]{2,1,0:T(8,128)S(1)} %get-tuple-element.33), channel_id=1, source_target_pairs={{0,7},{1,0},{2,1},{3,2},{4,3},{5,4},{6,5},{7,6},{8,15},{9,8},{10,9... | collective-permute-start | bytes 737288 | tf_op jit(solution)/shard_map/ppermute | solution.py:176
  177.3 68.4 %collective-permute-start.9 = (f32[3,40,512]{2,1,0:T(8,128)S(1)}, f32[3,40,512]{2,1,0:T(8,128)S(1)}, u32[]{:S(2)}, u32[]{:S(2)}) collective-permute-start(f32[3,40,512]{2,1,0:T(8,128)S(1)} %pad_maximum_fusion.2), channel_id=1, source_target_pairs={{0,24},{8,0},{16,8},{24,16},{1,25},{9,1},{17,9},{25,17},{2,26},{10... | collective-permute-start | bytes 737288 | tf_op jit(solution)/shard_map/ppermute | solution.py:176
  177.3 14.1 %slice-start.2 = ((s8[4718592]{0:T(1024)(128)(4,1)}), s8[4194304]{0:T(1024)(128)(4,1)S(1)}, s32[]{:S(2)}) async-start(s8[4718592]{0:T(1024)(128)(4,1)} %bitcast.15), calls=%async_computation.5 | async-start | bytes 8388608
  177.4 68.3 %collective-permute-start.10 = (f32[3,40,512]{2,1,0:T(8,128)S(1)}, f32[3,40,512]{2,1,0:T(8,128)S(1)}, u32[]{:S(2)}, u32[]{:S(2)}) collective-permute-start(f32[3,40,512]{2,1,0:T(8,128)S(1)} %pad_maximum_fusion.3), channel_id=1, source_target_pairs={{0,8},{8,16},{16,24},{24,0},{1,9},{9,17},{17,25},{25,1},{2,10},{10... | collective-permute-start | bytes 737288 | tf_op jit(solution)/shard_map/ppermute | solution.py:176
  179.6 1.6 copy-start.12
  181.2 1.6 copy-start.16
  182.8 1.6 copy-start.20
  184.4 1.2 copy-start.27
  185.6 5.8 %slice-start.3 = ((s8[4718592]{0:T(1024)(128)(4,1)}), s8[524288]{0:T(1024)(128)(4,1)S(1)}, s32[]{:S(2)}) async-start(s8[4718592]{0:T(1024)(128)(4,1)} %bitcast.15), calls=%async_computation.6 | async-start | bytes 1048576
  185.6 5.8 %copy-start.7 = (f32[189,40,128]{2,1,0:T(8,128)S(1)}, f32[189,40,128]{2,1,0:T(8,128)}, u32[]{:S(2)}) copy-start(f32[189,40,128]{2,1,0:T(8,128)} %copy-done.5) | copy-start | bytes 11612164
  185.6 5.8 %copy-start.34 = (s32[256,128]{1,0:T(8,128)S(1)}, s32[256,128]{1,0:T(8,128)}, u32[]{:S(2)}) copy-start(s32[256,128]{1,0:T(8,128)} %get-tuple-element.35.source_ref) | copy-start | bytes 393220
  191.5 65.4 %copy-start.17 = (f32[4104,128]{1,0:T(8,128)S(1)}, f32[4104,128]{1,0:T(8,128)}, u32[]{:S(2)}) copy-start(f32[4104,128]{1,0:T(8,128)} %copy-done.15) | copy-start | bytes 6303748
  191.5 65.4 %copy-start.21 = (f32[4104,128]{1,0:T(8,128)S(1)}, f32[4104,128]{1,0:T(8,128)}, u32[]{:S(2)}) copy-start(f32[4104,128]{1,0:T(8,128)} %copy-done.19) | copy-start | bytes 6303748
  231.6 25.3 %copy-start.13 = (f32[4104,128]{1,0:T(8,128)S(1)}, f32[4104,128]{1,0:T(8,128)}, u32[]{:S(2)}) copy-start(f32[4104,128]{1,0:T(8,128)} %copy-done.11) | copy-start | bytes 6303748
  231.6 25.3 %copy-start.28 = (bf16[2,512,512]{2,1,0:T(8,128)(2,1)S(1)}, bf16[2,512,512]{2,1,0:T(8,128)(2,1)}, u32[]{:S(2)}) copy-start(bf16[2,512,512]{2,1,0:T(8,128)(2,1)} %constant.39.clone.refs_5_) | copy-start | bytes 3145732
  256.9 9.3 %copy-start.10 = (f32[4104,128]{1,0:T(8,128)S(1)}, f32[4104,128]{1,0:T(8,128)}, u32[]{:S(2)}) copy-start(f32[4104,128]{1,0:T(8,128)} %copy-done.8) | copy-start | bytes 6303748
  266.2 1.6 copy-start.14
  267.8 1.6 copy-start.18
  269.4 1.6 copy-start.22
  271.0 1.2 copy-start.29

commit v7 on v4

--- a/solution.py
+++ b/solution.py
@@ -18,7 +18,7 @@
 SHIFT = 6
 LANE_SHIFT = 7
 VMEM_BYTES = 48 * 1024 * 1024
-CHUNKS = (1, 3, 3, 1)
+CHUNKS = (1, 4, 3)
 TOP_ROWS = TOP // 2
 
 DEPOSIT_SCALE = 8.0
@@ -170,12 +170,16 @@
     )(proxy_list, proxy_count, as_rows(table))
 
 
-def exchange(down, up, mid):
-    def shift(value, axis, by):
-        count = lax.axis_size(axis)
-        return lax.ppermute(value, axis, [(i, (i + by) % count) for i in range(count)])
-
-    down, up = shift(down, "gy", -1), shift(up, "gy", 1)
+def shift(value, axis, by):
+    count = lax.axis_size(axis)
+    return lax.ppermute(value, axis, [(i, (i + by) % count) for i in range(count)])
+
+
+def along_gy(down, up):
+    return shift(down, "gy", -1), shift(up, "gy", 1)
+
+
+def along_gx(down, up, mid):
     left = shift(jnp.stack([down[0], mid[0], up[0]]), "gx", -1)
     right = shift(jnp.stack([down[2], mid[1], up[2]]), "gx", 1)
     return down, up, left, right
@@ -209,6 +213,33 @@
         cost_estimate=cost(10**6, 20 * 10**6),
         name="order",
     )(packed)
+
+
+def split_kernel(ops_ref, out_ref, *, group):
+    coefs = ops_ref.shape[1]
+
+    @pl.loop(0, ops_ref.shape[0], step=group)
+    def _(c):
+        at = pl.ds(c, group)
+        value = ops_ref[at]
+        high = value.astype(jnp.bfloat16).astype(jnp.float32)
+        out_ref[at] = jnp.zeros((group, KPAD, LANES), jnp.float32)
+        out_ref[at, :coefs, :coefs] = high
+        out_ref[at, :coefs, KPAD : KPAD + coefs] = value - high
+
+
+def split(turned_ops):
+    classes = turned_ops.shape[0]
+    group = max(size for size in range(1, 10) if classes % size == 0)
+    return pl.pallas_call(
+        functools.partial(split_kernel, group=group),
+        out_shape=jax.ShapeDtypeStruct((classes, KPAD, LANES), jnp.float32),
+        in_specs=[VMEM_WHOLE],
+        out_specs=VMEM_WHOLE,
+        compiler_params=params(),
+        cost_estimate=cost(10**6, 12 * 10**6),
+        name="split",
+    )(turned_ops)
 
 
 def m2l_kernel(source_ref, class_ref, table_ref, ops_ref, out_ref, *gathered, first, turned):
@@ -363,12 +394,15 @@
     )(mesh)
 
 
-def first_part_kernel(mesh_ref, place_ref, cells_ref, out_ref, sems, *, rows):
+def first_part_kernel(mesh_ref, place_ref, cells_ref, out_ref, sems, *, count, rows):
     sources, _, width = out_ref.shape
     copies = [
         pltpu.make_async_copy(
-            mesh_ref.at[0, pl.ds(s * rows, rows), :], out_ref.at[s, pl.ds(0, rows), :], sems.at[s]
+            mesh_ref.at[p, pl.ds(s * rows, rows), :],
+            out_ref.at[s, pl.ds(p * rows, rows), :],
+            sems.at[p, s],
         )
+        for p in range(count)
         for s in range(sources)
     ]
     for copy in copies:
@@ -378,7 +412,7 @@
     table = spread(jnp.concatenate([cells_ref[:, :LANES], rest], axis=0))
     top = jnp.where(is_first, table[:TOP_ROWS, :], table[TOP_ROWS : 2 * TOP_ROWS, :])
     blocks = [place_ref[...].astype(jnp.float32), cell_lines(cells_ref), top]
-    at = rows
+    at = count * rows
     for block in blocks:
         high = block.shape[0] * LANES // width
         for h in range(width // LANES):
@@ -396,16 +430,16 @@
     return DEPOSIT_SCALE * jnp.concatenate(lines, axis=0)
 
 
-def first_part(mesh, place, multipoles, sources):
+def first_part(mesh, place, multipoles, sources, count):
     rows, width = mesh.shape[1] // sources, mesh.shape[2]
     extra = (2 * place.size + TOP_ROWS * LANES) // width
     return pl.pallas_call(
-        functools.partial(first_part_kernel, rows=rows),
-        out_shape=jax.ShapeDtypeStruct((sources, rows + extra, width), jnp.float32),
+        functools.partial(first_part_kernel, count=count, rows=rows),
+        out_shape=jax.ShapeDtypeStruct((sources, count * rows + extra, width), jnp.float32),
         in_specs=[pl.BlockSpec(memory_space=pl.ANY), VMEM_WHOLE, VMEM_WHOLE],
         out_specs=VMEM_WHOLE,
         scratch_shapes=[
-            pltpu.SemaphoreType.DMA((sources,)),
+            pltpu.SemaphoreType.DMA((count, sources)),
         ],
         compiler_params=params(),
         cost_estimate=cost(0, 8 * sources * rows * width),
@@ -417,10 +451,10 @@
     return value.bit_length() - 1
 
 
-def sift_kernel(mine_ref, part_ref, code_ref, value_ref, bound_ref, top_ref, ride, sem, *, planes, rows):
+def sift_kernel(mine_ref, part_ref, code_ref, value_ref, bound_ref, top_ref, ride, sem, *, count, planes, rows):
     sources, extra, width = ride.shape
     lines = code_ref.shape[0] // sources
-    copy = pltpu.make_async_copy(part_ref.at[:, pl.ds(rows, extra), :], ride, sem)
+    copy = pltpu.make_async_copy(part_ref.at[:, pl.ds(count * rows, extra), :], ride, sem)
     copy.start()
     copy.wait()
 
@@ -470,12 +504,12 @@
     bound_ref[...] = jnp.max(counts, axis=0).astype(jnp.int32)
 
 
-def sift(part, mine, planes, rows, lines):
+def sift(part, mine, count, planes, rows, lines):
     sources, whole_rows, width = part.shape
-    extra = whole_rows - rows
+    extra = whole_rows - count * rows
     shape = (sources * lines, LANES)
     return pl.pallas_call(
-        functools.partial(sift_kernel, planes=planes, rows=rows),
+        functools.partial(sift_kernel, count=count, planes=planes, rows=rows),
         out_shape=(
             jax.ShapeDtypeStruct(shape, jnp.int32),
             jax.ShapeDtypeStruct(shape, jnp.float32),
@@ -687,7 +721,7 @@
         spans.append((first, size))
         first += size
 
-    parts = [send(first_part(pm_density, cell_mesh, multipoles, n_gx))]
+    parts = [send(first_part(pm_density, cell_mesh, multipoles, n_gx, spans[0][1]))]
     carved = [
         carve(pm_density, at, size, n_gx).reshape(n_gx, size * own_rows, width)
         for at, size in spans[1:]
@@ -697,7 +731,6 @@
     base = cell_count + 8 * slots
     table = own_table(cells, base + TOP * domains)
     outgoing = pack(table, cell_count, lists, counts)
-    arrived = exchange(*outgoing)
 
     top = pair_source - base
     domain = top >> log2(TOP)
@@ -707,40 +740,37 @@
     wanted = jnp.where(pair_source < base, pair_source, top)
     sources = order(((wanted << SHIFT) | (pair_target & (BLOCK - 1))).reshape(-1, LANES))
 
-    turned_ops = jnp.pad(
-        m2l_ops.transpose(0, 2, 1), ((0, 0), (0, KPAD - coef_count), (0, KPAD - coef_count))
-    )
-    high = lax.reduce_precision(turned_ops, 8, 7)
-    ops = jnp.concatenate([high, turned_ops - high], axis=2)
-    ops = jnp.pad(ops, ((0, 0), (0, 0), (0, LANES - 2 * KPAD)))
+    arrived = along_gx(*along_gy(*outgoing[:2]), after(outgoing[2], sources))
+
+    ops = split(m2l_ops.transpose(0, 2, 1))
 
     tiles = width // LANES
     add_rows = planes * tiles * own_rows
     mine = lax.axis_index("gx").astype(jnp.int32).reshape(1)
-    codes, amounts, bounds, top_own = sift(parts[0], mine, planes, own_rows, cell_count // LANES)
+    codes, amounts, bounds, top_own = sift(
+        parts[0], mine, spans[0][1], planes, own_rows, cell_count // LANES
+    )
     tops = [top_own]
     for bit in range(log2(n_gy)):
         held = jnp.concatenate(tops, axis=0) if bit else top_own
         tops.append(lax.ppermute(held, "gy", [(i, i ^ (1 << bit)) for i in range(n_gy)]))
 
-    parts.append(send(after(carved[0], parts[0], *arrived)))
+    parts.append(send(after(carved[0], parts[0], ops, *arrived)))
     adds = deposit(codes, amounts, bounds, add_rows + 8, n_gx)
     table = whole_table(table, arrived, tops)
     cell_steps = cell_count // LANES
     slot_steps = 8 * slots // LANES
     slot_fields = m2l(sources, block_class, table, ops, cell_steps, slot_steps, True, slots)
-    returned = exchange(slot_fields[:3], slot_fields[3:6], slot_fields[6:])
-    parts.append(send(after(carved[1], parts[1], slot_fields)))
+    tables = fourier_tables(n_gx * width)
+    spectrum = fourier(parts[0], spans[0][1], adds, tables, 0, planes, None, own_rows)
+    crossed = along_gy(slot_fields[:3], slot_fields[3:6])
+    parts.append(send(after(carved[1], parts[1], spectrum, *crossed)))
+    returned = along_gx(*crossed, slot_fields[6:])
     own_fields = m2l(sources, block_class, table, ops, 0, cell_steps, False, slots)
-
-    tables = fourier_tables(n_gx * width)
-    spectrum = None
-    for i, (at, size) in enumerate(spans):
-        if i == 2:
-            parts.append(send(after(carved[2], parts[2], own_fields, spectrum, *returned)))
-        spectrum = fourier(parts[i], size, adds, tables, at, planes, spectrum, own_rows)
-
+    spectrum = fourier(parts[1], spans[1][1], adds, tables, spans[1][0], planes, spectrum, own_rows)
+    own_fields = after(own_fields, spectrum)
     field_tensors = add_back(lists, counts, own_fields, returned, coef_count)
+    spectrum = fourier(parts[2], spans[2][1], adds, tables, spans[2][0], planes, spectrum, own_rows)
     return (field_tensors, spectrum)
 
 

time: 267 us -> 262 us (0.981)
  other arithmetic: 9.2 us -> 0.27 us
  local copies, waits for them, and re-layouts: 19.5 us -> 25.5 us
  waiting for transfers between devices: 26.5 us -> 32.2 us
  starting transfers between devices: 32.6 us -> 27.3 us
  Pallas kernels: 176 us -> 173 us
    ppermute x3, waiting for transfers between devices: 0.87 us -> 9.21 us  [on_device(): lax.ppermute(held, 'gy', [(i, i ^ 1 << bit) for i in range(n_gy)])]
    reduce_precision x1 -> x0, other arithmetic: 5.72 us -> none  [on_device(): high = lax.reduce_precision(turned_ops, 8, 7)]
    all_to_all x4 -> x3, starting transfers between devices: 23.3 us -> 18.4 us  [send(): return lax.all_to_all(part, 'gx', 0, 0, tiled=True)]
    pallas_call x3 -> x2, Pallas kernels: 8.85 us -> 4.08 us  [carve(): pl.pallas_call(functools.partial(carve_kernel, first=first), out_shape=ja...]
    pallas_call x2 -> x3, Pallas kernels: 3.7 us -> 8.36 us  [the longest x1 4.65 us: split(): pl.pallas_call(functools.partial(split_kernel, group=group), out_shape=ja...]
    unnamed x69 -> x49, local copies, waits for them, and re-layouts: 19.3 us -> 22.6 us
    pallas_call x4 -> x3, Pallas kernels: 28.6 us -> 25.4 us  [fourier(): pl.pallas_call(functools.partial(fourier_kernel, sources=sources), grid=(...]
    concatenate x1 -> x0, other arithmetic: 3.22 us -> none  [on_device(): ops = jnp.concatenate([high, turned_ops - high], axis=2)]
  transfers between devices with their start and end apart: 15 -> 14, of which waited for: 7 -> 5; matrix products, arithmetic and copies ran while one was open for 6% -> 3% of each run, Pallas kernels for 64% -> 62%
where the time goes in v7:
time: 262 us; the launch traced here: 259 us
  Pallas kernels  173 us (66%)
  waiting for transfers between devices  32.2 us (12%)
  starting transfers between devices  27.3 us (10%)
  local copies, waits for them, and re-layouts  25.5 us (10%)
    pallas_call x2, Pallas kernels, m2l(): pl.pallas_call(functools.partial(m2l_kernel, first=first, turned=turned),...  80 us
    pallas_call x3, Pallas kernels, fourier(): pl.pallas_call(functools.partial(fourier_kernel, sources=sources), grid=(...  25.4 us
    ppermute x8, waiting for transfers between devices, shift(): lax.ppermute(value, axis, [(i, (i + by) % count) for i in range(count)])  23 us
    unnamed x49, local copies, waits for them, and re-layouts  22.6 us
    pallas_call x1, Pallas kernels, deposit(): pl.pallas_call(deposit_kernel, out_shape=(jax.ShapeDtypeStruct((rows, LAN...  21.6 us
    all_to_all x3, starting transfers between devices, send(): return lax.all_to_all(part, 'gx', 0, 0, tiled=True)  18.4 us
    pallas_call x1, Pallas kernels, add_back(): pl.pallas_call(add_back_kernel, out_shape=jax.ShapeDtypeStruct((coef_coun...  11.5 us
    pallas_call x1, Pallas kernels, pack(): pl.pallas_call(pack_kernel, grid=(1,), out_shape=tuple((jax.ShapeDtypeStr...  9.99 us
  transfers between devices with their start and end apart: 14, of which 5 were waited for; matrix products, arithmetic and copies ran while one was open for 3% of the time, Pallas kernels for 62%

profile of v7, /device:TPU:8, one launch (start us, length us, event | category | flops | bytes accessed | tf_op | source)
XLA Modules:
  0.0 259.3 jit_solution(1860249542179741287)
XLA Ops:
  0.6 1.1 copy-done.13
  1.7 0.7 copy-done.19
  2.4 2.4 first_part.1
  4.8 5.3 %all-to-all-start = ((f32[4,296,256]{2,1,0:T(8,128)}), f32[4,296,256]{2,1,0:T(8,128)S(1)}, u32[]{:S(2)}, u32[]{:S(2)}) async-start(f32[4,296,256]{2,1,0:T(8,128)} %first_part.1), calls=%async_computation | async-start | bytes 2424832 | tf_op jit(solution)/shard_map/all_to_all | solution.py:716
  10.2 0.0 copy-start.22
  10.2 0.0 copy-start.23
  10.2 3.3 %own_table.1.refs_8_ = f32[9216,128]{1,0:T(8,128)S(1)} custom-call(f32[40,4096]{1,0:T(8,128)S(1)} %pad.4.cells_ref), custom_call_target="tpu_custom_call" | custom-call | flops 1000000 | bytes 12000000 | tf_op jit(solution)/shard_map/own_table/pallas_call | solution.py:59
  13.6 10.0 %pack.1 = (f32[3,40,512]{2,1,0:T(8,128)S(1)}, f32[3,40,512]{2,1,0:T(8,128)S(1)}, f32[2,40,512]{2,1,0:T(8,128)S(1)}) custom-call(s32[8,512]{1,0:T(8,128)S(1)} %bitcast.16, s32[8]{0:T(128)S(1)} %bitcast.19, f32[9216,1,128]{2,1,0:T(1,128)S(1)} %bitcast.11), custom_call_target="tpu_custom_call" | custom-call | flops 1000000 | bytes 25000000 | tf_op jit(solution)/shard_map/pack/pallas_call | solution.py:154
  23.6 2.2 copy-done
  25.8 1.3 collective-permute-start
  27.1 0.0 collective-permute-start.1
  27.1 0.2 fusion.2.packed_ref
  27.3 7.4 %order.1.source_ref = s32[512,128]{1,0:T(8,128)S(1)} custom-call(s32[512,128]{1,0:T(8,128)S(1)} %fusion.2.packed_ref), custom_call_target="tpu_custom_call" | custom-call | flops 1000000 | bytes 20000000 | tf_op jit(solution)/shard_map/order/pallas_call | solution.py:207
  34.7 0.0 collective-permute-done.refs_0_
  34.7 0.3 collective-permute-done.1.refs_1_
  35.1 0.1 collective-permute-start.2
  35.2 2.0 collective-permute-start.3
  37.2 2.2 carve.2
  39.4 2.1 copy-done.6
  41.5 5.2 %copy.16 = f32[189,35,35]{1,2,0:T(8,128)} copy(f32[189,35,35]{0,2,1:T(8,128)} %param.17) | data formatting | bytes 1852200 | tf_op args[6]
  46.8 4.7 %split.1.ops_ref = f32[189,40,128]{2,1,0:T(8,128)S(1)} custom-call(f32[189,35,35]{2,1,0:T(8,128)} %bitcast.21), custom_call_target="tpu_custom_call" | custom-call | flops 1000000 | bytes 12000000 | tf_op jit(solution)/shard_map/split/pallas_call | solution.py:234
  51.4 1.8 copy-done.3
  53.3 0.0 collective-permute-done.2.refs_2_
  53.3 0.0 collective-permute-done.3.refs_3_
  53.3 0.0 all-to-all-done.part_ref.refs_0_
  53.3 6.9 %all-to-all-start.1 = ((f32[4,1024,256]{2,1,0:T(8,128)}), f32[4,1024,256]{2,1,0:T(8,128)}, u32[]{:S(2)}, u32[]{:S(2)}) async-start(f32[4,1024,256]{2,1,0:T(8,128)} %bitcast.14), calls=%async_computation.1 | async-start | bytes 8388608 | tf_op jit(solution)/shard_map/all_to_all | solution.py:716
  60.2 1.3 sift.1
  61.5 0.1 collective-permute-start.4
  61.6 1.2 collective-permute-done.4.refs_5_
  62.8 0.7 collective-permute-start.5
  63.5 3.6 %collective-permute-done.5.refs_6_ = f32[128,128]{1,0:T(8,128)S(1)} collective-permute-done((f32[128,128]{1,0:T(8,128)S(1)}, f32[128,128]{1,0:T(8,128)S(1)}, u32[]{:S(2)}, u32[]{:S(2)}) %collective-permute-start.5) | collective-permute-done | bytes 65568 | tf_op jit(solution)/shard_map/ppermute | solution.py:756
  67.1 0.6 collective-permute-start.6
  67.7 4.4 %collective-permute-done.6.refs_7_ = f32[256,128]{1,0:T(8,128)S(1)} collective-permute-done((f32[256,128]{1,0:T(8,128)S(1)}, f32[256,128]{1,0:T(8,128)S(1)}, u32[]{:S(2)}, u32[]{:S(2)}) %collective-permute-start.6) | collective-permute-done | bytes 131104 | tf_op jit(solution)/shard_map/ppermute | solution.py:756
  72.1 2.3 copy-done.1
  74.5 1.3 whole_table.1
  75.8 2.1 copy-done.2
  78.0 40.1 %m2l_slots.1 = f32[8,40,512]{2,1,0:T(8,128)S(1)} custom-call(s32[512,128]{1,0:T(8,128)S(1)} %order.1.source_ref, s32[1024]{0:T(1024)S(1)} %copy-done.20, f32[9216,1,128]{2,1,0:T(1,128)} %bitcast.12, f32[189,40,128]{2,1,0:T(8,128)S(1)} %copy-done.4), custom_call_target="tpu_custom_call" | custom-call | flops 1000000 | bytes 150000000 | tf_op jit(solution)/shard_map/m2l_slots/pallas_call | solution.py:302
  118.1 0.0 copy-start.15
  118.1 0.1 collective-permute-start.8
  118.2 0.7 copy-done.15
  118.9 1.9 collective-permute-start.7
  120.8 1.9 carve.3
  122.7 1.6 copy-done.7
  124.3 21.6 %deposit.1 = (f32[4104,128]{1,0:T(8,128)S(1)}, f32[4104,128]{1,0:T(8,128)S(1)}, f32[4104,128]{1,0:T(8,128)}, f32[4104,128]{1,0:T(8,128)}) custom-call(s32[128,128]{1,0:T(8,128)S(1)} %get-tuple-element.23.code_ref, f32[128,128]{1,0:T(8,128)S(1)} %get-tuple-element.24.value_ref, s32[16,128]{1,0:T(8,128)S(1)} %get-tuple-element.25.bound_ref), custom_call_target="tpu_custom_call" | custom-call | flops 1000000 | bytes 40000000 | tf_op jit(solution)/shard_map/deposit/pallas_call | solution.py:562
  145.9 1.4 copy-done.5
  147.3 4.6 %fourier.3.refs_7_ = f32[2,8,256,1024]{3,2,1,0:T(8,128)} custom-call(f32[4,296,256]{2,1,0:T(8,128)S(1)} %all-to-all-done.part_ref.refs_0_, f32[4104,128]{1,0:T(8,128)S(1)} %get-tuple-element.26.refs_1_, f32[4104,128]{1,0:T(8,128)} %copy-done.5, f32[4104,128]{1,0:T(8,128)} %get-tuple-element.28.refs_3_, f32[4104,128]{1,0:T(8,128)} %get-tuple-element.29.refs_4_, ...), custom_call_target="tpu_custom_call" | custom-call | flops 1000000 | bytes 10000000 | tf_op jit(solution)/shard_map/fourier/pallas_call | solution.py:677
  151.9 0.0 collective-permute-done.8.refs_1_
  151.9 0.0 collective-permute-done.7.refs_0_
  151.9 0.0 all-to-all-done.1.refs_0_
  151.9 6.2 %all-to-all-start.2 = ((f32[4,768,256]{2,1,0:T(8,128)}), f32[4,768,256]{2,1,0:T(8,128)}, u32[]{:S(2)}, u32[]{:S(2)}) async-start(f32[4,768,256]{2,1,0:T(8,128)} %bitcast.15), calls=%async_computation.2 | async-start | bytes 6291456 | tf_op jit(solution)/shard_map/all_to_all | solution.py:716
  158.1 0.9 fusion.6
  159.0 0.9 fusion.9
  160.0 0.9 fusion.8
  161.0 0.1 collective-permute-start.9
  161.1 0.0 copy-start.9
  161.1 0.0 copy-start.11
  161.1 2.0 collective-permute-start.10
  163.1 39.9 %m2l_cells.1.own_ref = f32[4096,128]{1,0:T(8,128)S(1)} custom-call(s32[512,128]{1,0:T(8,128)S(1)} %copy-done.17, s32[1024]{0:T(1024)S(1)} %copy-done.20, f32[9216,1,128]{2,1,0:T(1,128)} %bitcast.13, f32[189,40,128]{2,1,0:T(8,128)} %copy-done.3), custom_call_target="tpu_custom_call" | custom-call | flops 1000000 | bytes 150000000 | tf_op jit(solution)/shard_map/m2l_cells/pallas_call | solution.py:302
  203.1 11.5 %fourier.4.refs_7_ = f32[2,8,256,1024]{3,2,1,0:T(8,128)} custom-call(f32[4,1024,256]{2,1,0:T(8,128)} %all-to-all-done.1.refs_0_, f32[4104,128]{1,0:T(8,128)S(1)} %get-tuple-element.26.refs_1_, f32[4104,128]{1,0:T(8,128)} %copy-done.5, f32[4104,128]{1,0:T(8,128)} %get-tuple-element.28.refs_3_, ...), custom_call_target="tpu_custom_call", output_to_operand_aliasing={{}: (7, {})} | custom-call | flops 1000000 | bytes 40000000 | tf_op jit(solution)/shard_map/fourier/pallas_call | solution.py:677
  214.6 22.7 %collective-permute-done.9.refs_2_ = f32[3,40,512]{2,1,0:T(8,128)S(1)} collective-permute-done((f32[3,40,512]{2,1,0:T(8,128)S(1)}, f32[3,40,512]{2,1,0:T(8,128)S(1)}, u32[]{:S(2)}, u32[]{:S(2)}) %collective-permute-start.9) | collective-permute-done | bytes 245792 | tf_op jit(solution)/shard_map/ppermute | solution.py:175
  237.3 0.0 collective-permute-done.10.refs_3_
  237.3 11.5 %add_back.1 = f32[35,4096]{1,0:T(8,128)} custom-call(s32[8,512]{1,0:T(8,128)S(1)} %bitcast.17, s32[8]{0:T(128)S(1)} %bitcast.20, f32[4096,128]{1,0:T(8,128)S(1)} %m2l_cells.1.own_ref, f32[3,40,512]{2,1,0:T(8,128)} %collective-permute-done.7.refs_0_, f32[3,40,512]{2,1,0:T(8,128)} %collective-permute-done.8.refs_1_, ...), custom_call_target="tpu_custom_call" | custom-call | flops 1000000 | bytes 30000000 | tf_op jit(solution)/shard_map/add_back/pallas_call | solution.py:356
  248.8 1.2 copy-done.12
  250.1 9.3 %fourier.5 = f32[2,8,256,1024]{3,2,1,0:T(8,128)} custom-call(f32[4,768,256]{2,1,0:T(8,128)} %all-to-all-done.2.refs_0_, f32[4104,128]{1,0:T(8,128)S(1)} %get-tuple-element.26.refs_1_, f32[4104,128]{1,0:T(8,128)} %copy-done.5, f32[4104,128]{1,0:T(8,128)} %get-tuple-element.28.refs_3_, ...), custom_call_target="tpu_custom_call", output_to_operand_aliasing={{}: (7, {})} | custom-call | flops 1000000 | bytes 30000000 | tf_op jit(solution)/shard_map/fourier/pallas_call | solution.py:677
  (44 shorter events, 0.3 us)
Async XLA Ops:
  0.6 1.1 copy-start.13
  1.7 0.7 copy-start.19
  2.4 7.7 %copy-start.14 = (f32[35,4096]{1,0:T(8,128)S(1)}, f32[35,4096]{1,0:T(8,128)}, u32[]{:S(2)}) copy-start(f32[35,4096]{1,0:T(8,128)} %cells_ref.1) | copy-start | bytes 1720324
  4.8 48.5 %all-to-all-start = ((f32[4,296,256]{2,1,0:T(8,128)}), f32[4,296,256]{2,1,0:T(8,128)S(1)}, u32[]{:S(2)}, u32[]{:S(2)}) async-start(f32[4,296,256]{2,1,0:T(8,128)} %first_part.1), calls=%async_computation | async-start | bytes 2424832 | tf_op jit(solution)/shard_map/all_to_all | solution.py:716
  10.1 3.4 %copy-start.18 = (s32[1,8,512]{2,1,0:T(8,128)S(1)}, s32[1,8,512]{2,1,0:T(8,128)}, u32[]{:S(2)}) copy-start(s32[1,8,512]{2,1,0:T(8,128)} %param.12) | copy-start | bytes 49156
  10.1 3.4 %copy-start.21 = (s32[1,8]{1,0:T(1,128)S(1)}, s32[1,8]{1,0:T(1,128)}, u32[]{:S(2)}) copy-start(s32[1,8]{1,0:T(1,128)} %param.13) | copy-start | bytes 100
  10.2 16.9 %copy-start.22 = (s32[65536]{0:T(1024)S(1)}, s32[65536]{0:T(1024)}, u32[]{:S(2)}) copy-start(s32[65536]{0:T(1024)} %param.14) | copy-start | bytes 786436
  10.2 16.9 %copy-start.23 = (s32[65536]{0:T(1024)S(1)}, s32[65536]{0:T(1024)}, u32[]{:S(2)}) copy-start(s32[65536]{0:T(1024)} %param.15) | copy-start | bytes 786436
  23.6 2.2 copy-start
  25.8 9.0 %collective-permute-start = (f32[3,40,512]{2,1,0:T(8,128)S(1)}, f32[3,40,512]{2,1,0:T(8,128)S(1)}, u32[]{:S(2)}, u32[]{:S(2)}) collective-permute-start(f32[3,40,512]{2,1,0:T(8,128)S(1)} %get-tuple-element.17), channel_id=1, source_target_pairs={{0,7},{1,0},{2,1},{3,2},{4,3},{5,4},{6,5},{7,6},{8,15},{9,8},{10,9... | collective-permute-start | bytes 737288 | tf_op jit(solution)/shard_map/ppermute | solution.py:175
  27.1 7.9 %collective-permute-start.1 = (f32[3,40,512]{2,1,0:T(8,128)S(1)}, f32[3,40,512]{2,1,0:T(8,128)S(1)}, u32[]{:S(2)}, u32[]{:S(2)}) collective-permute-start(f32[3,40,512]{2,1,0:T(8,128)S(1)} %get-tuple-element.18), channel_id=1, source_target_pairs={{0,1},{1,2},{2,3},{3,4},{4,5},{5,6},{6,7},{7,0},{8,9},{9,10},{10,1... | collective-permute-start | bytes 737288 | tf_op jit(solution)/shard_map/ppermute | solution.py:175
  34.7 43.3 %copy-start.16 = (s32[512,128]{1,0:T(8,128)}, s32[512,128]{1,0:T(8,128)S(1)}, u32[]{:S(2)}) copy-start(s32[512,128]{1,0:T(8,128)S(1)} %order.1.source_ref) | copy-start | bytes 786436
  35.1 18.2 %collective-permute-start.2 = (f32[3,40,512]{2,1,0:T(8,128)S(1)}, f32[3,40,512]{2,1,0:T(8,128)S(1)}, u32[]{:S(2)}, u32[]{:S(2)}) collective-permute-start(f32[3,40,512]{2,1,0:T(8,128)S(1)} %pad_maximum_fusion), channel_id=1, source_target_pairs={{0,24},{8,0},{16,8},{24,16},{1,25},{9,1},{17,9},{25,17},{2,26},{10... | collective-permute-start | bytes 737288 | tf_op jit(solution)/shard_map/ppermute | solution.py:175
  35.2 18.1 %collective-permute-start.3 = (f32[3,40,512]{2,1,0:T(8,128)S(1)}, f32[3,40,512]{2,1,0:T(8,128)S(1)}, u32[]{:S(2)}, u32[]{:S(2)}) collective-permute-start(f32[3,40,512]{2,1,0:T(8,128)S(1)} %pad_maximum_fusion.1), channel_id=1, source_target_pairs={{0,8},{8,16},{16,24},{24,0},{1,9},{9,17},{17,25},{25,1},{2,10},{10... | collective-permute-start | bytes 737288 | tf_op jit(solution)/shard_map/ppermute | solution.py:175
  39.4 2.1 copy-start.6
  51.4 1.8 copy-start.3
  53.3 98.6 %all-to-all-start.1 = ((f32[4,1024,256]{2,1,0:T(8,128)}), f32[4,1024,256]{2,1,0:T(8,128)}, u32[]{:S(2)}, u32[]{:S(2)}) async-start(f32[4,1024,256]{2,1,0:T(8,128)} %bitcast.14), calls=%async_computation.1 | async-start | bytes 8388608 | tf_op jit(solution)/shard_map/all_to_all | solution.py:716
  61.5 1.3 collective-permute-start.4
  62.8 4.3 %collective-permute-start.5 = (f32[128,128]{1,0:T(8,128)S(1)}, f32[128,128]{1,0:T(8,128)S(1)}, u32[]{:S(2)}, u32[]{:S(2)}) collective-permute-start(f32[128,128]{1,0:T(8,128)S(1)} %pad_maximum_fusion.5), channel_id=1, source_target_pairs={{0,2},{1,3},{2,0},{3,1},{4,6},{5,7},{6,4},{7,5},{8,10},{9,11},{10,... | collective-permute-start | bytes 196616 | tf_op jit(solution)/shard_map/ppermute | solution.py:756
  67.1 10.9 %copy-start.20 = (s32[1024]{0:T(1024)S(1)}, s32[1024]{0:T(1024)}, u32[]{:S(2)}) copy-start(s32[1024]{0:T(1024)} %class_ref.3) | copy-start | bytes 12292
  67.1 5.0 %collective-permute-start.6 = (f32[256,128]{1,0:T(8,128)S(1)}, f32[256,128]{1,0:T(8,128)S(1)}, u32[]{:S(2)}, u32[]{:S(2)}) collective-permute-start(f32[256,128]{1,0:T(8,128)S(1)} %pad_maximum_fusion.4), channel_id=1, source_target_pairs={{0,4},{1,5},{2,6},{3,7},{4,0},{5,1},{6,2},{7,3},{8,12},{9,13},{10,... | collective-permute-start | bytes 393224 | tf_op jit(solution)/shard_map/ppermute | solution.py:756
  72.1 2.3 copy-start.1
  74.5 3.5 %copy-start.4 = (f32[189,40,128]{2,1,0:T(8,128)S(1)}, f32[189,40,128]{2,1,0:T(8,128)}, u32[]{:S(2)}) copy-start(f32[189,40,128]{2,1,0:T(8,128)} %copy-done.3) | copy-start | bytes 11612164
  75.8 2.2 copy-start.2
  118.1 0.8 copy-start.15
  118.1 33.7 %collective-permute-start.8 = (f32[3,40,512]{2,1,0:T(8,128)S(1)}, f32[3,40,512]{2,1,0:T(8,128)}, u32[]{:S(2)}, u32[]{:S(2)}) collective-permute-start(f32[3,40,512]{2,1,0:T(8,128)S(1)} %get-tuple-element.34), channel_id=1, source_target_pairs={{0,1},{1,2},{2,3},{3,4},{4,5},{5,6},{6,7},{7,0},{8,9},{9,10},{10,1... | collective-permute-start | bytes 737288 | tf_op jit(solution)/shard_map/ppermute | solution.py:175
  118.9 28.4 %copy-start.8 = (bf16[2,512,512]{2,1,0:T(8,128)(2,1)S(1)}, bf16[2,512,512]{2,1,0:T(8,128)(2,1)}, u32[]{:S(2)}) copy-start(bf16[2,512,512]{2,1,0:T(8,128)(2,1)} %constant.40.clone.refs_6_) | copy-start | bytes 3145732
  118.9 28.4 %copy-start.10 = (bf16[2,512,512]{2,1,0:T(8,128)(2,1)S(1)}, bf16[2,512,512]{2,1,0:T(8,128)(2,1)}, u32[]{:S(2)}) copy-start(bf16[2,512,512]{2,1,0:T(8,128)(2,1)} %constant.39.clone.refs_5_) | copy-start | bytes 3145732
  118.9 33.0 %collective-permute-start.7 = (f32[3,40,512]{2,1,0:T(8,128)S(1)}, f32[3,40,512]{2,1,0:T(8,128)}, u32[]{:S(2)}, u32[]{:S(2)}) collective-permute-start(f32[3,40,512]{2,1,0:T(8,128)S(1)} %get-tuple-element.35), channel_id=1, source_target_pairs={{0,7},{1,0},{2,1},{3,2},{4,3},{5,4},{6,5},{7,6},{8,15},{9,8},{10,9... | collective-permute-start | bytes 737288 | tf_op jit(solution)/shard_map/ppermute | solution.py:175
  122.7 1.6 copy-start.7
  145.9 1.4 copy-start.5
  151.9 11.2 %copy-start.17 = (s32[512,128]{1,0:T(8,128)S(1)}, s32[512,128]{1,0:T(8,128)}, u32[]{:S(2)}) copy-start(s32[512,128]{1,0:T(8,128)} %copy-done.16) | copy-start | bytes 786436
  151.9 96.9 %all-to-all-start.2 = ((f32[4,768,256]{2,1,0:T(8,128)}), f32[4,768,256]{2,1,0:T(8,128)}, u32[]{:S(2)}, u32[]{:S(2)}) async-start(f32[4,768,256]{2,1,0:T(8,128)} %bitcast.15), calls=%async_computation.2 | async-start | bytes 6291456 | tf_op jit(solution)/shard_map/all_to_all | solution.py:716
  161.0 76.4 %collective-permute-start.9 = (f32[3,40,512]{2,1,0:T(8,128)S(1)}, f32[3,40,512]{2,1,0:T(8,128)S(1)}, u32[]{:S(2)}, u32[]{:S(2)}) collective-permute-start(f32[3,40,512]{2,1,0:T(8,128)S(1)} %pad_maximum_fusion.2), channel_id=1, source_target_pairs={{0,24},{8,0},{16,8},{24,16},{1,25},{9,1},{17,9},{25,17},{2,26},{10... | collective-permute-start | bytes 737288 | tf_op jit(solution)/shard_map/ppermute | solution.py:175
  161.1 42.0 %copy-start.9 = (bf16[2,512,512]{2,1,0:T(8,128)(2,1)S(1)}, bf16[2,512,512]{2,1,0:T(8,128)(2,1)}, u32[]{:S(2)}) copy-start(bf16[2,512,512]{2,1,0:T(8,128)(2,1)} %constant.40.clone.refs_6_) | copy-start | bytes 3145732
  161.1 42.0 %copy-start.11 = (bf16[2,512,512]{2,1,0:T(8,128)(2,1)S(1)}, bf16[2,512,512]{2,1,0:T(8,128)(2,1)}, u32[]{:S(2)}) copy-start(bf16[2,512,512]{2,1,0:T(8,128)(2,1)} %constant.39.clone.refs_5_) | copy-start | bytes 3145732
  161.1 76.2 %collective-permute-start.10 = (f32[3,40,512]{2,1,0:T(8,128)S(1)}, f32[3,40,512]{2,1,0:T(8,128)S(1)}, u32[]{:S(2)}, u32[]{:S(2)}) collective-permute-start(f32[3,40,512]{2,1,0:T(8,128)S(1)} %pad_maximum_fusion.3), channel_id=1, source_target_pairs={{0,8},{8,16},{16,24},{24,0},{1,9},{9,17},{17,25},{25,1},{2,10},{10... | collective-permute-start | bytes 737288 | tf_op jit(solution)/shard_map/ppermute | solution.py:175
  248.8 1.2 copy-start.12

commit v8 on v7

--- a/solution.py
+++ b/solution.py
@@ -761,11 +761,10 @@
     cell_steps = cell_count // LANES
     slot_steps = 8 * slots // LANES
     slot_fields = m2l(sources, block_class, table, ops, cell_steps, slot_steps, True, slots)
+    returned = along_gx(*along_gy(slot_fields[:3], slot_fields[3:6]), slot_fields[6:])
+    parts.append(send(after(carved[1], parts[1], adds[0], *returned)))
     tables = fourier_tables(n_gx * width)
     spectrum = fourier(parts[0], spans[0][1], adds, tables, 0, planes, None, own_rows)
-    crossed = along_gy(slot_fields[:3], slot_fields[3:6])
-    parts.append(send(after(carved[1], parts[1], spectrum, *crossed)))
-    returned = along_gx(*crossed, slot_fields[6:])
     own_fields = m2l(sources, block_class, table, ops, 0, cell_steps, False, slots)
     spectrum = fourier(parts[1], spans[1][1], adds, tables, spans[1][0], planes, spectrum, own_rows)
     own_fields = after(own_fields, spectrum)

time: 262 us -> 251 us (0.958)
  waiting for transfers between devices: 32.2 us -> 22.3 us
    ppermute x8, waiting for transfers between devices: 23 us -> 13 us  [shift(): lax.ppermute(value, axis, [(i, (i + by) % count) for i in range(count)])]
    unnamed x49 -> x63, local copies, waits for them, and re-layouts: 22.6 us -> 25.8 us
    slice x6, local copies, waits for them, and re-layouts: 2.86 us -> 0.07 us  [along_gx(): right = shift(jnp.stack([down[2], mid[1], up[2]]), 'gx', 1)]
  transfers between devices with their start and end apart: 14 -> 14, of which waited for: 5 -> 6; matrix products, arithmetic and copies ran while one was open for 3% -> 2% of each run, Pallas kernels for 62% -> 65%
where the time goes in v8:
time: 251 us; the launch traced here: 249 us
  Pallas kernels  173 us (69%)
  starting transfers between devices  26.6 us (11%)
  local copies, waits for them, and re-layouts  25.9 us (10%)
  waiting for transfers between devices  22.3 us (9%)
    pallas_call x2, Pallas kernels, m2l(): pl.pallas_call(functools.partial(m2l_kernel, first=first, turned=turned),...  80.2 us
    unnamed x63, local copies, waits for them, and re-layouts  25.8 us
    pallas_call x3, Pallas kernels, fourier(): pl.pallas_call(functools.partial(fourier_kernel, sources=sources), grid=(...  25.5 us
    pallas_call x1, Pallas kernels, deposit(): pl.pallas_call(deposit_kernel, out_shape=(jax.ShapeDtypeStruct((rows, LAN...  21.4 us
    all_to_all x3, starting transfers between devices, send(): return lax.all_to_all(part, 'gx', 0, 0, tiled=True)  16.9 us
    ppermute x8, waiting for transfers between devices, shift(): lax.ppermute(value, axis, [(i, (i + by) % count) for i in range(count)])  13 us
    pallas_call x1, Pallas kernels, add_back(): pl.pallas_call(add_back_kernel, out_shape=jax.ShapeDtypeStruct((coef_coun...  11.2 us
    pallas_call x1, Pallas kernels, pack(): pl.pallas_call(pack_kernel, grid=(1,), out_shape=tuple((jax.ShapeDtypeStr...  9.99 us
  transfers between devices with their start and end apart: 14, of which 6 were waited for; matrix products, arithmetic and copies ran while one was open for 2% of the time, Pallas kernels for 65%

profile of v8, /device:TPU:8, one launch (start us, length us, event | category | flops | bytes accessed | tf_op | source)
XLA Modules:
  0.0 249.0 jit_solution(7554219877911216294)
XLA Ops:
  0.6 1.1 copy-done.13
  1.7 0.7 copy-done.26
  2.4 2.4 first_part.1
  4.8 5.3 %all-to-all-start = ((f32[4,296,256]{2,1,0:T(8,128)}), f32[4,296,256]{2,1,0:T(8,128)S(1)}, u32[]{:S(2)}, u32[]{:S(2)}) async-start(f32[4,296,256]{2,1,0:T(8,128)} %first_part.1), calls=%async_computation | async-start | bytes 2424832 | tf_op jit(solution)/shard_map/all_to_all | solution.py:716
  10.2 0.0 copy-start.29
  10.2 0.0 copy-start.30
  10.2 3.3 %own_table.1.refs_8_ = f32[9216,128]{1,0:T(8,128)S(1)} custom-call(f32[40,4096]{1,0:T(8,128)S(1)} %pad.4.cells_ref), custom_call_target="tpu_custom_call" | custom-call | flops 1000000 | bytes 12000000 | tf_op jit(solution)/shard_map/own_table/pallas_call | solution.py:59
  13.6 10.0 %pack.1 = (f32[3,40,512]{2,1,0:T(8,128)S(1)}, f32[3,40,512]{2,1,0:T(8,128)S(1)}, f32[2,40,512]{2,1,0:T(8,128)S(1)}) custom-call(s32[8,512]{1,0:T(8,128)S(1)} %bitcast.16, s32[8]{0:T(128)S(1)} %bitcast.19, f32[9216,1,128]{2,1,0:T(1,128)S(1)} %bitcast.11), custom_call_target="tpu_custom_call" | custom-call | flops 1000000 | bytes 25000000 | tf_op jit(solution)/shard_map/pack/pallas_call | solution.py:154
  23.6 2.2 copy-done
  25.7 1.3 collective-permute-start
  27.1 0.0 collective-permute-start.1
  27.1 0.2 fusion.2.packed_ref
  27.3 7.4 %order.1.source_ref = s32[512,128]{1,0:T(8,128)S(1)} custom-call(s32[512,128]{1,0:T(8,128)S(1)} %fusion.2.packed_ref), custom_call_target="tpu_custom_call" | custom-call | flops 1000000 | bytes 20000000 | tf_op jit(solution)/shard_map/order/pallas_call | solution.py:207
  34.7 0.0 copy-start.15
  34.7 0.0 collective-permute-done.refs_0_
  34.7 0.3 collective-permute-done.1.refs_1_
  35.0 0.1 collective-permute-start.2
  35.2 2.0 collective-permute-start.3
  37.2 2.2 carve.2
  39.4 2.0 copy-done.6
  41.5 5.3 %copy.16 = f32[189,35,35]{1,2,0:T(8,128)} copy(f32[189,35,35]{0,2,1:T(8,128)} %param.17) | data formatting | bytes 1852200 | tf_op args[6]
  46.7 4.7 %split.1.ops_ref = f32[189,40,128]{2,1,0:T(8,128)S(1)} custom-call(f32[189,35,35]{2,1,0:T(8,128)} %bitcast.21), custom_call_target="tpu_custom_call" | custom-call | flops 1000000 | bytes 12000000 | tf_op jit(solution)/shard_map/split/pallas_call | solution.py:234
  51.4 1.8 copy-done.3
  53.3 0.0 collective-permute-done.2.refs_2_
  53.3 0.0 collective-permute-done.3.refs_3_
  53.3 0.0 all-to-all-done.part_ref.refs_0_
  53.3 6.9 %all-to-all-start.1 = ((f32[4,1024,256]{2,1,0:T(8,128)}), f32[4,1024,256]{2,1,0:T(8,128)}, u32[]{:S(2)}, u32[]{:S(2)}) async-start(f32[4,1024,256]{2,1,0:T(8,128)} %bitcast.14), calls=%async_computation.1 | async-start | bytes 8388608 | tf_op jit(solution)/shard_map/all_to_all | solution.py:716
  60.2 1.3 sift.1
  61.5 0.1 collective-permute-start.4
  61.6 1.2 collective-permute-done.4.refs_5_
  62.8 0.7 collective-permute-start.5
  63.5 3.6 %collective-permute-done.5.refs_6_ = f32[128,128]{1,0:T(8,128)S(1)} collective-permute-done((f32[128,128]{1,0:T(8,128)S(1)}, f32[128,128]{1,0:T(8,128)S(1)}, u32[]{:S(2)}, u32[]{:S(2)}) %collective-permute-start.5) | collective-permute-done | bytes 65568 | tf_op jit(solution)/shard_map/ppermute | solution.py:756
  67.1 0.6 collective-permute-start.6
  67.7 4.5 %collective-permute-done.6.refs_7_ = f32[256,128]{1,0:T(8,128)S(1)} collective-permute-done((f32[256,128]{1,0:T(8,128)S(1)}, f32[256,128]{1,0:T(8,128)S(1)}, u32[]{:S(2)}, u32[]{:S(2)}) %collective-permute-start.6) | collective-permute-done | bytes 131104 | tf_op jit(solution)/shard_map/ppermute | solution.py:756
  72.1 2.3 copy-done.1
  74.5 1.3 whole_table.1
  75.8 2.2 copy-done.2
  78.0 40.1 %m2l_slots.1 = f32[8,40,512]{2,1,0:T(8,128)S(1)} custom-call(s32[512,128]{1,0:T(8,128)S(1)} %order.1.source_ref, s32[1024]{0:T(1024)S(1)} %copy-done.27, f32[9216,1,128]{2,1,0:T(1,128)} %bitcast.12, f32[189,40,128]{2,1,0:T(8,128)S(1)} %copy-done.4), custom_call_target="tpu_custom_call" | custom-call | flops 1000000 | bytes 150000000 | tf_op jit(solution)/shard_map/m2l_slots/pallas_call | solution.py:302
  118.2 0.1 collective-permute-start.8
  118.2 2.6 %collective-permute-start.7 = (f32[3,40,512]{2,1,0:T(8,128)S(1)}, f32[3,40,512]{2,1,0:T(8,128)S(1)}, u32[]{:S(2)}, u32[]{:S(2)}) collective-permute-start(f32[3,40,512]{2,1,0:T(8,128)S(1)} %get-tuple-element.35), channel_id=1, source_target_pairs={{0,7},{1,0},{2,1},{3,2},{4,3},{5,4},{6,5},{7,6},{8,15},{9,8},{10,9... | collective-permute-start | bytes 737288 | tf_op jit(solution)/shard_map/ppermute | solution.py:175
  120.9 5.3 %collective-permute-done.8.refs_1_ = f32[3,40,512]{2,1,0:T(8,128)S(1)} collective-permute-done((f32[3,40,512]{2,1,0:T(8,128)S(1)}, f32[3,40,512]{2,1,0:T(8,128)S(1)}, u32[]{:S(2)}, u32[]{:S(2)}) %collective-permute-start.8) | collective-permute-done | bytes 245792 | tf_op jit(solution)/shard_map/ppermute | solution.py:175
  126.2 0.0 collective-permute-done.7.refs_0_
  126.2 0.1 collective-permute-start.9
  126.3 2.2 collective-permute-start.10
  128.6 1.9 carve.3
  130.5 1.6 copy-done.7
  132.1 21.4 %deposit.1 = (f32[4104,128]{1,0:T(8,128)S(1)}, f32[4104,128]{1,0:T(8,128)S(1)}, f32[4104,128]{1,0:T(8,128)}, f32[4104,128]{1,0:T(8,128)}) custom-call(s32[128,128]{1,0:T(8,128)S(1)} %get-tuple-element.23.code_ref, f32[128,128]{1,0:T(8,128)S(1)} %get-tuple-element.24.value_ref, s32[16,128]{1,0:T(8,128)S(1)} %get-tuple-element.25.bound_ref), custom_call_target="tpu_custom_call" | custom-call | flops 1000000 | bytes 40000000 | tf_op jit(solution)/shard_map/deposit/pallas_call | solution.py:562
  153.5 1.4 copy-done.5
  154.9 7.4 %collective-permute-done.9.refs_2_ = f32[3,40,512]{2,1,0:T(8,128)S(1)} collective-permute-done((f32[3,40,512]{2,1,0:T(8,128)S(1)}, f32[3,40,512]{2,1,0:T(8,128)S(1)}, u32[]{:S(2)}, u32[]{:S(2)}) %collective-permute-start.9) | collective-permute-done | bytes 245792 | tf_op jit(solution)/shard_map/ppermute | solution.py:175
  162.4 0.7 copy-done.21
  163.1 0.0 collective-permute-done.10.refs_3_
  163.1 0.7 copy-done.23
  163.8 0.0 all-to-all-done.1.refs_0_
  163.8 4.6 %all-to-all-start.2 = ((f32[4,768,256]{2,1,0:T(8,128)}), f32[4,768,256]{2,1,0:T(8,128)}, u32[]{:S(2)}, u32[]{:S(2)}) async-start(f32[4,768,256]{2,1,0:T(8,128)} %bitcast.15), calls=%async_computation.2 | async-start | bytes 6291456 | tf_op jit(solution)/shard_map/all_to_all | solution.py:716
  168.4 0.0 copy-start.8
  168.4 1.2 copy-done.8
  169.6 1.2 copy-done.10
  170.9 4.6 %fourier.3.refs_7_ = f32[2,8,256,1024]{3,2,1,0:T(8,128)} custom-call(f32[4,296,256]{2,1,0:T(8,128)S(1)} %all-to-all-done.part_ref.refs_0_, f32[4104,128]{1,0:T(8,128)S(1)} %get-tuple-element.26.refs_1_, f32[4104,128]{1,0:T(8,128)} %copy-done.5, f32[4104,128]{1,0:T(8,128)} %get-tuple-element.28.refs_3_, f32[4104,128]{1,0:T(8,128)} %get-tuple-element.29.refs_4_, ...), custom_call_target="tpu_custom_call" | custom-call | flops 1000000 | bytes 10000000 | tf_op jit(solution)/shard_map/fourier/pallas_call | solution.py:677
  175.5 40.1 %m2l_cells.1.own_ref = f32[4096,128]{1,0:T(8,128)S(1)} custom-call(s32[512,128]{1,0:T(8,128)S(1)} %copy-done.16, s32[1024]{0:T(1024)S(1)} %copy-done.27, f32[9216,1,128]{2,1,0:T(1,128)} %bitcast.13, f32[189,40,128]{2,1,0:T(8,128)} %copy-done.3), custom_call_target="tpu_custom_call" | custom-call | flops 1000000 | bytes 150000000 | tf_op jit(solution)/shard_map/m2l_cells/pallas_call | solution.py:302
  215.6 11.6 %fourier.4.refs_7_ = f32[2,8,256,1024]{3,2,1,0:T(8,128)} custom-call(f32[4,1024,256]{2,1,0:T(8,128)} %all-to-all-done.1.refs_0_, f32[4104,128]{1,0:T(8,128)S(1)} %get-tuple-element.26.refs_1_, f32[4104,128]{1,0:T(8,128)} %copy-done.5, f32[4104,128]{1,0:T(8,128)} %get-tuple-element.28.refs_3_, ...), custom_call_target="tpu_custom_call", output_to_operand_aliasing={{}: (7, {})} | custom-call | flops 1000000 | bytes 40000000 | tf_op jit(solution)/shard_map/fourier/pallas_call | solution.py:677
  227.3 11.2 %add_back.1 = f32[35,4096]{1,0:T(8,128)} custom-call(s32[8,512]{1,0:T(8,128)S(1)} %bitcast.17, s32[8]{0:T(128)S(1)} %bitcast.20, f32[4096,128]{1,0:T(8,128)S(1)} %m2l_cells.1.own_ref, f32[3,40,512]{2,1,0:T(8,128)S(1)} %copy-done.20, f32[3,40,512]{2,1,0:T(8,128)S(1)} %copy-done.18, f32[3,40,512]{2,1,0:T(8,128)S(1)} %copy-done.22, f32[3,40,512]{2,1,0:T(8,128)S(1)} %copy-done.24), custom_call_target="tpu_custom_call" | custom-call | flops 1000000 | bytes 30000000 | tf_op jit(solution)/shard_map/add_back/pallas_call | solution.py:356
  238.5 0.0 all-to-all-done.2.refs_0_
  238.5 1.2 copy-done.12
  239.7 9.3 %fourier.5 = f32[2,8,256,1024]{3,2,1,0:T(8,128)} custom-call(f32[4,768,256]{2,1,0:T(8,128)} %all-to-all-done.2.refs_0_, f32[4104,128]{1,0:T(8,128)S(1)} %get-tuple-element.26.refs_1_, f32[4104,128]{1,0:T(8,128)} %copy-done.5, f32[4104,128]{1,0:T(8,128)} %get-tuple-element.28.refs_3_, ...), custom_call_target="tpu_custom_call", output_to_operand_aliasing={{}: (7, {})} | custom-call | flops 1000000 | bytes 30000000 | tf_op jit(solution)/shard_map/fourier/pallas_call | solution.py:677
  (58 shorter events, 0.3 us)
Async XLA Ops:
  0.6 1.1 copy-start.13
  1.7 0.7 copy-start.26
  2.4 7.7 %copy-start.14 = (f32[35,4096]{1,0:T(8,128)S(1)}, f32[35,4096]{1,0:T(8,128)}, u32[]{:S(2)}) copy-start(f32[35,4096]{1,0:T(8,128)} %cells_ref.1) | copy-start | bytes 1720324
  4.8 48.5 %all-to-all-start = ((f32[4,296,256]{2,1,0:T(8,128)}), f32[4,296,256]{2,1,0:T(8,128)S(1)}, u32[]{:S(2)}, u32[]{:S(2)}) async-start(f32[4,296,256]{2,1,0:T(8,128)} %first_part.1), calls=%async_computation | async-start | bytes 2424832 | tf_op jit(solution)/shard_map/all_to_all | solution.py:716
  10.1 3.4 %copy-start.25 = (s32[1,8,512]{2,1,0:T(8,128)S(1)}, s32[1,8,512]{2,1,0:T(8,128)}, u32[]{:S(2)}) copy-start(s32[1,8,512]{2,1,0:T(8,128)} %param.12) | copy-start | bytes 49156
  10.1 3.4 %copy-start.28 = (s32[1,8]{1,0:T(1,128)S(1)}, s32[1,8]{1,0:T(1,128)}, u32[]{:S(2)}) copy-start(s32[1,8]{1,0:T(1,128)} %param.13) | copy-start | bytes 100
  10.2 16.9 %copy-start.29 = (s32[65536]{0:T(1024)S(1)}, s32[65536]{0:T(1024)}, u32[]{:S(2)}) copy-start(s32[65536]{0:T(1024)} %param.14) | copy-start | bytes 786436
  10.2 16.9 %copy-start.30 = (s32[65536]{0:T(1024)S(1)}, s32[65536]{0:T(1024)}, u32[]{:S(2)}) copy-start(s32[65536]{0:T(1024)} %param.15) | copy-start | bytes 786436
  23.6 2.2 copy-start
  25.7 9.0 %collective-permute-start = (f32[3,40,512]{2,1,0:T(8,128)S(1)}, f32[3,40,512]{2,1,0:T(8,128)S(1)}, u32[]{:S(2)}, u32[]{:S(2)}) collective-permute-start(f32[3,40,512]{2,1,0:T(8,128)S(1)} %get-tuple-element.17), channel_id=1, source_target_pairs={{0,7},{1,0},{2,1},{3,2},{4,3},{5,4},{6,5},{7,6},{8,15},{9,8},{10,9... | collective-permute-start | bytes 737288 | tf_op jit(solution)/shard_map/ppermute | solution.py:175
  27.1 7.9 %collective-permute-start.1 = (f32[3,40,512]{2,1,0:T(8,128)S(1)}, f32[3,40,512]{2,1,0:T(8,128)S(1)}, u32[]{:S(2)}, u32[]{:S(2)}) collective-permute-start(f32[3,40,512]{2,1,0:T(8,128)S(1)} %get-tuple-element.18), channel_id=1, source_target_pairs={{0,1},{1,2},{2,3},{3,4},{4,5},{5,6},{6,7},{7,0},{8,9},{9,10},{10,1... | collective-permute-start | bytes 737288 | tf_op jit(solution)/shard_map/ppermute | solution.py:175
  34.7 43.3 %copy-start.15 = (s32[512,128]{1,0:T(8,128)}, s32[512,128]{1,0:T(8,128)S(1)}, u32[]{:S(2)}) copy-start(s32[512,128]{1,0:T(8,128)S(1)} %order.1.source_ref) | copy-start | bytes 786436
  35.0 18.2 %collective-permute-start.2 = (f32[3,40,512]{2,1,0:T(8,128)S(1)}, f32[3,40,512]{2,1,0:T(8,128)S(1)}, u32[]{:S(2)}, u32[]{:S(2)}) collective-permute-start(f32[3,40,512]{2,1,0:T(8,128)S(1)} %pad_maximum_fusion), channel_id=1, source_target_pairs={{0,24},{8,0},{16,8},{24,16},{1,25},{9,1},{17,9},{25,17},{2,26},{10... | collective-permute-start | bytes 737288 | tf_op jit(solution)/shard_map/ppermute | solution.py:175
  35.2 18.1 %collective-permute-start.3 = (f32[3,40,512]{2,1,0:T(8,128)S(1)}, f32[3,40,512]{2,1,0:T(8,128)S(1)}, u32[]{:S(2)}, u32[]{:S(2)}) collective-permute-start(f32[3,40,512]{2,1,0:T(8,128)S(1)} %pad_maximum_fusion.1), channel_id=1, source_target_pairs={{0,8},{8,16},{16,24},{24,0},{1,9},{9,17},{17,25},{25,1},{2,10},{10... | collective-permute-start | bytes 737288 | tf_op jit(solution)/shard_map/ppermute | solution.py:175
  39.4 2.0 copy-start.6
  51.4 1.9 copy-start.3
  53.3 110.5 %all-to-all-start.1 = ((f32[4,1024,256]{2,1,0:T(8,128)}), f32[4,1024,256]{2,1,0:T(8,128)}, u32[]{:S(2)}, u32[]{:S(2)}) async-start(f32[4,1024,256]{2,1,0:T(8,128)} %bitcast.14), calls=%async_computation.1 | async-start | bytes 8388608 | tf_op jit(solution)/shard_map/all_to_all | solution.py:716
  61.5 1.3 collective-permute-start.4
  62.8 4.3 %collective-permute-start.5 = (f32[128,128]{1,0:T(8,128)S(1)}, f32[128,128]{1,0:T(8,128)S(1)}, u32[]{:S(2)}, u32[]{:S(2)}) collective-permute-start(f32[128,128]{1,0:T(8,128)S(1)} %pad_maximum_fusion.5), channel_id=1, source_target_pairs={{0,2},{1,3},{2,0},{3,1},{4,6},{5,7},{6,4},{7,5},{8,10},{9,11},{10,... | collective-permute-start | bytes 196616 | tf_op jit(solution)/shard_map/ppermute | solution.py:756
  67.1 10.9 %copy-start.27 = (s32[1024]{0:T(1024)S(1)}, s32[1024]{0:T(1024)}, u32[]{:S(2)}) copy-start(s32[1024]{0:T(1024)} %class_ref.3) | copy-start | bytes 12292
  67.1 5.0 %collective-permute-start.6 = (f32[256,128]{1,0:T(8,128)S(1)}, f32[256,128]{1,0:T(8,128)S(1)}, u32[]{:S(2)}, u32[]{:S(2)}) collective-permute-start(f32[256,128]{1,0:T(8,128)S(1)} %pad_maximum_fusion.4), channel_id=1, source_target_pairs={{0,4},{1,5},{2,6},{3,7},{4,0},{5,1},{6,2},{7,3},{8,12},{9,13},{10,... | collective-permute-start | bytes 393224 | tf_op jit(solution)/shard_map/ppermute | solution.py:756
  72.1 2.3 copy-start.1
  74.5 3.5 %copy-start.4 = (f32[189,40,128]{2,1,0:T(8,128)S(1)}, f32[189,40,128]{2,1,0:T(8,128)}, u32[]{:S(2)}) copy-start(f32[189,40,128]{2,1,0:T(8,128)} %copy-done.3) | copy-start | bytes 11612164
  75.8 2.2 copy-start.2
  118.2 8.0 %collective-permute-start.8 = (f32[3,40,512]{2,1,0:T(8,128)S(1)}, f32[3,40,512]{2,1,0:T(8,128)S(1)}, u32[]{:S(2)}, u32[]{:S(2)}) collective-permute-start(f32[3,40,512]{2,1,0:T(8,128)S(1)} %get-tuple-element.34), channel_id=1, source_target_pairs={{0,1},{1,2},{2,3},{3,4},{4,5},{5,6},{6,7},{7,0},{8,9},{9,10},{10,1... | collective-permute-start | bytes 737288 | tf_op jit(solution)/shard_map/ppermute | solution.py:175
  118.2 8.0 %collective-permute-start.7 = (f32[3,40,512]{2,1,0:T(8,128)S(1)}, f32[3,40,512]{2,1,0:T(8,128)S(1)}, u32[]{:S(2)}, u32[]{:S(2)}) collective-permute-start(f32[3,40,512]{2,1,0:T(8,128)S(1)} %get-tuple-element.35), channel_id=1, source_target_pairs={{0,7},{1,0},{2,1},{3,2},{4,3},{5,4},{6,5},{7,6},{8,15},{9,8},{10,9... | collective-permute-start | bytes 737288 | tf_op jit(solution)/shard_map/ppermute | solution.py:175
  126.2 4.3 %copy-start.17 = (f32[3,40,512]{2,1,0:T(8,128)}, f32[3,40,512]{2,1,0:T(8,128)S(1)}, u32[]{:S(2)}) copy-start(f32[3,40,512]{2,1,0:T(8,128)S(1)} %collective-permute-done.8.refs_1_) | copy-start | bytes 737284
  126.2 4.3 %copy-start.19 = (f32[3,40,512]{2,1,0:T(8,128)}, f32[3,40,512]{2,1,0:T(8,128)S(1)}, u32[]{:S(2)}) copy-start(f32[3,40,512]{2,1,0:T(8,128)S(1)} %collective-permute-done.7.refs_0_) | copy-start | bytes 737284
  126.2 36.1 %collective-permute-start.9 = (f32[3,40,512]{2,1,0:T(8,128)S(1)}, f32[3,40,512]{2,1,0:T(8,128)S(1)}, u32[]{:S(2)}, u32[]{:S(2)}) collective-permute-start(f32[3,40,512]{2,1,0:T(8,128)S(1)} %pad_maximum_fusion.2), channel_id=1, source_target_pairs={{0,24},{8,0},{16,8},{24,16},{1,25},{9,1},{17,9},{25,17},{2,26},{10... | collective-permute-start | bytes 737288 | tf_op jit(solution)/shard_map/ppermute | solution.py:175
  126.3 36.7 %collective-permute-start.10 = (f32[3,40,512]{2,1,0:T(8,128)S(1)}, f32[3,40,512]{2,1,0:T(8,128)S(1)}, u32[]{:S(2)}, u32[]{:S(2)}) collective-permute-start(f32[3,40,512]{2,1,0:T(8,128)S(1)} %pad_maximum_fusion.3), channel_id=1, source_target_pairs={{0,8},{8,16},{16,24},{24,0},{1,9},{9,17},{17,25},{25,1},{2,10},{10... | collective-permute-start | bytes 737288 | tf_op jit(solution)/shard_map/ppermute | solution.py:175
  130.5 1.6 copy-start.7
  153.5 1.4 copy-start.5
  162.4 0.7 copy-start.21
  163.1 0.7 copy-start.23
  163.8 74.7 %all-to-all-start.2 = ((f32[4,768,256]{2,1,0:T(8,128)}), f32[4,768,256]{2,1,0:T(8,128)}, u32[]{:S(2)}, u32[]{:S(2)}) async-start(f32[4,768,256]{2,1,0:T(8,128)} %bitcast.15), calls=%async_computation.2 | async-start | bytes 6291456 | tf_op jit(solution)/shard_map/all_to_all | solution.py:716
  168.4 1.2 copy-start.8
  169.6 1.2 copy-start.10
  170.9 4.6 %copy-start.16 = (s32[512,128]{1,0:T(8,128)S(1)}, s32[512,128]{1,0:T(8,128)}, u32[]{:S(2)}) copy-start(s32[512,128]{1,0:T(8,128)} %copy-done.15) | copy-start | bytes 786436
  175.5 40.1 %copy-start.9 = (bf16[2,512,512]{2,1,0:T(8,128)(2,1)S(1)}, bf16[2,512,512]{2,1,0:T(8,128)(2,1)}, u32[]{:S(2)}) copy-start(bf16[2,512,512]{2,1,0:T(8,128)(2,1)} %constant.40.clone.refs_6_) | copy-start | bytes 3145732
  175.5 40.1 %copy-start.11 = (bf16[2,512,512]{2,1,0:T(8,128)(2,1)S(1)}, bf16[2,512,512]{2,1,0:T(8,128)(2,1)}, u32[]{:S(2)}) copy-start(bf16[2,512,512]{2,1,0:T(8,128)(2,1)} %constant.39.clone.refs_5_) | copy-start | bytes 3145732
  215.6 11.7 %copy-start.18 = (f32[3,40,512]{2,1,0:T(8,128)S(1)}, f32[3,40,512]{2,1,0:T(8,128)}, u32[]{:S(2)}) copy-start(f32[3,40,512]{2,1,0:T(8,128)} %copy-done.17) | copy-start | bytes 737284
  215.6 11.7 %copy-start.20 = (f32[3,40,512]{2,1,0:T(8,128)S(1)}, f32[3,40,512]{2,1,0:T(8,128)}, u32[]{:S(2)}) copy-start(f32[3,40,512]{2,1,0:T(8,128)} %copy-done.19) | copy-start | bytes 737284
  215.6 11.7 %copy-start.22 = (f32[3,40,512]{2,1,0:T(8,128)S(1)}, f32[3,40,512]{2,1,0:T(8,128)}, u32[]{:S(2)}) copy-start(f32[3,40,512]{2,1,0:T(8,128)} %copy-done.21) | copy-start | bytes 737284
  215.6 11.7 %copy-start.24 = (f32[3,40,512]{2,1,0:T(8,128)S(1)}, f32[3,40,512]{2,1,0:T(8,128)}, u32[]{:S(2)}) copy-start(f32[3,40,512]{2,1,0:T(8,128)} %copy-done.23) | copy-start | bytes 737284
  238.5 1.2 copy-start.12

commit v9 on v8

--- a/solution.py
+++ b/solution.py
@@ -755,13 +755,14 @@
         held = jnp.concatenate(tops, axis=0) if bit else top_own
         tops.append(lax.ppermute(held, "gy", [(i, i ^ (1 << bit)) for i in range(n_gy)]))
 
-    parts.append(send(after(carved[0], parts[0], ops, *arrived)))
+    parts.append(send(after(carved[0], parts[0], *arrived)))
     adds = deposit(codes, amounts, bounds, add_rows + 8, n_gx)
     table = whole_table(table, arrived, tops)
     cell_steps = cell_count // LANES
     slot_steps = 8 * slots // LANES
     slot_fields = m2l(sources, block_class, table, ops, cell_steps, slot_steps, True, slots)
-    returned = along_gx(*along_gy(slot_fields[:3], slot_fields[3:6]), slot_fields[6:])
+    mid = after(slot_fields[6:], carved[1])
+    returned = along_gx(*along_gy(slot_fields[:3], slot_fields[3:6]), mid)
     parts.append(send(after(carved[1], parts[1], adds[0], *returned)))
     tables = fourier_tables(n_gx * width)
     spectrum = fourier(parts[0], spans[0][1], adds, tables, 0, planes, None, own_rows)

time: 251 us -> 248 us (0.988)
  local copies, waits for them, and re-layouts: 25.9 us -> 21.9 us
    ppermute x3, waiting for transfers between devices: 9.26 us -> 4.46 us  [on_device(): lax.ppermute(held, 'gy', [(i, i ^ 1 << bit) for i in range(n_gy)])]
    unnamed x63, local copies, waits for them, and re-layouts: 25.8 us -> 21.7 us
    ppermute x8, waiting for transfers between devices: 13 us -> 16.3 us  [shift(): lax.ppermute(value, axis, [(i, (i + by) % count) for i in range(count)])]
  transfers between devices with their start and end apart: 14 -> 14, of which waited for: 6 -> 8; matrix products, arithmetic and copies ran while one was open for 2% -> 3% of each run, Pallas kernels for 65% -> 66%
where the time goes in v9:
time: 248 us; the launch traced here: 245 us
  Pallas kernels  173 us (70%)
  starting transfers between devices  27.6 us (11%)
  local copies, waits for them, and re-layouts  21.9 us (9%)
  waiting for transfers between devices  20.8 us (8%)
    pallas_call x2, Pallas kernels, m2l(): pl.pallas_call(functools.partial(m2l_kernel, first=first, turned=turned),...  80.2 us
    pallas_call x3, Pallas kernels, fourier(): pl.pallas_call(functools.partial(fourier_kernel, sources=sources), grid=(...  25.5 us
    unnamed x63, local copies, waits for them, and re-layouts  21.7 us
    pallas_call x1, Pallas kernels, deposit(): pl.pallas_call(deposit_kernel, out_shape=(jax.ShapeDtypeStruct((rows, LAN...  21.4 us
    all_to_all x3, starting transfers between devices, send(): return lax.all_to_all(part, 'gx', 0, 0, tiled=True)  16.7 us
    ppermute x8, waiting for transfers between devices, shift(): lax.ppermute(value, axis, [(i, (i + by) % count) for i in range(count)])  16.3 us
    pallas_call x1, Pallas kernels, add_back(): pl.pallas_call(add_back_kernel, out_shape=jax.ShapeDtypeStruct((coef_coun...  11.2 us
    pallas_call x1, Pallas kernels, pack(): pl.pallas_call(pack_kernel, grid=(1,), out_shape=tuple((jax.ShapeDtypeStr...  9.99 us
  transfers between devices with their start and end apart: 14, of which 8 were waited for; matrix products, arithmetic and copies ran while one was open for 3% of the time, Pallas kernels for 66%

profile of v9, /device:TPU:8, one launch (start us, length us, event | category | flops | bytes accessed | tf_op | source)
XLA Modules:
  0.0 245.3 jit_solution(1950540086051820005)
XLA Ops:
  0.6 1.1 copy-done.11
  1.7 0.7 copy-done.24
  2.4 2.4 first_part.1
  4.8 5.3 %all-to-all-start = ((f32[4,296,256]{2,1,0:T(8,128)}), f32[4,296,256]{2,1,0:T(8,128)S(1)}, u32[]{:S(2)}, u32[]{:S(2)}) async-start(f32[4,296,256]{2,1,0:T(8,128)} %first_part.1), calls=%async_computation | async-start | bytes 2424832 | tf_op jit(solution)/shard_map/all_to_all | solution.py:716
  10.2 0.0 copy-start.27
  10.2 3.3 %own_table.1.refs_8_ = f32[9216,128]{1,0:T(8,128)S(1)} custom-call(f32[40,4096]{1,0:T(8,128)S(1)} %pad.4.cells_ref), custom_call_target="tpu_custom_call" | custom-call | flops 1000000 | bytes 12000000 | tf_op jit(solution)/shard_map/own_table/pallas_call | solution.py:59
  13.6 0.0 copy-start.28
  13.6 10.0 %pack.1 = (f32[3,40,512]{2,1,0:T(8,128)S(1)}, f32[3,40,512]{2,1,0:T(8,128)S(1)}, f32[2,40,512]{2,1,0:T(8,128)S(1)}) custom-call(s32[8,512]{1,0:T(8,128)S(1)} %bitcast.18, s32[8]{0:T(128)S(1)} %bitcast.21, f32[9216,1,128]{2,1,0:T(1,128)S(1)} %bitcast.11), custom_call_target="tpu_custom_call" | custom-call | flops 1000000 | bytes 25000000 | tf_op jit(solution)/shard_map/pack/pallas_call | solution.py:154
  23.6 2.2 copy-done
  25.8 1.3 collective-permute-start
  27.1 0.0 collective-permute-start.1
  27.1 0.0 copy-done.28
  27.1 0.2 fusion.2.packed_ref
  27.3 7.4 %order.1.source_ref = s32[512,128]{1,0:T(8,128)S(1)} custom-call(s32[512,128]{1,0:T(8,128)S(1)} %fusion.2.packed_ref), custom_call_target="tpu_custom_call" | custom-call | flops 1000000 | bytes 20000000 | tf_op jit(solution)/shard_map/order/pallas_call | solution.py:207
  34.7 0.0 copy-start.13
  34.7 0.0 collective-permute-done.refs_0_
  34.8 0.3 collective-permute-done.1.refs_1_
  35.1 0.1 collective-permute-start.2
  35.2 2.0 collective-permute-start.3
  37.2 2.2 carve.2
  39.4 2.1 copy-done.4
  41.5 1.9 collective-permute-done.2.refs_2_
  43.4 6.7 %collective-permute-done.3.refs_3_ = f32[3,40,512]{2,1,0:T(8,128)S(1)} collective-permute-done((f32[3,40,512]{2,1,0:T(8,128)S(1)}, f32[3,40,512]{2,1,0:T(8,128)S(1)}, u32[]{:S(2)}, u32[]{:S(2)}) %collective-permute-start.3) | collective-permute-done | bytes 245792 | tf_op jit(solution)/shard_map/ppermute | solution.py:175
  50.1 0.0 all-to-all-done.part_ref.refs_0_
  50.1 5.3 %all-to-all-start.1 = ((f32[4,1024,256]{2,1,0:T(8,128)}), f32[4,1024,256]{2,1,0:T(8,128)}, u32[]{:S(2)}, u32[]{:S(2)}) async-start(f32[4,1024,256]{2,1,0:T(8,128)} %bitcast.16), calls=%async_computation.1 | async-start | bytes 8388608 | tf_op jit(solution)/shard_map/all_to_all | solution.py:716
  55.4 1.3 sift.1
  56.8 0.1 collective-permute-start.4
  56.9 1.2 collective-permute-done.4.refs_5_
  58.1 1.0 collective-permute-start.5
  59.1 3.3 %collective-permute-done.5.refs_6_ = f32[128,128]{1,0:T(8,128)S(1)} collective-permute-done((f32[128,128]{1,0:T(8,128)S(1)}, f32[128,128]{1,0:T(8,128)S(1)}, u32[]{:S(2)}, u32[]{:S(2)}) %collective-permute-start.5) | collective-permute-done | bytes 65568 | tf_op jit(solution)/shard_map/ppermute | solution.py:756
  62.3 0.7 pad_maximum_fusion.4
  63.0 1.4 collective-permute-start.6
  64.4 5.4 %copy.16 = f32[189,35,35]{1,2,0:T(8,128)} copy(f32[189,35,35]{0,2,1:T(8,128)} %param.17) | data formatting | bytes 1852200 | tf_op args[6]
  69.7 4.8 %split.1.ops_ref = f32[189,40,128]{2,1,0:T(8,128)S(1)} custom-call(f32[189,35,35]{2,1,0:T(8,128)} %bitcast.23), custom_call_target="tpu_custom_call" | custom-call | flops 1000000 | bytes 12000000 | tf_op jit(solution)/shard_map/split/pallas_call | solution.py:234
  74.6 0.0 copy-start.25
  74.6 0.0 collective-permute-done.6.refs_7_
  74.6 1.3 whole_table.1
  76.0 2.2 copy-done.1
  78.2 40.1 %m2l_slots.1 = f32[8,40,512]{2,1,0:T(8,128)S(1)} custom-call(s32[512,128]{1,0:T(8,128)S(1)} %order.1.source_ref, s32[1024]{0:T(1024)S(1)} %copy-done.25, f32[9216,1,128]{2,1,0:T(1,128)} %bitcast.14, f32[189,40,128]{2,1,0:T(8,128)S(1)} %split.1.ops_ref), custom_call_target="tpu_custom_call" | custom-call | flops 1000000 | bytes 150000000 | tf_op jit(solution)/shard_map/m2l_slots/pallas_call | solution.py:302
  118.3 0.1 collective-permute-start.8
  118.4 1.9 carve.3
  120.3 1.6 copy-done.5
  121.9 2.7 %collective-permute-start.7 = (f32[3,40,512]{2,1,0:T(8,128)S(1)}, f32[3,40,512]{2,1,0:T(8,128)S(1)}, u32[]{:S(2)}, u32[]{:S(2)}) collective-permute-start(f32[3,40,512]{2,1,0:T(8,128)S(1)} %get-tuple-element.35), channel_id=1, source_target_pairs={{0,7},{1,0},{2,1},{3,2},{4,3},{5,4},{6,5},{7,6},{8,15},{9,8},{10,9... | collective-permute-start | bytes 737288 | tf_op jit(solution)/shard_map/ppermute | solution.py:175
  124.6 0.3 collective-permute-done.8.refs_1_
  124.9 3.4 %collective-permute-done.7.refs_0_ = f32[3,40,512]{2,1,0:T(8,128)S(1)} collective-permute-done((f32[3,40,512]{2,1,0:T(8,128)S(1)}, f32[3,40,512]{2,1,0:T(8,128)S(1)}, u32[]{:S(2)}, u32[]{:S(2)}) %collective-permute-start.7) | collective-permute-done | bytes 245792 | tf_op jit(solution)/shard_map/ppermute | solution.py:175
  128.4 0.1 collective-permute-start.9
  128.5 2.2 collective-permute-start.10
  130.7 21.4 %deposit.1 = (f32[4104,128]{1,0:T(8,128)S(1)}, f32[4104,128]{1,0:T(8,128)S(1)}, f32[4104,128]{1,0:T(8,128)}, f32[4104,128]{1,0:T(8,128)}) custom-call(s32[128,128]{1,0:T(8,128)S(1)} %get-tuple-element.24.code_ref, f32[128,128]{1,0:T(8,128)S(1)} %get-tuple-element.25.value_ref, s32[16,128]{1,0:T(8,128)S(1)} %get-tuple-element.26.bound_ref), custom_call_target="tpu_custom_call" | custom-call | flops 1000000 | bytes 40000000 | tf_op jit(solution)/shard_map/deposit/pallas_call | solution.py:562
  152.1 1.4 copy-done.3
  153.5 3.8 %collective-permute-done.9.refs_2_ = f32[3,40,512]{2,1,0:T(8,128)S(1)} collective-permute-done((f32[3,40,512]{2,1,0:T(8,128)S(1)}, f32[3,40,512]{2,1,0:T(8,128)S(1)}, u32[]{:S(2)}, u32[]{:S(2)}) %collective-permute-start.9) | collective-permute-done | bytes 245792 | tf_op jit(solution)/shard_map/ppermute | solution.py:175
  157.3 0.7 copy-done.19
  158.0 0.0 collective-permute-done.10.refs_3_
  158.0 0.7 copy-done.21
  158.7 0.0 all-to-all-done.1.refs_0_
  158.7 6.0 %all-to-all-start.2 = ((f32[4,768,256]{2,1,0:T(8,128)}), f32[4,768,256]{2,1,0:T(8,128)}, u32[]{:S(2)}, u32[]{:S(2)}) async-start(f32[4,768,256]{2,1,0:T(8,128)} %bitcast.17), calls=%async_computation.2 | async-start | bytes 6291456 | tf_op jit(solution)/shard_map/all_to_all | solution.py:716
  164.7 1.2 copy-done.6
  165.9 1.2 copy-done.8
  167.2 4.6 %fourier.3.refs_7_ = f32[2,8,256,1024]{3,2,1,0:T(8,128)} custom-call(f32[4,296,256]{2,1,0:T(8,128)S(1)} %all-to-all-done.part_ref.refs_0_, f32[4104,128]{1,0:T(8,128)S(1)} %get-tuple-element.27.refs_1_, f32[4104,128]{1,0:T(8,128)} %copy-done.3, f32[4104,128]{1,0:T(8,128)} %get-tuple-element.29.refs_3_, f32[4104,128]{1,0:T(8,128)} %get-tuple-element.30.refs_4_, ...), custom_call_target="tpu_custom_call" | custom-call | flops 1000000 | bytes 10000000 | tf_op jit(solution)/shard_map/fourier/pallas_call | solution.py:677
  171.8 40.1 %m2l_cells.1.own_ref = f32[4096,128]{1,0:T(8,128)S(1)} custom-call(s32[512,128]{1,0:T(8,128)S(1)} %copy-done.14, s32[1024]{0:T(1024)S(1)} %copy-done.25, f32[9216,1,128]{2,1,0:T(1,128)} %bitcast.15, f32[189,40,128]{2,1,0:T(8,128)} %copy-done.2), custom_call_target="tpu_custom_call" | custom-call | flops 1000000 | bytes 150000000 | tf_op jit(solution)/shard_map/m2l_cells/pallas_call | solution.py:302
  211.9 11.6 %fourier.4.refs_7_ = f32[2,8,256,1024]{3,2,1,0:T(8,128)} custom-call(f32[4,1024,256]{2,1,0:T(8,128)} %all-to-all-done.1.refs_0_, f32[4104,128]{1,0:T(8,128)S(1)} %get-tuple-element.27.refs_1_, f32[4104,128]{1,0:T(8,128)} %copy-done.3, f32[4104,128]{1,0:T(8,128)} %get-tuple-element.29.refs_3_, ...), custom_call_target="tpu_custom_call", output_to_operand_aliasing={{}: (7, {})} | custom-call | flops 1000000 | bytes 40000000 | tf_op jit(solution)/shard_map/fourier/pallas_call | solution.py:677
  223.6 11.2 %add_back.1 = f32[35,4096]{1,0:T(8,128)} custom-call(s32[8,512]{1,0:T(8,128)S(1)} %bitcast.19, s32[8]{0:T(128)S(1)} %bitcast.22, f32[4096,128]{1,0:T(8,128)S(1)} %m2l_cells.1.own_ref, f32[3,40,512]{2,1,0:T(8,128)S(1)} %copy-done.18, f32[3,40,512]{2,1,0:T(8,128)S(1)} %copy-done.16, f32[3,40,512]{2,1,0:T(8,128)S(1)} %copy-done.20, f32[3,40,512]{2,1,0:T(8,128)S(1)} %copy-done.22), custom_call_target="tpu_custom_call" | custom-call | flops 1000000 | bytes 30000000 | tf_op jit(solution)/shard_map/add_back/pallas_call | solution.py:356
  234.8 0.0 all-to-all-done.2.refs_0_
  234.8 1.2 copy-done.10
  236.0 9.3 %fourier.5 = f32[2,8,256,1024]{3,2,1,0:T(8,128)} custom-call(f32[4,768,256]{2,1,0:T(8,128)} %all-to-all-done.2.refs_0_, f32[4104,128]{1,0:T(8,128)S(1)} %get-tuple-element.27.refs_1_, f32[4104,128]{1,0:T(8,128)} %copy-done.3, f32[4104,128]{1,0:T(8,128)} %get-tuple-element.29.refs_3_, ...), custom_call_target="tpu_custom_call", output_to_operand_aliasing={{}: (7, {})} | custom-call | flops 1000000 | bytes 30000000 | tf_op jit(solution)/shard_map/fourier/pallas_call | solution.py:677
  (60 shorter events, 0.3 us)
Async XLA Ops:
  0.6 1.1 copy-start.11
  1.7 0.7 copy-start.24
  2.4 7.7 %copy-start.12 = (f32[35,4096]{1,0:T(8,128)S(1)}, f32[35,4096]{1,0:T(8,128)}, u32[]{:S(2)}) copy-start(f32[35,4096]{1,0:T(8,128)} %cells_ref.1) | copy-start | bytes 1720324
  4.8 45.3 %all-to-all-start = ((f32[4,296,256]{2,1,0:T(8,128)}), f32[4,296,256]{2,1,0:T(8,128)S(1)}, u32[]{:S(2)}, u32[]{:S(2)}) async-start(f32[4,296,256]{2,1,0:T(8,128)} %first_part.1), calls=%async_computation | async-start | bytes 2424832 | tf_op jit(solution)/shard_map/all_to_all | solution.py:716
  10.1 3.4 %copy-start.23 = (s32[1,8,512]{2,1,0:T(8,128)S(1)}, s32[1,8,512]{2,1,0:T(8,128)}, u32[]{:S(2)}) copy-start(s32[1,8,512]{2,1,0:T(8,128)} %param.12) | copy-start | bytes 49156
  10.1 3.4 %copy-start.26 = (s32[1,8]{1,0:T(1,128)S(1)}, s32[1,8]{1,0:T(1,128)}, u32[]{:S(2)}) copy-start(s32[1,8]{1,0:T(1,128)} %param.13) | copy-start | bytes 100
  10.2 16.9 %copy-start.27 = (s32[65536]{0:T(1024)S(1)}, s32[65536]{0:T(1024)}, u32[]{:S(2)}) copy-start(s32[65536]{0:T(1024)} %param.14) | copy-start | bytes 786436
  13.6 13.5 %copy-start.28 = (s32[65536]{0:T(1024)S(1)}, s32[65536]{0:T(1024)}, u32[]{:S(2)}) copy-start(s32[65536]{0:T(1024)} %param.15) | copy-start | bytes 786436
  23.6 2.2 copy-start
  25.8 9.0 %collective-permute-start = (f32[3,40,512]{2,1,0:T(8,128)S(1)}, f32[3,40,512]{2,1,0:T(8,128)S(1)}, u32[]{:S(2)}, u32[]{:S(2)}) collective-permute-start(f32[3,40,512]{2,1,0:T(8,128)S(1)} %get-tuple-element.18), channel_id=1, source_target_pairs={{0,7},{1,0},{2,1},{3,2},{4,3},{5,4},{6,5},{7,6},{8,15},{9,8},{10,9... | collective-permute-start | bytes 737288 | tf_op jit(solution)/shard_map/ppermute | solution.py:175
  27.1 7.9 %collective-permute-start.1 = (f32[3,40,512]{2,1,0:T(8,128)S(1)}, f32[3,40,512]{2,1,0:T(8,128)S(1)}, u32[]{:S(2)}, u32[]{:S(2)}) collective-permute-start(f32[3,40,512]{2,1,0:T(8,128)S(1)} %get-tuple-element.19), channel_id=1, source_target_pairs={{0,1},{1,2},{2,3},{3,4},{4,5},{5,6},{6,7},{7,0},{8,9},{9,10},{10,1... | collective-permute-start | bytes 737288 | tf_op jit(solution)/shard_map/ppermute | solution.py:175
  34.7 43.5 %copy-start.13 = (s32[512,128]{1,0:T(8,128)}, s32[512,128]{1,0:T(8,128)S(1)}, u32[]{:S(2)}) copy-start(s32[512,128]{1,0:T(8,128)S(1)} %order.1.source_ref) | copy-start | bytes 786436
  35.1 8.4 %collective-permute-start.2 = (f32[3,40,512]{2,1,0:T(8,128)S(1)}, f32[3,40,512]{2,1,0:T(8,128)S(1)}, u32[]{:S(2)}, u32[]{:S(2)}) collective-permute-start(f32[3,40,512]{2,1,0:T(8,128)S(1)} %pad_maximum_fusion), channel_id=1, source_target_pairs={{0,24},{8,0},{16,8},{24,16},{1,25},{9,1},{17,9},{25,17},{2,26},{10... | collective-permute-start | bytes 737288 | tf_op jit(solution)/shard_map/ppermute | solution.py:175
  35.2 14.9 %collective-permute-start.3 = (f32[3,40,512]{2,1,0:T(8,128)S(1)}, f32[3,40,512]{2,1,0:T(8,128)S(1)}, u32[]{:S(2)}, u32[]{:S(2)}) collective-permute-start(f32[3,40,512]{2,1,0:T(8,128)S(1)} %pad_maximum_fusion.1), channel_id=1, source_target_pairs={{0,8},{8,16},{16,24},{24,0},{1,9},{9,17},{17,25},{25,1},{2,10},{10... | collective-permute-start | bytes 737288 | tf_op jit(solution)/shard_map/ppermute | solution.py:175
  39.4 2.1 copy-start.4
  50.1 108.6 %all-to-all-start.1 = ((f32[4,1024,256]{2,1,0:T(8,128)}), f32[4,1024,256]{2,1,0:T(8,128)}, u32[]{:S(2)}, u32[]{:S(2)}) async-start(f32[4,1024,256]{2,1,0:T(8,128)} %bitcast.16), calls=%async_computation.1 | async-start | bytes 8388608 | tf_op jit(solution)/shard_map/all_to_all | solution.py:716
  56.8 1.3 collective-permute-start.4
  58.1 4.3 %collective-permute-start.5 = (f32[128,128]{1,0:T(8,128)S(1)}, f32[128,128]{1,0:T(8,128)S(1)}, u32[]{:S(2)}, u32[]{:S(2)}) collective-permute-start(f32[128,128]{1,0:T(8,128)S(1)} %pad_maximum_fusion.5), channel_id=1, source_target_pairs={{0,2},{1,3},{2,0},{3,1},{4,6},{5,7},{6,4},{7,5},{8,10},{9,11},{10,... | collective-permute-start | bytes 196616 | tf_op jit(solution)/shard_map/ppermute | solution.py:756
  63.0 11.6 %collective-permute-start.6 = (f32[256,128]{1,0:T(8,128)}, f32[256,128]{1,0:T(8,128)S(1)}, u32[]{:S(2)}, u32[]{:S(2)}) collective-permute-start(f32[256,128]{1,0:T(8,128)} %pad_maximum_fusion.4), channel_id=1, source_target_pairs={{0,4},{1,5},{2,6},{3,7},{4,0},{5,1},{6,2},{7,3},{8,12},{9,13},{10,... | collective-permute-start | bytes 393224 | tf_op jit(solution)/shard_map/ppermute | solution.py:756
  64.4 10.2 %slice-start = ((s8[4718592]{0:T(1024)(128)(4,1)}), s8[524288]{0:T(1024)(128)(4,1)S(1)}, s32[]{:S(2)}) async-start(s8[4718592]{0:T(1024)(128)(4,1)} %bitcast.12), calls=%async_computation.3 | async-start | bytes 1048576
  69.7 4.9 %slice-start.1 = ((s8[4718592]{0:T(1024)(128)(4,1)}), s8[4194304]{0:T(1024)(128)(4,1)S(1)}, s32[]{:S(2)}) async-start(s8[4718592]{0:T(1024)(128)(4,1)} %bitcast.12), calls=%async_computation.4 | async-start | bytes 8388608
  74.6 3.6 %copy-start.2 = (f32[189,40,128]{2,1,0:T(8,128)}, f32[189,40,128]{2,1,0:T(8,128)S(1)}, u32[]{:S(2)}) copy-start(f32[189,40,128]{2,1,0:T(8,128)S(1)} %split.1.ops_ref) | copy-start | bytes 11612164
  74.6 3.6 %copy-start.25 = (s32[1024]{0:T(1024)S(1)}, s32[1024]{0:T(1024)}, u32[]{:S(2)}) copy-start(s32[1024]{0:T(1024)} %class_ref.3) | copy-start | bytes 12292
  76.0 2.2 copy-start.1
  118.3 6.6 %collective-permute-start.8 = (f32[3,40,512]{2,1,0:T(8,128)S(1)}, f32[3,40,512]{2,1,0:T(8,128)S(1)}, u32[]{:S(2)}, u32[]{:S(2)}) collective-permute-start(f32[3,40,512]{2,1,0:T(8,128)S(1)} %get-tuple-element.34), channel_id=1, source_target_pairs={{0,1},{1,2},{2,3},{3,4},{4,5},{5,6},{6,7},{7,0},{8,9},{9,10},{10,1... | collective-permute-start | bytes 737288 | tf_op jit(solution)/shard_map/ppermute | solution.py:175
  120.3 1.6 copy-start.5
  121.9 6.4 %collective-permute-start.7 = (f32[3,40,512]{2,1,0:T(8,128)S(1)}, f32[3,40,512]{2,1,0:T(8,128)S(1)}, u32[]{:S(2)}, u32[]{:S(2)}) collective-permute-start(f32[3,40,512]{2,1,0:T(8,128)S(1)} %get-tuple-element.35), channel_id=1, source_target_pairs={{0,7},{1,0},{2,1},{3,2},{4,3},{5,4},{6,5},{7,6},{8,15},{9,8},{10,9... | collective-permute-start | bytes 737288 | tf_op jit(solution)/shard_map/ppermute | solution.py:175
  124.9 27.2 %copy-start.15 = (f32[3,40,512]{2,1,0:T(8,128)}, f32[3,40,512]{2,1,0:T(8,128)S(1)}, u32[]{:S(2)}) copy-start(f32[3,40,512]{2,1,0:T(8,128)S(1)} %collective-permute-done.8.refs_1_) | copy-start | bytes 737284
  128.3 29.0 %copy-start.17 = (f32[3,40,512]{2,1,0:T(8,128)}, f32[3,40,512]{2,1,0:T(8,128)S(1)}, u32[]{:S(2)}) copy-start(f32[3,40,512]{2,1,0:T(8,128)S(1)} %collective-permute-done.7.refs_0_) | copy-start | bytes 737284
  128.4 28.9 %collective-permute-start.9 = (f32[3,40,512]{2,1,0:T(8,128)S(1)}, f32[3,40,512]{2,1,0:T(8,128)S(1)}, u32[]{:S(2)}, u32[]{:S(2)}) collective-permute-start(f32[3,40,512]{2,1,0:T(8,128)S(1)} %pad_maximum_fusion.2), channel_id=1, source_target_pairs={{0,24},{8,0},{16,8},{24,16},{1,25},{9,1},{17,9},{25,17},{2,26},{10... | collective-permute-start | bytes 737288 | tf_op jit(solution)/shard_map/ppermute | solution.py:175
  128.5 29.5 %collective-permute-start.10 = (f32[3,40,512]{2,1,0:T(8,128)S(1)}, f32[3,40,512]{2,1,0:T(8,128)S(1)}, u32[]{:S(2)}, u32[]{:S(2)}) collective-permute-start(f32[3,40,512]{2,1,0:T(8,128)S(1)} %pad_maximum_fusion.3), channel_id=1, source_target_pairs={{0,8},{8,16},{16,24},{24,0},{1,9},{9,17},{17,25},{25,1},{2,10},{10... | collective-permute-start | bytes 737288 | tf_op jit(solution)/shard_map/ppermute | solution.py:175
  152.1 1.4 copy-start.3
  157.3 0.7 copy-start.19
  158.0 0.7 copy-start.21
  158.7 76.1 %all-to-all-start.2 = ((f32[4,768,256]{2,1,0:T(8,128)}), f32[4,768,256]{2,1,0:T(8,128)}, u32[]{:S(2)}, u32[]{:S(2)}) async-start(f32[4,768,256]{2,1,0:T(8,128)} %bitcast.17), calls=%async_computation.2 | async-start | bytes 6291456 | tf_op jit(solution)/shard_map/all_to_all | solution.py:716
  164.7 1.2 copy-start.6
  165.9 1.2 copy-start.8
  167.2 4.6 %copy-start.14 = (s32[512,128]{1,0:T(8,128)S(1)}, s32[512,128]{1,0:T(8,128)}, u32[]{:S(2)}) copy-start(s32[512,128]{1,0:T(8,128)} %copy-done.13) | copy-start | bytes 786436
  171.8 40.1 %copy-start.7 = (bf16[2,512,512]{2,1,0:T(8,128)(2,1)S(1)}, bf16[2,512,512]{2,1,0:T(8,128)(2,1)}, u32[]{:S(2)}) copy-start(bf16[2,512,512]{2,1,0:T(8,128)(2,1)} %constant.40.clone.refs_6_) | copy-start | bytes 3145732
  171.8 40.1 %copy-start.9 = (bf16[2,512,512]{2,1,0:T(8,128)(2,1)S(1)}, bf16[2,512,512]{2,1,0:T(8,128)(2,1)}, u32[]{:S(2)}) copy-start(bf16[2,512,512]{2,1,0:T(8,128)(2,1)} %constant.39.clone.refs_5_) | copy-start | bytes 3145732
  211.9 11.7 %copy-start.16 = (f32[3,40,512]{2,1,0:T(8,128)S(1)}, f32[3,40,512]{2,1,0:T(8,128)}, u32[]{:S(2)}) copy-start(f32[3,40,512]{2,1,0:T(8,128)} %copy-done.15) | copy-start | bytes 737284
  211.9 11.7 %copy-start.18 = (f32[3,40,512]{2,1,0:T(8,128)S(1)}, f32[3,40,512]{2,1,0:T(8,128)}, u32[]{:S(2)}) copy-start(f32[3,40,512]{2,1,0:T(8,128)} %copy-done.17) | copy-start | bytes 737284
  211.9 11.7 %copy-start.20 = (f32[3,40,512]{2,1,0:T(8,128)S(1)}, f32[3,40,512]{2,1,0:T(8,128)}, u32[]{:S(2)}) copy-start(f32[3,40,512]{2,1,0:T(8,128)} %copy-done.19) | copy-start | bytes 737284
  211.9 11.7 %copy-start.22 = (f32[3,40,512]{2,1,0:T(8,128)S(1)}, f32[3,40,512]{2,1,0:T(8,128)}, u32[]{:S(2)}) copy-start(f32[3,40,512]{2,1,0:T(8,128)} %copy-done.21) | copy-start | bytes 737284
  234.8 1.2 copy-start.10

commit v10 on v9

--- a/solution.py
+++ b/solution.py
@@ -763,9 +763,9 @@
     slot_fields = m2l(sources, block_class, table, ops, cell_steps, slot_steps, True, slots)
     mid = after(slot_fields[6:], carved[1])
     returned = along_gx(*along_gy(slot_fields[:3], slot_fields[3:6]), mid)
-    parts.append(send(after(carved[1], parts[1], adds[0], *returned)))
     tables = fourier_tables(n_gx * width)
     spectrum = fourier(parts[0], spans[0][1], adds, tables, 0, planes, None, own_rows)
+    parts.append(send(after(carved[1], parts[1], spectrum, *returned)))
     own_fields = m2l(sources, block_class, table, ops, 0, cell_steps, False, slots)
     spectrum = fourier(parts[1], spans[1][1], adds, tables, spans[1][0], planes, spectrum, own_rows)
     own_fields = after(own_fields, spectrum)

time: 248 us -> 250 us (level)
    all_to_all x3, waiting for transfers between devices: 0.01 us -> 5.15 us  [send(): return lax.all_to_all(part, 'gx', 0, 0, tiled=True)]
    ppermute x8, waiting for transfers between devices: 16.3 us -> 12.5 us  [shift(): lax.ppermute(value, axis, [(i, (i + by) % count) for i in range(count)])]
where the time goes in v10:
time: 250 us; the launch traced here: 245 us
  Pallas kernels  173 us (69%)
  starting transfers between devices  28.3 us (11%)
  waiting for transfers between devices  22.1 us (9%)
  local copies, waits for them, and re-layouts  19.5 us (8%)
    pallas_call x2, Pallas kernels, m2l(): pl.pallas_call(functools.partial(m2l_kernel, first=first, turned=turned),...  80.2 us
    pallas_call x3, Pallas kernels, fourier(): pl.pallas_call(functools.partial(fourier_kernel, sources=sources), grid=(...  25.4 us
    pallas_call x1, Pallas kernels, deposit(): pl.pallas_call(deposit_kernel, out_shape=(jax.ShapeDtypeStruct((rows, LAN...  21.8 us
    unnamed x63, local copies, waits for them, and re-layouts  19.3 us
    all_to_all x3, starting transfers between devices, send(): return lax.all_to_all(part, 'gx', 0, 0, tiled=True)  17.5 us
    ppermute x8, waiting for transfers between devices, shift(): lax.ppermute(value, axis, [(i, (i + by) % count) for i in range(count)])  12.5 us
    pallas_call x1, Pallas kernels, add_back(): pl.pallas_call(add_back_kernel, out_shape=jax.ShapeDtypeStruct((coef_coun...  11.2 us
    pallas_call x1, Pallas kernels, pack(): pl.pallas_call(pack_kernel, grid=(1,), out_shape=tuple((jax.ShapeDtypeStr...  9.99 us
  transfers between devices with their start and end apart: 14, of which 8 were waited for; matrix products, arithmetic and copies ran while one was open for 3% of the time, Pallas kernels for 66%

profile of v10, /device:TPU:8, one launch (start us, length us, event | category | flops | bytes accessed | tf_op | source)
XLA Modules:
  0.0 245.4 jit_solution(8441924483743143745)
XLA Ops:
  0.6 0.0 copy-start.11
  0.6 1.1 copy-done.11
  1.7 0.7 copy-done.24
  2.4 2.4 first_part.1
  4.8 5.3 %all-to-all-start = ((f32[4,296,256]{2,1,0:T(8,128)}), f32[4,296,256]{2,1,0:T(8,128)S(1)}, u32[]{:S(2)}, u32[]{:S(2)}) async-start(f32[4,296,256]{2,1,0:T(8,128)} %first_part.1), calls=%async_computation | async-start | bytes 2424832 | tf_op jit(solution)/shard_map/all_to_all | solution.py:716
  10.2 0.0 copy-start.27
  10.2 3.3 %own_table.1.refs_8_ = f32[9216,128]{1,0:T(8,128)S(1)} custom-call(f32[40,4096]{1,0:T(8,128)S(1)} %pad.4.cells_ref), custom_call_target="tpu_custom_call" | custom-call | flops 1000000 | bytes 12000000 | tf_op jit(solution)/shard_map/own_table/pallas_call | solution.py:59
  13.6 0.0 copy-start.28
  13.6 10.0 %pack.1 = (f32[3,40,512]{2,1,0:T(8,128)S(1)}, f32[3,40,512]{2,1,0:T(8,128)S(1)}, f32[2,40,512]{2,1,0:T(8,128)S(1)}) custom-call(s32[8,512]{1,0:T(8,128)S(1)} %bitcast.18, s32[8]{0:T(128)S(1)} %bitcast.21, f32[9216,1,128]{2,1,0:T(1,128)S(1)} %bitcast.11), custom_call_target="tpu_custom_call" | custom-call | flops 1000000 | bytes 25000000 | tf_op jit(solution)/shard_map/pack/pallas_call | solution.py:154
  23.6 2.2 copy-done
  25.8 1.3 collective-permute-start
  27.1 0.0 collective-permute-start.1
  27.1 0.2 fusion.2.packed_ref
  27.3 7.4 %order.1.source_ref = s32[512,128]{1,0:T(8,128)S(1)} custom-call(s32[512,128]{1,0:T(8,128)S(1)} %fusion.2.packed_ref), custom_call_target="tpu_custom_call" | custom-call | flops 1000000 | bytes 20000000 | tf_op jit(solution)/shard_map/order/pallas_call | solution.py:207
  34.7 0.0 copy-start.13
  34.7 0.0 collective-permute-done.refs_0_
  34.8 0.3 collective-permute-done.1.refs_1_
  35.1 0.1 collective-permute-start.2
  35.2 2.0 collective-permute-start.3
  37.2 2.2 carve.2
  39.4 2.1 copy-done.4
  41.5 1.9 collective-permute-done.2.refs_2_
  43.4 6.7 %collective-permute-done.3.refs_3_ = f32[3,40,512]{2,1,0:T(8,128)S(1)} collective-permute-done((f32[3,40,512]{2,1,0:T(8,128)S(1)}, f32[3,40,512]{2,1,0:T(8,128)S(1)}, u32[]{:S(2)}, u32[]{:S(2)}) %collective-permute-start.3) | collective-permute-done | bytes 245792 | tf_op jit(solution)/shard_map/ppermute | solution.py:175
  50.1 0.0 all-to-all-done.part_ref.refs_0_
  50.1 5.3 %all-to-all-start.1 = ((f32[4,1024,256]{2,1,0:T(8,128)}), f32[4,1024,256]{2,1,0:T(8,128)}, u32[]{:S(2)}, u32[]{:S(2)}) async-start(f32[4,1024,256]{2,1,0:T(8,128)} %bitcast.16), calls=%async_computation.1 | async-start | bytes 8388608 | tf_op jit(solution)/shard_map/all_to_all | solution.py:716
  55.4 1.3 sift.1
  56.8 0.1 collective-permute-start.4
  56.9 1.2 collective-permute-done.4.refs_5_
  58.1 1.0 collective-permute-start.5
  59.1 3.3 %collective-permute-done.5.refs_6_ = f32[128,128]{1,0:T(8,128)S(1)} collective-permute-done((f32[128,128]{1,0:T(8,128)S(1)}, f32[128,128]{1,0:T(8,128)S(1)}, u32[]{:S(2)}, u32[]{:S(2)}) %collective-permute-start.5) | collective-permute-done | bytes 65568 | tf_op jit(solution)/shard_map/ppermute | solution.py:756
  62.3 0.7 pad_maximum_fusion.4
  63.0 1.4 collective-permute-start.6
  64.4 5.4 %copy.16 = f32[189,35,35]{1,2,0:T(8,128)} copy(f32[189,35,35]{0,2,1:T(8,128)} %param.17) | data formatting | bytes 1852200 | tf_op args[6]
  69.8 4.8 %split.1.ops_ref = f32[189,40,128]{2,1,0:T(8,128)S(1)} custom-call(f32[189,35,35]{2,1,0:T(8,128)} %bitcast.23), custom_call_target="tpu_custom_call" | custom-call | flops 1000000 | bytes 12000000 | tf_op jit(solution)/shard_map/split/pallas_call | solution.py:234
  74.6 0.0 copy-start.25
  74.6 0.0 collective-permute-done.6.refs_7_
  74.6 1.3 whole_table.1
  76.0 2.2 copy-done.1
  78.2 40.1 %m2l_slots.1 = f32[8,40,512]{2,1,0:T(8,128)S(1)} custom-call(s32[512,128]{1,0:T(8,128)S(1)} %order.1.source_ref, s32[1024]{0:T(1024)S(1)} %copy-done.25, f32[9216,1,128]{2,1,0:T(1,128)} %bitcast.14, f32[189,40,128]{2,1,0:T(8,128)S(1)} %split.1.ops_ref), custom_call_target="tpu_custom_call" | custom-call | flops 1000000 | bytes 150000000 | tf_op jit(solution)/shard_map/m2l_slots/pallas_call | solution.py:302
  118.3 0.0 copy-start.6
  118.3 0.0 copy-start.8
  118.4 0.1 collective-permute-start.8
  118.4 2.0 carve.3
  120.4 1.6 copy-done.5
  122.1 2.5 %collective-permute-start.7 = (f32[3,40,512]{2,1,0:T(8,128)S(1)}, f32[3,40,512]{2,1,0:T(8,128)S(1)}, u32[]{:S(2)}, u32[]{:S(2)}) collective-permute-start(f32[3,40,512]{2,1,0:T(8,128)S(1)} %get-tuple-element.35), channel_id=1, source_target_pairs={{0,7},{1,0},{2,1},{3,2},{4,3},{5,4},{6,5},{7,6},{8,15},{9,8},{10,9... | collective-permute-start | bytes 737288 | tf_op jit(solution)/shard_map/ppermute | solution.py:175
  124.6 0.3 collective-permute-done.8.refs_1_
  124.9 3.4 %collective-permute-done.7.refs_0_ = f32[3,40,512]{2,1,0:T(8,128)S(1)} collective-permute-done((f32[3,40,512]{2,1,0:T(8,128)S(1)}, f32[3,40,512]{2,1,0:T(8,128)S(1)}, u32[]{:S(2)}, u32[]{:S(2)}) %collective-permute-start.7) | collective-permute-done | bytes 245792 | tf_op jit(solution)/shard_map/ppermute | solution.py:175
  128.4 0.2 collective-permute-start.9
  128.6 2.2 collective-permute-start.10
  130.7 21.8 %deposit.1 = (f32[4104,128]{1,0:T(8,128)S(1)}, f32[4104,128]{1,0:T(8,128)S(1)}, f32[4104,128]{1,0:T(8,128)}, f32[4104,128]{1,0:T(8,128)}) custom-call(s32[128,128]{1,0:T(8,128)S(1)} %get-tuple-element.24.code_ref, f32[128,128]{1,0:T(8,128)S(1)} %get-tuple-element.25.value_ref, s32[16,128]{1,0:T(8,128)S(1)} %get-tuple-element.26.bound_ref), custom_call_target="tpu_custom_call" | custom-call | flops 1000000 | bytes 40000000 | tf_op jit(solution)/shard_map/deposit/pallas_call | solution.py:562
  152.5 1.4 copy-done.3
  153.9 4.5 %fourier.3.refs_7_ = f32[2,8,256,1024]{3,2,1,0:T(8,128)} custom-call(f32[4,296,256]{2,1,0:T(8,128)S(1)} %all-to-all-done.part_ref.refs_0_, f32[4104,128]{1,0:T(8,128)S(1)} %get-tuple-element.27.refs_1_, f32[4104,128]{1,0:T(8,128)} %copy-done.3, f32[4104,128]{1,0:T(8,128)} %get-tuple-element.29.refs_3_, f32[4104,128]{1,0:T(8,128)} %get-tuple-element.30.refs_4_, ...), custom_call_target="tpu_custom_call" | custom-call | flops 1000000 | bytes 10000000 | tf_op jit(solution)/shard_map/fourier/pallas_call | solution.py:677
  158.5 0.0 collective-permute-done.9.refs_2_
  158.5 0.7 copy-done.19
  159.2 0.0 collective-permute-done.10.refs_3_
  159.2 0.7 copy-done.21
  159.9 0.0 all-to-all-done.1.refs_0_
  159.9 6.8 %all-to-all-start.2 = ((f32[4,768,256]{2,1,0:T(8,128)}), f32[4,768,256]{2,1,0:T(8,128)}, u32[]{:S(2)}, u32[]{:S(2)}) async-start(f32[4,768,256]{2,1,0:T(8,128)} %bitcast.17), calls=%async_computation.2 | async-start | bytes 6291456 | tf_op jit(solution)/shard_map/all_to_all | solution.py:716
  166.7 40.1 %m2l_cells.1.own_ref = f32[4096,128]{1,0:T(8,128)S(1)} custom-call(s32[512,128]{1,0:T(8,128)S(1)} %copy-done.14, s32[1024]{0:T(1024)S(1)} %copy-done.25, f32[9216,1,128]{2,1,0:T(1,128)} %bitcast.15, f32[189,40,128]{2,1,0:T(8,128)} %copy-done.2), custom_call_target="tpu_custom_call" | custom-call | flops 1000000 | bytes 150000000 | tf_op jit(solution)/shard_map/m2l_cells/pallas_call | solution.py:302
  206.8 11.6 %fourier.4.refs_7_ = f32[2,8,256,1024]{3,2,1,0:T(8,128)} custom-call(f32[4,1024,256]{2,1,0:T(8,128)} %all-to-all-done.1.refs_0_, f32[4104,128]{1,0:T(8,128)S(1)} %get-tuple-element.27.refs_1_, f32[4104,128]{1,0:T(8,128)} %copy-done.3, f32[4104,128]{1,0:T(8,128)} %get-tuple-element.29.refs_3_, ...), custom_call_target="tpu_custom_call", output_to_operand_aliasing={{}: (7, {})} | custom-call | flops 1000000 | bytes 40000000 | tf_op jit(solution)/shard_map/fourier/pallas_call | solution.py:677
  218.5 11.2 %add_back.1 = f32[35,4096]{1,0:T(8,128)} custom-call(s32[8,512]{1,0:T(8,128)S(1)} %bitcast.19, s32[8]{0:T(128)S(1)} %bitcast.22, f32[4096,128]{1,0:T(8,128)S(1)} %m2l_cells.1.own_ref, f32[3,40,512]{2,1,0:T(8,128)S(1)} %copy-done.18, f32[3,40,512]{2,1,0:T(8,128)S(1)} %copy-done.16, f32[3,40,512]{2,1,0:T(8,128)S(1)} %copy-done.20, f32[3,40,512]{2,1,0:T(8,128)S(1)} %copy-done.22), custom_call_target="tpu_custom_call" | custom-call | flops 1000000 | bytes 30000000 | tf_op jit(solution)/shard_map/add_back/pallas_call | solution.py:356
  229.7 5.1 %all-to-all-done.2.refs_0_ = f32[4,768,256]{2,1,0:T(8,128)} async-done(((f32[4,768,256]{2,1,0:T(8,128)}), f32[4,768,256]{2,1,0:T(8,128)}, u32[]{:S(2)}, u32[]{:S(2)}) %all-to-all-start.2) | async-done | bytes 3145760 | tf_op jit(solution)/shard_map/all_to_all | solution.py:716
  234.9 1.2 copy-done.10
  236.1 9.3 %fourier.5 = f32[2,8,256,1024]{3,2,1,0:T(8,128)} custom-call(f32[4,768,256]{2,1,0:T(8,128)} %all-to-all-done.2.refs_0_, f32[4104,128]{1,0:T(8,128)S(1)} %get-tuple-element.27.refs_1_, f32[4104,128]{1,0:T(8,128)} %copy-done.3, f32[4104,128]{1,0:T(8,128)} %get-tuple-element.29.refs_3_, ...), custom_call_target="tpu_custom_call", output_to_operand_aliasing={{}: (7, {})} | custom-call | flops 1000000 | bytes 30000000 | tf_op jit(solution)/shard_map/fourier/pallas_call | solution.py:677
  (60 shorter events, 0.3 us)
Async XLA Ops:
  0.6 1.1 copy-start.11
  1.7 0.7 copy-start.24
  2.4 7.7 %copy-start.12 = (f32[35,4096]{1,0:T(8,128)S(1)}, f32[35,4096]{1,0:T(8,128)}, u32[]{:S(2)}) copy-start(f32[35,4096]{1,0:T(8,128)} %cells_ref.1) | copy-start | bytes 1720324
  4.8 45.3 %all-to-all-start = ((f32[4,296,256]{2,1,0:T(8,128)}), f32[4,296,256]{2,1,0:T(8,128)S(1)}, u32[]{:S(2)}, u32[]{:S(2)}) async-start(f32[4,296,256]{2,1,0:T(8,128)} %first_part.1), calls=%async_computation | async-start | bytes 2424832 | tf_op jit(solution)/shard_map/all_to_all | solution.py:716
  10.1 3.4 %copy-start.23 = (s32[1,8,512]{2,1,0:T(8,128)S(1)}, s32[1,8,512]{2,1,0:T(8,128)}, u32[]{:S(2)}) copy-start(s32[1,8,512]{2,1,0:T(8,128)} %param.12) | copy-start | bytes 49156
  10.1 3.4 %copy-start.26 = (s32[1,8]{1,0:T(1,128)S(1)}, s32[1,8]{1,0:T(1,128)}, u32[]{:S(2)}) copy-start(s32[1,8]{1,0:T(1,128)} %param.13) | copy-start | bytes 100
  10.2 16.9 %copy-start.27 = (s32[65536]{0:T(1024)S(1)}, s32[65536]{0:T(1024)}, u32[]{:S(2)}) copy-start(s32[65536]{0:T(1024)} %param.14) | copy-start | bytes 786436
  13.6 13.5 %copy-start.28 = (s32[65536]{0:T(1024)S(1)}, s32[65536]{0:T(1024)}, u32[]{:S(2)}) copy-start(s32[65536]{0:T(1024)} %param.15) | copy-start | bytes 786436
  23.6 2.2 copy-start
  25.8 9.0 %collective-permute-start = (f32[3,40,512]{2,1,0:T(8,128)S(1)}, f32[3,40,512]{2,1,0:T(8,128)S(1)}, u32[]{:S(2)}, u32[]{:S(2)}) collective-permute-start(f32[3,40,512]{2,1,0:T(8,128)S(1)} %get-tuple-element.18), channel_id=1, source_target_pairs={{0,7},{1,0},{2,1},{3,2},{4,3},{5,4},{6,5},{7,6},{8,15},{9,8},{10,9... | collective-permute-start | bytes 737288 | tf_op jit(solution)/shard_map/ppermute | solution.py:175
  27.1 7.9 %collective-permute-start.1 = (f32[3,40,512]{2,1,0:T(8,128)S(1)}, f32[3,40,512]{2,1,0:T(8,128)S(1)}, u32[]{:S(2)}, u32[]{:S(2)}) collective-permute-start(f32[3,40,512]{2,1,0:T(8,128)S(1)} %get-tuple-element.19), channel_id=1, source_target_pairs={{0,1},{1,2},{2,3},{3,4},{4,5},{5,6},{6,7},{7,0},{8,9},{9,10},{10,1... | collective-permute-start | bytes 737288 | tf_op jit(solution)/shard_map/ppermute | solution.py:175
  34.7 43.5 %copy-start.13 = (s32[512,128]{1,0:T(8,128)}, s32[512,128]{1,0:T(8,128)S(1)}, u32[]{:S(2)}) copy-start(s32[512,128]{1,0:T(8,128)S(1)} %order.1.source_ref) | copy-start | bytes 786436
  35.1 8.3 %collective-permute-start.2 = (f32[3,40,512]{2,1,0:T(8,128)S(1)}, f32[3,40,512]{2,1,0:T(8,128)S(1)}, u32[]{:S(2)}, u32[]{:S(2)}) collective-permute-start(f32[3,40,512]{2,1,0:T(8,128)S(1)} %pad_maximum_fusion), channel_id=1, source_target_pairs={{0,24},{8,0},{16,8},{24,16},{1,25},{9,1},{17,9},{25,17},{2,26},{10... | collective-permute-start | bytes 737288 | tf_op jit(solution)/shard_map/ppermute | solution.py:175
  35.2 14.9 %collective-permute-start.3 = (f32[3,40,512]{2,1,0:T(8,128)S(1)}, f32[3,40,512]{2,1,0:T(8,128)S(1)}, u32[]{:S(2)}, u32[]{:S(2)}) collective-permute-start(f32[3,40,512]{2,1,0:T(8,128)S(1)} %pad_maximum_fusion.1), channel_id=1, source_target_pairs={{0,8},{8,16},{16,24},{24,0},{1,9},{9,17},{17,25},{25,1},{2,10},{10... | collective-permute-start | bytes 737288 | tf_op jit(solution)/shard_map/ppermute | solution.py:175
  39.4 2.1 copy-start.4
  50.1 109.8 %all-to-all-start.1 = ((f32[4,1024,256]{2,1,0:T(8,128)}), f32[4,1024,256]{2,1,0:T(8,128)}, u32[]{:S(2)}, u32[]{:S(2)}) async-start(f32[4,1024,256]{2,1,0:T(8,128)} %bitcast.16), calls=%async_computation.1 | async-start | bytes 8388608 | tf_op jit(solution)/shard_map/all_to_all | solution.py:716
  56.8 1.3 collective-permute-start.4
  58.1 4.3 %collective-permute-start.5 = (f32[128,128]{1,0:T(8,128)S(1)}, f32[128,128]{1,0:T(8,128)S(1)}, u32[]{:S(2)}, u32[]{:S(2)}) collective-permute-start(f32[128,128]{1,0:T(8,128)S(1)} %pad_maximum_fusion.5), channel_id=1, source_target_pairs={{0,2},{1,3},{2,0},{3,1},{4,6},{5,7},{6,4},{7,5},{8,10},{9,11},{10,... | collective-permute-start | bytes 196616 | tf_op jit(solution)/shard_map/ppermute | solution.py:756
  63.0 11.6 %collective-permute-start.6 = (f32[256,128]{1,0:T(8,128)}, f32[256,128]{1,0:T(8,128)S(1)}, u32[]{:S(2)}, u32[]{:S(2)}) collective-permute-start(f32[256,128]{1,0:T(8,128)} %pad_maximum_fusion.4), channel_id=1, source_target_pairs={{0,4},{1,5},{2,6},{3,7},{4,0},{5,1},{6,2},{7,3},{8,12},{9,13},{10,... | collective-permute-start | bytes 393224 | tf_op jit(solution)/shard_map/ppermute | solution.py:756
  64.4 10.2 %slice-start = ((s8[4718592]{0:T(1024)(128)(4,1)}), s8[524288]{0:T(1024)(128)(4,1)S(1)}, s32[]{:S(2)}) async-start(s8[4718592]{0:T(1024)(128)(4,1)} %bitcast.12), calls=%async_computation.3 | async-start | bytes 1048576
  69.7 4.9 %slice-start.1 = ((s8[4718592]{0:T(1024)(128)(4,1)}), s8[4194304]{0:T(1024)(128)(4,1)S(1)}, s32[]{:S(2)}) async-start(s8[4718592]{0:T(1024)(128)(4,1)} %bitcast.12), calls=%async_computation.4 | async-start | bytes 8388608
  74.6 3.6 %copy-start.2 = (f32[189,40,128]{2,1,0:T(8,128)}, f32[189,40,128]{2,1,0:T(8,128)S(1)}, u32[]{:S(2)}) copy-start(f32[189,40,128]{2,1,0:T(8,128)S(1)} %split.1.ops_ref) | copy-start | bytes 11612164
  74.6 3.6 %copy-start.25 = (s32[1024]{0:T(1024)S(1)}, s32[1024]{0:T(1024)}, u32[]{:S(2)}) copy-start(s32[1024]{0:T(1024)} %class_ref.3) | copy-start | bytes 12292
  76.0 2.2 copy-start.1
  118.3 35.6 %copy-start.6 = (bf16[2,512,512]{2,1,0:T(8,128)(2,1)S(1)}, bf16[2,512,512]{2,1,0:T(8,128)(2,1)}, u32[]{:S(2)}) copy-start(bf16[2,512,512]{2,1,0:T(8,128)(2,1)} %constant.40.clone.refs_6_) | copy-start | bytes 3145732
  118.3 35.6 %copy-start.8 = (bf16[2,512,512]{2,1,0:T(8,128)(2,1)S(1)}, bf16[2,512,512]{2,1,0:T(8,128)(2,1)}, u32[]{:S(2)}) copy-start(bf16[2,512,512]{2,1,0:T(8,128)(2,1)} %constant.39.clone.refs_5_) | copy-start | bytes 3145732
  118.4 6.6 %collective-permute-start.8 = (f32[3,40,512]{2,1,0:T(8,128)S(1)}, f32[3,40,512]{2,1,0:T(8,128)S(1)}, u32[]{:S(2)}, u32[]{:S(2)}) collective-permute-start(f32[3,40,512]{2,1,0:T(8,128)S(1)} %get-tuple-element.34), channel_id=1, source_target_pairs={{0,1},{1,2},{2,3},{3,4},{4,5},{5,6},{6,7},{7,0},{8,9},{9,10},{10,1... | collective-permute-start | bytes 737288 | tf_op jit(solution)/shard_map/ppermute | solution.py:175
  120.4 1.6 copy-start.5
  122.1 6.3 %collective-permute-start.7 = (f32[3,40,512]{2,1,0:T(8,128)S(1)}, f32[3,40,512]{2,1,0:T(8,128)S(1)}, u32[]{:S(2)}, u32[]{:S(2)}) collective-permute-start(f32[3,40,512]{2,1,0:T(8,128)S(1)} %get-tuple-element.35), channel_id=1, source_target_pairs={{0,7},{1,0},{2,1},{3,2},{4,3},{5,4},{6,5},{7,6},{8,15},{9,8},{10,9... | collective-permute-start | bytes 737288 | tf_op jit(solution)/shard_map/ppermute | solution.py:175
  124.9 33.5 %copy-start.15 = (f32[3,40,512]{2,1,0:T(8,128)}, f32[3,40,512]{2,1,0:T(8,128)S(1)}, u32[]{:S(2)}) copy-start(f32[3,40,512]{2,1,0:T(8,128)S(1)} %collective-permute-done.8.refs_1_) | copy-start | bytes 737284
  128.3 30.1 %copy-start.17 = (f32[3,40,512]{2,1,0:T(8,128)}, f32[3,40,512]{2,1,0:T(8,128)S(1)}, u32[]{:S(2)}) copy-start(f32[3,40,512]{2,1,0:T(8,128)S(1)} %collective-permute-done.7.refs_0_) | copy-start | bytes 737284
  128.4 30.1 %collective-permute-start.9 = (f32[3,40,512]{2,1,0:T(8,128)S(1)}, f32[3,40,512]{2,1,0:T(8,128)S(1)}, u32[]{:S(2)}, u32[]{:S(2)}) collective-permute-start(f32[3,40,512]{2,1,0:T(8,128)S(1)} %pad_maximum_fusion.2), channel_id=1, source_target_pairs={{0,24},{8,0},{16,8},{24,16},{1,25},{9,1},{17,9},{25,17},{2,26},{10... | collective-permute-start | bytes 737288 | tf_op jit(solution)/shard_map/ppermute | solution.py:175
  128.6 30.6 %collective-permute-start.10 = (f32[3,40,512]{2,1,0:T(8,128)S(1)}, f32[3,40,512]{2,1,0:T(8,128)S(1)}, u32[]{:S(2)}, u32[]{:S(2)}) collective-permute-start(f32[3,40,512]{2,1,0:T(8,128)S(1)} %pad_maximum_fusion.3), channel_id=1, source_target_pairs={{0,8},{8,16},{16,24},{24,0},{1,9},{9,17},{17,25},{25,1},{2,10},{10... | collective-permute-start | bytes 737288 | tf_op jit(solution)/shard_map/ppermute | solution.py:175
  152.5 1.4 copy-start.3
  158.5 8.2 %copy-start.14 = (s32[512,128]{1,0:T(8,128)S(1)}, s32[512,128]{1,0:T(8,128)}, u32[]{:S(2)}) copy-start(s32[512,128]{1,0:T(8,128)} %copy-done.13) | copy-start | bytes 786436
  158.5 0.7 copy-start.19
  159.2 0.7 copy-start.21
  159.9 75.0 %all-to-all-start.2 = ((f32[4,768,256]{2,1,0:T(8,128)}), f32[4,768,256]{2,1,0:T(8,128)}, u32[]{:S(2)}, u32[]{:S(2)}) async-start(f32[4,768,256]{2,1,0:T(8,128)} %bitcast.17), calls=%async_computation.2 | async-start | bytes 6291456 | tf_op jit(solution)/shard_map/all_to_all | solution.py:716
  166.7 40.1 %copy-start.7 = (bf16[2,512,512]{2,1,0:T(8,128)(2,1)S(1)}, bf16[2,512,512]{2,1,0:T(8,128)(2,1)}, u32[]{:S(2)}) copy-start(bf16[2,512,512]{2,1,0:T(8,128)(2,1)} %constant.40.clone.refs_6_) | copy-start | bytes 3145732
  166.7 40.1 %copy-start.9 = (bf16[2,512,512]{2,1,0:T(8,128)(2,1)S(1)}, bf16[2,512,512]{2,1,0:T(8,128)(2,1)}, u32[]{:S(2)}) copy-start(bf16[2,512,512]{2,1,0:T(8,128)(2,1)} %constant.39.clone.refs_5_) | copy-start | bytes 3145732
  206.8 11.7 %copy-start.16 = (f32[3,40,512]{2,1,0:T(8,128)S(1)}, f32[3,40,512]{2,1,0:T(8,128)}, u32[]{:S(2)}) copy-start(f32[3,40,512]{2,1,0:T(8,128)} %copy-done.15) | copy-start | bytes 737284
  206.8 11.7 %copy-start.18 = (f32[3,40,512]{2,1,0:T(8,128)S(1)}, f32[3,40,512]{2,1,0:T(8,128)}, u32[]{:S(2)}) copy-start(f32[3,40,512]{2,1,0:T(8,128)} %copy-done.17) | copy-start | bytes 737284
  206.8 11.7 %copy-start.20 = (f32[3,40,512]{2,1,0:T(8,128)S(1)}, f32[3,40,512]{2,1,0:T(8,128)}, u32[]{:S(2)}) copy-start(f32[3,40,512]{2,1,0:T(8,128)} %copy-done.19) | copy-start | bytes 737284
  206.8 11.7 %copy-start.22 = (f32[3,40,512]{2,1,0:T(8,128)S(1)}, f32[3,40,512]{2,1,0:T(8,128)}, u32[]{:S(2)}) copy-start(f32[3,40,512]{2,1,0:T(8,128)} %copy-done.21) | copy-start | bytes 737284
  234.9 1.2 copy-start.10

commit v11 on v9

--- a/solution.py
+++ b/solution.py
@@ -740,7 +740,7 @@
     wanted = jnp.where(pair_source < base, pair_source, top)
     sources = order(((wanted << SHIFT) | (pair_target & (BLOCK - 1))).reshape(-1, LANES))
 
-    arrived = along_gx(*along_gy(*outgoing[:2]), after(outgoing[2], sources))
+    arrived = along_gx(*along_gy(*outgoing[:2]), outgoing[2])
 
     ops = split(m2l_ops.transpose(0, 2, 1))
 
@@ -755,7 +755,7 @@
         held = jnp.concatenate(tops, axis=0) if bit else top_own
         tops.append(lax.ppermute(held, "gy", [(i, i ^ (1 << bit)) for i in range(n_gy)]))
 
-    parts.append(send(after(carved[0], parts[0], *arrived)))
+    parts.append(send(after(carved[0], parts[0], sources, *arrived)))
     adds = deposit(codes, amounts, bounds, add_rows + 8, n_gx)
     table = whole_table(table, arrived, tops)
     cell_steps = cell_count // LANES

time: 248 us -> 248 us (level)
  transfers between devices with their start and end apart: 14 -> 14, of which waited for: 8 -> 7; matrix products, arithmetic and copies ran while one was open for 3% -> 3% of each run, Pallas kernels for 66% -> 66%
where the time goes in v11:
time: 248 us; the launch traced here: 245 us
  Pallas kernels  173 us (70%)
  starting transfers between devices  27.4 us (11%)
  local copies, waits for them, and re-layouts  21.9 us (9%)
  waiting for transfers between devices  19.5 us (8%)
    pallas_call x2, Pallas kernels, m2l(): pl.pallas_call(functools.partial(m2l_kernel, first=first, turned=turned),...  80.2 us
    pallas_call x3, Pallas kernels, fourier(): pl.pallas_call(functools.partial(fourier_kernel, sources=sources), grid=(...  25.5 us
    unnamed x63, local copies, waits for them, and re-layouts  21.7 us
    pallas_call x1, Pallas kernels, deposit(): pl.pallas_call(deposit_kernel, out_shape=(jax.ShapeDtypeStruct((rows, LAN...  21.7 us
    all_to_all x3, starting transfers between devices, send(): return lax.all_to_all(part, 'gx', 0, 0, tiled=True)  18.2 us
    ppermute x8, waiting for transfers between devices, shift(): lax.ppermute(value, axis, [(i, (i + by) % count) for i in range(count)])  14.2 us
    pallas_call x1, Pallas kernels, add_back(): pl.pallas_call(add_back_kernel, out_shape=jax.ShapeDtypeStruct((coef_coun...  11.2 us
    pallas_call x1, Pallas kernels, pack(): pl.pallas_call(pack_kernel, grid=(1,), out_shape=tuple((jax.ShapeDtypeStr...  9.99 us
  transfers between devices with their start and end apart: 14, of which 7 were waited for; matrix products, arithmetic and copies ran while one was open for 3% of the time, Pallas kernels for 66%

profile of v11, /device:TPU:8, one launch (start us, length us, event | category | flops | bytes accessed | tf_op | source)
XLA Modules:
  0.0 245.4 jit_solution(6679591261068844334)
XLA Ops:
  0.6 0.0 copy-start.11
  0.6 1.1 copy-done.11
  1.7 0.7 copy-done.24
  2.4 2.4 first_part.1
  4.8 5.3 %all-to-all-start = ((f32[4,296,256]{2,1,0:T(8,128)}), f32[4,296,256]{2,1,0:T(8,128)S(1)}, u32[]{:S(2)}, u32[]{:S(2)}) async-start(f32[4,296,256]{2,1,0:T(8,128)} %first_part.1), calls=%async_computation | async-start | bytes 2424832 | tf_op jit(solution)/shard_map/all_to_all | solution.py:716
  10.2 3.3 %own_table.1.refs_8_ = f32[9216,128]{1,0:T(8,128)S(1)} custom-call(f32[40,4096]{1,0:T(8,128)S(1)} %pad.4.cells_ref), custom_call_target="tpu_custom_call" | custom-call | flops 1000000 | bytes 12000000 | tf_op jit(solution)/shard_map/own_table/pallas_call | solution.py:59
  13.6 10.0 %pack.1 = (f32[3,40,512]{2,1,0:T(8,128)S(1)}, f32[3,40,512]{2,1,0:T(8,128)S(1)}, f32[2,40,512]{2,1,0:T(8,128)S(1)}) custom-call(s32[8,512]{1,0:T(8,128)S(1)} %bitcast.18, s32[8]{0:T(128)S(1)} %bitcast.21, f32[9216,1,128]{2,1,0:T(1,128)S(1)} %bitcast.11), custom_call_target="tpu_custom_call" | custom-call | flops 1000000 | bytes 25000000 | tf_op jit(solution)/shard_map/pack/pallas_call | solution.py:154
  23.6 2.2 copy-done
  25.7 1.3 collective-permute-start
  27.1 0.0 collective-permute-start.1
  27.1 5.9 %collective-permute-done.refs_0_ = f32[3,40,512]{2,1,0:T(8,128)S(1)} collective-permute-done((f32[3,40,512]{2,1,0:T(8,128)S(1)}, f32[3,40,512]{2,1,0:T(8,128)S(1)}, u32[]{:S(2)}, u32[]{:S(2)}) %collective-permute-start) | collective-permute-done | bytes 245792 | tf_op jit(solution)/shard_map/ppermute | solution.py:175
  33.0 2.0 collective-permute-done.1.refs_1_
  35.0 0.7 pad_maximum_fusion
  35.7 0.0 collective-permute-start.2
  35.8 0.7 pad_maximum_fusion.1
  36.5 2.0 collective-permute-start.3
  38.5 2.3 carve.2
  40.8 2.1 copy-done.4
  42.8 0.2 fusion.2.packed_ref
  43.0 7.4 %order.1.source_ref = s32[512,128]{1,0:T(8,128)S(1)} custom-call(s32[512,128]{1,0:T(8,128)S(1)} %fusion.2.packed_ref), custom_call_target="tpu_custom_call" | custom-call | flops 1000000 | bytes 20000000 | tf_op jit(solution)/shard_map/order/pallas_call | solution.py:207
  50.4 0.0 copy-start.13
  50.4 0.0 collective-permute-done.2.refs_2_
  50.4 0.0 collective-permute-done.3.refs_3_
  50.5 0.0 all-to-all-done.part_ref.refs_0_
  50.5 6.9 %all-to-all-start.1 = ((f32[4,1024,256]{2,1,0:T(8,128)}), f32[4,1024,256]{2,1,0:T(8,128)}, u32[]{:S(2)}, u32[]{:S(2)}) async-start(f32[4,1024,256]{2,1,0:T(8,128)} %bitcast.16), calls=%async_computation.1 | async-start | bytes 8388608 | tf_op jit(solution)/shard_map/all_to_all | solution.py:716
  57.4 1.3 sift.1
  58.7 0.1 collective-permute-start.4
  58.8 1.2 collective-permute-done.4.refs_5_
  60.0 0.2 collective-permute-start.5
  60.2 4.1 %collective-permute-done.5.refs_6_ = f32[128,128]{1,0:T(8,128)S(1)} collective-permute-done((f32[128,128]{1,0:T(8,128)S(1)}, f32[128,128]{1,0:T(8,128)S(1)}, u32[]{:S(2)}, u32[]{:S(2)}) %collective-permute-start.5) | collective-permute-done | bytes 65568 | tf_op jit(solution)/shard_map/ppermute | solution.py:756
  64.3 0.7 pad_maximum_fusion.4
  64.9 0.5 collective-permute-start.6
  65.4 5.4 %copy.16 = f32[189,35,35]{1,2,0:T(8,128)} copy(f32[189,35,35]{0,2,1:T(8,128)} %param.17) | data formatting | bytes 1852200 | tf_op args[6]
  70.8 4.8 %split.1.ops_ref = f32[189,40,128]{2,1,0:T(8,128)S(1)} custom-call(f32[189,35,35]{2,1,0:T(8,128)} %bitcast.23), custom_call_target="tpu_custom_call" | custom-call | flops 1000000 | bytes 12000000 | tf_op jit(solution)/shard_map/split/pallas_call | solution.py:234
  75.6 0.0 copy-start.25
  75.6 0.0 collective-permute-done.6.refs_7_
  75.7 1.3 whole_table.1
  77.0 2.2 copy-done.1
  79.2 40.1 %m2l_slots.1 = f32[8,40,512]{2,1,0:T(8,128)S(1)} custom-call(s32[512,128]{1,0:T(8,128)S(1)} %order.1.source_ref, s32[1024]{0:T(1024)S(1)} %copy-done.25, f32[9216,1,128]{2,1,0:T(1,128)} %bitcast.14, f32[189,40,128]{2,1,0:T(8,128)S(1)} %split.1.ops_ref), custom_call_target="tpu_custom_call" | custom-call | flops 1000000 | bytes 150000000 | tf_op jit(solution)/shard_map/m2l_slots/pallas_call | solution.py:302
  119.4 0.1 collective-permute-start.8
  119.5 1.9 carve.3
  121.4 1.6 copy-done.5
  123.0 2.7 %collective-permute-start.7 = (f32[3,40,512]{2,1,0:T(8,128)S(1)}, f32[3,40,512]{2,1,0:T(8,128)S(1)}, u32[]{:S(2)}, u32[]{:S(2)}) collective-permute-start(f32[3,40,512]{2,1,0:T(8,128)S(1)} %get-tuple-element.33), channel_id=1, source_target_pairs={{0,7},{1,0},{2,1},{3,2},{4,3},{5,4},{6,5},{7,6},{8,15},{9,8},{10,9... | collective-permute-start | bytes 737288 | tf_op jit(solution)/shard_map/ppermute | solution.py:175
  125.7 0.3 collective-permute-done.8.refs_1_
  126.0 3.4 %collective-permute-done.7.refs_0_ = f32[3,40,512]{2,1,0:T(8,128)S(1)} collective-permute-done((f32[3,40,512]{2,1,0:T(8,128)S(1)}, f32[3,40,512]{2,1,0:T(8,128)S(1)}, u32[]{:S(2)}, u32[]{:S(2)}) %collective-permute-start.7) | collective-permute-done | bytes 245792 | tf_op jit(solution)/shard_map/ppermute | solution.py:175
  129.4 0.1 collective-permute-start.9
  129.5 2.2 collective-permute-start.10
  131.8 21.7 %deposit.1 = (f32[4104,128]{1,0:T(8,128)S(1)}, f32[4104,128]{1,0:T(8,128)S(1)}, f32[4104,128]{1,0:T(8,128)}, f32[4104,128]{1,0:T(8,128)}) custom-call(s32[128,128]{1,0:T(8,128)S(1)} %get-tuple-element.22.code_ref, f32[128,128]{1,0:T(8,128)S(1)} %get-tuple-element.23.value_ref, s32[16,128]{1,0:T(8,128)S(1)} %get-tuple-element.24.bound_ref), custom_call_target="tpu_custom_call" | custom-call | flops 1000000 | bytes 40000000 | tf_op jit(solution)/shard_map/deposit/pallas_call | solution.py:562
  153.5 1.4 copy-done.3
  154.8 2.6 %collective-permute-done.9.refs_2_ = f32[3,40,512]{2,1,0:T(8,128)S(1)} collective-permute-done((f32[3,40,512]{2,1,0:T(8,128)S(1)}, f32[3,40,512]{2,1,0:T(8,128)S(1)}, u32[]{:S(2)}, u32[]{:S(2)}) %collective-permute-start.9) | collective-permute-done | bytes 245792 | tf_op jit(solution)/shard_map/ppermute | solution.py:175
  157.4 0.7 copy-done.19
  158.1 0.0 collective-permute-done.10.refs_3_
  158.1 0.7 copy-done.21
  158.8 0.0 all-to-all-done.1.refs_0_
  158.8 6.0 %all-to-all-start.2 = ((f32[4,768,256]{2,1,0:T(8,128)}), f32[4,768,256]{2,1,0:T(8,128)}, u32[]{:S(2)}, u32[]{:S(2)}) async-start(f32[4,768,256]{2,1,0:T(8,128)} %bitcast.17), calls=%async_computation.2 | async-start | bytes 6291456 | tf_op jit(solution)/shard_map/all_to_all | solution.py:716
  164.9 1.2 copy-done.6
  166.1 1.2 copy-done.8
  167.3 4.6 %fourier.3.refs_7_ = f32[2,8,256,1024]{3,2,1,0:T(8,128)} custom-call(f32[4,296,256]{2,1,0:T(8,128)S(1)} %all-to-all-done.part_ref.refs_0_, f32[4104,128]{1,0:T(8,128)S(1)} %get-tuple-element.25.refs_1_, f32[4104,128]{1,0:T(8,128)} %copy-done.3, f32[4104,128]{1,0:T(8,128)} %get-tuple-element.27.refs_3_, f32[4104,128]{1,0:T(8,128)} %get-tuple-element.28.refs_4_, ...), custom_call_target="tpu_custom_call" | custom-call | flops 1000000 | bytes 10000000 | tf_op jit(solution)/shard_map/fourier/pallas_call | solution.py:677
  171.9 40.1 %m2l_cells.1.own_ref = f32[4096,128]{1,0:T(8,128)S(1)} custom-call(s32[512,128]{1,0:T(8,128)S(1)} %copy-done.14, s32[1024]{0:T(1024)S(1)} %copy-done.25, f32[9216,1,128]{2,1,0:T(1,128)} %bitcast.15, f32[189,40,128]{2,1,0:T(8,128)} %copy-done.2), custom_call_target="tpu_custom_call" | custom-call | flops 1000000 | bytes 150000000 | tf_op jit(solution)/shard_map/m2l_cells/pallas_call | solution.py:302
  212.0 11.6 %fourier.4.refs_7_ = f32[2,8,256,1024]{3,2,1,0:T(8,128)} custom-call(f32[4,1024,256]{2,1,0:T(8,128)} %all-to-all-done.1.refs_0_, f32[4104,128]{1,0:T(8,128)S(1)} %get-tuple-element.25.refs_1_, f32[4104,128]{1,0:T(8,128)} %copy-done.3, f32[4104,128]{1,0:T(8,128)} %get-tuple-element.27.refs_3_, ...), custom_call_target="tpu_custom_call", output_to_operand_aliasing={{}: (7, {})} | custom-call | flops 1000000 | bytes 40000000 | tf_op jit(solution)/shard_map/fourier/pallas_call | solution.py:677
  223.7 11.2 %add_back.1 = f32[35,4096]{1,0:T(8,128)} custom-call(s32[8,512]{1,0:T(8,128)S(1)} %bitcast.19, s32[8]{0:T(128)S(1)} %bitcast.22, f32[4096,128]{1,0:T(8,128)S(1)} %m2l_cells.1.own_ref, f32[3,40,512]{2,1,0:T(8,128)S(1)} %copy-done.18, f32[3,40,512]{2,1,0:T(8,128)S(1)} %copy-done.16, f32[3,40,512]{2,1,0:T(8,128)S(1)} %copy-done.20, f32[3,40,512]{2,1,0:T(8,128)S(1)} %copy-done.22), custom_call_target="tpu_custom_call" | custom-call | flops 1000000 | bytes 30000000 | tf_op jit(solution)/shard_map/add_back/pallas_call | solution.py:356
  234.9 0.0 all-to-all-done.2.refs_0_
  234.9 1.2 copy-done.10
  236.1 9.3 %fourier.5 = f32[2,8,256,1024]{3,2,1,0:T(8,128)} custom-call(f32[4,768,256]{2,1,0:T(8,128)} %all-to-all-done.2.refs_0_, f32[4104,128]{1,0:T(8,128)S(1)} %get-tuple-element.25.refs_1_, f32[4104,128]{1,0:T(8,128)} %copy-done.3, f32[4104,128]{1,0:T(8,128)} %get-tuple-element.27.refs_3_, ...), custom_call_target="tpu_custom_call", output_to_operand_aliasing={{}: (7, {})} | custom-call | flops 1000000 | bytes 30000000 | tf_op jit(solution)/shard_map/fourier/pallas_call | solution.py:677
  (60 shorter events, 0.3 us)
Async XLA Ops:
  0.6 1.1 copy-start.11
  1.7 0.7 copy-start.24
  2.4 7.7 %copy-start.12 = (f32[35,4096]{1,0:T(8,128)S(1)}, f32[35,4096]{1,0:T(8,128)}, u32[]{:S(2)}) copy-start(f32[35,4096]{1,0:T(8,128)} %cells_ref.1) | copy-start | bytes 1720324
  4.8 45.6 %all-to-all-start = ((f32[4,296,256]{2,1,0:T(8,128)}), f32[4,296,256]{2,1,0:T(8,128)S(1)}, u32[]{:S(2)}, u32[]{:S(2)}) async-start(f32[4,296,256]{2,1,0:T(8,128)} %first_part.1), calls=%async_computation | async-start | bytes 2424832 | tf_op jit(solution)/shard_map/all_to_all | solution.py:716
  10.1 3.4 %copy-start.23 = (s32[1,8,512]{2,1,0:T(8,128)S(1)}, s32[1,8,512]{2,1,0:T(8,128)}, u32[]{:S(2)}) copy-start(s32[1,8,512]{2,1,0:T(8,128)} %param.12) | copy-start | bytes 49156
  10.1 3.4 %copy-start.26 = (s32[1,8]{1,0:T(1,128)S(1)}, s32[1,8]{1,0:T(1,128)}, u32[]{:S(2)}) copy-start(s32[1,8]{1,0:T(1,128)} %param.13) | copy-start | bytes 100
  23.6 2.2 copy-start
  25.7 7.3 %collective-permute-start = (f32[3,40,512]{2,1,0:T(8,128)S(1)}, f32[3,40,512]{2,1,0:T(8,128)S(1)}, u32[]{:S(2)}, u32[]{:S(2)}) collective-permute-start(f32[3,40,512]{2,1,0:T(8,128)S(1)} %get-tuple-element.17), channel_id=1, source_target_pairs={{0,7},{1,0},{2,1},{3,2},{4,3},{5,4},{6,5},{7,6},{8,15},{9,8},{10,9... | collective-permute-start | bytes 737288 | tf_op jit(solution)/shard_map/ppermute | solution.py:175
  27.1 7.9 %collective-permute-start.1 = (f32[3,40,512]{2,1,0:T(8,128)S(1)}, f32[3,40,512]{2,1,0:T(8,128)S(1)}, u32[]{:S(2)}, u32[]{:S(2)}) collective-permute-start(f32[3,40,512]{2,1,0:T(8,128)S(1)} %get-tuple-element.18), channel_id=1, source_target_pairs={{0,1},{1,2},{2,3},{3,4},{4,5},{5,6},{6,7},{7,0},{8,9},{9,10},{10,1... | collective-permute-start | bytes 737288 | tf_op jit(solution)/shard_map/ppermute | solution.py:175
  35.7 14.7 %collective-permute-start.2 = (f32[3,40,512]{2,1,0:T(8,128)}, f32[3,40,512]{2,1,0:T(8,128)S(1)}, u32[]{:S(2)}, u32[]{:S(2)}) collective-permute-start(f32[3,40,512]{2,1,0:T(8,128)} %pad_maximum_fusion), channel_id=1, source_target_pairs={{0,24},{8,0},{16,8},{24,16},{1,25},{9,1},{17,9},{25,17},{2,26},{10... | collective-permute-start | bytes 737288 | tf_op jit(solution)/shard_map/ppermute | solution.py:175
  36.5 14.0 %collective-permute-start.3 = (f32[3,40,512]{2,1,0:T(8,128)}, f32[3,40,512]{2,1,0:T(8,128)S(1)}, u32[]{:S(2)}, u32[]{:S(2)}) collective-permute-start(f32[3,40,512]{2,1,0:T(8,128)} %pad_maximum_fusion.1), channel_id=1, source_target_pairs={{0,8},{8,16},{16,24},{24,0},{1,9},{9,17},{17,25},{25,1},{2,10},{10... | collective-permute-start | bytes 737288 | tf_op jit(solution)/shard_map/ppermute | solution.py:175
  38.5 4.4 %copy-start.27 = (s32[65536]{0:T(1024)S(1)}, s32[65536]{0:T(1024)}, u32[]{:S(2)}) copy-start(s32[65536]{0:T(1024)} %param.14) | copy-start | bytes 786436
  38.5 4.4 %copy-start.28 = (s32[65536]{0:T(1024)S(1)}, s32[65536]{0:T(1024)}, u32[]{:S(2)}) copy-start(s32[65536]{0:T(1024)} %param.15) | copy-start | bytes 786436
  40.7 2.1 copy-start.4
  50.4 28.8 %copy-start.13 = (s32[512,128]{1,0:T(8,128)}, s32[512,128]{1,0:T(8,128)S(1)}, u32[]{:S(2)}) copy-start(s32[512,128]{1,0:T(8,128)S(1)} %order.1.source_ref) | copy-start | bytes 786436
  50.5 108.4 %all-to-all-start.1 = ((f32[4,1024,256]{2,1,0:T(8,128)}), f32[4,1024,256]{2,1,0:T(8,128)}, u32[]{:S(2)}, u32[]{:S(2)}) async-start(f32[4,1024,256]{2,1,0:T(8,128)} %bitcast.16), calls=%async_computation.1 | async-start | bytes 8388608 | tf_op jit(solution)/shard_map/all_to_all | solution.py:716
  58.7 1.3 collective-permute-start.4
  60.0 4.3 %collective-permute-start.5 = (f32[128,128]{1,0:T(8,128)S(1)}, f32[128,128]{1,0:T(8,128)S(1)}, u32[]{:S(2)}, u32[]{:S(2)}) collective-permute-start(f32[128,128]{1,0:T(8,128)S(1)} %pad_maximum_fusion.5), channel_id=1, source_target_pairs={{0,2},{1,3},{2,0},{3,1},{4,6},{5,7},{6,4},{7,5},{8,10},{9,11},{10,... | collective-permute-start | bytes 196616 | tf_op jit(solution)/shard_map/ppermute | solution.py:756
  64.9 10.7 %collective-permute-start.6 = (f32[256,128]{1,0:T(8,128)}, f32[256,128]{1,0:T(8,128)S(1)}, u32[]{:S(2)}, u32[]{:S(2)}) collective-permute-start(f32[256,128]{1,0:T(8,128)} %pad_maximum_fusion.4), channel_id=1, source_target_pairs={{0,4},{1,5},{2,6},{3,7},{4,0},{5,1},{6,2},{7,3},{8,12},{9,13},{10,... | collective-permute-start | bytes 393224 | tf_op jit(solution)/shard_map/ppermute | solution.py:756
  65.4 10.2 %slice-start = ((s8[4718592]{0:T(1024)(128)(4,1)}), s8[524288]{0:T(1024)(128)(4,1)S(1)}, s32[]{:S(2)}) async-start(s8[4718592]{0:T(1024)(128)(4,1)} %bitcast.12), calls=%async_computation.3 | async-start | bytes 1048576
  70.8 4.9 %slice-start.1 = ((s8[4718592]{0:T(1024)(128)(4,1)}), s8[4194304]{0:T(1024)(128)(4,1)S(1)}, s32[]{:S(2)}) async-start(s8[4718592]{0:T(1024)(128)(4,1)} %bitcast.12), calls=%async_computation.4 | async-start | bytes 8388608
  75.6 3.6 %copy-start.2 = (f32[189,40,128]{2,1,0:T(8,128)}, f32[189,40,128]{2,1,0:T(8,128)S(1)}, u32[]{:S(2)}) copy-start(f32[189,40,128]{2,1,0:T(8,128)S(1)} %split.1.ops_ref) | copy-start | bytes 11612164
  75.6 3.6 %copy-start.25 = (s32[1024]{0:T(1024)S(1)}, s32[1024]{0:T(1024)}, u32[]{:S(2)}) copy-start(s32[1024]{0:T(1024)} %class_ref.3) | copy-start | bytes 12292
  77.0 2.2 copy-start.1
  119.4 6.6 %collective-permute-start.8 = (f32[3,40,512]{2,1,0:T(8,128)S(1)}, f32[3,40,512]{2,1,0:T(8,128)S(1)}, u32[]{:S(2)}, u32[]{:S(2)}) collective-permute-start(f32[3,40,512]{2,1,0:T(8,128)S(1)} %get-tuple-element.32), channel_id=1, source_target_pairs={{0,1},{1,2},{2,3},{3,4},{4,5},{5,6},{6,7},{7,0},{8,9},{9,10},{10,1... | collective-permute-start | bytes 737288 | tf_op jit(solution)/shard_map/ppermute | solution.py:175
  121.4 1.6 copy-start.5
  123.0 6.4 %collective-permute-start.7 = (f32[3,40,512]{2,1,0:T(8,128)S(1)}, f32[3,40,512]{2,1,0:T(8,128)S(1)}, u32[]{:S(2)}, u32[]{:S(2)}) collective-permute-start(f32[3,40,512]{2,1,0:T(8,128)S(1)} %get-tuple-element.33), channel_id=1, source_target_pairs={{0,7},{1,0},{2,1},{3,2},{4,3},{5,4},{6,5},{7,6},{8,15},{9,8},{10,9... | collective-permute-start | bytes 737288 | tf_op jit(solution)/shard_map/ppermute | solution.py:175
  126.0 27.5 %copy-start.15 = (f32[3,40,512]{2,1,0:T(8,128)}, f32[3,40,512]{2,1,0:T(8,128)S(1)}, u32[]{:S(2)}) copy-start(f32[3,40,512]{2,1,0:T(8,128)S(1)} %collective-permute-done.8.refs_1_) | copy-start | bytes 737284
  129.4 28.1 %copy-start.17 = (f32[3,40,512]{2,1,0:T(8,128)}, f32[3,40,512]{2,1,0:T(8,128)S(1)}, u32[]{:S(2)}) copy-start(f32[3,40,512]{2,1,0:T(8,128)S(1)} %collective-permute-done.7.refs_0_) | copy-start | bytes 737284
  129.4 28.0 %collective-permute-start.9 = (f32[3,40,512]{2,1,0:T(8,128)S(1)}, f32[3,40,512]{2,1,0:T(8,128)S(1)}, u32[]{:S(2)}, u32[]{:S(2)}) collective-permute-start(f32[3,40,512]{2,1,0:T(8,128)S(1)} %pad_maximum_fusion.2), channel_id=1, source_target_pairs={{0,24},{8,0},{16,8},{24,16},{1,25},{9,1},{17,9},{25,17},{2,26},{10... | collective-permute-start | bytes 737288 | tf_op jit(solution)/shard_map/ppermute | solution.py:175
  129.5 28.6 %collective-permute-start.10 = (f32[3,40,512]{2,1,0:T(8,128)S(1)}, f32[3,40,512]{2,1,0:T(8,128)S(1)}, u32[]{:S(2)}, u32[]{:S(2)}) collective-permute-start(f32[3,40,512]{2,1,0:T(8,128)S(1)} %pad_maximum_fusion.3), channel_id=1, source_target_pairs={{0,8},{8,16},{16,24},{24,0},{1,9},{9,17},{17,25},{25,1},{2,10},{10... | collective-permute-start | bytes 737288 | tf_op jit(solution)/shard_map/ppermute | solution.py:175
  153.5 1.4 copy-start.3
  157.4 0.7 copy-start.19
  158.1 0.7 copy-start.21
  158.8 76.1 %all-to-all-start.2 = ((f32[4,768,256]{2,1,0:T(8,128)}), f32[4,768,256]{2,1,0:T(8,128)}, u32[]{:S(2)}, u32[]{:S(2)}) async-start(f32[4,768,256]{2,1,0:T(8,128)} %bitcast.17), calls=%async_computation.2 | async-start | bytes 6291456 | tf_op jit(solution)/shard_map/all_to_all | solution.py:716
  164.9 1.2 copy-start.6
  166.1 1.2 copy-start.8
  167.3 4.6 %copy-start.14 = (s32[512,128]{1,0:T(8,128)S(1)}, s32[512,128]{1,0:T(8,128)}, u32[]{:S(2)}) copy-start(s32[512,128]{1,0:T(8,128)} %copy-done.13) | copy-start | bytes 786436
  171.9 40.1 %copy-start.7 = (bf16[2,512,512]{2,1,0:T(8,128)(2,1)S(1)}, bf16[2,512,512]{2,1,0:T(8,128)(2,1)}, u32[]{:S(2)}) copy-start(bf16[2,512,512]{2,1,0:T(8,128)(2,1)} %constant.40.clone.refs_6_) | copy-start | bytes 3145732
  171.9 40.1 %copy-start.9 = (bf16[2,512,512]{2,1,0:T(8,128)(2,1)S(1)}, bf16[2,512,512]{2,1,0:T(8,128)(2,1)}, u32[]{:S(2)}) copy-start(bf16[2,512,512]{2,1,0:T(8,128)(2,1)} %constant.39.clone.refs_5_) | copy-start | bytes 3145732
  212.0 11.7 %copy-start.16 = (f32[3,40,512]{2,1,0:T(8,128)S(1)}, f32[3,40,512]{2,1,0:T(8,128)}, u32[]{:S(2)}) copy-start(f32[3,40,512]{2,1,0:T(8,128)} %copy-done.15) | copy-start | bytes 737284
  212.0 11.7 %copy-start.18 = (f32[3,40,512]{2,1,0:T(8,128)S(1)}, f32[3,40,512]{2,1,0:T(8,128)}, u32[]{:S(2)}) copy-start(f32[3,40,512]{2,1,0:T(8,128)} %copy-done.17) | copy-start | bytes 737284
  212.0 11.7 %copy-start.20 = (f32[3,40,512]{2,1,0:T(8,128)S(1)}, f32[3,40,512]{2,1,0:T(8,128)}, u32[]{:S(2)}) copy-start(f32[3,40,512]{2,1,0:T(8,128)} %copy-done.19) | copy-start | bytes 737284
  212.0 11.7 %copy-start.22 = (f32[3,40,512]{2,1,0:T(8,128)S(1)}, f32[3,40,512]{2,1,0:T(8,128)}, u32[]{:S(2)}) copy-start(f32[3,40,512]{2,1,0:T(8,128)} %copy-done.21) | copy-start | bytes 737284
  234.9 1.2 copy-start.10
